TPU v7x, 32 devices: a whole 2x2x4 slice. The times are simulated.
32 devices in a mesh: wide: 8 (over z, y), narrow: 4 (over x, core).
Axes of the slice: x: 2, y: 2, z: 4, core: 2. Of those that a mesh axis runs over, the one named last changes fastest.
Arguments:
- activations: bfloat16 [512, 8192], P(('wide', 'narrow')), may hold values from -6 to 6
- cotangent: bfloat16 [512, 8192], P('wide', 'narrow'), may hold values from -6 to 6
- gate_proj: bfloat16 [8192, 26624], P('narrow', 'wide'), may hold values from -0.0625 to 0.0625
- up_proj: bfloat16 [8192, 26624], P('narrow', 'wide'), may hold values from -0.0625 to 0.0625
- down_proj: bfloat16 [26624, 8192], P('wide', 'narrow'), may hold values from -0.0390625 to 0.0390625
Outputs:
- block_output: bfloat16 [512, 8192], P('wide', 'narrow')
- input_gradient: bfloat16 [512, 8192], P(('wide', 'narrow'))
- gate_gradient: bfloat16 [8192, 26624], P('narrow', 'wide')
- up_gradient: bfloat16 [8192, 26624], P('narrow', 'wide')
- down_gradient: bfloat16 [26624, 8192], P('wide', 'narrow')
All inputs are finite; a program needn't handle non-finite values.
Results may differ from a plain program's by a relative error of at most 0.005.
Values may be sent and summed in bfloat16 or wider, within the bound.
No kernel may reach another device: no remote copies, remote signals or barrier semaphores. Data moves between devices by JAX's collectives and lax.ppermute only.
A program may use at most 192 MiB of HBM per device.

v0:
```python
import jax
import jax.numpy as jnp
from jax import lax
from jax.sharding import PartitionSpec as P


def silu_parts(gate):
    sigma = jax.nn.sigmoid(gate)
    return (gate * sigma, sigma * (1.0 + gate * (1.0 - sigma)))


def contract_rows(left, right):
    return lax.dot_general(
        left, right, (((0,), (0,)), ((), ())), preferred_element_type=jnp.float32
    )


def contract_cols(left, right):
    return lax.dot_general(
        left, right, (((1,), (1,)), ((), ())), preferred_element_type=jnp.float32
    )


def local(activations, cotangent, gate_proj, up_proj, down_proj):
    whole_rows = lax.all_gather(activations, ("wide", "narrow"), axis=0, tiled=True)
    tile_width = whole_rows.shape[1] // lax.axis_size("narrow")
    features = lax.dynamic_slice_in_dim(
        whole_rows, lax.axis_index("narrow") * tile_width, tile_width, 1
    )
    gate_part = jnp.dot(features, gate_proj, preferred_element_type=jnp.float32)
    up_part = jnp.dot(features, up_proj, preferred_element_type=jnp.float32)
    gate, up = lax.psum((gate_part, up_part), "narrow")
    active, slope = silu_parts(gate)
    hidden = (active * up).astype(jnp.bfloat16)
    block_output = lax.psum_scatter(
        jnp.dot(hidden, down_proj, preferred_element_type=jnp.float32),
        "wide",
        scatter_dimension=0,
        tiled=True,
    ).astype(jnp.bfloat16)
    upstream = lax.all_gather(cotangent, "wide", axis=0, tiled=True)
    down_gradient = contract_rows(hidden, upstream).astype(jnp.bfloat16)
    back_part = contract_cols(upstream, down_proj)
    back = lax.psum(back_part, "narrow")
    gate_delta = (back * up * slope).astype(jnp.bfloat16)
    up_delta = (back * active).astype(jnp.bfloat16)
    gate_gradient = contract_rows(features, gate_delta).astype(jnp.bfloat16)
    up_gradient = contract_rows(features, up_delta).astype(jnp.bfloat16)
    grad_tile = lax.psum_scatter(
        contract_cols(gate_delta, gate_proj) + contract_cols(up_delta, up_proj),
        "wide",
        scatter_dimension=0,
        tiled=True,
    ).astype(jnp.bfloat16)
    input_gradient = lax.all_to_all(grad_tile, "narrow", split_axis=0, concat_axis=1, tiled=True)
    return (block_output, input_gradient, gate_gradient, up_gradient, down_gradient)


def solution(mesh):
    placed = (
        P(("wide", "narrow"), None),
        P("wide", "narrow"),
        P("narrow", "wide"),
        P("narrow", "wide"),
        P("wide", "narrow"),
    )
    return jax.shard_map(
        local,
        mesh=mesh,
        in_specs=placed,
        out_specs=(
            P("wide", "narrow"),
            P(("wide", "narrow"), None),
            P("narrow", "wide"),
            P("narrow", "wide"),
            P("wide", "narrow"),
        ),
        check_vma=False,
    )
```

profile of v0, /device:TPU:0, one launch (start us, length us, event | category | flops | bytes accessed | tf_op | source)
XLA Modules:
  0.0 734.9 jit_solution(10258739851633141904)
XLA Ops:
  7.2 0.0 all-gather.5.cloned.1.call-start
  7.2 0.7 all-gather.5.cloned.1.call-update
  7.9 0.0 all-gather.3.cloned.1.call-start
  7.9 0.7 all-gather.3.cloned.1.call-update
  8.6 0.0 all-reduce.3.cloned.1.call-start
  8.7 53.4 %all-gather.5.cloned.1.call-done = bf16[512,2048]{1,0:T(8,128)(2,1)} async-done(((bf16[64,2048]{1,0:T(8,128)(2,1)}), bf16[512,2048]{1,0:T(8,128)(2,1)}) %all-gather.5.cloned.1.call-update) | async-done | bytes 2097168 | tf_op jit(solution)/shard_map/all_gather | solution.py:41
  62.1 13.3 %fusion.12 = f32[512,3328]{1,0:T(8,128)} fusion(bf16[512,2048]{1,0:T(8,128)(2,1)} %all-gather.5.cloned.1.call-done, bf16[3328,2048]{1,0:T(8,128)(2,1)} %param.9), kind=kOutput, calls=%fused_computation.20 | convolution fusion | flops 6979321856 | bytes 22544384 | tf_op jit(solution)/shard_map/dot_general | solution.py:19
  75.4 65.5 %all-gather.3.cloned.1.call-done = bf16[512,8192]{1,0:T(8,128)(2,1)} async-done(((bf16[16,8192]{1,0:T(8,128)(2,1)}), bf16[512,8192]{1,0:T(8,128)(2,1)}) %all-gather.3.cloned.1.call-update) | async-done | bytes 8388624 | tf_op jit(solution)/shard_map/all_gather | solution.py:25
  141.0 0.0 copy-start.2
  141.0 13.3 %fusion.3 = f32[512,3328]{1,0:T(8,128)} fusion(bf16[2048,3328]{1,0:T(8,128)(2,1)} %param.8, bf16[512,8192]{1,0:T(8,128)(2,1)} %all-gather.3.cloned.1.call-done, s32[]{:T(128)S(6)} %select_n.3), kind=kOutput, calls=%fused_computation.11 | convolution fusion | flops 6979321856 | bytes 22544388 | tf_op jit(solution)/shard_map/dot_general | solution.py:31
  154.3 0.0 copy-done.2
  154.3 10.5 %fusion.5 = f32[512,3328]{1,0:T(8,128)} fusion(bf16[2048,3328]{1,0:T(8,128)(2,1)S(1)} %copy-done.2, bf16[512,8192]{1,0:T(8,128)(2,1)} %all-gather.3.cloned.1.call-done, s32[]{:T(128)S(6)} %select_n.3), kind=kOutput, calls=%fused_computation.13 | convolution fusion | flops 6979321856 | bytes 22544388 | tf_op jit(solution)/shard_map/dot_general | solution.py:30
  164.9 0.0 all-reduce.3.cloned.1.call-update
  164.9 0.2 reduce-scatter.5.cloned.1.call-start
  165.1 346.7 %all-reduce.3.cloned.1.call-done = (f32[512,3328]{1,0:T(8,128)}, f32[512,3328]{1,0:T(8,128)}, f32[512,3328]{1,0:T(8,128)}) async-done(((f32[512,3328]{1,0:T(8,128)}, f32[512,3328]{1,0:T(8,128)}, f32[512,3328]{1,0:T(8,128)}), (f32[512,3328]{1,0:T(8,128)}, f32[512,3328]{1,0:T(8,128)}, f32[512,3328]{1,0:T(8,128)})) %all-reduce.3.cloned.1.call-update) | async-done | bytes 20447248 | tf_op jit(solution)/shard_map/psum | solution.py:32
  511.9 10.1 %multiply_convert_fusion = (bf16[512,3328]{1,0:T(8,128)(2,1)S(1)}, bf16[512,3328]{1,0:T(8,128)(2,1)S(1)}, bf16[512,3328]{1,0:T(8,128)(2,1)}) fusion(f32[512,3328]{1,0:T(8,128)} %get-tuple-element.7, f32[512,3328]{1,0:T(8,128)} %get-tuple-element.6, f32[512,3328]{1,0:T(8,128)} %get-tuple-element.5), kind=kLoop, calls=%fused_computation.3 | loop fusion | flops 25559040 | bytes 30670848 | tf_op jit(solution)/shard_map/convert_element_type | solution.py:46
  521.9 0.0 copy-start.1
  521.9 11.6 %fusion.13 = f32[512,2048]{1,0:T(8,128)S(1)} fusion(bf16[512,3328]{1,0:T(8,128)(2,1)S(1)} %get-tuple-element.9, bf16[2048,3328]{1,0:T(8,128)(2,1)} %param.7), kind=kOutput, calls=%fused_computation.21 | convolution fusion | flops 6979321856 | bytes 21233664 | tf_op jit(solution)/shard_map/dot_general | solution.py:19
  533.5 0.0 copy-done.1
  533.5 11.7 %convolution_add_fusion = f32[512,2048]{1,0:T(8,128)} fusion(f32[512,2048]{1,0:T(8,128)S(1)} %fusion.13, bf16[512,3328]{1,0:T(8,128)(2,1)S(1)} %get-tuple-element.8, bf16[2048,3328]{1,0:T(8,128)(2,1)} %param.8), kind=kOutput, calls=%fused_computation.8 | convolution fusion | flops 6980370432 | bytes 25427968 | tf_op jit(solution)/shard_map/dot_general | solution.py:19
  545.3 0.0 reduce-scatter.5.cloned.1.call-update
  545.3 0.3 reduce-scatter.3.cloned.1.call-start
  545.6 12.6 %fusion.11 = f32[512,2048]{1,0:T(8,128)} fusion(bf16[512,3328]{1,0:T(8,128)(2,1)} %get-tuple-element.10, bf16[3328,2048]{1,0:T(8,128)(2,1)} %param.9), kind=kOutput, calls=%fused_computation.19 | convolution fusion | flops 6979321856 | bytes 21233664 | tf_op jit(solution)/shard_map/dot_general | solution.py:36
  558.2 0.0 reduce-scatter.3.cloned.1.call-update
  558.2 0.0 copy-start
  558.2 0.0 copy-start.3
  558.2 12.9 %convolution_convert_fusion.2 = bf16[2048,3328]{1,0:T(8,128)(2,1)} fusion(bf16[512,3328]{1,0:T(8,128)(2,1)} %copy-done.1, bf16[512,8192]{1,0:T(8,128)(2,1)} %all-gather.3.cloned.1.call-done, s32[]{:T(128)S(6)} %select_n.3), kind=kOutput, calls=%fused_computation.2 | convolution fusion | flops 6986137600 | bytes 19136516 | tf_op jit(solution)/shard_map/dot_general | solution.py:13
  571.1 0.0 copy-done
  571.1 0.0 copy-done.3
  571.1 10.5 %convolution_convert_fusion = bf16[3328,2048]{1,0:T(8,128)(2,1)} fusion(bf16[512,3328]{1,0:T(8,128)(2,1)S(1)} %copy-done, bf16[512,2048]{1,0:T(8,128)(2,1)S(1)} %copy-done.3), kind=kOutput, calls=%fused_computation | convolution fusion | flops 6986137600 | bytes 19136512 | tf_op jit(solution)/shard_map/dot_general | solution.py:13
  581.6 52.1 %reduce-scatter.5.cloned.1.call-done = f32[64,2048]{1,0:T(8,128)} async-done(((f32[512,2048]{1,0:T(8,128)}), f32[64,2048]{1,0:T(8,128)}) %reduce-scatter.5.cloned.1.call-update) | async-done | bytes 524304 | tf_op jit(solution)/shard_map/reduce_scatter | solution.py:49
  633.7 1.8 convert_element_type.28
  635.5 4.3 all-to-all-start
  639.8 12.6 %convolution_convert_fusion.1 = bf16[2048,3328]{1,0:T(8,128)(2,1)} fusion(bf16[512,3328]{1,0:T(8,128)(2,1)S(1)} %get-tuple-element.8, bf16[512,8192]{1,0:T(8,128)(2,1)} %all-gather.3.cloned.1.call-done, s32[]{:T(128)S(6)} %select_n.3), kind=kOutput, calls=%fused_computation.1 | convolution fusion | flops 6986137600 | bytes 19136516 | tf_op jit(solution)/shard_map/dot_general | solution.py:13
  652.4 72.5 %reduce-scatter.3.cloned.1.call-done = f32[64,2048]{1,0:T(8,128)} async-done(((f32[512,2048]{1,0:T(8,128)}), f32[64,2048]{1,0:T(8,128)}) %reduce-scatter.3.cloned.1.call-update) | async-done | bytes 524304 | tf_op jit(solution)/shard_map/reduce_scatter | solution.py:35
  724.9 1.8 convert_element_type.25
  726.7 0.0 all-to-all-done
  726.7 1.7 copy.11
Async XLA Ops:
  7.2 55.0 %all-gather.5.cloned.1.call-start = ((), (), s32[]{:S(2)}) async-start(), calls=%async_computation.5 | async-start | bytes 2359296 | tf_op jit(solution)/shard_map/all_gather | solution.py:41
  7.9 133.1 %all-gather.3.cloned.1.call-start = ((), (), s32[]{:S(2)}) async-start(), calls=%async_computation.3 | async-start | bytes 8650752 | tf_op jit(solution)/shard_map/all_gather | solution.py:25
  8.6 503.2 %all-reduce.3.cloned.1.call-start = ((), (), s32[]{:S(2)}) async-start(), calls=%async_computation.7 | async-start | bytes 40894464 | tf_op jit(solution)/shard_map/psum | solution.py:32
  141.0 13.4 %copy-start.2 = (bf16[2048,3328]{1,0:T(8,128)(2,1)S(1)}, bf16[2048,3328]{1,0:T(8,128)(2,1)}, u32[]{:S(2)}) copy-start(bf16[2048,3328]{1,0:T(8,128)(2,1)} %param.7) | copy-start | bytes 40894468
  164.9 468.8 %reduce-scatter.5.cloned.1.call-start = ((), (), s32[]{:S(2)}) async-start(), calls=%async_computation.6 | async-start | bytes 4718592 | tf_op jit(solution)/shard_map/reduce_scatter | solution.py:49
  521.9 11.6 %copy-start.1 = (bf16[512,3328]{1,0:T(8,128)(2,1)}, bf16[512,3328]{1,0:T(8,128)(2,1)S(1)}, u32[]{:S(2)}) copy-start(bf16[512,3328]{1,0:T(8,128)(2,1)S(1)} %get-tuple-element.9) | copy-start | bytes 10223620
  545.3 179.6 %reduce-scatter.3.cloned.1.call-start = ((), (), s32[]{:S(2)}) async-start(), calls=%async_computation.4 | async-start | bytes 4718592 | tf_op jit(solution)/shard_map/reduce_scatter | solution.py:35
  558.2 12.9 %copy-start = (bf16[512,3328]{1,0:T(8,128)(2,1)S(1)}, bf16[512,3328]{1,0:T(8,128)(2,1)}, u32[]{:S(2)}) copy-start(bf16[512,3328]{1,0:T(8,128)(2,1)} %get-tuple-element.10) | copy-start | bytes 10223620
  558.2 12.9 %copy-start.3 = (bf16[512,2048]{1,0:T(8,128)(2,1)S(1)}, bf16[512,2048]{1,0:T(8,128)(2,1)}, u32[]{:S(2)}) copy-start(bf16[512,2048]{1,0:T(8,128)(2,1)} %all-gather.5.cloned.1.call-done) | copy-start | bytes 6291460
  635.5 91.2 %all-to-all-start = ((bf16[4,16,2048]{2,1,0:T(8,128)(2,1)}), bf16[4,16,2048]{2,1,0:T(8,128)(2,1)}, u32[]{:S(2)}, u32[]{:S(2)}) async-start(bf16[4,16,2048]{2,1,0:T(8,128)(2,1)} %bitcast.18), calls=%async_computation.2 | async-start | bytes 524288 | tf_op jit(solution)/shard_map/all_to_all | solution.py:55
Sparse Core Ops, SparseCore 0:
  10.1 51.9 all-gather.4
  65.0 75.9 all-gather.2
  165.0 346.8 all-reduce.2
  545.4 88.2 reduce-scatter.4
  637.2 87.6 reduce-scatter.2
where the time goes:
time: 735 us
  waiting for transfers between devices  592 us (81%)
  matrix products  109 us (15%)
  between operations  13.8 us (2%)
  other arithmetic  13.6 us (2%)
    psum x1, waiting for transfers between devices, local(): gate, up = lax.psum((gate_part, up_part), 'narrow')  347 us
    reduce_scatter x1, waiting for transfers between devices, local(): lax.psum_scatter(jnp.dot(hidden, down_proj, preferred_element_type=jnp.fl...  72.5 us
    all_gather x1, waiting for transfers between devices, local(): lax.all_gather(activations, ('wide', 'narrow'), axis=0, tiled=True)  65.5 us
    all_gather x1, waiting for transfers between devices, local(): upstream = lax.all_gather(cotangent, 'wide', axis=0, tiled=True)  53.4 us
    reduce_scatter x1, waiting for transfers between devices, local(): lax.psum_scatter(contract_cols(gate_delta, gate_proj) + contract_cols(up_...  52.1 us
    dot_general x3, matrix products, contract_cols(): lax.dot_general(left, right, (((1,), (1,)), ((), ())), preferred_element_...  36.6 us
    dot_general x3, matrix products, contract_rows(): lax.dot_general(left, right, (((0,), (0,)), ((), ())), preferred_element_...  35.9 us
  transfers between devices with their start and end apart: 6, of which 5 were waited for; matrix products, arithmetic and copies ran while one was open for 9% of the time, Pallas kernels for 0%

commit v1 on v0

v1 whole, which is shorter than its diff:
```python
import jax
import jax.numpy as jnp
from jax import lax
from jax.sharding import PartitionSpec as P

CHUNKS = 2


def silu_parts(gate):
    sigma = jax.nn.sigmoid(gate)
    return (gate * sigma, sigma * (1.0 + gate * (1.0 - sigma)))


def contract_rows(left, right):
    return lax.dot_general(
        left, right, (((0,), (0,)), ((), ())), preferred_element_type=jnp.float32
    )


def contract_cols(left, right):
    return lax.dot_general(
        left, right, (((1,), (1,)), ((), ())), preferred_element_type=jnp.float32
    )


def swap(value, mask):
    return lax.ppermute(value, "narrow", [(i, i ^ mask) for i in range(4)])


def scatter_sum(part, wide):
    split = part.reshape(wide, 4, -1, part.shape[-1])
    got = swap(jnp.stack([split[:, 1], split[:, 3]]), 1)
    away = (split[:, 2] + got[1]).astype(jnp.bfloat16)
    return (split[:, 0] + got[0]) + swap(away, 2).astype(jnp.float32)


def spread(own):
    far = swap(own, 2)
    pair = swap(jnp.stack([own, far]), 1)
    whole = jnp.stack([own, pair[0], far, pair[1]], axis=1)
    return whole.reshape(-1, own.shape[-1])


def local(activations, cotangent, gate_proj, up_proj, down_proj):
    wide = lax.axis_size("wide")
    me = lax.axis_index("narrow")
    rows = activations.shape[0]
    tile = activations.shape[1] // 4
    half = rows // CHUNKS

    pieces = [lax.dynamic_slice_in_dim(activations, (me ^ g) * tile, tile, 1) for g in range(4)]
    pieces = [pieces[0]] + [swap(pieces[g], g) for g in range(1, 4)]
    cots = [lax.dynamic_slice_in_dim(cotangent, (me ^ g) * rows, rows, 0) for g in range(4)]

    def gathered(parts, c):
        mine = jnp.stack([p[c * half : (c + 1) * half] for p in parts])
        return lax.all_gather(mine, "wide", axis=0, tiled=True).reshape(-1, tile)

    features, upstream = [], []
    for c in range(CHUNKS):
        features.append(gathered(pieces, c))
        upstream.append(gathered(cots, c))

    hidden, gate_delta, up_delta, outs, tiles = [], [], [], [], []
    for c in range(CHUNKS):
        gate = scatter_sum(jnp.dot(features[c], gate_proj, preferred_element_type=jnp.float32), wide)
        up = scatter_sum(jnp.dot(features[c], up_proj, preferred_element_type=jnp.float32), wide)
        back = scatter_sum(contract_cols(upstream[c], down_proj), wide)
        active, slope = silu_parts(gate)
        gate_delta.append(spread((back * up * slope).astype(jnp.bfloat16)))
        up_delta.append(spread((back * active).astype(jnp.bfloat16)))
        hidden.append(spread((active * up).astype(jnp.bfloat16)))

    def landed(total):
        got = lax.psum_scatter(total, "wide", scatter_dimension=0, tiled=True)
        return got.astype(jnp.bfloat16).reshape(4, half, tile)

    for c in range(CHUNKS):
        tiles.append(
            landed(contract_cols(gate_delta[c], gate_proj) + contract_cols(up_delta[c], up_proj))
        )
        outs.append(landed(jnp.dot(hidden[c], down_proj, preferred_element_type=jnp.float32)))

    features, upstream = jnp.concatenate(features), jnp.concatenate(upstream)
    gate_gradient = contract_rows(features, jnp.concatenate(gate_delta)).astype(jnp.bfloat16)
    up_gradient = contract_rows(features, jnp.concatenate(up_delta)).astype(jnp.bfloat16)
    down_gradient = contract_rows(jnp.concatenate(hidden), upstream).astype(jnp.bfloat16)

    out = jnp.concatenate(outs, axis=1)
    block_output = jnp.concatenate(
        [lax.dynamic_index_in_dim(out, me ^ g, 0, keepdims=False) for g in range(4)]
    )
    grad = jnp.concatenate(tiles, axis=1)
    grads = jnp.stack([grad[0]] + [swap(grad[g], g) for g in range(1, 4)])
    input_gradient = jnp.concatenate(
        [lax.dynamic_index_in_dim(grads, me ^ g, 0, keepdims=False) for g in range(4)], axis=1
    )
    return (block_output, input_gradient, gate_gradient, up_gradient, down_gradient)


def solution(mesh):
    placed = (
        P(("wide", "narrow"), None),
        P("wide", "narrow"),
        P("narrow", "wide"),
        P("narrow", "wide"),
        P("wide", "narrow"),
    )
    return jax.shard_map(
        local,
        mesh=mesh,
        in_specs=placed,
        out_specs=(
            P("wide", "narrow"),
            P(("wide", "narrow"), None),
            P("narrow", "wide"),
            P("narrow", "wide"),
            P("wide", "narrow"),
        ),
        check_vma=False,
    )
```

time: 735 us -> 620 us (0.84); the launches traced: 735 us -> 611 us
  waiting for transfers between devices: 592 us -> 391 us
  matrix products: 109 us -> 137 us
  starting transfers between devices: 4.9 us -> 22 us
  other arithmetic: 13.6 us -> 29.6 us
  local copies, waits for them, and re-layouts: 1.69 us -> 15.6 us
    psum x1 -> x0, waiting for transfers between devices: 347 us -> none  [local(): gate, up = lax.psum((gate_part, up_part), 'narrow')]
    ppermute x0 -> x30, waiting for transfers between devices: none -> 85.1 us  [swap(): return lax.ppermute(value, 'narrow', [(i, i ^ mask) for i in range(4)])]
    reduce_scatter x2 -> x4, waiting for transfers between devices: 125 us -> 186 us  [landed(): got = lax.psum_scatter(total, 'wide', scatter_dimension=0, tiled=True)]
    ppermute x0 -> x30, starting transfers between devices: none -> 21.6 us  [swap(): return lax.ppermute(value, 'narrow', [(i, i ^ mask) for i in range(4)])]
    dot_general x3 -> x6, matrix products: 36.5 us -> 53.5 us  [the longest x2 20.1 us: local(): jnp.dot(features[c], up_proj, preferred_element_type=jnp.float32)]
    dot_general x3 -> x6, matrix products: 36.6 us -> 50.1 us  [contract_cols(): lax.dot_general(left, right, (((1,), (1,)), ((), ())), preferred_element_...]
    another operation x0 -> x23, other arithmetic: none -> 12.9 us  [the longest x6 4.34 us: spread(): pair = swap(jnp.stack([own, far]), 1)]
    unnamed x8 -> x44, local copies, waits for them, and re-layouts: 0.02 us -> 8.24 us
  transfers between devices with their start and end apart: 6 -> 38, of which waited for: 5 -> 18; matrix products, arithmetic and copies ran while one was open for 9% -> 28% of each run, Pallas kernels for 0% -> 0%
where the time goes in v1:
time: 620 us; the launch traced here: 611 us
  waiting for transfers between devices  391 us (63%)
  matrix products  137 us (22%)
  other arithmetic  29.6 us (5%)
  starting transfers between devices  22 us (4%)
  local copies, waits for them, and re-layouts  15.6 us (3%)
  between operations  15.4 us (2%)
    reduce_scatter x4, waiting for transfers between devices, landed(): got = lax.psum_scatter(total, 'wide', scatter_dimension=0, tiled=True)  186 us
    all_gather x4, waiting for transfers between devices, gathered(): return lax.all_gather(mine, 'wide', axis=0, tiled=True).reshape(-1, tile)  120 us
    ppermute x30, waiting for transfers between devices, swap(): return lax.ppermute(value, 'narrow', [(i, i ^ mask) for i in range(4)])  85.1 us
    dot_general x6, matrix products, contract_cols(): lax.dot_general(left, right, (((1,), (1,)), ((), ())), preferred_element_...  50.1 us
    dot_general x3, matrix products, contract_rows(): lax.dot_general(left, right, (((0,), (0,)), ((), ())), preferred_element_...  33.6 us
    ppermute x30, starting transfers between devices, swap(): return lax.ppermute(value, 'narrow', [(i, i ^ mask) for i in range(4)])  21.6 us
    dot_general x2, matrix products, local(): jnp.dot(features[c], up_proj, preferred_element_type=jnp.float32)  20.1 us
    dot_general x2, matrix products, local(): jnp.dot(hidden[c], down_proj, preferred_element_type=jnp.float32)  17.6 us
  transfers between devices with their start and end apart: 38, of which 18 were waited for; matrix products, arithmetic and copies ran while one was open for 28% of the time, Pallas kernels for 0%

profile of v1, /device:TPU:0, one launch (start us, length us, event | category | flops | bytes accessed | tf_op | source)
XLA Modules:
  0.0 610.9 jit_solution(16331561379731377631)
XLA Ops:
  11.1 2.6 collective-permute-start.2
  14.6 1.6 collective-permute-done.2
  16.2 1.8 collective-permute-done.1
  19.5 34.0 %all-gather.9.cloned.1.call-done = bf16[32,8,2048]{2,1,0:T(8,128)(2,1)} async-done(((bf16[4,8,2048]{2,1,0:T(8,128)(2,1)}), bf16[32,8,2048]{2,1,0:T(8,128)(2,1)}) %all-gather.9.cloned.1.call-update) | async-done | bytes 1048592 | tf_op jit(solution)/shard_map/all_gather | solution.py:57
  53.6 7.4 %fusion.4 = f32[8,4,8,3328]{3,2,0,1:T(8,128)S(1)} fusion(bf16[3328,2048]{1,0:T(8,128)(2,1)} %param.9, bf16[8,4,8,2048]{3,2,1,0:T(8,128)(2,1)} %bitcast.378), kind=kOutput, calls=%fused_computation.7 | convolution fusion | flops 3489660928 | bytes 18087936 | tf_op jit(solution)/shard_map/dot_general | solution.py:21
  61.1 1.5 pad_maximum_fusion.7
  63.3 31.9 %all-gather.11.cloned.1.call-done = bf16[32,8,2048]{2,1,0:T(8,128)(2,1)} async-done(((bf16[4,8,2048]{2,1,0:T(8,128)(2,1)}), bf16[32,8,2048]{2,1,0:T(8,128)(2,1)}) %all-gather.11.cloned.1.call-update) | async-done | bytes 1048592 | tf_op jit(solution)/shard_map/all_gather | solution.py:57
  95.2 7.4 %fusion.2 = f32[8,4,8,3328]{3,2,0,1:T(8,128)S(1)} fusion(bf16[3328,2048]{1,0:T(8,128)(2,1)} %param.9, bf16[8,4,8,2048]{3,2,1,0:T(8,128)(2,1)} %bitcast.380), kind=kOutput, calls=%fused_computation.5 | convolution fusion | flops 3489660928 | bytes 18087936 | tf_op jit(solution)/shard_map/dot_general | solution.py:21
  104.0 32.8 %all-gather.5.cloned.1.call-done = bf16[32,8,2048]{2,1,0:T(8,128)(2,1)} async-done(((bf16[4,8,2048]{2,1,0:T(8,128)(2,1)}), bf16[32,8,2048]{2,1,0:T(8,128)(2,1)}) %all-gather.5.cloned.1.call-update) | async-done | bytes 1048592 | tf_op jit(solution)/shard_map/all_gather | solution.py:57
  136.9 10.7 %fusion.8 = f32[8,4,8,3328]{3,2,0,1:T(8,128)} fusion(bf16[2048,3328]{1,0:T(8,128)(2,1)} %param.8, bf16[8,4,8,2048]{3,2,1,0:T(8,128)(2,1)} %bitcast.382), kind=kOutput, calls=%fused_computation.11 | convolution fusion | flops 3489660928 | bytes 18087936 | tf_op jit(solution)/shard_map/dot_general | solution.py:67
  147.6 8.6 %fusion = f32[8,4,8,3328]{3,2,1,0:T(8,128)} fusion(bf16[8,4,8,2048]{3,2,1,0:T(8,128)(2,1)S(1)} %bitcast.383, bf16[2048,3328]{1,0:T(8,128)(2,1)} %param.7), kind=kOutput, calls=%fused_computation.3 | convolution fusion | flops 3489660928 | bytes 18087936 | tf_op jit(solution)/shard_map/dot_general | solution.py:66
  156.2 21.6 %all-gather.7.cloned.1.call-done = bf16[32,8,2048]{2,1,0:T(8,128)(2,1)} async-done(((bf16[4,8,2048]{2,1,0:T(8,128)(2,1)}), bf16[32,8,2048]{2,1,0:T(8,128)(2,1)}) %all-gather.7.cloned.1.call-update) | async-done | bytes 1048592 | tf_op jit(solution)/shard_map/all_gather | solution.py:57
  177.8 9.4 %fusion.6 = f32[8,4,8,3328]{3,2,0,1:T(8,128)S(1)} fusion(bf16[2048,3328]{1,0:T(8,128)(2,1)} %param.8, bf16[8,4,8,2048]{3,2,1,0:T(8,128)(2,1)} %bitcast.386), kind=kOutput, calls=%fused_computation.9 | convolution fusion | flops 3489660928 | bytes 18087936 | tf_op jit(solution)/shard_map/dot_general | solution.py:67
  187.2 7.3 %fusion.10 = f32[8,4,8,3328]{3,2,0,1:T(8,128)S(1)} fusion(bf16[2048,3328]{1,0:T(8,128)(2,1)} %param.7, bf16[8,4,8,2048]{3,2,1,0:T(8,128)(2,1)S(1)} %bitcast.387), kind=kOutput, calls=%fused_computation.13 | convolution fusion | flops 3489660928 | bytes 18087936 | tf_op jit(solution)/shard_map/dot_general | solution.py:66
  194.8 1.8 copy-done.8
  198.1 1.7 copy-done.1
  201.1 1.5 collective-permute-start.16
  204.6 1.5 collective-permute-start.6
  207.1 1.5 collective-permute-start.12
  208.7 5.2 collective-permute-done.16
  213.9 1.5 collective-permute-start.10
  215.3 25.9 %collective-permute-done.4 = bf16[8,8,3328]{2,1,0:T(8,128)(2,1)S(1)} collective-permute-done((bf16[8,8,3328]{2,1,0:T(8,128)(2,1)S(1)}, bf16[8,8,3328]{2,1,0:T(8,128)(2,1)S(1)}, u32[]{:S(2)}, u32[]{:S(2)}) %collective-permute-start.4) | collective-permute-done | bytes 426016 | tf_op jit(solution)/shard_map/ppermute | solution.py:27
  241.3 1.6 multiply_convert_fusion.2
  242.8 2.5 multiply_convert_fusion.3
  247.4 1.5 collective-permute-start.19
  248.9 10.7 %collective-permute-done.10 = bf16[8,8,3328]{2,1,0:T(8,128)(2,1)S(1)} collective-permute-done((bf16[8,8,3328]{2,1,0:T(8,128)(2,1)S(1)}, bf16[8,8,3328]{2,1,0:T(8,128)(2,1)S(1)}, u32[]{:S(2)}, u32[]{:S(2)}) %collective-permute-start.10) | collective-permute-done | bytes 426016 | tf_op jit(solution)/shard_map/ppermute | solution.py:27
  259.5 1.5 multiply_convert_fusion
  261.1 2.7 multiply_convert_fusion.1
  265.8 2.9 collective-permute-done.17
  268.8 18.1 %collective-permute-done.19 = bf16[8,8,3328]{2,1,0:T(8,128)(2,1)S(1)} collective-permute-done((bf16[8,8,3328]{2,1,0:T(8,128)(2,1)S(1)}, bf16[8,8,3328]{2,1,0:T(8,128)(2,1)S(1)}, u32[]{:S(2)}, u32[]{:S(2)}) %collective-permute-start.19) | collective-permute-done | bytes 426016 | tf_op jit(solution)/shard_map/ppermute | solution.py:27
  287.1 9.0 %collective-permute-done.23 = bf16[8,8,3328]{2,1,0:T(8,128)(2,1)S(1)} collective-permute-done((bf16[8,8,3328]{2,1,0:T(8,128)(2,1)S(1)}, bf16[8,8,3328]{2,1,0:T(8,128)(2,1)S(1)}, u32[]{:S(2)}, u32[]{:S(2)}) %collective-permute-start.23) | collective-permute-done | bytes 426016 | tf_op jit(solution)/shard_map/ppermute | solution.py:27
  297.0 7.2 %collective-permute-done.25 = bf16[8,8,3328]{2,1,0:T(8,128)(2,1)S(1)} collective-permute-done((bf16[8,8,3328]{2,1,0:T(8,128)(2,1)S(1)}, bf16[8,8,3328]{2,1,0:T(8,128)(2,1)S(1)}, u32[]{:S(2)}, u32[]{:S(2)}) %collective-permute-start.25) | collective-permute-done | bytes 426016 | tf_op jit(solution)/shard_map/ppermute | solution.py:27
  306.1 7.7 %fusion.76 = f32[256,2048]{1,0:T(8,128)S(1)} fusion(bf16[256,3328]{1,0:T(8,128)(2,1)S(1)} %bitcast.353, bf16[2048,3328]{1,0:T(8,128)(2,1)} %param.7), kind=kOutput, calls=%fused_computation.203 | convolution fusion | flops 3489660928 | bytes 17432576 | tf_op jit(solution)/shard_map/dot_general | solution.py:21
  313.8 9.9 %convolution_add_fusion.1 = f32[256,2048]{1,0:T(8,128)} fusion(f32[256,2048]{1,0:T(8,128)S(1)} %fusion.76, bf16[256,3328]{1,0:T(8,128)(2,1)S(1)} %bitcast.355, bf16[2048,3328]{1,0:T(8,128)(2,1)} %param.8), kind=kOutput, calls=%fused_computation.25 | convolution fusion | flops 3490185216 | bytes 19529728 | tf_op jit(solution)/shard_map/dot_general | solution.py:21
  325.4 1.8 slice_bitcast_fusion.37
  327.6 7.7 %fusion.77 = f32[256,2048]{1,0:T(8,128)S(1)} fusion(bf16[256,3328]{1,0:T(8,128)(2,1)S(1)} %bitcast.357, bf16[2048,3328]{1,0:T(8,128)(2,1)} %param.7), kind=kOutput, calls=%fused_computation.204 | convolution fusion | flops 3489660928 | bytes 17432576 | tf_op jit(solution)/shard_map/dot_general | solution.py:21
  335.3 10.1 %convolution_add_fusion = f32[256,2048]{1,0:T(8,128)} fusion(f32[256,2048]{1,0:T(8,128)S(1)} %fusion.77, bf16[256,3328]{1,0:T(8,128)(2,1)S(1)} %bitcast.359, bf16[2048,3328]{1,0:T(8,128)(2,1)} %param.8), kind=kOutput, calls=%fused_computation.24 | convolution fusion | flops 3490185216 | bytes 19529728 | tf_op jit(solution)/shard_map/dot_general | solution.py:21
  352.1 8.7 %fusion.74 = f32[256,2048]{1,0:T(8,128)} fusion(bf16[256,3328]{1,0:T(8,128)(2,1)S(1)} %bitcast.361, bf16[3328,2048]{1,0:T(8,128)(2,1)} %param.9), kind=kOutput, calls=%fused_computation.201 | convolution fusion | flops 3489660928 | bytes 17432576 | tf_op jit(solution)/shard_map/dot_general | solution.py:82
  362.2 2.2 collective-permute-done.14
  366.1 8.9 %fusion.75 = f32[256,2048]{1,0:T(8,128)} fusion(bf16[256,3328]{1,0:T(8,128)(2,1)S(1)} %bitcast.363, bf16[3328,2048]{1,0:T(8,128)(2,1)} %param.9), kind=kOutput, calls=%fused_computation.202 | convolution fusion | flops 3489660928 | bytes 17432576 | tf_op jit(solution)/shard_map/dot_general | solution.py:82
  375.0 1.6 copy-done.16
  376.6 12.3 %convolution_convert_fusion = bf16[3328,2048]{1,0:T(8,128)(2,1)} fusion(bf16[256,3328]{1,0:T(8,128)(2,1)} %bitcast.364, bf16[256,3328]{1,0:T(8,128)(2,1)S(1)} %bitcast.362, bf16[256,2048]{1,0:T(8,128)(2,1)} %bitcast.381, bf16[256,2048]{1,0:T(8,128)(2,1)} %bitcast.379), kind=kOutput, calls=%fused_computation | convolution fusion | flops 6997147648 | bytes 19136512 | tf_op jit(solution)/shard_map/dot_general | solution.py:15
  389.0 10.5 %convolution_convert_fusion.1 = bf16[2048,3328]{1,0:T(8,128)(2,1)} fusion(bf16[256,3328]{1,0:T(8,128)(2,1)S(1)} %bitcast.360, bf16[256,3328]{1,0:T(8,128)(2,1)S(1)} %bitcast.356, bf16[256,2048]{1,0:T(8,128)(2,1)S(1)} %bitcast.388, bf16[256,2048]{1,0:T(8,128)(2,1)S(1)} %bitcast.384), kind=kOutput, calls=%fused_computation.1 | convolution fusion | flops 6997147648 | bytes 19136512 | tf_op jit(solution)/shard_map/dot_general | solution.py:15
  399.5 10.8 %convolution_convert_fusion.2 = bf16[2048,3328]{1,0:T(8,128)(2,1)} fusion(bf16[256,3328]{1,0:T(8,128)(2,1)S(1)} %bitcast.358, bf16[256,3328]{1,0:T(8,128)(2,1)S(1)} %bitcast.354, bf16[256,2048]{1,0:T(8,128)(2,1)S(1)} %bitcast.389, bf16[256,2048]{1,0:T(8,128)(2,1)S(1)} %bitcast.385), kind=kOutput, calls=%fused_computation.2 | convolution fusion | flops 6997147648 | bytes 19136512 | tf_op jit(solution)/shard_map/dot_general | solution.py:15
  411.3 49.2 %reduce-scatter.11.cloned.1.call-done = f32[32,2048]{1,0:T(8,128)} async-done(((f32[256,2048]{1,0:T(8,128)}), f32[32,2048]{1,0:T(8,128)}) %reduce-scatter.11.cloned.1.call-update) | async-done | bytes 262160 | tf_op jit(solution)/shard_map/reduce_scatter | solution.py:75
  461.5 1.7 collective-permute-start.29
  463.7 67.1 %reduce-scatter.5.cloned.1.call-done = f32[32,2048]{1,0:T(8,128)} async-done(((f32[256,2048]{1,0:T(8,128)}), f32[32,2048]{1,0:T(8,128)}) %reduce-scatter.5.cloned.1.call-update) | async-done | bytes 262160 | tf_op jit(solution)/shard_map/reduce_scatter | solution.py:75
  531.8 69.3 %reduce-scatter.7.cloned.1.call-done = f32[32,2048]{1,0:T(8,128)} async-done(((f32[256,2048]{1,0:T(8,128)}), f32[32,2048]{1,0:T(8,128)}) %reduce-scatter.7.cloned.1.call-update) | async-done | bytes 262160 | tf_op jit(solution)/shard_map/reduce_scatter | solution.py:75
  (160 shorter events, 39.2 us)
Async XLA Ops:
  7.2 46.4 %all-gather.9.cloned.1.call-start = ((), (), s32[]{:S(2)}) async-start(), calls=%async_computation.8 | async-start | bytes 1179648 | tf_op jit(solution)/shard_map/all_gather | solution.py:57
  8.8 86.4 %all-gather.11.cloned.1.call-start = ((), (), s32[]{:S(2)}) async-start(), calls=%async_computation.10 | async-start | bytes 1179648 | tf_op jit(solution)/shard_map/all_gather | solution.py:57
  9.6 127.3 %all-gather.5.cloned.1.call-start = ((), (), s32[]{:S(2)}) async-start(), calls=%async_computation.4 | async-start | bytes 1179648 | tf_op jit(solution)/shard_map/all_gather | solution.py:57
  10.6 4.0 collective-permute-start
  11.1 5.0 collective-permute-start.2
  13.7 4.3 collective-permute-start.1
  18.7 159.1 %all-gather.7.cloned.1.call-start = ((), (), s32[]{:S(2)}) async-start(), calls=%async_computation.6 | async-start | bytes 1179648 | tf_op jit(solution)/shard_map/all_gather | solution.py:57
  19.5 390.8 %reduce-scatter.9.cloned.1.call-start = ((), (), s32[]{:S(2)}) async-start(), calls=%async_computation.9 | async-start | bytes 2359296 | tf_op jit(solution)/shard_map/reduce_scatter | solution.py:75
  63.3 134.7 %collective-permute-start.15 = (f32[2,8,8,3328]{3,2,1,0:T(8,128)}, f32[2,8,8,3328]{3,2,1,0:T(8,128)}, u32[]{:S(2)}, u32[]{:S(2)}) collective-permute-start(f32[2,8,8,3328]{3,2,1,0:T(8,128)} %pad_maximum_fusion.7), channel_id=1, source_target_pairs={{0,1},{1,0},{2,3},{3,2},{4,5},{5,4},{6,7},{7,6},{8,9},{9,8},{10,11... | collective-permute-start | bytes 5111816 | tf_op jit(solution)/shard_map/ppermute | solution.py:27
  104.0 97.1 %collective-permute-start.21 = (f32[2,8,8,3328]{3,2,1,0:T(8,128)}, f32[2,8,8,3328]{3,2,1,0:T(8,128)}, u32[]{:S(2)}, u32[]{:S(2)}) collective-permute-start(f32[2,8,8,3328]{3,2,1,0:T(8,128)} %pad_maximum_fusion.10), channel_id=1, source_target_pairs={{0,1},{1,0},{2,3},{3,2},{4,5},{5,4},{6,7},{7,6},{8,9},{9,8},{10,11... | collective-permute-start | bytes 5111816 | tf_op jit(solution)/shard_map/ppermute | solution.py:27
  136.9 10.7 %copy-start.18 = (bf16[32,8,2048]{2,1,0:T(8,128)(2,1)S(1)}, bf16[32,8,2048]{2,1,0:T(8,128)(2,1)}, u32[]{:S(2)}) copy-start(bf16[32,8,2048]{2,1,0:T(8,128)(2,1)} %all-gather.5.cloned.1.call-done) | copy-start | bytes 3145732
  177.8 9.4 %copy-start.20 = (bf16[32,8,2048]{2,1,0:T(8,128)(2,1)S(1)}, bf16[32,8,2048]{2,1,0:T(8,128)(2,1)}, u32[]{:S(2)}) copy-start(bf16[32,8,2048]{2,1,0:T(8,128)(2,1)} %all-gather.7.cloned.1.call-done) | copy-start | bytes 3145732
  194.7 9.2 %collective-permute-start.5 = (f32[2,8,8,3328]{3,2,1,0:T(8,128)S(1)}, f32[2,8,8,3328]{3,2,1,0:T(8,128)S(1)}, u32[]{:S(2)}, u32[]{:S(2)}) collective-permute-start(f32[2,8,8,3328]{3,2,1,0:T(8,128)S(1)} %pad_maximum_fusion.2), channel_id=1, source_target_pairs={{0,1},{1,0},{2,3},{3,2},{4,5},{5,4},{6,7},{7,6},{8,9},{9,8},{10,11... | collective-permute-start | bytes 5111816 | tf_op jit(solution)/shard_map/ppermute | solution.py:27
  196.8 7.9 %collective-permute-start.3 = (f32[2,8,8,3328]{3,2,1,0:T(8,128)S(1)}, f32[2,8,8,3328]{3,2,1,0:T(8,128)S(1)}, u32[]{:S(2)}, u32[]{:S(2)}) collective-permute-start(f32[2,8,8,3328]{3,2,1,0:T(8,128)S(1)} %pad_maximum_fusion.1), channel_id=1, source_target_pairs={{0,1},{1,0},{2,3},{3,2},{4,5},{5,4},{6,7},{7,6},{8,9},{9,8},{10,11... | collective-permute-start | bytes 5111816 | tf_op jit(solution)/shard_map/ppermute | solution.py:27
  197.2 9.1 %collective-permute-start.11 = (f32[2,8,8,3328]{3,2,1,0:T(8,128)S(1)}, f32[2,8,8,3328]{3,2,1,0:T(8,128)S(1)}, u32[]{:S(2)}, u32[]{:S(2)}) collective-permute-start(f32[2,8,8,3328]{3,2,1,0:T(8,128)S(1)} %pad_maximum_fusion.5), channel_id=1, source_target_pairs={{0,1},{1,0},{2,3},{3,2},{4,5},{5,4},{6,7},{7,6},{8,9},{9,8},{10,11... | collective-permute-start | bytes 5111816 | tf_op jit(solution)/shard_map/ppermute | solution.py:27
  198.0 9.1 %collective-permute-start.9 = (f32[2,8,8,3328]{3,2,1,0:T(8,128)S(1)}, f32[2,8,8,3328]{3,2,1,0:T(8,128)S(1)}, u32[]{:S(2)}, u32[]{:S(2)}) collective-permute-start(f32[2,8,8,3328]{3,2,1,0:T(8,128)S(1)} %pad_maximum_fusion.4), channel_id=1, source_target_pairs={{0,1},{1,0},{2,3},{3,2},{4,5},{5,4},{6,7},{7,6},{8,9},{9,8},{10,11... | collective-permute-start | bytes 5111816 | tf_op jit(solution)/shard_map/ppermute | solution.py:27
  201.1 12.7 %collective-permute-start.16 = (bf16[8,8,3328]{2,1,0:T(8,128)(2,1)S(1)}, bf16[8,8,3328]{2,1,0:T(8,128)(2,1)S(1)}, u32[]{:S(2)}, u32[]{:S(2)}) collective-permute-start(bf16[8,8,3328]{2,1,0:T(8,128)(2,1)S(1)} %fusion.34), channel_id=1, source_target_pairs={{0,2},{1,3},{2,0},{3,1},{4,6},{5,7},{6,4},{7,5},{8,10},{9,11},{10,... | collective-permute-start | bytes 1277960 | tf_op jit(solution)/shard_map/ppermute | solution.py:27
  203.9 43.5 %collective-permute-start.22 = (bf16[8,8,3328]{2,1,0:T(8,128)(2,1)S(1)}, bf16[8,8,3328]{2,1,0:T(8,128)(2,1)S(1)}, u32[]{:S(2)}, u32[]{:S(2)}) collective-permute-start(bf16[8,8,3328]{2,1,0:T(8,128)(2,1)S(1)} %fusion.30), channel_id=1, source_target_pairs={{0,2},{1,3},{2,0},{3,1},{4,6},{5,7},{6,4},{7,5},{8,10},{9,11},{10,... | collective-permute-start | bytes 1277960 | tf_op jit(solution)/shard_map/ppermute | solution.py:27
  204.6 38.2 %collective-permute-start.6 = (bf16[8,8,3328]{2,1,0:T(8,128)(2,1)S(1)}, bf16[8,8,3328]{2,1,0:T(8,128)(2,1)S(1)}, u32[]{:S(2)}, u32[]{:S(2)}) collective-permute-start(bf16[8,8,3328]{2,1,0:T(8,128)(2,1)S(1)} %fusion.46), channel_id=1, source_target_pairs={{0,2},{1,3},{2,0},{3,1},{4,6},{5,7},{6,4},{7,5},{8,10},{9,11},{10,... | collective-permute-start | bytes 1277960 | tf_op jit(solution)/shard_map/ppermute | solution.py:27
  206.3 34.9 %collective-permute-start.4 = (bf16[8,8,3328]{2,1,0:T(8,128)(2,1)S(1)}, bf16[8,8,3328]{2,1,0:T(8,128)(2,1)S(1)}, u32[]{:S(2)}, u32[]{:S(2)}) collective-permute-start(bf16[8,8,3328]{2,1,0:T(8,128)(2,1)S(1)} %fusion.50), channel_id=1, source_target_pairs={{0,2},{1,3},{2,0},{3,1},{4,6},{5,7},{6,4},{7,5},{8,10},{9,11},{10,... | collective-permute-start | bytes 1277960 | tf_op jit(solution)/shard_map/ppermute | solution.py:27
  207.1 54.0 %collective-permute-start.12 = (bf16[8,8,3328]{2,1,0:T(8,128)(2,1)S(1)}, bf16[8,8,3328]{2,1,0:T(8,128)(2,1)S(1)}, u32[]{:S(2)}, u32[]{:S(2)}) collective-permute-start(bf16[8,8,3328]{2,1,0:T(8,128)(2,1)S(1)} %fusion.38), channel_id=1, source_target_pairs={{0,2},{1,3},{2,0},{3,1},{4,6},{5,7},{6,4},{7,5},{8,10},{9,11},{10,... | collective-permute-start | bytes 1277960 | tf_op jit(solution)/shard_map/ppermute | solution.py:27
  213.9 45.6 %collective-permute-start.10 = (bf16[8,8,3328]{2,1,0:T(8,128)(2,1)S(1)}, bf16[8,8,3328]{2,1,0:T(8,128)(2,1)S(1)}, u32[]{:S(2)}, u32[]{:S(2)}) collective-permute-start(bf16[8,8,3328]{2,1,0:T(8,128)(2,1)S(1)} %fusion.42), channel_id=1, source_target_pairs={{0,2},{1,3},{2,0},{3,1},{4,6},{5,7},{6,4},{7,5},{8,10},{9,11},{10,... | collective-permute-start | bytes 1277960 | tf_op jit(solution)/shard_map/ppermute | solution.py:27
  245.3 23.3 %collective-permute-start.17 = (bf16[8,8,3328]{2,1,0:T(8,128)(2,1)S(1)}, bf16[8,8,3328]{2,1,0:T(8,128)(2,1)S(1)}, u32[]{:S(2)}, u32[]{:S(2)}) collective-permute-start(bf16[8,8,3328]{2,1,0:T(8,128)(2,1)S(1)} %get-tuple-element.9), channel_id=1, source_target_pairs={{0,2},{1,3},{2,0},{3,1},{4,6},{5,7},{6,4},{7,5},{8,10},{9,11},{10,... | collective-permute-start | bytes 1277960 | tf_op jit(solution)/shard_map/ppermute | solution.py:27
  246.8 98.6 %collective-permute-start.7 = (bf16[8,8,3328]{2,1,0:T(8,128)(2,1)}, bf16[8,8,3328]{2,1,0:T(8,128)(2,1)}, u32[]{:S(2)}, u32[]{:S(2)}) collective-permute-start(bf16[8,8,3328]{2,1,0:T(8,128)(2,1)} %get-tuple-element.10), channel_id=1, source_target_pairs={{0,2},{1,3},{2,0},{3,1},{4,6},{5,7},{6,4},{7,5},{8,10},{9,11},{10,... | collective-permute-start | bytes 1277960 | tf_op jit(solution)/shard_map/ppermute | solution.py:27
  247.4 39.5 %collective-permute-start.19 = (bf16[8,8,3328]{2,1,0:T(8,128)(2,1)S(1)}, bf16[8,8,3328]{2,1,0:T(8,128)(2,1)S(1)}, u32[]{:S(2)}, u32[]{:S(2)}) collective-permute-start(bf16[8,8,3328]{2,1,0:T(8,128)(2,1)S(1)} %get-tuple-element.5), channel_id=1, source_target_pairs={{0,2},{1,3},{2,0},{3,1},{4,6},{5,7},{6,4},{7,5},{8,10},{9,11},{10,... | collective-permute-start | bytes 1277960 | tf_op jit(solution)/shard_map/ppermute | solution.py:27
  261.1 43.2 %copy-start.5 = (bf16[8,8,3328]{2,1,0:T(8,128)(2,1)}, bf16[8,8,3328]{2,1,0:T(8,128)(2,1)S(1)}, u32[]{:S(2)}) copy-start(bf16[8,8,3328]{2,1,0:T(8,128)(2,1)S(1)} %get-tuple-element.7) | copy-start | bytes 1277956
  263.8 33.2 %copy-start.3 = (bf16[8,8,3328]{2,1,0:T(8,128)(2,1)}, bf16[8,8,3328]{2,1,0:T(8,128)(2,1)S(1)}, u32[]{:S(2)}) copy-start(bf16[8,8,3328]{2,1,0:T(8,128)(2,1)S(1)} %get-tuple-element.11) | copy-start | bytes 1277956
  263.8 32.3 %collective-permute-start.23 = (bf16[8,8,3328]{2,1,0:T(8,128)(2,1)S(1)}, bf16[8,8,3328]{2,1,0:T(8,128)(2,1)S(1)}, u32[]{:S(2)}, u32[]{:S(2)}) collective-permute-start(bf16[8,8,3328]{2,1,0:T(8,128)(2,1)S(1)} %get-tuple-element.11), channel_id=1, source_target_pairs={{0,2},{1,3},{2,0},{3,1},{4,6},{5,7},{6,4},{7,5},{8,10},{9,11},{10,... | collective-permute-start | bytes 1277960 | tf_op jit(solution)/shard_map/ppermute | solution.py:27
  265.2 39.0 %collective-permute-start.25 = (bf16[8,8,3328]{2,1,0:T(8,128)(2,1)S(1)}, bf16[8,8,3328]{2,1,0:T(8,128)(2,1)S(1)}, u32[]{:S(2)}, u32[]{:S(2)}) collective-permute-start(bf16[8,8,3328]{2,1,0:T(8,128)(2,1)S(1)} %get-tuple-element.7), channel_id=1, source_target_pairs={{0,2},{1,3},{2,0},{3,1},{4,6},{5,7},{6,4},{7,5},{8,10},{9,11},{10,... | collective-permute-start | bytes 1277960 | tf_op jit(solution)/shard_map/ppermute | solution.py:27
  268.7 36.5 %collective-permute-start.18 = (bf16[2,8,8,3328]{3,2,1,0:T(8,128)(2,1)S(1)}, bf16[2,8,8,3328]{3,2,1,0:T(8,128)(2,1)S(1)}, u32[]{:S(2)}, u32[]{:S(2)}) collective-permute-start(bf16[2,8,8,3328]{3,2,1,0:T(8,128)(2,1)S(1)} %pad_maximum_fusion.17), channel_id=1, source_target_pairs={{0,1},{1,0},{2,3},{3,2},{4,5},{5,4},{6,7},{7,6},{8,9},{9,8},{10,11... | collective-permute-start | bytes 2555912 | tf_op jit(solution)/shard_map/ppermute | solution.py:27
  287.0 18.6 %collective-permute-start.20 = (bf16[2,8,8,3328]{3,2,1,0:T(8,128)(2,1)S(1)}, bf16[2,8,8,3328]{3,2,1,0:T(8,128)(2,1)S(1)}, u32[]{:S(2)}, u32[]{:S(2)}) collective-permute-start(bf16[2,8,8,3328]{3,2,1,0:T(8,128)(2,1)S(1)} %pad_maximum_fusion.18), channel_id=1, source_target_pairs={{0,1},{1,0},{2,3},{3,2},{4,5},{5,4},{6,7},{7,6},{8,9},{9,8},{10,11... | collective-permute-start | bytes 2555912 | tf_op jit(solution)/shard_map/ppermute | solution.py:27
  297.0 26.8 %collective-permute-start.24 = (bf16[2,8,8,3328]{3,2,1,0:T(8,128)(2,1)}, bf16[2,8,8,3328]{3,2,1,0:T(8,128)(2,1)}, u32[]{:S(2)}, u32[]{:S(2)}) collective-permute-start(bf16[2,8,8,3328]{3,2,1,0:T(8,128)(2,1)} %pad_maximum_fusion.19), channel_id=1, source_target_pairs={{0,1},{1,0},{2,3},{3,2},{4,5},{5,4},{6,7},{7,6},{8,9},{9,8},{10,11... | collective-permute-start | bytes 2555912 | tf_op jit(solution)/shard_map/ppermute | solution.py:27
  305.2 20.2 %collective-permute-start.26 = (bf16[2,8,8,3328]{3,2,1,0:T(8,128)(2,1)}, bf16[2,8,8,3328]{3,2,1,0:T(8,128)(2,1)}, u32[]{:S(2)}, u32[]{:S(2)}) collective-permute-start(bf16[2,8,8,3328]{3,2,1,0:T(8,128)(2,1)} %pad_maximum_fusion.20), channel_id=1, source_target_pairs={{0,1},{1,0},{2,3},{3,2},{4,5},{5,4},{6,7},{7,6},{8,9},{9,8},{10,11... | collective-permute-start | bytes 2555912 | tf_op jit(solution)/shard_map/ppermute | solution.py:27
  306.1 7.7 %copy-start.9 = (bf16[8,4,8,3328]{3,2,1,0:T(8,128)(2,1)}, bf16[8,4,8,3328]{3,2,1,0:T(8,128)(2,1)S(1)}, u32[]{:S(2)}) copy-start(bf16[8,4,8,3328]{3,2,1,0:T(8,128)(2,1)S(1)} %copy.84) | copy-start | bytes 5111812
  323.7 136.7 %reduce-scatter.11.cloned.1.call-start = ((), (), s32[]{:S(2)}) async-start(), calls=%async_computation.11 | async-start | bytes 2359296 | tf_op jit(solution)/shard_map/reduce_scatter | solution.py:75
  345.4 185.4 %reduce-scatter.5.cloned.1.call-start = ((), (), s32[]{:S(2)}) async-start(), calls=%async_computation.5 | async-start | bytes 2359296 | tf_op jit(solution)/shard_map/reduce_scatter | solution.py:75
  346.7 2.6 collective-permute-start.8
  347.4 13.5 %collective-permute-start.13 = (bf16[8,8,3328]{2,1,0:T(8,128)(2,1)S(1)}, bf16[8,8,3328]{2,1,0:T(8,128)(2,1)S(1)}, u32[]{:S(2)}, u32[]{:S(2)}) collective-permute-start(bf16[8,8,3328]{2,1,0:T(8,128)(2,1)S(1)} %copy-done.2), channel_id=1, source_target_pairs={{0,2},{1,3},{2,0},{3,1},{4,6},{5,7},{6,4},{7,5},{8,10},{9,11},{10,... | collective-permute-start | bytes 1277960 | tf_op jit(solution)/shard_map/ppermute | solution.py:27
  360.8 240.2 %reduce-scatter.7.cloned.1.call-start = ((), (), s32[]{:S(2)}) async-start(), calls=%async_computation.7 | async-start | bytes 2359296 | tf_op jit(solution)/shard_map/reduce_scatter | solution.py:75
  361.8 2.6 collective-permute-start.14
  376.6 12.3 %copy-start.10 = (bf16[8,4,8,3328]{3,2,1,0:T(8,128)(2,1)S(1)}, bf16[8,4,8,3328]{3,2,1,0:T(8,128)(2,1)}, u32[]{:S(2)}) copy-start(bf16[8,4,8,3328]{3,2,1,0:T(8,128)(2,1)} %copy-done.9) | copy-start | bytes 5111812
  376.6 12.3 %copy-start.14 = (bf16[8,4,8,3328]{3,2,1,0:T(8,128)(2,1)S(1)}, bf16[8,4,8,3328]{3,2,1,0:T(8,128)(2,1)}, u32[]{:S(2)}) copy-start(bf16[8,4,8,3328]{3,2,1,0:T(8,128)(2,1)} %copy-done.13) | copy-start | bytes 5111812
  376.6 12.4 %copy-start.19 = (bf16[32,8,2048]{2,1,0:T(8,128)(2,1)S(1)}, bf16[32,8,2048]{2,1,0:T(8,128)(2,1)}, u32[]{:S(2)}) copy-start(bf16[32,8,2048]{2,1,0:T(8,128)(2,1)} %all-gather.5.cloned.1.call-done) | copy-start | bytes 3145732
  376.6 12.4 %copy-start.21 = (bf16[32,8,2048]{2,1,0:T(8,128)(2,1)S(1)}, bf16[32,8,2048]{2,1,0:T(8,128)(2,1)}, u32[]{:S(2)}) copy-start(bf16[32,8,2048]{2,1,0:T(8,128)(2,1)} %all-gather.7.cloned.1.call-done) | copy-start | bytes 3145732
  389.0 10.5 %copy-start.12 = (bf16[8,4,8,3328]{3,2,1,0:T(8,128)(2,1)S(1)}, bf16[8,4,8,3328]{3,2,1,0:T(8,128)(2,1)}, u32[]{:S(2)}) copy-start(bf16[8,4,8,3328]{3,2,1,0:T(8,128)(2,1)} %copy-done.11) | copy-start | bytes 5111812
  461.4 140.6 %collective-permute-start.27 = (bf16[16,2048]{1,0:T(8,128)(2,1)S(1)}, bf16[16,2048]{1,0:T(8,128)(2,1)S(1)}, u32[]{:S(2)}, u32[]{:S(2)}) collective-permute-start(bf16[16,2048]{1,0:T(8,128)(2,1)S(1)} %get-tuple-element.42), channel_id=1, source_target_pairs={{0,1},{1,0},{2,3},{3,2},{4,5},{5,4},{6,7},{7,6},{8,9},{9,8},{10,11... | collective-permute-start | bytes 196616 | tf_op jit(solution)/shard_map/ppermute | solution.py:27
  461.5 140.5 %collective-permute-start.29 = (bf16[16,2048]{1,0:T(8,128)(2,1)S(1)}, bf16[16,2048]{1,0:T(8,128)(2,1)S(1)}, u32[]{:S(2)}, u32[]{:S(2)}) collective-permute-start(bf16[16,2048]{1,0:T(8,128)(2,1)S(1)} %get-tuple-element.43), channel_id=1, source_target_pairs={{0,3},{1,2},{2,1},{3,0},{4,7},{5,6},{6,5},{7,4},{8,11},{9,10},{10,... | collective-permute-start | bytes 196616 | tf_op jit(solution)/shard_map/ppermute | solution.py:27
  463.2 138.8 %collective-permute-start.28 = (bf16[16,2048]{1,0:T(8,128)(2,1)S(1)}, bf16[16,2048]{1,0:T(8,128)(2,1)S(1)}, u32[]{:S(2)}, u32[]{:S(2)}) collective-permute-start(bf16[16,2048]{1,0:T(8,128)(2,1)S(1)} %get-tuple-element.44), channel_id=1, source_target_pairs={{0,2},{1,3},{2,0},{3,1},{4,6},{5,7},{6,4},{7,5},{8,10},{9,11},{10,... | collective-permute-start | bytes 196616 | tf_op jit(solution)/shard_map/ppermute | solution.py:27
  (12 other events, 32.8 us)
Sparse Core Ops, SparseCore 0:
  10.7 42.8 all-gather.8
  56.3 38.8 all-gather.10
  97.9 38.8 all-gather.4
  138.8 38.8 all-gather.6
  323.8 66.4 reduce-scatter.8
  393.7 66.6 reduce-scatter.10
  464.0 66.7 reduce-scatter.4
  534.3 66.6 reduce-scatter.6

commit v2 on v1

v2 whole, which is shorter than its diff:
```python
import functools

import jax
import jax.numpy as jnp
from jax import lax
from jax.experimental import pallas as pl
from jax.experimental.pallas import tpu as pltpu
from jax.sharding import PartitionSpec as P

BF16, F32 = jnp.bfloat16, jnp.float32
BLOCK = 256
VMEM_LIMIT = 48 * 1024 * 1024
NN = (((1,), (0,)), ((), ()))
NT = (((1,), (1,)), ((), ()))
TN = (((0,), (0,)), ((), ()))


def dot(left, right, dims):
    return lax.dot_general(left, right, dims, preferred_element_type=F32)


def silu_parts(gate):
    sigma = jax.nn.sigmoid(gate)
    return (gate * sigma, sigma * (1.0 + gate * (1.0 - sigma)))


def swap(value, mask):
    return lax.ppermute(value, "narrow", [(i, i ^ mask) for i in range(4)])


def swap_wide(value, mask):
    return lax.ppermute(value, "wide", [(i, i ^ mask) for i in range(8)])


class Chain:
    def __init__(self):
        self.token = None
        self.waits = []

    def after(self, *arrays):
        self.waits += arrays

    def __call__(self, body, grid, ins, outs, scratch=(), flops=0, alias=None, scalar=None):
        lead = 0 if scalar is None else 1
        arrays = [a for a, _, _ in ins]
        specs = [pl.BlockSpec(block, index) for _, block, index in ins]
        unread = self.waits + ([] if self.token is None else [self.token])
        self.waits = []
        arrays += unread
        specs += [pl.BlockSpec(memory_space=pl.ANY)] * len(unread)
        shapes = [jax.ShapeDtypeStruct(shape, dtype) for shape, dtype, _, _ in outs]
        out_specs = [pl.BlockSpec(block, index) for _, _, block, index in outs]
        shapes.append(jax.ShapeDtypeStruct((8, 128), F32))
        out_specs.append(pl.BlockSpec((8, 128), lambda *i: (0, 0)))
        n_in, n_out = len(ins), len(outs)

        def kernel(*refs):
            head, refs = refs[:lead], refs[lead:]
            in_refs = refs[:n_in]
            rest = refs[n_in + len(unread) :]
            out_refs, token, scratch_refs = rest[:n_out], rest[n_out], rest[n_out + 1 :]
            token[...] = jnp.zeros(token.shape, F32)
            body(*head, *in_refs, *out_refs, *scratch_refs)

        res = pl.pallas_call(
            kernel,
            grid_spec=pltpu.PrefetchScalarGridSpec(
                num_scalar_prefetch=lead,
                grid=grid,
                in_specs=specs,
                out_specs=out_specs,
                scratch_shapes=list(scratch),
            ),
            out_shape=shapes,
            input_output_aliases={k + lead: v for k, v in (alias or {}).items()},
            compiler_params=pltpu.CompilerParams(vmem_limit_bytes=VMEM_LIMIT),
            cost_estimate=pl.CostEstimate(flops=1, bytes_accessed=1, transcendentals=0),
        )(*(() if scalar is None else (scalar,)), *arrays)
        self.token = res[-1]
        return res[:-1]


def arrange(chain, me, pieces, rows, tile):
    def body(_, *refs):
        out = refs[8]
        for k in range(8):
            out[0, k] = refs[k][...]

    (out,) = chain(
        body,
        (4,),
        [(p, (rows, tile), lambda g, s: (s[0] ^ g, 0)) for p in pieces],
        [((4, 8, rows, tile), BF16, (1, 8, rows, tile), lambda g, s: (g, 0, 0, 0))],
        scalar=me,
    )
    return out.reshape(32 * rows, tile)


def parted(acc, q, keep, send):
    for i in range(2):
        keep[i] = acc[2 * i * q : (2 * i + 1) * q]
        send[i] = acc[(2 * i + 1) * q : (2 * i + 2) * q]


def back_part(chain, cot, down, base, blocks):
    tokens, tile = cot.shape
    q, n = tokens // 4, blocks * BLOCK

    def body(c, w, keep, send):
        parted(dot(c[...], w[...], NT), q, keep, send)

    out = ((2, q, n), F32, (2, q, BLOCK), lambda j: (0, 0, j))
    return chain(
        body,
        (blocks,),
        [(cot, cot.shape, lambda j: (0, 0)), (down, (BLOCK, tile), lambda j: (base + j, 0))],
        [out, out],
        flops=2 * tokens * tile * n,
    )


def gate_up_part(chain, act, gate, up, base, blocks):
    tokens, tile = act.shape
    q, n = tokens // 4, blocks * BLOCK

    def body(a, wg, wu, keep, send):
        parted(dot(a[...], wg[...], NN), q, keep.at[:, 0], send.at[:, 0])
        parted(dot(a[...], wu[...], NN), q, keep.at[:, 1], send.at[:, 1])

    weight = ((tile, BLOCK), lambda j: (0, base + j))
    out = ((2, 2, q, n), F32, (2, 2, q, BLOCK), lambda j: (0, 0, 0, j))
    return chain(
        body,
        (blocks,),
        [(act, act.shape, lambda j: (0, 0)), (gate, *weight), (up, *weight)],
        [out, out],
        flops=4 * tokens * tile * n,
    )


def add_away(chain, keep, got):
    shape = keep.shape[1:]
    zeros = (0,) * (len(shape) - 1)
    block = (1, *shape[:-1], BLOCK)

    def body(a, b, out):
        out[...] = (a[0] + b[0]).astype(BF16)

    def at(j):
        return (1, *zeros, j)

    (out,) = chain(
        body,
        (shape[-1] // BLOCK,),
        [(keep, block, at), (got, block, at)],
        [(shape, BF16, block[1:], lambda j: (*zeros, j))],
    )
    return out


def activate(chain, keep_gu, got_gu, far_gu, keep_b, got_b, far_b, merged):
    q, n = far_b.shape

    def body(kg, gg, fg, kb, gb, fb, deltas, *rest):
        gate = kg[0, 0] + gg[0, 0] + fg[0].astype(F32)
        up = kg[0, 1] + gg[0, 1] + fg[1].astype(F32)
        back = kb[0] + gb[0] + fb[...].astype(F32)
        active, slope = silu_parts(gate)
        if merged:
            deltas[2] = (active * up).astype(BF16)
        else:
            rest[0][0] = (active * up).astype(BF16)
        deltas[0] = (back * up * slope).astype(BF16)
        deltas[1] = (back * active).astype(BF16)

    four = ((1, 2, q, BLOCK), lambda j: (0, 0, 0, j))
    three = ((1, q, BLOCK), lambda j: (0, 0, j))
    return chain(
        body,
        (n // BLOCK,),
        [
            (keep_gu, *four),
            (got_gu, *four),
            (far_gu, (2, q, BLOCK), lambda j: (0, 0, j)),
            (keep_b, *three),
            (got_b, *three),
            (far_b, (q, BLOCK), lambda j: (0, j)),
        ],
        [
            ((k, q, n), BF16, (k, q, BLOCK), lambda j: (0, 0, j))
            for k in ((3,) if merged else (2, 1))
        ],
    )


def split_slots(acc, rows, keep, sends):
    view = acc.reshape(4, 8, rows, acc.shape[-1])
    for s in range(4):
        keep[s] = view[:, 2 * s]
        sends[s][...] = view[:, 2 * s + 1].astype(BF16)


def summed(chain, quarters, at, weights, base, blocks, dims, prev, last, tile):
    count = len(weights)
    q, n = quarters[0].shape[-2:]
    rows = q // 8
    wide_block = min(2 * BLOCK, tile)

    def body(*refs):
        parts, w = refs[:4], refs[4 : 4 + count * blocks]
        rest = refs[4 + count * blocks :]
        scratch = rest[-1]
        if prev is not None:
            total, rest = rest[0][...], rest[1:]
        else:
            total = None

        @pl.when(pl.program_id(0) == 0)
        def _():
            for g in range(4):
                for k in range(count):
                    scratch[k, g * q : (g + 1) * q] = parts[g][k]

        for k in range(count):
            for i in range(blocks):
                left = scratch[k, :, i * BLOCK : (i + 1) * BLOCK]
                term = dot(left, w[k * blocks + i][...], dims)
                total = term if total is None else total + term
        if last:
            split_slots(total, rows, rest[0], rest[1:5])
        else:
            rest[0][...] = total

    ins = [(p, (count, q, n), lambda j: (at, 0, 0)) for p in quarters]
    for w in weights:
        for i in range(blocks):
            if dims is NN:
                ins.append((w, (BLOCK, wide_block), functools.partial(lambda i, j: (base + i, j), i)))
            else:
                ins.append((w, (wide_block, BLOCK), functools.partial(lambda i, j: (j, base + i), i)))
    whole = ((4 * q, tile), F32, (4 * q, wide_block), lambda j: (0, j))
    alias = {}
    if prev is not None:
        ins.append((prev, whole[2], whole[3]))
        if not last:
            alias = {len(ins) - 1: 0}
    if last:
        outs = [((4, 4, rows, tile), F32, (4, 4, rows, wide_block), lambda j: (0, 0, 0, j))]
        outs += [((4, rows, tile), BF16, (4, rows, wide_block), lambda j: (0, 0, j))] * 4
    else:
        outs = [whole]
    return chain(
        body,
        (tile // wide_block,),
        ins,
        outs,
        scratch=[pltpu.VMEM((count, 4 * q, n), BF16)],
        flops=2 * count * 4 * q * n * tile,
        alias=alias,
    )


def delta_gradients(chain, act_t, quarters, base, blocks, prev, hidden_units):
    tile, tokens = act_t.shape
    q, n = quarters[0].shape[-2:]

    def body(*refs):
        a, parts = refs[0], refs[1:5]
        outs = refs[-2:]
        for k in range(2):
            right = jnp.concatenate([p[k] for p in parts], axis=0)
            outs[k][...] = dot(a[...], right, NN).astype(BF16)

    ins = [(act_t, act_t.shape, lambda j: (0, 0))]
    ins += [(p, (2, q, BLOCK), lambda j: (0, 0, j)) for p in quarters]
    out = ((tile, hidden_units), BF16, (tile, BLOCK), lambda j: (0, base + j))
    return filled(chain, body, blocks, ins, [out, out], prev, 4 * tokens * tile * n)


def down_gradient_rows(chain, cot, quarters, at, base, blocks, prev, hidden_units):
    tokens, tile = cot.shape
    q, n = quarters[0].shape[-2:]

    def body(*refs):
        c, parts = refs[0], refs[1:5]
        left = jnp.concatenate([p[0] for p in parts], axis=0)
        refs[-1][...] = dot(left, c[...], TN).astype(BF16)

    ins = [(cot, cot.shape, lambda j: (0, 0))]
    ins += [(p, (1, q, BLOCK), lambda j: (at, 0, j)) for p in quarters]
    out = ((hidden_units, tile), BF16, (BLOCK, tile), lambda j: (base + j, 0))
    return filled(chain, body, blocks, ins, [out], prev, 2 * tokens * tile * n)


def filled(chain, body, blocks, ins, outs, prev, flops):
    lead = len(ins)
    if prev is None:
        return chain(body, (blocks,), ins, outs, flops=flops)

    def aliased(*refs):
        body(*refs[:lead], *refs[lead + len(prev) :])

    spot = ((16, 128), lambda j: (0, 0))
    return chain(
        aliased,
        (blocks,),
        ins + [(p, *spot) for p in prev],
        outs,
        flops=flops,
        alias={lead + i: i for i in range(len(prev))},
    )


def over_z(chain, keep, got):
    _, four, rows, tile = keep.shape
    block = min(tile, 512)

    def body(k, *refs):
        g, outs = refs[:4], refs[4:]
        for s in range(4):
            outs[s][...] = (k[s] + g[s][...].astype(F32)).astype(outs[s].dtype)

    one = ((four, rows, block), lambda j: (0, 0, j))
    return chain(
        body,
        (tile // block,),
        [(keep, (4, four, rows, block), lambda j: (0, 0, 0, j))] + [(x, *one) for x in got],
        [((four, rows, tile), F32 if s == 0 else BF16, *one) for s in range(4)],
    )


def finish_rows(chain, me, own, got):
    four, rows, tile = own.shape

    def body(s, o, *refs):
        total = o[...]
        for x in refs[:3]:
            total = total + x[...].astype(F32)
        refs[3][...] = total.astype(BF16)

    one = ((1, rows, tile), lambda g, s: (g, 0, 0))
    (out,) = chain(
        body,
        (4,),
        [(x, *one) for x in (own, *got)],
        [((four, rows, tile), BF16, (1, rows, tile), lambda g, s: (s[0] ^ g, 0, 0))],
        scalar=me,
    )
    return out.reshape(four * rows, tile)


def finish_groups(chain, own, got):
    four, rows, tile = own.shape
    block = min(tile, 512)

    def body(o, *refs):
        total = o[...]
        for x in refs[:3]:
            total = total + x[...].astype(F32)
        for g in range(4):
            refs[3 + g][...] = total[g].astype(BF16)

    one = ((four, rows, block), lambda j: (0, 0, j))
    return chain(
        body,
        (tile // block,),
        [(x, *one) for x in (own, *got)],
        [((rows, tile), BF16, (rows, block), lambda j: (0, j))] * 4,
    )


def place_columns(chain, me, groups):
    rows, tile = groups[0].shape

    def body(s, *refs):
        for g in range(4):

            @pl.when(pl.program_id(0) == g)
            def _():
                refs[4][...] = refs[g][...]

    (out,) = chain(
        body,
        (4,),
        [(x, (rows, tile), lambda g, s: (0, 0)) for x in groups],
        [((rows, 4 * tile), BF16, (rows, tile), lambda g, s: (0, s[0] ^ g))],
        scalar=me,
    )
    return out


def gather_wide(own):
    pieces = {0: own}
    pieces[1] = swap_wide(own, 1)
    for k in (2, 4, 6):
        pieces[k] = swap_wide(own, k)
    for k in (2, 4, 6):
        pieces[k + 1] = swap_wide(pieces[k], 1)
    return [pieces[k] for k in range(8)]


def spread(own):
    far = swap(own, 2)
    return [own, swap(own, 1), far, swap(far, 1)]


def chunk_sizes(total):
    count = min(4, total)
    return [total // count + (1 if i < total % count else 0) for i in range(count)]


def local_eight(activations, cotangent, gate_proj, up_proj, down_proj):
    me = lax.axis_index("narrow").astype(jnp.int32).reshape(1)
    rows = activations.shape[0]
    tile, units = gate_proj.shape
    sizes = chunk_sizes(units // BLOCK)
    count = len(sizes)
    bases = [sum(sizes[:c]) for c in range(count)]
    chunks = list(zip(bases, sizes))
    chain = Chain()

    cot_pieces = gather_wide(cotangent)
    tiles = lax.all_to_all(activations, "narrow", split_axis=1, concat_axis=0, tiled=True)
    act_pieces = gather_wide(tiles)

    keep_b, got_b, far_b = {}, {}, {}
    keep_gu, got_gu, far_gu = {}, {}, {}
    hid, delta, at = {}, {}, {}
    out = grad = down_grad = None
    gate_up_grads = None
    last = count - 1

    def back(c):
        keep_b[c], send = back_part(chain, cot, down_proj, *chunks[c])
        got_b[c] = swap(send, 1)

    def back_x(c):
        far_b[c] = swap(add_away(chain, keep_b[c], got_b[c]), 2)

    def gate_up(c):
        keep_gu[c], send = gate_up_part(chain, act, gate_proj, up_proj, *chunks[c])
        got_gu[c] = swap(send, 1)

    def gate_up_x(c):
        far_gu[c] = swap(add_away(chain, keep_gu[c], got_gu[c]), 2)

    def elementwise(c):
        merged = c < count - 2
        res = activate(
            chain, keep_gu[c], got_gu[c], far_gu[c], keep_b[c], got_b[c], far_b[c], merged
        )
        delta[c] = spread(res[0])
        hid[c], at[c] = (delta[c], 2) if merged else (spread(res[1]), 0)

    def add_out(c):
        nonlocal out
        res = summed(chain, hid[c], at[c], [down_proj], *chunks[c], NN, out, c == last, tile)
        out = res if c == last else res[0]

    def add_grad(c):
        nonlocal grad
        weights = [gate_proj, up_proj]
        res = summed(chain, delta[c], 0, weights, *chunks[c], NT, grad, c == last, tile)
        grad = res if c == last else res[0]

    def down_grads(c):
        nonlocal down_grad
        down_grad = down_gradient_rows(chain, cot, hid[c], at[c], *chunks[c], down_grad, units)

    def delta_grads(c):
        nonlocal gate_up_grads
        gate_up_grads = delta_gradients(chain, act_t, delta[c], *chunks[c], gate_up_grads, units)

    def over_y(sends):
        return [swap_wide(s, 1) for s in sends]

    def across_z(keep, got):
        own, *away = over_z(chain, keep, got)
        return own, [swap_wide(a, 2 * (i + 1)) for i, a in enumerate(away)]

    chain.after(tiles)
    cot = arrange(chain, me, cot_pieces, rows, tile)
    arrived = [act_pieces[k] for k in (2, 4, 1, 6, 3, 5, 7)]
    for c in range(count):
        chain.after(*arrived[:1])
        arrived = arrived[1:]
        back(c)
        if c > 0:
            chain.after(*arrived[:1])
            arrived = arrived[1:]
            if c > 2:
                chain.after(far_b[c - 3])
            back_x(c - 1)
    if count > 2:
        chain.after(far_b[count - 3])
    back_x(last)
    if last > 0:
        chain.after(far_b[last - 1])
    act = arrange(chain, me, act_pieces, rows, tile)
    chain.after(far_b[last])
    act_t = act.T
    for c in range(count):
        gate_up(c)
        if c >= 1:
            gate_up_x(c - 1)
        if c >= 2:
            elementwise(c - 2)
    gate_up_x(last)
    if last >= 1:
        elementwise(last - 1)
    todo = list(range(count))
    early = todo[: max(count - 2, 0)]
    late = todo[max(count - 2, 0) :]
    for i, c in enumerate(early):
        if i == len(early) - 1:
            elementwise(last)
        add_out(c)
        add_grad(c)
        if i == len(early) - 1:
            chain.after(hid[late[0]][2])
        down_grads(c)
        if i == len(early) - 1:
            chain.after(hid[last][2])
        delta_grads(c)
    if not early:
        elementwise(last)
    for c in late:
        if c == last:
            chain.after(delta[late[0]][2])
        add_out(c)
    out_keep, *out_sends = out
    out_got = over_y(out_sends)
    for c in late[:-1]:
        add_grad(c)
    down_grads(late[0])
    chain.after(delta[last][2])
    out_own, out_far = across_z(out_keep, out_got)
    add_grad(last)
    grad_keep, *grad_sends = grad
    grad_got = over_y(grad_sends)
    for c in late[1:]:
        down_grads(c)
    delta_grads(late[0])
    block_output = finish_rows(chain, me, out_own, out_far)
    for c in late[1:]:
        delta_grads(c)
    grad_own, grad_far = across_z(grad_keep, grad_got)
    groups = finish_groups(chain, grad_own, grad_far)
    groups = [groups[0]] + [swap(groups[g], g) for g in range(1, 4)]
    input_gradient = place_columns(chain, me, groups)
    return (block_output, input_gradient, *gate_up_grads, down_grad[0])


def scatter_sum(part):
    split = part.reshape(-1, 4, part.shape[0] // 4 // lax.axis_size("wide"), part.shape[-1])
    got = swap(jnp.stack([split[:, 1], split[:, 3]]), 1)
    away = (split[:, 2] + got[1]).astype(BF16)
    return (split[:, 0] + got[0]) + swap(away, 2).astype(F32)


def spread_rows(own):
    return jnp.stack(spread(own), axis=1).reshape(-1, own.shape[-1])


def local_any(activations, cotangent, gate_proj, up_proj, down_proj):
    me = lax.axis_index("narrow")
    rows = activations.shape[0]
    tile = gate_proj.shape[0]
    pieces = [lax.dynamic_slice_in_dim(activations, (me ^ g) * tile, tile, 1) for g in range(4)]
    pieces = [pieces[0]] + [swap(pieces[g], g) for g in range(1, 4)]
    cots = [lax.dynamic_slice_in_dim(cotangent, (me ^ g) * rows, rows, 0) for g in range(4)]

    def gathered(parts):
        return lax.all_gather(jnp.stack(parts), "wide", axis=0, tiled=True).reshape(-1, tile)

    features, upstream = gathered(pieces), gathered(cots)
    gate = scatter_sum(dot(features, gate_proj, NN))
    up = scatter_sum(dot(features, up_proj, NN))
    back = scatter_sum(dot(upstream, down_proj, NT))
    active, slope = silu_parts(gate)
    gate_delta = spread_rows((back * up * slope).astype(BF16))
    up_delta = spread_rows((back * active).astype(BF16))
    hidden = spread_rows((active * up).astype(BF16))

    def landed(total):
        got = lax.psum_scatter(total, "wide", scatter_dimension=0, tiled=True)
        return got.astype(BF16).reshape(4, rows, tile)

    grad = landed(dot(gate_delta, gate_proj, NT) + dot(up_delta, up_proj, NT))
    out = landed(dot(hidden, down_proj, NN))
    gate_gradient = dot(features, gate_delta, TN).astype(BF16)
    up_gradient = dot(features, up_delta, TN).astype(BF16)
    down_gradient = dot(hidden, upstream, TN).astype(BF16)

    block_output = jnp.concatenate(
        [lax.dynamic_index_in_dim(out, me ^ g, 0, keepdims=False) for g in range(4)]
    )
    grads = jnp.stack([grad[0]] + [swap(grad[g], g) for g in range(1, 4)])
    input_gradient = jnp.concatenate(
        [lax.dynamic_index_in_dim(grads, me ^ g, 0, keepdims=False) for g in range(4)], axis=1
    )
    return (block_output, input_gradient, gate_gradient, up_gradient, down_gradient)


def local(activations, cotangent, gate_proj, up_proj, down_proj):
    args = (activations, cotangent, gate_proj, up_proj, down_proj)
    rows, (tile, units) = activations.shape[0], gate_proj.shape
    fits = lax.axis_size("wide") == 8 and rows % 16 == 0
    if fits and tile % BLOCK == 0 and units % BLOCK == 0:
        return local_eight(*args)
    return local_any(*args)


def solution(mesh):
    placed = (
        P(("wide", "narrow"), None),
        P("wide", "narrow"),
        P("narrow", "wide"),
        P("narrow", "wide"),
        P("wide", "narrow"),
    )
    return jax.shard_map(
        local,
        mesh=mesh,
        in_specs=placed,
        out_specs=(
            P("wide", "narrow"),
            P(("wide", "narrow"), None),
            P("narrow", "wide"),
            P("narrow", "wide"),
            P("wide", "narrow"),
        ),
        check_vma=False,
    )
```

time: 620 us -> 421 us (0.68)
  waiting for transfers between devices: 391 us -> 149 us
  Pallas kernels: 0 us -> 167 us
  matrix products: 137 us -> 0 us
  starting transfers between devices: 22 us -> 66 us
  other arithmetic: 29.6 us -> 0 us
  local copies, waits for them, and re-layouts: 15.6 us -> 35.2 us
  between operations: 15.4 us -> 1.39 us
    reduce_scatter x4 -> x0, waiting for transfers between devices: 186 us -> none  [landed(): got = lax.psum_scatter(total, 'wide', scatter_dimension=0, tiled=True)]
    pallas_call x0 -> x43, Pallas kernels: none -> 167 us  [__call__(): pl.pallas_call(kernel, grid_spec=pltpu.PrefetchScalarGridSpec(num_scalar_...]
    dot_general x15 -> x0, matrix products: 137 us -> none  [the longest x6 50.1 us: contract_cols(): lax.dot_general(left, right, (((1,), (1,)), ((), ())), preferred_element_...]
    all_gather x4 -> x0, waiting for transfers between devices: 120 us -> none  [gathered(): return lax.all_gather(mine, 'wide', axis=0, tiled=True).reshape(-1, tile)]
    ppermute x0 -> x28, waiting for transfers between devices: none -> 77 us  [swap_wide(): return lax.ppermute(value, 'wide', [(i, i ^ mask) for i in range(8)])]
    ppermute x0 -> x28, starting transfers between devices: none -> 43.2 us  [swap_wide(): return lax.ppermute(value, 'wide', [(i, i ^ mask) for i in range(8)])]
    unnamed x44 -> x144, local copies, waits for them, and re-layouts: 8.24 us -> 29.6 us
    ppermute x30 -> x37, waiting for transfers between devices: 85.1 us -> 71.5 us  [swap(): return lax.ppermute(value, 'narrow', [(i, i ^ mask) for i in range(4)])]
  transfers between devices with their start and end apart: 38 -> 66, of which waited for: 18 -> 26; matrix products, arithmetic and copies ran while one was open for 28% -> 1% of each run, Pallas kernels for 0% -> 36%
where the time goes in v2:
time: 421 us; the launch traced here: 418 us
  Pallas kernels  167 us (40%)
  waiting for transfers between devices  149 us (35%)
  starting transfers between devices  66 us (16%)
  local copies, waits for them, and re-layouts  35.2 us (8%)
    pallas_call x43, Pallas kernels, __call__(): pl.pallas_call(kernel, grid_spec=pltpu.PrefetchScalarGridSpec(num_scalar_...  167 us
    ppermute x28, waiting for transfers between devices, swap_wide(): return lax.ppermute(value, 'wide', [(i, i ^ mask) for i in range(8)])  77 us
    ppermute x37, waiting for transfers between devices, swap(): return lax.ppermute(value, 'narrow', [(i, i ^ mask) for i in range(4)])  71.5 us
    ppermute x28, starting transfers between devices, swap_wide(): return lax.ppermute(value, 'wide', [(i, i ^ mask) for i in range(8)])  43.2 us
    unnamed x144, local copies, waits for them, and re-layouts  29.6 us
    ppermute x37, starting transfers between devices, swap(): return lax.ppermute(value, 'narrow', [(i, i ^ mask) for i in range(4)])  19.4 us
  transfers between devices with their start and end apart: 66, of which 26 were waited for; matrix products, arithmetic and copies ran while one was open for 1% of the time, Pallas kernels for 36%

profile of v2, /device:TPU:0, one launch (start us, length us, event | category | flops | bytes accessed | tf_op | source)
XLA Modules:
  0.0 417.6 jit_solution(6780559246102581589)
XLA Ops:
  0.6 4.1 collective-permute-start.10
  8.0 3.4 all-to-all-start
  13.0 10.4 %collective-permute-done.10.refs_5_ = bf16[64,2048]{1,0:T(8,128)(2,1)S(1)} collective-permute-done((bf16[64,2048]{1,0:T(8,128)(2,1)}, bf16[64,2048]{1,0:T(8,128)(2,1)S(1)}, u32[]{:S(2)}, u32[]{:S(2)}) %collective-permute-start.10) | collective-permute-done | bytes 262176 | tf_op jit(solution)/shard_map/ppermute | solution.py:32
  27.3 3.7 collective-permute-start.1
  33.3 4.9 %collective-permute-done.13.refs_8_ = bf16[64,2048]{1,0:T(8,128)(2,1)S(1)} collective-permute-done((bf16[64,2048]{1,0:T(8,128)(2,1)S(1)}, bf16[64,2048]{1,0:T(8,128)(2,1)S(1)}, u32[]{:S(2)}, u32[]{:S(2)}) %collective-permute-start.13) | collective-permute-done | bytes 262176 | tf_op jit(solution)/shard_map/ppermute | solution.py:32
  46.9 4.9 %shard_map.93 = (f32[2,128,1024]{2,1,0:T(8,128)S(1)}, f32[2,128,1024]{2,1,0:T(8,128)S(1)}, f32[8,128]{1,0:T(8,128)S(1)}) custom-call(bf16[512,2048]{1,0:T(8,128)(2,1)S(1)} %bitcast.12, bf16[3328,2048]{1,0:T(8,128)(2,1)} %refs_6_.13, bf16[64,2048]{1,0:T(8,128)(2,1)S(1)} %collective-permute-done.1.refs_2_.refs_3_, f32[8,128]{1,0:T(8,128)S(1)} %get-tuple-element.122.refs_3_), custom_call_target="tpu_custom_call" | custom-call | flops 1 | bytes 1 | tf_op jit(solution)/shard_map/pallas_call | solution.py:65
  51.9 3.4 collective-permute-start.3
  55.3 12.5 %collective-permute-done.3.refs_2_.refs_5_ = bf16[64,2048]{1,0:T(8,128)(2,1)S(1)} collective-permute-done((bf16[64,2048]{1,0:T(8,128)(2,1)S(1)}, bf16[64,2048]{1,0:T(8,128)(2,1)S(1)}, u32[]{:S(2)}, u32[]{:S(2)}) %collective-permute-start.3) | collective-permute-done | bytes 262176 | tf_op jit(solution)/shard_map/ppermute | solution.py:32
  67.8 4.0 shard_map.94
  73.5 3.6 collective-permute-start.5
  77.6 3.5 collective-permute-done.refs_2_
  83.8 4.0 shard_map.96
  88.2 3.7 collective-permute-done.4.refs_2_.refs_6_
  91.9 4.0 shard_map.98
  99.6 5.1 %collective-permute-done.6.refs_2_.refs_8_ = bf16[64,2048]{1,0:T(8,128)(2,1)S(1)} collective-permute-done((bf16[64,2048]{1,0:T(8,128)(2,1)S(1)}, bf16[64,2048]{1,0:T(8,128)(2,1)S(1)}, u32[]{:S(2)}, u32[]{:S(2)}) %collective-permute-start.6) | collective-permute-done | bytes 262176 | tf_op jit(solution)/shard_map/ppermute | solution.py:32
  118.6 9.2 %shard_map.102 = (f32[2,2,128,1024]{3,2,1,0:T(8,128)S(1)}, f32[2,2,128,1024]{3,2,1,0:T(8,128)}, f32[8,128]{1,0:T(8,128)S(1)}) custom-call(bf16[512,2048]{1,0:T(8,128)(2,1)} %bitcast.24, bf16[2048,3328]{1,0:T(8,128)(2,1)} %refs_6_.15, bf16[2048,3328]{1,0:T(8,128)(2,1)} %refs_9_.7, bf16[128,768]{1,0:T(8,128)(2,1)S(1)} %collective-permute-done.21.refs_3_.refs_5_, ...), custom_call_target="tpu_custom_call" | custom-call | flops 1 | bytes 1 | tf_op jit(solution)/shard_map/pallas_call | solution.py:65
  127.9 6.7 %shard_map.103 = (f32[2,2,128,768]{3,2,1,0:T(8,128)S(1)}, f32[2,2,128,768]{3,2,1,0:T(8,128)}, f32[8,128]{1,0:T(8,128)S(1)}) custom-call(bf16[512,2048]{1,0:T(8,128)(2,1)S(1)} %bitcast.26, bf16[2048,3328]{1,0:T(8,128)(2,1)} %refs_6_.15, bf16[2048,3328]{1,0:T(8,128)(2,1)} %refs_9_.7, f32[8,128]{1,0:T(8,128)S(1)} %get-tuple-element.147.refs_3_), custom_call_target="tpu_custom_call" | custom-call | flops 1 | bytes 1 | tf_op jit(solution)/shard_map/pallas_call | solution.py:65
  138.4 6.7 %shard_map.105 = (f32[2,2,128,768]{3,2,1,0:T(8,128)S(1)}, f32[2,2,128,768]{3,2,1,0:T(8,128)}, f32[8,128]{1,0:T(8,128)S(1)}) custom-call(bf16[512,2048]{1,0:T(8,128)(2,1)S(1)} %bitcast.27, bf16[2048,3328]{1,0:T(8,128)(2,1)} %refs_6_.15, bf16[2048,3328]{1,0:T(8,128)(2,1)} %refs_9_.7, f32[8,128]{1,0:T(8,128)S(1)} %get-tuple-element.152.refs_3_), custom_call_target="tpu_custom_call" | custom-call | flops 1 | bytes 1 | tf_op jit(solution)/shard_map/pallas_call | solution.py:65
  146.7 4.6 %collective-permute-done.23.refs_2_ = bf16[2,128,1024]{2,1,0:T(8,128)(2,1)S(1)} collective-permute-done((bf16[2,128,1024]{2,1,0:T(8,128)(2,1)}, bf16[2,128,1024]{2,1,0:T(8,128)(2,1)S(1)}, u32[]{:S(2)}, u32[]{:S(2)}) %collective-permute-start.23) | collective-permute-done | bytes 524320 | tf_op jit(solution)/shard_map/ppermute | solution.py:28
  158.0 6.8 %shard_map.108 = (f32[2,2,128,768]{3,2,1,0:T(8,128)S(1)}, f32[2,2,128,768]{3,2,1,0:T(8,128)}, f32[8,128]{1,0:T(8,128)S(1)}) custom-call(bf16[512,2048]{1,0:T(8,128)(2,1)S(1)} %bitcast.28, bf16[2048,3328]{1,0:T(8,128)(2,1)} %refs_6_.15, bf16[2048,3328]{1,0:T(8,128)(2,1)} %refs_9_.7, f32[8,128]{1,0:T(8,128)S(1)} %get-tuple-element.155.refs_3_), custom_call_target="tpu_custom_call" | custom-call | flops 1 | bytes 1 | tf_op jit(solution)/shard_map/pallas_call | solution.py:65
  166.9 18.3 %collective-permute-done.30.refs_2_.refs_3_ = bf16[3,128,1024]{2,1,0:T(8,128)(2,1)S(1)} collective-permute-done((bf16[3,128,1024]{2,1,0:T(8,128)(2,1)S(1)}, bf16[3,128,1024]{2,1,0:T(8,128)(2,1)S(1)}, u32[]{:S(2)}, u32[]{:S(2)}) %collective-permute-start.30) | collective-permute-done | bytes 786464 | tf_op jit(solution)/shard_map/ppermute | solution.py:28
  187.6 5.7 %collective-permute-done.26.refs_2_ = bf16[2,128,768]{2,1,0:T(8,128)(2,1)S(1)} collective-permute-done((bf16[2,128,768]{2,1,0:T(8,128)(2,1)S(1)}, bf16[2,128,768]{2,1,0:T(8,128)(2,1)S(1)}, u32[]{:S(2)}, u32[]{:S(2)}) %collective-permute-start.26) | collective-permute-done | bytes 393248 | tf_op jit(solution)/shard_map/ppermute | solution.py:28
  202.3 19.6 %collective-permute-done.32.refs_2_ = bf16[2,128,768]{2,1,0:T(8,128)(2,1)S(1)} collective-permute-done((bf16[2,128,768]{2,1,0:T(8,128)(2,1)S(1)}, bf16[2,128,768]{2,1,0:T(8,128)(2,1)S(1)}, u32[]{:S(2)}, u32[]{:S(2)}) %collective-permute-start.32) | collective-permute-done | bytes 393248 | tf_op jit(solution)/shard_map/ppermute | solution.py:28
  233.2 5.1 %collective-permute-done.37.refs_6_.refs_2_.refs_3_ = bf16[1,128,768]{2,1,0:T(8,128)(2,1)} collective-permute-done((bf16[1,128,768]{2,1,0:T(8,128)(2,1)}, bf16[1,128,768]{2,1,0:T(8,128)(2,1)}, u32[]{:S(2)}, u32[]{:S(2)}) %collective-permute-start.37) | collective-permute-done | bytes 196640 | tf_op jit(solution)/shard_map/ppermute | solution.py:28
  238.3 3.9 copy.30
  245.6 6.1 %shard_map.113 = (f32[512,2048]{1,0:T(8,128)}, f32[8,128]{1,0:T(8,128)S(1)}) custom-call(bf16[3,128,1024]{2,1,0:T(8,128)(2,1)S(1)} %get-tuple-element.165.refs_0_.refs_1_, bf16[3,128,1024]{2,1,0:T(8,128)(2,1)S(1)} %copy-done.11, bf16[3,128,1024]{2,1,0:T(8,128)(2,1)S(1)} %copy-done.8, bf16[3,128,1024]{2,1,0:T(8,128)(2,1)S(1)} %copy-done.14, ...), custom_call_target="tpu_custom_call" | custom-call | flops 1 | bytes 1 | tf_op jit(solution)/shard_map/pallas_call | solution.py:65
  251.8 9.0 %shard_map.114 = (f32[512,2048]{1,0:T(8,128)}, f32[8,128]{1,0:T(8,128)S(1)}) custom-call(bf16[3,128,1024]{2,1,0:T(8,128)(2,1)S(1)} %get-tuple-element.165.refs_0_.refs_1_, bf16[3,128,1024]{2,1,0:T(8,128)(2,1)S(1)} %copy-done.11, bf16[3,128,1024]{2,1,0:T(8,128)(2,1)S(1)} %copy-done.8, bf16[3,128,1024]{2,1,0:T(8,128)(2,1)S(1)} %copy-done.14, ...), custom_call_target="tpu_custom_call" | custom-call | flops 1 | bytes 1 | tf_op jit(solution)/shard_map/pallas_call | solution.py:65
  260.8 4.3 %shard_map.115 = (bf16[3328,2048]{1,0:T(8,128)(2,1)}, f32[8,128]{1,0:T(8,128)S(1)}) custom-call(bf16[512,2048]{1,0:T(8,128)(2,1)S(1)} %bitcast.16, bf16[3,128,1024]{2,1,0:T(8,128)(2,1)S(1)} %get-tuple-element.165.refs_0_.refs_1_, bf16[3,128,1024]{2,1,0:T(8,128)(2,1)S(1)} %copy-done.12, bf16[3,128,1024]{2,1,0:T(8,128)(2,1)S(1)} %copy-done.9, ...), custom_call_target="tpu_custom_call" | custom-call | flops 1 | bytes 1 | tf_op jit(solution)/shard_map/pallas_call | solution.py:65
  265.1 6.7 %shard_map.116 = (bf16[2048,3328]{1,0:T(8,128)(2,1)}, bf16[2048,3328]{1,0:T(8,128)(2,1)}, f32[8,128]{1,0:T(8,128)S(1)}) custom-call(bf16[2048,512]{1,0:T(8,128)(2,1)S(1)} %bitcast.20, bf16[3,128,1024]{2,1,0:T(8,128)(2,1)S(1)} %get-tuple-element.165.refs_0_.refs_1_, bf16[3,128,1024]{2,1,0:T(8,128)(2,1)S(1)} %copy-done.12, ...), custom_call_target="tpu_custom_call" | custom-call | flops 1 | bytes 1 | tf_op jit(solution)/shard_map/pallas_call | solution.py:65
  276.4 5.7 %collective-permute-done.34.refs_7_.refs_2_.refs_3_ = bf16[1,128,768]{2,1,0:T(8,128)(2,1)S(1)} collective-permute-done((bf16[1,128,768]{2,1,0:T(8,128)(2,1)S(1)}, bf16[1,128,768]{2,1,0:T(8,128)(2,1)S(1)}, u32[]{:S(2)}, u32[]{:S(2)}) %collective-permute-start.34) | collective-permute-done | bytes 196640 | tf_op jit(solution)/shard_map/ppermute | solution.py:28
  282.7 7.0 %shard_map.118 = (f32[512,2048]{1,0:T(8,128)}, f32[8,128]{1,0:T(8,128)S(1)}) custom-call(bf16[3,128,768]{2,1,0:T(8,128)(2,1)S(1)} %get-tuple-element.175.refs_0_.refs_1_, bf16[3,128,768]{2,1,0:T(8,128)(2,1)} %collective-permute-done.39.refs_1_.refs_2_, bf16[3,128,768]{2,1,0:T(8,128)(2,1)} %collective-permute-done.40.refs_2_.refs_3_, ...), custom_call_target="tpu_custom_call", output_to_operand_aliasing={{0}: (7, {})} | custom-call | flops 1 | bytes 1 | tf_op jit(solution)/shard_map/pallas_call | solution.py:65
  289.7 9.1 %shard_map.119 = (f32[512,2048]{1,0:T(8,128)}, f32[8,128]{1,0:T(8,128)S(1)}) custom-call(bf16[3,128,768]{2,1,0:T(8,128)(2,1)S(1)} %get-tuple-element.175.refs_0_.refs_1_, bf16[3,128,768]{2,1,0:T(8,128)(2,1)} %collective-permute-done.39.refs_1_.refs_2_, ...), custom_call_target="tpu_custom_call", output_to_operand_aliasing={{0}: (10, {})} | custom-call | flops 1 | bytes 1 | tf_op jit(solution)/shard_map/pallas_call | solution.py:65
  298.7 4.6 %shard_map.120 = (bf16[3328,2048]{1,0:T(8,128)(2,1)}, f32[8,128]{1,0:T(8,128)S(1)}) custom-call(bf16[512,2048]{1,0:T(8,128)(2,1)S(1)} %bitcast.17, bf16[3,128,768]{2,1,0:T(8,128)(2,1)S(1)} %get-tuple-element.175.refs_0_.refs_1_, bf16[3,128,768]{2,1,0:T(8,128)(2,1)} %collective-permute-done.39.refs_1_.refs_2_, ...), custom_call_target="tpu_custom_call", output_to_operand_aliasing={{0}: (5, {})} | custom-call | flops 1 | bytes 1 | tf_op jit(solution)/shard_map/pallas_call | solution.py:65
  303.3 6.6 %shard_map.121 = (bf16[2048,3328]{1,0:T(8,128)(2,1)}, bf16[2048,3328]{1,0:T(8,128)(2,1)}, f32[8,128]{1,0:T(8,128)S(1)}) custom-call(bf16[2048,512]{1,0:T(8,128)(2,1)S(1)} %bitcast.21, bf16[3,128,768]{2,1,0:T(8,128)(2,1)S(1)} %get-tuple-element.175.refs_0_.refs_1_, ...), custom_call_target="tpu_custom_call", output_to_operand_aliasing={{0}: (5, {}), {1}: (6, {})} | custom-call | flops 1 | bytes 1 | tf_op jit(solution)/shard_map/pallas_call | solution.py:65
  309.9 4.8 %shard_map.122 = (f32[512,2048]{1,0:T(8,128)S(1)}, f32[8,128]{1,0:T(8,128)S(1)}) custom-call(bf16[1,128,768]{2,1,0:T(8,128)(2,1)} %get-tuple-element.174.refs_0_.refs_1_, bf16[1,128,768]{2,1,0:T(8,128)(2,1)} %collective-permute-done.36.refs_1_.refs_2_, ...), custom_call_target="tpu_custom_call", output_to_operand_aliasing={{0}: (7, {})} | custom-call | flops 1 | bytes 1 | tf_op jit(solution)/shard_map/pallas_call | solution.py:65
  316.9 5.5 %shard_map.123 = (f32[4,4,16,2048]{3,2,1,0:T(8,128)S(1)}, bf16[4,16,2048]{2,1,0:T(8,128)(2,1)S(1)}, bf16[4,16,2048]{2,1,0:T(8,128)(2,1)S(1)}, bf16[4,16,2048]{2,...) custom-call(bf16[1,128,768]{2,1,0:T(8,128)(2,1)S(1)} %get-tuple-element.173.refs_0_.refs_1_, ...), custom_call_target="tpu_custom_call" | custom-call | flops 1 | bytes 1 | tf_op jit(solution)/shard_map/pallas_call | solution.py:65
  326.5 5.1 %collective-permute-done.43.refs_1_ = bf16[4,16,2048]{2,1,0:T(8,128)(2,1)S(1)} collective-permute-done((bf16[4,16,2048]{2,1,0:T(8,128)(2,1)S(1)}, bf16[4,16,2048]{2,1,0:T(8,128)(2,1)S(1)}, u32[]{:S(2)}, u32[]{:S(2)}) %collective-permute-start.43) | collective-permute-done | bytes 262176 | tf_op jit(solution)/shard_map/ppermute | solution.py:32
  331.6 6.9 %shard_map.124 = (f32[512,2048]{1,0:T(8,128)S(1)}, f32[8,128]{1,0:T(8,128)S(1)}) custom-call(bf16[2,128,768]{2,1,0:T(8,128)(2,1)} %get-tuple-element.188.refs_0_.refs_1_, bf16[2,128,768]{2,1,0:T(8,128)(2,1)S(1)} %collective-permute-done.48.refs_1_.refs_2_, ...), custom_call_target="tpu_custom_call", output_to_operand_aliasing={{0}: (10, {})} | custom-call | flops 1 | bytes 1 | tf_op jit(solution)/shard_map/pallas_call | solution.py:65
  338.5 4.8 %shard_map.125 = (bf16[3328,2048]{1,0:T(8,128)(2,1)}, f32[8,128]{1,0:T(8,128)S(1)}) custom-call(bf16[512,2048]{1,0:T(8,128)(2,1)S(1)} %bitcast.18, bf16[1,128,768]{2,1,0:T(8,128)(2,1)} %get-tuple-element.174.refs_0_.refs_1_, bf16[1,128,768]{2,1,0:T(8,128)(2,1)} %collective-permute-done.36.refs_1_.refs_2_, ...), custom_call_target="tpu_custom_call", output_to_operand_aliasing={{0}: (5, {})} | custom-call | flops 1 | bytes 1 | tf_op jit(solution)/shard_map/pallas_call | solution.py:65
  343.3 4.3 %collective-permute-done.46.refs_4_ = bf16[4,16,2048]{2,1,0:T(8,128)(2,1)S(1)} collective-permute-done((bf16[4,16,2048]{2,1,0:T(8,128)(2,1)S(1)}, bf16[4,16,2048]{2,1,0:T(8,128)(2,1)S(1)}, u32[]{:S(2)}, u32[]{:S(2)}) %collective-permute-start.46) | collective-permute-done | bytes 262176 | tf_op jit(solution)/shard_map/ppermute | solution.py:32
  349.0 3.4 collective-permute-start.51
  352.7 7.6 %shard_map.127 = (f32[4,4,16,2048]{3,2,1,0:T(8,128)S(1)}, bf16[4,16,2048]{2,1,0:T(8,128)(2,1)S(1)}, bf16[4,16,2048]{2,1,0:T(8,128)(2,1)S(1)}, bf16[4,16,2048]{2,...) custom-call(bf16[2,128,768]{2,1,0:T(8,128)(2,1)} %get-tuple-element.195.refs_0_.refs_1_, ...), custom_call_target="tpu_custom_call" | custom-call | flops 1 | bytes 1 | tf_op jit(solution)/shard_map/pallas_call | solution.py:65
  363.0 7.9 %collective-permute-done.51.refs_3_ = bf16[4,16,2048]{2,1,0:T(8,128)(2,1)S(1)} collective-permute-done((bf16[4,16,2048]{2,1,0:T(8,128)(2,1)S(1)}, bf16[4,16,2048]{2,1,0:T(8,128)(2,1)S(1)}, u32[]{:S(2)}, u32[]{:S(2)}) %collective-permute-start.51) | collective-permute-done | bytes 262176 | tf_op jit(solution)/shard_map/ppermute | solution.py:32
  371.4 4.2 %shard_map.128 = (bf16[3328,2048]{1,0:T(8,128)(2,1)}, f32[8,128]{1,0:T(8,128)S(1)}) custom-call(bf16[512,2048]{1,0:T(8,128)(2,1)S(1)} %bitcast.19, bf16[1,128,768]{2,1,0:T(8,128)(2,1)S(1)} %copy-done.48, bf16[1,128,768]{2,1,0:T(8,128)(2,1)S(1)} %copy-done.50, bf16[1,128,768]{2,1,0:T(8,128)(2,1)S(1)} %copy-done.44, ...), custom_call_target="tpu_custom_call", output_to_operand_aliasing={{0}: (5, {})} | custom-call | flops 1 | bytes 1 | tf_op jit(solution)/shard_map/pallas_call | solution.py:65
  375.6 6.7 %shard_map.129 = (bf16[2048,3328]{1,0:T(8,128)(2,1)}, bf16[2048,3328]{1,0:T(8,128)(2,1)}, f32[8,128]{1,0:T(8,128)S(1)}) custom-call(bf16[2048,512]{1,0:T(8,128)(2,1)S(1)} %bitcast.22, bf16[2,128,768]{2,1,0:T(8,128)(2,1)} %get-tuple-element.188.refs_0_.refs_1_, bf16[2,128,768]{2,1,0:T(8,128)(2,1)S(1)} %copy-done.46, ...), custom_call_target="tpu_custom_call", output_to_operand_aliasing={{0}: (5, {}), {1}: (6, {})} | custom-call | flops 1 | bytes 1 | tf_op jit(solution)/shard_map/pallas_call | solution.py:65
  383.7 6.1 %shard_map.131 = (bf16[2048,3328]{1,0:T(8,128)(2,1)}, bf16[2048,3328]{1,0:T(8,128)(2,1)}, f32[8,128]{1,0:T(8,128)S(1)}) custom-call(bf16[2048,512]{1,0:T(8,128)(2,1)S(1)} %bitcast.23, bf16[2,128,768]{2,1,0:T(8,128)(2,1)} %get-tuple-element.195.refs_0_.refs_1_, ...), custom_call_target="tpu_custom_call", output_to_operand_aliasing={{0}: (5, {}), {1}: (6, {})} | custom-call | flops 1 | bytes 1 | tf_op jit(solution)/shard_map/pallas_call | solution.py:65
  394.9 3.4 collective-permute-done.59.refs_1_
  398.3 11.9 %collective-permute-done.60.refs_2_ = bf16[4,16,2048]{2,1,0:T(8,128)(2,1)S(1)} collective-permute-done((bf16[4,16,2048]{2,1,0:T(8,128)(2,1)S(1)}, bf16[4,16,2048]{2,1,0:T(8,128)(2,1)S(1)}, u32[]{:S(2)}, u32[]{:S(2)}) %collective-permute-start.60) | collective-permute-done | bytes 262176 | tf_op jit(solution)/shard_map/ppermute | solution.py:32
  (273 shorter events, 112.7 us)
Async XLA Ops:
  0.6 22.7 %collective-permute-start.10 = (bf16[64,2048]{1,0:T(8,128)(2,1)}, bf16[64,2048]{1,0:T(8,128)(2,1)S(1)}, u32[]{:S(2)}, u32[]{:S(2)}) collective-permute-start(bf16[64,2048]{1,0:T(8,128)(2,1)} %refs_1_.9), channel_id=1, source_target_pairs={{0,16},{4,20},{8,24},{12,28},{16,0},{20,4},{24,8},{28,12},{1,17},{... | collective-permute-start | bytes 786440 | tf_op jit(solution)/shard_map/ppermute | solution.py:32
  4.7 20.5 %collective-permute-start.12 = (bf16[64,2048]{1,0:T(8,128)(2,1)}, bf16[64,2048]{1,0:T(8,128)(2,1)S(1)}, u32[]{:S(2)}, u32[]{:S(2)}) collective-permute-start(bf16[64,2048]{1,0:T(8,128)(2,1)} %refs_1_.9), channel_id=1, source_target_pairs={{0,24},{4,28},{8,16},{12,20},{16,8},{20,12},{24,0},{28,4},{1,25},{... | collective-permute-start | bytes 786440 | tf_op jit(solution)/shard_map/ppermute | solution.py:32
  6.1 19.3 %collective-permute-start.8 = (bf16[64,2048]{1,0:T(8,128)(2,1)}, bf16[64,2048]{1,0:T(8,128)(2,1)S(1)}, u32[]{:S(2)}, u32[]{:S(2)}) collective-permute-start(bf16[64,2048]{1,0:T(8,128)(2,1)} %refs_1_.9), channel_id=1, source_target_pairs={{0,8},{4,12},{8,0},{12,4},{16,24},{20,28},{24,16},{28,20},{1,9},{5... | collective-permute-start | bytes 786440 | tf_op jit(solution)/shard_map/ppermute | solution.py:32
  8.0 19.3 %all-to-all-start = ((bf16[16,4,2048]{2,0,1:T(8,128)(2,1)}), bf16[16,4,2048]{2,0,1:T(8,128)(2,1)S(1)}, u32[]{:S(2)}, u32[]{:S(2)}) async-start(bf16[16,4,2048]{2,0,1:T(8,128)(2,1)} %bitcast.11), calls=%async_computation | async-start | bytes 524288 | tf_op jit(solution)/shard_map/all_to_all | solution.py:423
  11.4 19.6 %collective-permute-start.7 = (bf16[64,2048]{1,0:T(8,128)(2,1)}, bf16[64,2048]{1,0:T(8,128)(2,1)S(1)}, u32[]{:S(2)}, u32[]{:S(2)}) collective-permute-start(bf16[64,2048]{1,0:T(8,128)(2,1)} %refs_1_.9), channel_id=1, source_target_pairs={{0,4},{4,0},{8,12},{12,8},{16,20},{20,16},{24,28},{28,24},{1,5},{5... | collective-permute-start | bytes 786440 | tf_op jit(solution)/shard_map/ppermute | solution.py:32
  25.2 13.0 %collective-permute-start.13 = (bf16[64,2048]{1,0:T(8,128)(2,1)S(1)}, bf16[64,2048]{1,0:T(8,128)(2,1)S(1)}, u32[]{:S(2)}, u32[]{:S(2)}) collective-permute-start(bf16[64,2048]{1,0:T(8,128)(2,1)S(1)} %collective-permute-done.12.refs_7_), channel_id=1, source_target_pairs={{0,4},{4,0},{8,12},{12,8},{16,20},{20,16},{24,28},{28,24},{1,5},{5... | collective-permute-start | bytes 786440 | tf_op jit(solution)/shard_map/ppermute | solution.py:32
  25.4 15.9 %collective-permute-start.9 = (bf16[64,2048]{1,0:T(8,128)(2,1)S(1)}, bf16[64,2048]{1,0:T(8,128)(2,1)S(1)}, u32[]{:S(2)}, u32[]{:S(2)}) collective-permute-start(bf16[64,2048]{1,0:T(8,128)(2,1)S(1)} %collective-permute-done.8.refs_3_), channel_id=1, source_target_pairs={{0,4},{4,0},{8,12},{12,8},{16,20},{20,16},{24,28},{28,24},{1,5},{5... | collective-permute-start | bytes 786440 | tf_op jit(solution)/shard_map/ppermute | solution.py:32
  27.3 19.7 %collective-permute-start.1 = (bf16[64,2048]{1,0:T(8,128)(2,1)S(1)}, bf16[64,2048]{1,0:T(8,128)(2,1)S(1)}, u32[]{:S(2)}, u32[]{:S(2)}) collective-permute-start(bf16[64,2048]{1,0:T(8,128)(2,1)S(1)} %bitcast.29), channel_id=1, source_target_pairs={{0,8},{4,12},{8,0},{12,4},{16,24},{20,28},{24,16},{28,20},{1,9},{5... | collective-permute-start | bytes 786440 | tf_op jit(solution)/shard_map/ppermute | solution.py:32
  51.8 30.8 %collective-permute-start.14 = (f32[2,128,1024]{2,1,0:T(8,128)S(1)}, f32[2,128,1024]{2,1,0:T(8,128)S(1)}, u32[]{:S(2)}, u32[]{:S(2)}) collective-permute-start(f32[2,128,1024]{2,1,0:T(8,128)S(1)} %get-tuple-element.124), channel_id=1, source_target_pairs={{0,1},{1,0},{2,3},{3,2},{4,5},{5,4},{6,7},{7,6},{8,9},{9,8},{10,11... | collective-permute-start | bytes 3145736 | tf_op jit(solution)/shard_map/ppermute | solution.py:28
  51.9 16.0 %collective-permute-start.3 = (bf16[64,2048]{1,0:T(8,128)(2,1)S(1)}, bf16[64,2048]{1,0:T(8,128)(2,1)S(1)}, u32[]{:S(2)}, u32[]{:S(2)}) collective-permute-start(bf16[64,2048]{1,0:T(8,128)(2,1)S(1)} %bitcast.31), channel_id=1, source_target_pairs={{0,16},{4,20},{8,24},{12,28},{16,0},{20,4},{24,8},{28,12},{1,17},{... | collective-permute-start | bytes 786440 | tf_op jit(solution)/shard_map/ppermute | solution.py:32
  71.9 16.1 %collective-permute-start.17 = (f32[2,128,768]{2,1,0:T(8,128)S(1)}, f32[2,128,768]{2,1,0:T(8,128)S(1)}, u32[]{:S(2)}, u32[]{:S(2)}) collective-permute-start(f32[2,128,768]{2,1,0:T(8,128)S(1)} %get-tuple-element.132), channel_id=1, source_target_pairs={{0,1},{1,0},{2,3},{3,2},{4,5},{5,4},{6,7},{7,6},{8,9},{9,8},{10,11... | collective-permute-start | bytes 2359304 | tf_op jit(solution)/shard_map/ppermute | solution.py:28
  87.9 18.9 %collective-permute-start.15 = (f32[2,128,768]{2,1,0:T(8,128)S(1)}, f32[2,128,768]{2,1,0:T(8,128)S(1)}, u32[]{:S(2)}, u32[]{:S(2)}) collective-permute-start(f32[2,128,768]{2,1,0:T(8,128)S(1)} %get-tuple-element.129), channel_id=1, source_target_pairs={{0,1},{1,0},{2,3},{3,2},{4,5},{5,4},{6,7},{7,6},{8,9},{9,8},{10,11... | collective-permute-start | bytes 2359304 | tf_op jit(solution)/shard_map/ppermute | solution.py:28
  95.9 15.0 %collective-permute-start.19 = (f32[2,128,768]{2,1,0:T(8,128)S(1)}, f32[2,128,768]{2,1,0:T(8,128)S(1)}, u32[]{:S(2)}, u32[]{:S(2)}) collective-permute-start(f32[2,128,768]{2,1,0:T(8,128)S(1)} %get-tuple-element.138), channel_id=1, source_target_pairs={{0,1},{1,0},{2,3},{3,2},{4,5},{5,4},{6,7},{7,6},{8,9},{9,8},{10,11... | collective-permute-start | bytes 2359304 | tf_op jit(solution)/shard_map/ppermute | solution.py:28
  99.1 11.9 %collective-permute-start.20 = (bf16[128,768]{1,0:T(8,128)(2,1)S(1)}, bf16[128,768]{1,0:T(8,128)(2,1)S(1)}, u32[]{:S(2)}, u32[]{:S(2)}) collective-permute-start(bf16[128,768]{1,0:T(8,128)(2,1)S(1)} %get-tuple-element.139), channel_id=1, source_target_pairs={{0,2},{1,3},{2,0},{3,1},{4,6},{5,7},{6,4},{7,5},{8,10},{9,11},{10,... | collective-permute-start | bytes 589832 | tf_op jit(solution)/shard_map/ppermute | solution.py:28
  134.6 11.8 %collective-permute-start.24 = (f32[2,2,128,768]{3,2,1,0:T(8,128)}, f32[2,2,128,768]{3,2,1,0:T(8,128)S(1)}, u32[]{:S(2)}, u32[]{:S(2)}) collective-permute-start(f32[2,2,128,768]{3,2,1,0:T(8,128)} %get-tuple-element.151), channel_id=1, source_target_pairs={{0,1},{1,0},{2,3},{3,2},{4,5},{5,4},{6,7},{7,6},{8,9},{9,8},{10,11... | collective-permute-start | bytes 4718600 | tf_op jit(solution)/shard_map/ppermute | solution.py:28
  136.9 14.4 %collective-permute-start.23 = (bf16[2,128,1024]{2,1,0:T(8,128)(2,1)}, bf16[2,128,1024]{2,1,0:T(8,128)(2,1)S(1)}, u32[]{:S(2)}, u32[]{:S(2)}) collective-permute-start(bf16[2,128,1024]{2,1,0:T(8,128)(2,1)} %get-tuple-element.149), channel_id=1, source_target_pairs={{0,2},{1,3},{2,0},{3,1},{4,6},{5,7},{6,4},{7,5},{8,10},{9,11},{10,... | collective-permute-start | bytes 1572872 | tf_op jit(solution)/shard_map/ppermute | solution.py:28
  146.3 38.9 %collective-permute-start.27 = (f32[2,2,128,768]{3,2,1,0:T(8,128)}, f32[2,2,128,768]{3,2,1,0:T(8,128)}, u32[]{:S(2)}, u32[]{:S(2)}) collective-permute-start(f32[2,2,128,768]{3,2,1,0:T(8,128)} %get-tuple-element.160), channel_id=1, source_target_pairs={{0,1},{1,0},{2,3},{3,2},{4,5},{5,4},{6,7},{7,6},{8,9},{9,8},{10,11... | collective-permute-start | bytes 4718600 | tf_op jit(solution)/shard_map/ppermute | solution.py:28
  164.8 35.7 %collective-permute-start.25 = (f32[2,2,128,768]{3,2,1,0:T(8,128)}, f32[2,2,128,768]{3,2,1,0:T(8,128)S(1)}, u32[]{:S(2)}, u32[]{:S(2)}) collective-permute-start(f32[2,2,128,768]{3,2,1,0:T(8,128)} %get-tuple-element.157), channel_id=1, source_target_pairs={{0,1},{1,0},{2,3},{3,2},{4,5},{5,4},{6,7},{7,6},{8,9},{9,8},{10,11... | collective-permute-start | bytes 4718600 | tf_op jit(solution)/shard_map/ppermute | solution.py:28
  164.8 20.4 %collective-permute-start.30 = (bf16[3,128,1024]{2,1,0:T(8,128)(2,1)S(1)}, bf16[3,128,1024]{2,1,0:T(8,128)(2,1)S(1)}, u32[]{:S(2)}, u32[]{:S(2)}) collective-permute-start(bf16[3,128,1024]{2,1,0:T(8,128)(2,1)S(1)} %get-tuple-element.165.refs_0_.refs_1_), channel_id=1, source_target_pairs={{0,2},{1,3},{2,0},{3,1},{4,6},{5,7},{6,4},{7,5},{8,10},{9,11},{10,... | collective-permute-start | bytes 2359304 | tf_op jit(solution)/shard_map/ppermute | solution.py:28
  166.4 26.8 %collective-permute-start.26 = (bf16[2,128,768]{2,1,0:T(8,128)(2,1)S(1)}, bf16[2,128,768]{2,1,0:T(8,128)(2,1)S(1)}, u32[]{:S(2)}, u32[]{:S(2)}) collective-permute-start(bf16[2,128,768]{2,1,0:T(8,128)(2,1)S(1)} %get-tuple-element.158), channel_id=1, source_target_pairs={{0,2},{1,3},{2,0},{3,1},{4,6},{5,7},{6,4},{7,5},{8,10},{9,11},{10,... | collective-permute-start | bytes 1179656 | tf_op jit(solution)/shard_map/ppermute | solution.py:28
  166.9 62.5 %collective-permute-start.29 = (bf16[3,128,1024]{2,1,0:T(8,128)(2,1)S(1)}, bf16[3,128,1024]{2,1,0:T(8,128)(2,1)S(1)}, u32[]{:S(2)}, u32[]{:S(2)}) collective-permute-start(bf16[3,128,1024]{2,1,0:T(8,128)(2,1)S(1)} %get-tuple-element.165.refs_0_.refs_1_), channel_id=1, source_target_pairs={{0,1},{1,0},{2,3},{3,2},{4,5},{5,4},{6,7},{7,6},{8,9},{9,8},{10,11... | collective-permute-start | bytes 2359304 | tf_op jit(solution)/shard_map/ppermute | solution.py:28
  185.3 45.6 %collective-permute-start.31 = (bf16[3,128,1024]{2,1,0:T(8,128)(2,1)S(1)}, bf16[3,128,1024]{2,1,0:T(8,128)(2,1)S(1)}, u32[]{:S(2)}, u32[]{:S(2)}) collective-permute-start(bf16[3,128,1024]{2,1,0:T(8,128)(2,1)S(1)} %collective-permute-done.30.refs_2_.refs_3_), channel_id=1, source_target_pairs={{0,1},{1,0},{2,3},{3,2},{4,5},{5,4},{6,7},{7,6},{8,9},{9,8},{10,11... | collective-permute-start | bytes 2359304 | tf_op jit(solution)/shard_map/ppermute | solution.py:28
  198.5 24.9 %collective-permute-start.40 = (bf16[3,128,768]{2,1,0:T(8,128)(2,1)S(1)}, bf16[3,128,768]{2,1,0:T(8,128)(2,1)}, u32[]{:S(2)}, u32[]{:S(2)}) collective-permute-start(bf16[3,128,768]{2,1,0:T(8,128)(2,1)S(1)} %get-tuple-element.175.refs_0_.refs_1_), channel_id=1, source_target_pairs={{0,2},{1,3},{2,0},{3,1},{4,6},{5,7},{6,4},{7,5},{8,10},{9,11},{10,... | collective-permute-start | bytes 1769480 | tf_op jit(solution)/shard_map/ppermute | solution.py:28
  200.0 21.8 %collective-permute-start.32 = (bf16[2,128,768]{2,1,0:T(8,128)(2,1)S(1)}, bf16[2,128,768]{2,1,0:T(8,128)(2,1)S(1)}, u32[]{:S(2)}, u32[]{:S(2)}) collective-permute-start(bf16[2,128,768]{2,1,0:T(8,128)(2,1)S(1)} %get-tuple-element.166), channel_id=1, source_target_pairs={{0,2},{1,3},{2,0},{3,1},{4,6},{5,7},{6,4},{7,5},{8,10},{9,11},{10,... | collective-permute-start | bytes 1179656 | tf_op jit(solution)/shard_map/ppermute | solution.py:28
  200.6 74.6 %collective-permute-start.39 = (bf16[3,128,768]{2,1,0:T(8,128)(2,1)S(1)}, bf16[3,128,768]{2,1,0:T(8,128)(2,1)}, u32[]{:S(2)}, u32[]{:S(2)}) collective-permute-start(bf16[3,128,768]{2,1,0:T(8,128)(2,1)S(1)} %get-tuple-element.175.refs_0_.refs_1_), channel_id=1, source_target_pairs={{0,1},{1,0},{2,3},{3,2},{4,5},{5,4},{6,7},{7,6},{8,9},{9,8},{10,11... | collective-permute-start | bytes 1769480 | tf_op jit(solution)/shard_map/ppermute | solution.py:28
  221.9 50.0 %collective-permute-start.28 = (bf16[2,128,768]{2,1,0:T(8,128)(2,1)}, bf16[2,128,768]{2,1,0:T(8,128)(2,1)}, u32[]{:S(2)}, u32[]{:S(2)}) collective-permute-start(bf16[2,128,768]{2,1,0:T(8,128)(2,1)} %get-tuple-element.164), channel_id=1, source_target_pairs={{0,2},{1,3},{2,0},{3,1},{4,6},{5,7},{6,4},{7,5},{8,10},{9,11},{10,... | collective-permute-start | bytes 1179656 | tf_op jit(solution)/shard_map/ppermute | solution.py:28
  223.3 58.7 %collective-permute-start.41 = (bf16[3,128,768]{2,1,0:T(8,128)(2,1)}, bf16[3,128,768]{2,1,0:T(8,128)(2,1)}, u32[]{:S(2)}, u32[]{:S(2)}) collective-permute-start(bf16[3,128,768]{2,1,0:T(8,128)(2,1)} %collective-permute-done.40.refs_2_.refs_3_), channel_id=1, source_target_pairs={{0,1},{1,0},{2,3},{3,2},{4,5},{5,4},{6,7},{7,6},{8,9},{9,8},{10,11... | collective-permute-start | bytes 1769480 | tf_op jit(solution)/shard_map/ppermute | solution.py:28
  231.7 44.0 %collective-permute-start.42 = (bf16[2,128,768]{2,1,0:T(8,128)(2,1)}, bf16[2,128,768]{2,1,0:T(8,128)(2,1)}, u32[]{:S(2)}, u32[]{:S(2)}) collective-permute-start(bf16[2,128,768]{2,1,0:T(8,128)(2,1)} %get-tuple-element.188.refs_0_.refs_1_), channel_id=1, source_target_pairs={{0,2},{1,3},{2,0},{3,1},{4,6},{5,7},{6,4},{7,5},{8,10},{9,11},{10,... | collective-permute-start | bytes 1179656 | tf_op jit(solution)/shard_map/ppermute | solution.py:28
  238.3 37.4 %collective-permute-start.36 = (bf16[1,128,768]{2,1,0:T(8,128)(2,1)}, bf16[1,128,768]{2,1,0:T(8,128)(2,1)}, u32[]{:S(2)}, u32[]{:S(2)}) collective-permute-start(bf16[1,128,768]{2,1,0:T(8,128)(2,1)} %get-tuple-element.174.refs_0_.refs_1_), channel_id=1, source_target_pairs={{0,1},{1,0},{2,3},{3,2},{4,5},{5,4},{6,7},{7,6},{8,9},{9,8},{10,11... | collective-permute-start | bytes 589832 | tf_op jit(solution)/shard_map/ppermute | solution.py:28
  275.8 48.7 %collective-permute-start.48 = (bf16[2,128,768]{2,1,0:T(8,128)(2,1)}, bf16[2,128,768]{2,1,0:T(8,128)(2,1)S(1)}, u32[]{:S(2)}, u32[]{:S(2)}) collective-permute-start(bf16[2,128,768]{2,1,0:T(8,128)(2,1)} %get-tuple-element.188.refs_0_.refs_1_), channel_id=1, source_target_pairs={{0,1},{1,0},{2,3},{3,2},{4,5},{5,4},{6,7},{7,6},{8,9},{9,8},{10,11... | collective-permute-start | bytes 1179656 | tf_op jit(solution)/shard_map/ppermute | solution.py:28
  275.8 49.2 %collective-permute-start.49 = (bf16[2,128,768]{2,1,0:T(8,128)(2,1)}, bf16[2,128,768]{2,1,0:T(8,128)(2,1)}, u32[]{:S(2)}, u32[]{:S(2)}) collective-permute-start(bf16[2,128,768]{2,1,0:T(8,128)(2,1)} %collective-permute-done.42.refs_8_.refs_2_.refs_3_), channel_id=1, source_target_pairs={{0,1},{1,0},{2,3},{3,2},{4,5},{5,4},{6,7},{7,6},{8,9},{9,8},{10,11... | collective-permute-start | bytes 1179656 | tf_op jit(solution)/shard_map/ppermute | solution.py:28
  276.3 40.5 %collective-permute-start.33 = (bf16[1,128,768]{2,1,0:T(8,128)(2,1)S(1)}, bf16[1,128,768]{2,1,0:T(8,128)(2,1)S(1)}, u32[]{:S(2)}, u32[]{:S(2)}) collective-permute-start(bf16[1,128,768]{2,1,0:T(8,128)(2,1)S(1)} %get-tuple-element.173.refs_0_.refs_1_), channel_id=1, source_target_pairs={{0,1},{1,0},{2,3},{3,2},{4,5},{5,4},{6,7},{7,6},{8,9},{9,8},{10,11... | collective-permute-start | bytes 589832 | tf_op jit(solution)/shard_map/ppermute | solution.py:28
  282.1 34.8 %collective-permute-start.35 = (bf16[1,128,768]{2,1,0:T(8,128)(2,1)S(1)}, bf16[1,128,768]{2,1,0:T(8,128)(2,1)S(1)}, u32[]{:S(2)}, u32[]{:S(2)}) collective-permute-start(bf16[1,128,768]{2,1,0:T(8,128)(2,1)S(1)} %collective-permute-done.34.refs_7_.refs_2_.refs_3_), channel_id=1, source_target_pairs={{0,1},{1,0},{2,3},{3,2},{4,5},{5,4},{6,7},{7,6},{8,9},{9,8},{10,11... | collective-permute-start | bytes 589832 | tf_op jit(solution)/shard_map/ppermute | solution.py:28
  282.1 44.4 %collective-permute-start.47 = (bf16[2,128,768]{2,1,0:T(8,128)(2,1)}, bf16[2,128,768]{2,1,0:T(8,128)(2,1)S(1)}, u32[]{:S(2)}, u32[]{:S(2)}) collective-permute-start(bf16[2,128,768]{2,1,0:T(8,128)(2,1)} %get-tuple-element.195.refs_0_.refs_1_), channel_id=1, source_target_pairs={{0,2},{1,3},{2,0},{3,1},{4,6},{5,7},{6,4},{7,5},{8,10},{9,11},{10,... | collective-permute-start | bytes 1179656 | tf_op jit(solution)/shard_map/ppermute | solution.py:28
  322.9 20.4 %collective-permute-start.44 = (bf16[4,16,2048]{2,1,0:T(8,128)(2,1)S(1)}, bf16[4,16,2048]{2,1,0:T(8,128)(2,1)S(1)}, u32[]{:S(2)}, u32[]{:S(2)}) collective-permute-start(bf16[4,16,2048]{2,1,0:T(8,128)(2,1)S(1)} %get-tuple-element.192), channel_id=1, source_target_pairs={{0,4},{4,0},{8,12},{12,8},{16,20},{20,16},{24,28},{28,24},{1,5},{5... | collective-permute-start | bytes 786440 | tf_op jit(solution)/shard_map/ppermute | solution.py:32
  324.5 18.9 %collective-permute-start.45 = (bf16[4,16,2048]{2,1,0:T(8,128)(2,1)S(1)}, bf16[4,16,2048]{2,1,0:T(8,128)(2,1)S(1)}, u32[]{:S(2)}, u32[]{:S(2)}) collective-permute-start(bf16[4,16,2048]{2,1,0:T(8,128)(2,1)S(1)} %get-tuple-element.193), channel_id=1, source_target_pairs={{0,4},{4,0},{8,12},{12,8},{16,20},{20,16},{24,28},{28,24},{1,5},{5... | collective-permute-start | bytes 786440 | tf_op jit(solution)/shard_map/ppermute | solution.py:32
  325.0 22.7 %collective-permute-start.46 = (bf16[4,16,2048]{2,1,0:T(8,128)(2,1)S(1)}, bf16[4,16,2048]{2,1,0:T(8,128)(2,1)S(1)}, u32[]{:S(2)}, u32[]{:S(2)}) collective-permute-start(bf16[4,16,2048]{2,1,0:T(8,128)(2,1)S(1)} %get-tuple-element.194), channel_id=1, source_target_pairs={{0,4},{4,0},{8,12},{12,8},{16,20},{20,16},{24,28},{28,24},{1,5},{5... | collective-permute-start | bytes 786440 | tf_op jit(solution)/shard_map/ppermute | solution.py:32
  326.5 26.2 %collective-permute-start.53 = (bf16[2,128,768]{2,1,0:T(8,128)(2,1)}, bf16[2,128,768]{2,1,0:T(8,128)(2,1)S(1)}, u32[]{:S(2)}, u32[]{:S(2)}) collective-permute-start(bf16[2,128,768]{2,1,0:T(8,128)(2,1)} %get-tuple-element.195.refs_0_.refs_1_), channel_id=1, source_target_pairs={{0,1},{1,0},{2,3},{3,2},{4,5},{5,4},{6,7},{7,6},{8,9},{9,8},{10,11... | collective-permute-start | bytes 1179656 | tf_op jit(solution)/shard_map/ppermute | solution.py:28
  331.6 21.1 %collective-permute-start.54 = (bf16[2,128,768]{2,1,0:T(8,128)(2,1)S(1)}, bf16[2,128,768]{2,1,0:T(8,128)(2,1)S(1)}, u32[]{:S(2)}, u32[]{:S(2)}) collective-permute-start(bf16[2,128,768]{2,1,0:T(8,128)(2,1)S(1)} %collective-permute-done.47.refs_5_.refs_2_.refs_3_), channel_id=1, source_target_pairs={{0,1},{1,0},{2,3},{3,2},{4,5},{5,4},{6,7},{7,6},{8,9},{9,8},{10,11... | collective-permute-start | bytes 1179656 | tf_op jit(solution)/shard_map/ppermute | solution.py:28
  348.2 14.2 %collective-permute-start.50 = (bf16[4,16,2048]{2,1,0:T(8,128)(2,1)S(1)}, bf16[4,16,2048]{2,1,0:T(8,128)(2,1)S(1)}, u32[]{:S(2)}, u32[]{:S(2)}) collective-permute-start(bf16[4,16,2048]{2,1,0:T(8,128)(2,1)S(1)} %get-tuple-element.202), channel_id=1, source_target_pairs={{0,8},{4,12},{8,0},{12,4},{16,24},{20,28},{24,16},{28,20},{1,9},{5... | collective-permute-start | bytes 786440 | tf_op jit(solution)/shard_map/ppermute | solution.py:32
  349.0 21.8 %collective-permute-start.51 = (bf16[4,16,2048]{2,1,0:T(8,128)(2,1)S(1)}, bf16[4,16,2048]{2,1,0:T(8,128)(2,1)S(1)}, u32[]{:S(2)}, u32[]{:S(2)}) collective-permute-start(bf16[4,16,2048]{2,1,0:T(8,128)(2,1)S(1)} %get-tuple-element.203), channel_id=1, source_target_pairs={{0,16},{4,20},{8,24},{12,28},{16,0},{20,4},{24,8},{28,12},{1,17},{... | collective-permute-start | bytes 786440 | tf_op jit(solution)/shard_map/ppermute | solution.py:32
  352.4 29.8 %collective-permute-start.52 = (bf16[4,16,2048]{2,1,0:T(8,128)(2,1)S(1)}, bf16[4,16,2048]{2,1,0:T(8,128)(2,1)S(1)}, u32[]{:S(2)}, u32[]{:S(2)}) collective-permute-start(bf16[4,16,2048]{2,1,0:T(8,128)(2,1)S(1)} %get-tuple-element.204), channel_id=1, source_target_pairs={{0,24},{4,28},{8,16},{12,20},{16,8},{20,12},{24,0},{28,4},{1,25},{... | collective-permute-start | bytes 786440 | tf_op jit(solution)/shard_map/ppermute | solution.py:32
  360.4 29.4 %collective-permute-start.55 = (bf16[4,16,2048]{2,1,0:T(8,128)(2,1)S(1)}, bf16[4,16,2048]{2,1,0:T(8,128)(2,1)S(1)}, u32[]{:S(2)}, u32[]{:S(2)}) collective-permute-start(bf16[4,16,2048]{2,1,0:T(8,128)(2,1)S(1)} %get-tuple-element.215), channel_id=1, source_target_pairs={{0,4},{4,0},{8,12},{12,8},{16,20},{20,16},{24,28},{28,24},{1,5},{5... | collective-permute-start | bytes 786440 | tf_op jit(solution)/shard_map/ppermute | solution.py:32
  360.9 28.8 %collective-permute-start.56 = (bf16[4,16,2048]{2,1,0:T(8,128)(2,1)S(1)}, bf16[4,16,2048]{2,1,0:T(8,128)(2,1)S(1)}, u32[]{:S(2)}, u32[]{:S(2)}) collective-permute-start(bf16[4,16,2048]{2,1,0:T(8,128)(2,1)S(1)} %get-tuple-element.216), channel_id=1, source_target_pairs={{0,4},{4,0},{8,12},{12,8},{16,20},{20,16},{24,28},{28,24},{1,5},{5... | collective-permute-start | bytes 786440 | tf_op jit(solution)/shard_map/ppermute | solution.py:32
  362.5 27.3 %collective-permute-start.57 = (bf16[4,16,2048]{2,1,0:T(8,128)(2,1)S(1)}, bf16[4,16,2048]{2,1,0:T(8,128)(2,1)S(1)}, u32[]{:S(2)}, u32[]{:S(2)}) collective-permute-start(bf16[4,16,2048]{2,1,0:T(8,128)(2,1)S(1)} %get-tuple-element.217), channel_id=1, source_target_pairs={{0,4},{4,0},{8,12},{12,8},{16,20},{20,16},{24,28},{28,24},{1,5},{5... | collective-permute-start | bytes 786440 | tf_op jit(solution)/shard_map/ppermute | solution.py:32
  370.9 18.9 %collective-permute-start.58 = (bf16[4,16,2048]{2,1,0:T(8,128)(2,1)S(1)}, bf16[4,16,2048]{2,1,0:T(8,128)(2,1)S(1)}, u32[]{:S(2)}, u32[]{:S(2)}) collective-permute-start(bf16[4,16,2048]{2,1,0:T(8,128)(2,1)S(1)} %get-tuple-element.218), channel_id=1, source_target_pairs={{0,4},{4,0},{8,12},{12,8},{16,20},{20,16},{24,28},{28,24},{1,5},{5... | collective-permute-start | bytes 786440 | tf_op jit(solution)/shard_map/ppermute | solution.py:32
  390.5 19.7 %collective-permute-start.60 = (bf16[4,16,2048]{2,1,0:T(8,128)(2,1)S(1)}, bf16[4,16,2048]{2,1,0:T(8,128)(2,1)S(1)}, u32[]{:S(2)}, u32[]{:S(2)}) collective-permute-start(bf16[4,16,2048]{2,1,0:T(8,128)(2,1)S(1)} %get-tuple-element.225), channel_id=1, source_target_pairs={{0,16},{4,20},{8,24},{12,28},{16,0},{20,4},{24,8},{28,12},{1,17},{... | collective-permute-start | bytes 786440 | tf_op jit(solution)/shard_map/ppermute | solution.py:32
  393.5 16.7 %collective-permute-start.61 = (bf16[4,16,2048]{2,1,0:T(8,128)(2,1)S(1)}, bf16[4,16,2048]{2,1,0:T(8,128)(2,1)S(1)}, u32[]{:S(2)}, u32[]{:S(2)}) collective-permute-start(bf16[4,16,2048]{2,1,0:T(8,128)(2,1)S(1)} %get-tuple-element.226), channel_id=1, source_target_pairs={{0,24},{4,28},{8,16},{12,20},{16,8},{20,12},{24,0},{28,4},{1,25},{... | collective-permute-start | bytes 786440 | tf_op jit(solution)/shard_map/ppermute | solution.py:32
  (90 other events, 801.1 us)

commit v3 on v1

v3 whole, which is shorter than its diff:
```python
import functools

import jax
import jax.numpy as jnp
from jax import lax
from jax.experimental import pallas as pl
from jax.experimental.pallas import tpu as pltpu
from jax.sharding import PartitionSpec as P

BF16, F32 = jnp.bfloat16, jnp.float32
BLOCK = 256
VMEM_LIMIT = 64 * 1024 * 1024 - 256 * 1024
NN = (((1,), (0,)), ((), ()))
NT = (((1,), (1,)), ((), ()))
TN = (((0,), (0,)), ((), ()))


def dot(left, right, dims):
    return lax.dot_general(left, right, dims, preferred_element_type=F32)


def silu_parts(gate):
    sigma = jax.nn.sigmoid(gate)
    return (gate * sigma, sigma * (1.0 + gate * (1.0 - sigma)))


def swap(value, mask):
    return lax.ppermute(value, "narrow", [(i, i ^ mask) for i in range(4)])


def swap_wide(value, mask):
    return lax.ppermute(value, "wide", [(i, i ^ mask) for i in range(8)])


class Chain:
    def __init__(self):
        self.token = None
        self.waits = []

    def after(self, *arrays):
        self.waits += arrays

    def __call__(self, body, grid, ins, outs, scratch=(), flops=0, alias=None, scalar=None):
        lead = 0 if scalar is None else 1
        arrays = [a for a, _, _ in ins]
        specs = [pl.BlockSpec(block, index) for _, block, index in ins]
        unread = self.waits + ([] if self.token is None else [self.token])
        self.waits = []
        arrays += unread
        specs += [pl.BlockSpec(memory_space=pltpu.HBM)] * len(unread)
        shapes = [jax.ShapeDtypeStruct(shape, dtype) for shape, dtype, _, _ in outs]
        out_specs = [pl.BlockSpec(block, index) for _, _, block, index in outs]
        shapes.append(jax.ShapeDtypeStruct((8, 128), F32))
        out_specs.append(pl.BlockSpec((8, 128), lambda *i: (0, 0)))
        n_in, n_out = len(ins), len(outs)

        def kernel(*refs):
            head, refs = refs[:lead], refs[lead:]
            in_refs = refs[:n_in]
            rest = refs[n_in + len(unread) :]
            out_refs, token, scratch_refs = rest[:n_out], rest[n_out], rest[n_out + 1 :]
            token[...] = jnp.zeros(token.shape, F32)
            body(*head, *in_refs, *out_refs, *scratch_refs)

        res = pl.pallas_call(
            kernel,
            grid_spec=pltpu.PrefetchScalarGridSpec(
                num_scalar_prefetch=lead,
                grid=grid,
                in_specs=specs,
                out_specs=out_specs,
                scratch_shapes=list(scratch),
            ),
            out_shape=shapes,
            input_output_aliases={k + lead: v for k, v in (alias or {}).items()},
            compiler_params=pltpu.CompilerParams(vmem_limit_bytes=VMEM_LIMIT),
            cost_estimate=pl.CostEstimate(flops=1, bytes_accessed=1, transcendentals=0),
        )(*(() if scalar is None else (scalar,)), *arrays)
        self.token = res[-1]
        return res[:-1]


def join(chain, parts):
    rows, tile = parts[0].shape
    count, step = len(parts), rows // 4

    def body(*refs):
        for i in range(count):
            refs[count][i] = refs[i][...]

    (out,) = chain(
        body,
        (4,),
        [(p, (step, tile), lambda j: (j, 0)) for p in parts],
        [((count, rows, tile), BF16, (count, step, tile), lambda j: (0, j, 0))],
    )
    return out


def arrange(chain, me, even, first, odd, rows, tile, turned=False):
    q = 8 * rows

    def body(_, *refs):
        out = refs[8]
        for k in range(8):
            out[0, k] = refs[k][...]
        if turned:
            refs[9][...] = out[0].reshape(q, tile).T

    slots = [(even[0], 0), (first, 0), (even[1], 0), odd[0]]
    slots += [(even[2], 0), odd[1], (even[3], 0), odd[2]]
    outs = [((4, 8, rows, tile), BF16, (1, 8, rows, tile), lambda g, s: (g, 0, 0, 0))]
    if turned:
        outs.append(((tile, 4 * q), BF16, (tile, q), lambda g, s: (0, g)))
    out, *rest = chain(
        body,
        (4,),
        [
            (p, (rows, tile), functools.partial(lambda at, g, s: (at + (s[0] ^ g), 0), at))
            for p, at in slots
        ],
        outs,
        scalar=me,
    )
    return [out.reshape(4 * q, tile), *rest]


def parted(acc, q, keep, send):
    for i in range(2):
        keep[i] = acc[2 * i * q : (2 * i + 1) * q]
        send[i] = acc[(2 * i + 1) * q : (2 * i + 2) * q]


def back_part(chain, cot, down, base, blocks):
    tokens, tile = cot.shape
    q, n = tokens // 4, blocks * BLOCK

    def body(c, w, keep, send):
        parted(dot(c[...], w[...], NT), q, keep, send)

    out = ((2, q, n), F32, (2, q, BLOCK), lambda j: (0, 0, j))
    return chain(
        body,
        (blocks,),
        [(cot, cot.shape, lambda j: (0, 0)), (down, (BLOCK, tile), lambda j: (base + j, 0))],
        [out, out],
        flops=2 * tokens * tile * n,
    )


def gate_up_part(chain, act, gate, up, base, blocks):
    tokens, tile = act.shape
    q, n = tokens // 4, blocks * BLOCK

    def body(a, wg, wu, keep, send):
        parted(dot(a[...], wg[...], NN), q, keep.at[:, 0], send.at[:, 0])
        parted(dot(a[...], wu[...], NN), q, keep.at[:, 1], send.at[:, 1])

    weight = ((tile, BLOCK), lambda j: (0, base + j))
    out = ((2, 2, q, n), F32, (2, 2, q, BLOCK), lambda j: (0, 0, 0, j))
    return chain(
        body,
        (blocks,),
        [(act, act.shape, lambda j: (0, 0)), (gate, *weight), (up, *weight)],
        [out, out],
        flops=4 * tokens * tile * n,
    )


def add_away(chain, keep, got):
    shape = keep.shape[1:]
    zeros = (0,) * (len(shape) - 1)
    block = (1, *shape[:-1], BLOCK)

    def body(a, b, out):
        out[...] = (a[0] + b[0]).astype(BF16)

    def at(j):
        return (1, *zeros, j)

    (out,) = chain(
        body,
        (shape[-1] // BLOCK,),
        [(keep, block, at), (got, block, at)],
        [(shape, BF16, block[1:], lambda j: (*zeros, j))],
    )
    return out


def activate(chain, keep_gu, got_gu, far_gu, keep_b, got_b, far_b, off):
    n, q = far_gu.shape[-1], far_gu.shape[1]

    def body(kg, gg, fg, kb, gb, fb, deltas, hidden):
        gate = kg[0, 0] + gg[0, 0] + fg[0].astype(F32)
        up = kg[0, 1] + gg[0, 1] + fg[1].astype(F32)
        back = kb[0] + gb[0] + fb[...].astype(F32)
        active, slope = silu_parts(gate)
        deltas[0] = (back * up * slope).astype(BF16)
        deltas[1] = (back * active).astype(BF16)
        hidden[0] = (active * up).astype(BF16)

    four = ((1, 2, q, BLOCK), lambda j: (0, 0, 0, j))
    three = ((1, q, BLOCK), lambda j: (0, 0, off + j))
    return chain(
        body,
        (n // BLOCK,),
        [
            (keep_gu, *four),
            (got_gu, *four),
            (far_gu, (2, q, BLOCK), lambda j: (0, 0, j)),
            (keep_b, *three),
            (got_b, *three),
            (far_b, (q, BLOCK), lambda j: (0, off + j)),
        ],
        [((k, q, n), BF16, (k, q, BLOCK), lambda j: (0, 0, j)) for k in (2, 1)],
    )


def split_slots(acc, rows, keep, send):
    view = acc.reshape(4, 8, rows, acc.shape[-1])
    for s in range(4):
        keep[s] = view[:, 2 * s]
        send[s] = view[:, 2 * s + 1].astype(BF16)


def summed(chain, terms, base, blocks, halves=1, half=0, split=False):
    kinds = sum(len(t[1]) for t in terms)
    q, n = terms[0][0][0].shape[1:]
    rows = q // 8
    first_weight, dims = terms[0][1][0], terms[0][2]
    tile = first_weight.shape[1 if dims is NN else 0]
    width = tile // halves
    step = min(2 * BLOCK, width)
    off = half * (width // step)
    ins, outs, alias, plan, moves = [], [], {}, [], []
    for quarters, weights, dims, prev in terms:
        refs, first = [], len(moves) // 4
        for k in range(len(weights)):
            moves += [(first + k, g, len(ins) + g, k) for g in range(4)]
        ins += [(p, p.shape, lambda j: (0, 0, 0)) for p in quarters]
        for w in weights:
            for i in range(blocks):
                refs.append(len(ins))
                if dims is NN:
                    index = functools.partial(lambda i, j: (base + i, off + j), i)
                    ins.append((w, (BLOCK, step), index))
                else:
                    index = functools.partial(lambda i, j: (off + j, base + i), i)
                    ins.append((w, (step, BLOCK), index))
        before = None
        if prev is not None:
            before = len(ins)
            ins.append((prev, (4 * q, step), lambda j: (0, off + j)))
            if not split:
                alias[before] = len(outs)
        plan.append((first, len(weights), dims, refs, before, len(outs)))
        if split:
            shape, block = (4, 4, rows, width), (4, 4, rows, step)
            outs.append((shape, F32, block, lambda j: (0, 0, 0, j)))
            outs.append((shape, BF16, block, lambda j: (0, 0, 0, j)))
        else:
            outs.append(((4 * q, tile), F32, (4 * q, step), lambda j: (0, j)))
    n_in = len(ins)

    def body(*refs):
        out_refs, scratch = refs[n_in:-1], refs[-1]

        @pl.when(pl.program_id(0) == 0)
        def _():
            for to, g, at, k in moves:
                scratch[to, g * q : (g + 1) * q] = refs[at][k]

        for first, count, dims, at, before, out in plan:
            total = None if before is None else refs[before][...]
            for k in range(count):
                for i in range(blocks):
                    left = scratch[first + k, :, i * BLOCK : (i + 1) * BLOCK]
                    term = dot(left, refs[at[k * blocks + i]][...], dims)
                    total = term if total is None else total + term
            if split:
                split_slots(total, rows, out_refs[out], out_refs[out + 1])
            else:
                out_refs[out][...] = total

    return chain(
        body,
        (width // step,),
        ins,
        outs,
        scratch=[pltpu.VMEM((kinds, 4 * q, n), BF16)],
        flops=2 * kinds * 4 * q * n * width,
        alias=alias,
    )


def gradients(chain, act_t, cot, hidden, deltas, base, blocks, prev, units):
    tile, tokens = act_t.shape
    q = deltas[0].shape[1]
    lead = 10

    def body(*refs):
        a, c, hid, dl = refs[0], refs[1], refs[2:6], refs[6:10]
        outs = refs[-3:]
        for k in range(2):
            right = jnp.concatenate([p[k] for p in dl], axis=0)
            outs[k][...] = dot(a[...], right, NN).astype(BF16)
        left = jnp.concatenate([p[0] for p in hid], axis=0)
        outs[2][...] = dot(left, c[...], TN).astype(BF16)

    ins = [(act_t, act_t.shape, lambda j: (0, 0)), (cot, cot.shape, lambda j: (0, 0))]
    ins += [(p, (1, q, BLOCK), lambda j: (0, 0, j)) for p in hidden]
    ins += [(p, (2, q, BLOCK), lambda j: (0, 0, j)) for p in deltas]
    column = ((tile, units), BF16, (tile, BLOCK), lambda j: (0, base + j))
    outs = [column, column, ((units, tile), BF16, (BLOCK, tile), lambda j: (base + j, 0))]
    alias = {}
    if prev is not None:
        ins += [(p, (16, 128), lambda j: (0, 0)) for p in prev]
        alias = {lead + i: i for i in range(3)}
    return chain(body, (blocks,), ins, outs, flops=6 * tokens * tile * blocks * BLOCK, alias=alias)


def over_z(chain, keep, got):
    _, four, rows, width = keep.shape
    step = min(width, 512)

    def body(k, g, *outs):
        for s in range(4):
            outs[s][...] = (k[s] + g[s].astype(F32)).astype(outs[s].dtype)

    four_slots = ((4, four, rows, step), lambda j: (0, 0, 0, j))
    one = ((four, rows, step), lambda j: (0, 0, j))
    return chain(
        body,
        (width // step,),
        [(keep, *four_slots), (got, *four_slots)],
        [((four, rows, width), F32 if s == 0 else BF16, *one) for s in range(4)],
    )


def finish(chain, me, halves, by_rows):
    four, rows, width = halves[0][0].shape
    tile = width * len(halves)

    def body(s, *refs):
        outs = refs[4 * len(halves) :]
        for h in range(len(halves)):
            total = refs[4 * h][...]
            for x in refs[4 * h + 1 : 4 * h + 4]:
                total = total + x[...].astype(F32)
            columns = slice(h * width, (h + 1) * width)
            for g in range(4):
                rounded = total[g].astype(BF16)
                if by_rows:
                    outs[0][s[0] ^ g, :, columns] = rounded
                else:
                    outs[g][:, columns] = rounded

    ins = []
    for own, got in halves:
        ins += [(x, (four, rows, width), lambda j, s: (0, 0, 0)) for x in (own, *got)]
    if by_rows:
        outs = [((four, rows, tile), BF16, (four, rows, tile), lambda j, s: (0, 0, 0))]
    else:
        outs = [((rows, tile), BF16, (rows, tile), lambda j, s: (0, 0))] * 4
    res = chain(body, (1,), ins, outs, scalar=me)
    return res[0].reshape(four * rows, tile) if by_rows else res


def place_columns(chain, me, groups):
    rows, tile = groups[0].shape

    def body(s, *refs):
        for g in range(4):

            @pl.when(pl.program_id(0) == g)
            def _():
                refs[4][...] = refs[g][...]

    (out,) = chain(
        body,
        (4,),
        [(x, (rows, tile), lambda g, s: (0, 0)) for x in groups],
        [((rows, 4 * tile), BF16, (rows, tile), lambda g, s: (0, s[0] ^ g))],
        scalar=me,
    )
    return out


def gather_z(own):
    return [own] + [swap_wide(own, k) for k in (2, 4, 6)]


def spread(own):
    far = swap(own, 2)
    return [own, swap(own, 1), far, swap(far, 1)]


def chunk_sizes(total):
    first = max(1, total // 6)
    rest = total - first
    return [first, (rest + 2) // 3, (rest + 1) // 3, rest // 3]


def local_eight(activations, cotangent, gate_proj, up_proj, down_proj):
    me = lax.axis_index("narrow").astype(jnp.int32).reshape(1)
    rows = activations.shape[0]
    tile, units = gate_proj.shape
    sizes = chunk_sizes(units // BLOCK)
    chunks = [(sum(sizes[:c]), sizes[c]) for c in range(4)]
    backs = [(0, sizes[0] + sizes[1]), chunks[2], chunks[3]]
    back_of = [(0, 0), (0, sizes[0]), (1, 0), (2, 0)]
    chain = Chain()

    keep_b, got_b, far_b = {}, {}, {}
    keep_gu, got_gu, far_gu = {}, {}, {}
    own, near, far, diag = {}, {}, {}, {}
    out = grad = grads = None

    def back(p):
        keep_b[p], send = back_part(chain, cot, down_proj, *backs[p])
        got_b[p] = swap(send, 1)

    def back_x(p):
        far_b[p] = swap(add_away(chain, keep_b[p], got_b[p]), 2)

    def gate_up(c):
        keep_gu[c], send = gate_up_part(chain, act, gate_proj, up_proj, *chunks[c])
        got_gu[c] = swap(send, 1)

    def gate_up_x(c):
        far_gu[c] = swap(add_away(chain, keep_gu[c], got_gu[c]), 2)

    def elementwise(c):
        p, off = back_of[c]
        res = activate(
            chain, keep_gu[c], got_gu[c], far_gu[c], keep_b[p], got_b[p], far_b[p], off
        )
        for kind, value in zip("dh", res):
            name = (kind, c)
            own[name], near[name], far[name] = value, swap(value, 1), swap(value, 2)
            diag[name] = swap(far[name], 1)

    def gathered(kind, c):
        return [x[kind, c] for x in (own, near, far, diag)]

    def out_term(c):
        return (gathered("h", c), [down_proj], NN, out)

    def grad_term(c):
        return (gathered("d", c), [gate_proj, up_proj], NT, grad)

    def add_both(c):
        nonlocal out, grad
        out, grad = summed(chain, [out_term(c), grad_term(c)], *chunks[c])

    def all_grads(c):
        nonlocal grads
        hid, delta = gathered("h", c), gathered("d", c)
        grads = gradients(chain, act_t, cot, hid, delta, *chunks[c], grads, units)

    def last_part(term, half):
        keep, send = summed(chain, [term], *chunks[3], 2, half, True)
        return keep, swap_wide(send, 1)

    def across_z(keep, got):
        mine, *away = over_z(chain, keep, got)
        return mine, [swap_wide(a, 2 * (i + 1)) for i, a in enumerate(away)]

    cot_even, cot_first = gather_z(cotangent), swap_wide(cotangent, 1)
    tiles = lax.all_to_all(activations, "narrow", split_axis=1, concat_axis=0, tiled=True)
    act_even, act_first = gather_z(tiles), swap_wide(tiles, 1)
    act_odd = [swap_wide(x, 1) for x in act_even[1:]]
    chain.after(tiles, cot_first, act_first)
    cot_odd = swap_wide(join(chain, cot_even[1:]), 1)
    cot_odd = [(cot_odd.reshape(12 * rows, tile), 4 * i) for i in range(3)]
    chain.after(*act_even[1:])
    (cot,) = arrange(chain, me, cot_even, cot_first, cot_odd, rows, tile)
    back(0)
    chain.after(act_odd[0], act_odd[1])
    back(1)
    chain.after(act_odd[2])
    back_x(0)
    act_odd = [(x, 0) for x in act_odd]
    act, act_t = arrange(chain, me, act_even, act_first, act_odd, rows, tile, True)
    gate_up(0)
    chain.after(far_b[0])
    back_x(1)
    back(2)
    chain.after(far_b[1])
    gate_up_x(0)
    gate_up(1)
    chain.after(far_gu[0])
    back_x(2)
    elementwise(0)
    gate_up(2)
    chain.after(far["d", 0], far["h", 0], near["d", 0], near["h", 0])
    gate_up_x(1)
    chain.after(diag["d", 0], diag["h", 0])
    gate_up(3)
    chain.after(far_gu[1], far_b[2])
    gate_up_x(2)
    elementwise(1)
    add_both(0)
    chain.after(far["d", 1], near["d", 1], near["h", 1])
    gate_up_x(3)
    all_grads(0)
    chain.after(far["h", 1], far_gu[2], diag["d", 1])
    elementwise(2)
    chain.after(diag["h", 1])
    add_both(1)
    chain.after(far_gu[3], far["h", 2], near["h", 2], near["d", 2])
    elementwise(3)
    chain.after(diag["h", 2])
    all_grads(1)
    chain.after(far["h", 3], far["d", 2], near["h", 3], near["d", 3])
    (out,) = summed(chain, [out_term(2)], *chunks[2])
    chain.after(diag["h", 3], diag["d", 2], far["d", 3])
    pieces = [last_part(out_term(3), 0)]
    chain.after(diag["d", 3])
    (grad,) = summed(chain, [grad_term(2)], *chunks[2])
    landed = [across_z(*pieces[0])]
    pieces.append(last_part(out_term(3), 1))
    pieces.append(last_part(grad_term(3), 0))
    chain.after(*landed[-1][1])
    landed.append(across_z(*pieces[1]))
    pieces.append(last_part(grad_term(3), 1))
    chain.after(*landed[-1][1])
    landed.append(across_z(*pieces[2]))
    all_grads(2)
    chain.after(*landed[-1][1])
    landed.append(across_z(*pieces[3]))
    all_grads(3)
    chain.after(*landed[-1][1])
    block_output = finish(chain, me, landed[:2], True)
    groups = finish(chain, me, landed[2:], False)
    groups = [groups[0]] + [swap(groups[g], g) for g in range(1, 4)]
    input_gradient = place_columns(chain, me, groups)
    return (block_output, input_gradient, *grads)


def scatter_sum(part):
    split = part.reshape(-1, 4, part.shape[0] // 4 // lax.axis_size("wide"), part.shape[-1])
    got = swap(jnp.stack([split[:, 1], split[:, 3]]), 1)
    away = (split[:, 2] + got[1]).astype(BF16)
    return (split[:, 0] + got[0]) + swap(away, 2).astype(F32)


def spread_rows(own):
    return jnp.stack(spread(own), axis=1).reshape(-1, own.shape[-1])


def local_any(activations, cotangent, gate_proj, up_proj, down_proj):
    me = lax.axis_index("narrow")
    rows = activations.shape[0]
    tile = gate_proj.shape[0]
    pieces = [lax.dynamic_slice_in_dim(activations, (me ^ g) * tile, tile, 1) for g in range(4)]
    pieces = [pieces[0]] + [swap(pieces[g], g) for g in range(1, 4)]
    cots = [lax.dynamic_slice_in_dim(cotangent, (me ^ g) * rows, rows, 0) for g in range(4)]

    def gathered(parts):
        return lax.all_gather(jnp.stack(parts), "wide", axis=0, tiled=True).reshape(-1, tile)

    features, upstream = gathered(pieces), gathered(cots)
    gate = scatter_sum(dot(features, gate_proj, NN))
    up = scatter_sum(dot(features, up_proj, NN))
    back = scatter_sum(dot(upstream, down_proj, NT))
    active, slope = silu_parts(gate)
    gate_delta = spread_rows((back * up * slope).astype(BF16))
    up_delta = spread_rows((back * active).astype(BF16))
    hidden = spread_rows((active * up).astype(BF16))

    def landed(total):
        got = lax.psum_scatter(total, "wide", scatter_dimension=0, tiled=True)
        return got.astype(BF16).reshape(4, rows, tile)

    grad = landed(dot(gate_delta, gate_proj, NT) + dot(up_delta, up_proj, NT))
    out = landed(dot(hidden, down_proj, NN))
    gate_gradient = dot(features, gate_delta, TN).astype(BF16)
    up_gradient = dot(features, up_delta, TN).astype(BF16)
    down_gradient = dot(hidden, upstream, TN).astype(BF16)

    block_output = jnp.concatenate(
        [lax.dynamic_index_in_dim(out, me ^ g, 0, keepdims=False) for g in range(4)]
    )
    grads = jnp.stack([grad[0]] + [swap(grad[g], g) for g in range(1, 4)])
    input_gradient = jnp.concatenate(
        [lax.dynamic_index_in_dim(grads, me ^ g, 0, keepdims=False) for g in range(4)], axis=1
    )
    return (block_output, input_gradient, gate_gradient, up_gradient, down_gradient)


def local(activations, cotangent, gate_proj, up_proj, down_proj):
    args = (activations, cotangent, gate_proj, up_proj, down_proj)
    rows, (tile, units) = activations.shape[0], gate_proj.shape
    fits = lax.axis_size("wide") == 8 and rows % 16 == 0
    if fits and tile % (2 * BLOCK) == 0 and units % BLOCK == 0 and units >= 6 * BLOCK:
        return local_eight(*args)
    return local_any(*args)


def solution(mesh):
    placed = (
        P(("wide", "narrow"), None),
        P("wide", "narrow"),
        P("narrow", "wide"),
        P("narrow", "wide"),
        P("wide", "narrow"),
    )
    return jax.shard_map(
        local,
        mesh=mesh,
        in_specs=placed,
        out_specs=(
            P("wide", "narrow"),
            P(("wide", "narrow"), None),
            P("narrow", "wide"),
            P("narrow", "wide"),
            P("wide", "narrow"),
        ),
        check_vma=False,
    )
```

time: 620 us -> 454 us (0.73); the launches traced: 611 us -> 452 us
  waiting for transfers between devices: 391 us -> 164 us
  Pallas kernels: 0 us -> 214 us
  matrix products: 137 us -> 0 us
  starting transfers between devices: 22 us -> 66.4 us
  other arithmetic: 29.6 us -> 0 us
  between operations: 15.4 us -> 0.95 us
  local copies, waits for them, and re-layouts: 15.6 us -> 6.2 us
    pallas_call x0 -> x40, Pallas kernels: none -> 214 us  [__call__(): pl.pallas_call(kernel, grid_spec=pltpu.PrefetchScalarGridSpec(num_scalar_...]
    reduce_scatter x4 -> x0, waiting for transfers between devices: 186 us -> none  [landed(): got = lax.psum_scatter(total, 'wide', scatter_dimension=0, tiled=True)]
    dot_general x15 -> x0, matrix products: 137 us -> none  [the longest x6 50.1 us: contract_cols(): lax.dot_general(left, right, (((1,), (1,)), ((), ())), preferred_element_...]
    all_gather x4 -> x0, waiting for transfers between devices: 120 us -> none  [gathered(): return lax.all_gather(mine, 'wide', axis=0, tiled=True).reshape(-1, tile)]
    ppermute x0 -> x28, waiting for transfers between devices: none -> 69.7 us  [swap_wide(): return lax.ppermute(value, 'wide', [(i, i ^ mask) for i in range(8)])]
    ppermute x0 -> x28, starting transfers between devices: none -> 39.8 us  [swap_wide(): return lax.ppermute(value, 'wide', [(i, i ^ mask) for i in range(8)])]
    another operation x23 -> x0, other arithmetic: 12.9 us -> none  [the longest x6 4.34 us: spread(): pair = swap(jnp.stack([own, far]), 1)]
    convert_element_type x10 -> x0, other arithmetic: 11.3 us -> none  [the longest x2 5.19 us: local(): gate_delta.append(spread((back * up * slope).astype(jnp.bfloat16)))]
  transfers between devices with their start and end apart: 38 -> 70, of which waited for: 18 -> 26; matrix products, arithmetic and copies ran while one was open for 28% -> 0% of each run, Pallas kernels for 0% -> 39%
where the time goes in v3:
time: 454 us; the launch traced here: 452 us
  Pallas kernels  214 us (47%)
  waiting for transfers between devices  164 us (36%)
  starting transfers between devices  66.4 us (15%)
  local copies, waits for them, and re-layouts  6.2 us (1%)
    pallas_call x40, Pallas kernels, __call__(): pl.pallas_call(kernel, grid_spec=pltpu.PrefetchScalarGridSpec(num_scalar_...  214 us
    ppermute x41, waiting for transfers between devices, swap(): return lax.ppermute(value, 'narrow', [(i, i ^ mask) for i in range(4)])  94.7 us
    ppermute x28, waiting for transfers between devices, swap_wide(): return lax.ppermute(value, 'wide', [(i, i ^ mask) for i in range(8)])  69.7 us
    ppermute x28, starting transfers between devices, swap_wide(): return lax.ppermute(value, 'wide', [(i, i ^ mask) for i in range(8)])  39.8 us
    ppermute x41, starting transfers between devices, swap(): return lax.ppermute(value, 'narrow', [(i, i ^ mask) for i in range(4)])  22.3 us
  transfers between devices with their start and end apart: 70, of which 26 were waited for; matrix products, arithmetic and copies ran while one was open for 0% of the time, Pallas kernels for 39%

profile of v3, /device:TPU:0, one launch (start us, length us, event | category | flops | bytes accessed | tf_op | source)
XLA Modules:
  0.0 452.3 jit_solution(7874721077964844562)
XLA Ops:
  2.3 4.2 all-to-all-start
  6.5 4.3 collective-permute-start.10
  20.3 4.4 collective-permute-done.8.refs_0_.refs_3_
  24.7 9.3 %collective-permute-done.9.refs_1_.refs_5_ = bf16[64,2048]{1,0:T(8,128)(2,1)} collective-permute-done((bf16[64,2048]{1,0:T(8,128)(2,1)}, bf16[64,2048]{1,0:T(8,128)(2,1)}, u32[]{:S(2)}, u32[]{:S(2)}) %collective-permute-start.9) | collective-permute-done | bytes 262176 | tf_op jit(solution)/shard_map/ppermute | solution.py:32
  43.2 8.2 %collective-permute-done.1.refs_9_.refs_3_ = bf16[64,2048]{1,0:T(8,128)(2,1)} collective-permute-done((bf16[64,2048]{1,0:T(8,128)(2,1)}, bf16[64,2048]{1,0:T(8,128)(2,1)}, u32[]{:S(2)}, u32[]{:S(2)}) %collective-permute-start.1) | collective-permute-done | bytes 262176 | tf_op jit(solution)/shard_map/ppermute | solution.py:32
  51.3 9.3 %collective-permute-done.3.refs_10_.refs_5_ = bf16[64,2048]{1,0:T(8,128)(2,1)} collective-permute-done((bf16[64,2048]{1,0:T(8,128)(2,1)}, bf16[64,2048]{1,0:T(8,128)(2,1)}, u32[]{:S(2)}, u32[]{:S(2)}) %collective-permute-start.3) | collective-permute-done | bytes 262176 | tf_op jit(solution)/shard_map/ppermute | solution.py:32
  60.7 3.8 shard_map.93
  64.5 8.6 %shard_map.94 = (f32[2,128,1536]{2,1,0:T(8,128)}, f32[2,128,1536]{2,1,0:T(8,128)}, f32[8,128]{1,0:T(8,128)}) custom-call(bf16[512,2048]{1,0:T(8,128)(2,1)} %bitcast.12, bf16[3328,2048]{1,0:T(8,128)(2,1)} %refs_6_.11, f32[8,128]{1,0:T(8,128)} %get-tuple-element.128.refs_2_), custom_call_target="tpu_custom_call" | custom-call | flops 1 | bytes 1 | tf_op jit(solution)/shard_map/pallas_call | solution.py:65
  75.7 6.9 %collective-permute-done.2.refs_2_.refs_4_ = bf16[64,2048]{1,0:T(8,128)(2,1)} collective-permute-done((bf16[64,2048]{1,0:T(8,128)(2,1)}, bf16[64,2048]{1,0:T(8,128)(2,1)}, u32[]{:S(2)}, u32[]{:S(2)}) %collective-permute-start.2) | collective-permute-done | bytes 262176 | tf_op jit(solution)/shard_map/ppermute | solution.py:32
  82.6 5.6 %collective-permute-done.4.refs_3_.refs_6_ = bf16[64,2048]{1,0:T(8,128)(2,1)} collective-permute-done((bf16[64,2048]{1,0:T(8,128)(2,1)}, bf16[64,2048]{1,0:T(8,128)(2,1)}, u32[]{:S(2)}, u32[]{:S(2)}) %collective-permute-start.4) | collective-permute-done | bytes 262176 | tf_op jit(solution)/shard_map/ppermute | solution.py:32
  88.2 6.4 %shard_map.95 = (f32[2,128,1024]{2,1,0:T(8,128)}, f32[2,128,1024]{2,1,0:T(8,128)}, f32[8,128]{1,0:T(8,128)}) custom-call(bf16[512,2048]{1,0:T(8,128)(2,1)} %bitcast.13, bf16[3328,2048]{1,0:T(8,128)(2,1)} %refs_6_.11, bf16[64,2048]{1,0:T(8,128)(2,1)} %collective-permute-done.2.refs_2_.refs_4_, bf16[64,2048]{1,0:T(8,128)(2,1)} %collective-permute-done.4.refs_3_.refs_6_, ...), custom_call_target="tpu_custom_call" | custom-call | flops 1 | bytes 1 | tf_op jit(solution)/shard_map/pallas_call | solution.py:65
  94.6 4.4 shard_map.96
  99.0 4.4 shard_map.97
  103.4 6.1 %shard_map.98 = (f32[2,2,128,512]{3,2,1,0:T(8,128)}, f32[2,2,128,512]{3,2,1,0:T(8,128)}, f32[8,128]{1,0:T(8,128)}) custom-call(bf16[512,2048]{1,0:T(8,128)(2,1)} %bitcast.19, bf16[2048,3328]{1,0:T(8,128)(2,1)} %refs_6_.13, bf16[2048,3328]{1,0:T(8,128)(2,1)} %refs_9_.5, f32[8,128]{1,0:T(8,128)} %get-tuple-element.135.refs_3_), custom_call_target="tpu_custom_call" | custom-call | flops 1 | bytes 1 | tf_op jit(solution)/shard_map/pallas_call | solution.py:65
  111.6 9.8 %collective-permute-done.15.refs_2_.refs_5_ = bf16[128,1536]{1,0:T(8,128)(2,1)} collective-permute-done((bf16[128,1536]{1,0:T(8,128)(2,1)}, bf16[128,1536]{1,0:T(8,128)(2,1)}, u32[]{:S(2)}, u32[]{:S(2)}) %collective-permute-start.15) | collective-permute-done | bytes 393248 | tf_op jit(solution)/shard_map/ppermute | solution.py:28
  121.4 3.3 shard_map.99
  126.3 5.6 %shard_map.100 = (f32[2,128,768]{2,1,0:T(8,128)}, f32[2,128,768]{2,1,0:T(8,128)}, f32[8,128]{1,0:T(8,128)}) custom-call(bf16[512,2048]{1,0:T(8,128)(2,1)} %bitcast.14, bf16[3328,2048]{1,0:T(8,128)(2,1)} %refs_6_.11, f32[8,128]{1,0:T(8,128)} %get-tuple-element.143.refs_2_), custom_call_target="tpu_custom_call" | custom-call | flops 1 | bytes 1 | tf_op jit(solution)/shard_map/pallas_call | solution.py:65
  134.3 9.1 %shard_map.102 = (f32[2,2,128,1024]{3,2,1,0:T(8,128)}, f32[2,2,128,1024]{3,2,1,0:T(8,128)}, f32[8,128]{1,0:T(8,128)}) custom-call(bf16[512,2048]{1,0:T(8,128)(2,1)} %bitcast.20, bf16[2048,3328]{1,0:T(8,128)(2,1)} %refs_6_.13, bf16[2048,3328]{1,0:T(8,128)(2,1)} %refs_9_.5, f32[8,128]{1,0:T(8,128)} %get-tuple-element.148.refs_3_), custom_call_target="tpu_custom_call" | custom-call | flops 1 | bytes 1 | tf_op jit(solution)/shard_map/pallas_call | solution.py:65
  145.0 7.4 %collective-permute-done.17.refs_2_ = bf16[2,128,512]{2,1,0:T(8,128)(2,1)} collective-permute-done((bf16[2,128,512]{2,1,0:T(8,128)(2,1)}, bf16[2,128,512]{2,1,0:T(8,128)(2,1)}, u32[]{:S(2)}, u32[]{:S(2)}) %collective-permute-start.17) | collective-permute-done | bytes 262176 | tf_op jit(solution)/shard_map/ppermute | solution.py:28
  157.3 9.2 %shard_map.105 = (f32[2,2,128,1024]{3,2,1,0:T(8,128)}, f32[2,2,128,1024]{3,2,1,0:T(8,128)}, f32[8,128]{1,0:T(8,128)}) custom-call(bf16[512,2048]{1,0:T(8,128)(2,1)} %bitcast.21, bf16[2048,3328]{1,0:T(8,128)(2,1)} %refs_6_.13, bf16[2048,3328]{1,0:T(8,128)(2,1)} %refs_9_.5, f32[8,128]{1,0:T(8,128)} %get-tuple-element.155.refs_3_), custom_call_target="tpu_custom_call" | custom-call | flops 1 | bytes 1 | tf_op jit(solution)/shard_map/pallas_call | solution.py:65
  168.6 9.8 %collective-permute-done.21.refs_3_.refs_2_.refs_4_ = bf16[1,128,512]{2,1,0:T(8,128)(2,1)} collective-permute-done((bf16[1,128,512]{2,1,0:T(8,128)(2,1)S(1)}, bf16[1,128,512]{2,1,0:T(8,128)(2,1)}, u32[]{:S(2)}, u32[]{:S(2)}) %collective-permute-start.21) | collective-permute-done | bytes 131104 | tf_op jit(solution)/shard_map/ppermute | solution.py:28
  180.1 3.5 shard_map.106
  184.2 7.6 %shard_map.107 = (f32[2,2,128,768]{3,2,1,0:T(8,128)}, f32[2,2,128,768]{3,2,1,0:T(8,128)}, f32[8,128]{1,0:T(8,128)}) custom-call(bf16[512,2048]{1,0:T(8,128)(2,1)} %bitcast.22, bf16[2048,3328]{1,0:T(8,128)(2,1)} %refs_6_.13, bf16[2048,3328]{1,0:T(8,128)(2,1)} %refs_9_.5, bf16[2,128,512]{2,1,0:T(8,128)(2,1)} %collective-permute-done.20.refs_3_.refs_9_, ...), custom_call_target="tpu_custom_call" | custom-call | flops 1 | bytes 1 | tf_op jit(solution)/shard_map/pallas_call | solution.py:65
  194.3 16.4 %collective-permute-done.29.refs_3_.refs_5_ = bf16[128,768]{1,0:T(8,128)(2,1)S(1)} collective-permute-done((bf16[128,768]{1,0:T(8,128)(2,1)}, bf16[128,768]{1,0:T(8,128)(2,1)S(1)}, u32[]{:S(2)}, u32[]{:S(2)}) %collective-permute-start.29) | collective-permute-done | bytes 196640 | tf_op jit(solution)/shard_map/ppermute | solution.py:28
  211.3 3.5 shard_map.108
  214.8 4.0 shard_map.109
  221.3 12.6 %collective-permute-done.30.refs_2_.refs_11_.refs_8_ = bf16[2,128,1024]{2,1,0:T(8,128)(2,1)} collective-permute-done((bf16[2,128,1024]{2,1,0:T(8,128)(2,1)}, bf16[2,128,1024]{2,1,0:T(8,128)(2,1)}, u32[]{:S(2)}, u32[]{:S(2)}) %collective-permute-start.30) | collective-permute-done | bytes 524320 | tf_op jit(solution)/shard_map/ppermute | solution.py:28
  235.6 8.8 %shard_map.110 = (f32[512,2048]{1,0:T(8,128)}, f32[512,2048]{1,0:T(8,128)}, f32[8,128]{1,0:T(8,128)}) custom-call(bf16[1,128,512]{2,1,0:T(8,128)(2,1)} %get-tuple-element.152.refs_0_.refs_2_, bf16[1,128,512]{2,1,0:T(8,128)(2,1)} %collective-permute-done.25.refs_5_.refs_1_.refs_3_, bf16[1,128,512]{2,1,0:T(8,128)(2,1)} %collective-permute-done.21.refs_3_.refs_2_.refs_4_, ...), custom_call_target="tpu_custom_call" | custom-call | flops 1 | bytes 1 | tf_op jit(solution)/shard_map/pallas_call | solution.py:65
  247.3 7.5 %shard_map.112 = (bf16[2048,3328]{1,0:T(8,128)(2,1)}, bf16[2048,3328]{1,0:T(8,128)(2,1)}, bf16[3328,2048]{1,0:T(8,128)(2,1)}, f32[8,128]{1,0:T(8,128)}) custom-call(bf16[2048,512]{1,0:T(8,128)(2,1)} %get-tuple-element.172.refs_0_, bf16[512,2048]{1,0:T(8,128)(2,1)} %bitcast.15, bf16[1,128,512]{2,1,0:T(8,128)(2,1)} %get-tuple-element.152.refs_0_.refs_2_, ...), custom_call_target="tpu_custom_call" | custom-call | flops 1 | bytes 1 | tf_op jit(solution)/shard_map/pallas_call | solution.py:65
  254.8 4.0 shard_map.113
  261.8 12.1 %collective-permute-done.45.refs_10_.refs_2_.refs_8_ = bf16[2,128,1024]{2,1,0:T(8,128)(2,1)} collective-permute-done((bf16[2,128,1024]{2,1,0:T(8,128)(2,1)}, bf16[2,128,1024]{2,1,0:T(8,128)(2,1)}, u32[]{:S(2)}, u32[]{:S(2)}) %collective-permute-start.45) | collective-permute-done | bytes 524320 | tf_op jit(solution)/shard_map/ppermute | solution.py:28
  273.9 13.3 %collective-permute-done.37.refs_7_.refs_2_.refs_4_ = bf16[1,128,1024]{2,1,0:T(8,128)(2,1)} collective-permute-done((bf16[1,128,1024]{2,1,0:T(8,128)(2,1)}, bf16[1,128,1024]{2,1,0:T(8,128)(2,1)}, u32[]{:S(2)}, u32[]{:S(2)}) %collective-permute-start.37) | collective-permute-done | bytes 262176 | tf_op jit(solution)/shard_map/ppermute | solution.py:28
  287.3 13.9 %shard_map.114 = (f32[512,2048]{1,0:T(8,128)}, f32[512,2048]{1,0:T(8,128)}, f32[8,128]{1,0:T(8,128)}) custom-call(bf16[1,128,1024]{2,1,0:T(8,128)(2,1)} %get-tuple-element.167.refs_0_.refs_2_, bf16[1,128,1024]{2,1,0:T(8,128)(2,1)} %collective-permute-done.32.refs_4_.refs_1_.refs_3_, ...), custom_call_target="tpu_custom_call", output_to_operand_aliasing={{0}: (8, {}), {1}: (21, {})} | custom-call | flops 1 | bytes 1 | tf_op jit(solution)/shard_map/pallas_call | solution.py:65
  301.2 3.5 shard_map.115
  307.2 6.0 %collective-permute-done.42.refs_9_.refs_2_.refs_4_ = bf16[1,128,768]{2,1,0:T(8,128)(2,1)} collective-permute-done((bf16[1,128,768]{2,1,0:T(8,128)(2,1)}, bf16[1,128,768]{2,1,0:T(8,128)(2,1)}, u32[]{:S(2)}, u32[]{:S(2)}) %collective-permute-start.42) | collective-permute-done | bytes 196640 | tf_op jit(solution)/shard_map/ppermute | solution.py:28
  313.2 11.3 %shard_map.116 = (bf16[2048,3328]{1,0:T(8,128)(2,1)}, bf16[2048,3328]{1,0:T(8,128)(2,1)}, bf16[3328,2048]{1,0:T(8,128)(2,1)}, f32[8,128]{1,0:T(8,128)}) custom-call(bf16[2048,512]{1,0:T(8,128)(2,1)} %get-tuple-element.172.refs_0_, bf16[512,2048]{1,0:T(8,128)(2,1)} %bitcast.16, ...), custom_call_target="tpu_custom_call", output_to_operand_aliasing={{0}: (10, {}), {1}: (11, {}), {2}: (12, {})} | custom-call | flops 1 | bytes 1 | tf_op jit(solution)/shard_map/pallas_call | solution.py:65
  324.5 7.6 %shard_map.117 = (f32[512,2048]{1,0:T(8,128)}, f32[8,128]{1,0:T(8,128)}) custom-call(bf16[1,128,1024]{2,1,0:T(8,128)(2,1)} %get-tuple-element.175.refs_0_.refs_2_, bf16[1,128,1024]{2,1,0:T(8,128)(2,1)} %collective-permute-done.38.refs_8_.refs_1_.refs_3_, ...), custom_call_target="tpu_custom_call", output_to_operand_aliasing={{0}: (8, {})} | custom-call | flops 1 | bytes 1 | tf_op jit(solution)/shard_map/pallas_call | solution.py:65
  332.8 4.0 shard_map.118
  339.4 10.6 %shard_map.119 = (f32[512,2048]{1,0:T(8,128)}, f32[8,128]{1,0:T(8,128)}) custom-call(bf16[2,128,1024]{2,1,0:T(8,128)(2,1)} %get-tuple-element.176.refs_0_.refs_6_, bf16[2,128,1024]{2,1,0:T(8,128)(2,1)} %collective-permute-done.39.refs_9_.refs_1_.refs_7_, ...), custom_call_target="tpu_custom_call", output_to_operand_aliasing={{0}: (12, {})} | custom-call | flops 1 | bytes 1 | tf_op jit(solution)/shard_map/pallas_call | solution.py:65
  353.6 3.9 shard_map.121
  358.1 5.6 %shard_map.122 = (f32[4,4,16,1024]{3,2,1,0:T(8,128)}, bf16[4,4,16,1024]{3,2,1,0:T(8,128)(2,1)}, f32[8,128]{1,0:T(8,128)}) custom-call(bf16[2,128,768]{2,1,0:T(8,128)(2,1)} %get-tuple-element.183.refs_0_.refs_6_, bf16[2,128,768]{2,1,0:T(8,128)(2,1)} %collective-permute-done.46.refs_12_.refs_1_.refs_7_, ...), custom_call_target="tpu_custom_call" | custom-call | flops 1 | bytes 1 | tf_op jit(solution)/shard_map/pallas_call | solution.py:65
  365.2 4.2 collective-permute-start.51
  373.8 8.2 %collective-permute-done.52.refs_3_ = bf16[4,16,1024]{2,1,0:T(8,128)(2,1)} collective-permute-done((bf16[4,16,1024]{2,1,0:T(8,128)(2,1)}, bf16[4,16,1024]{2,1,0:T(8,128)(2,1)}, u32[]{:S(2)}, u32[]{:S(2)}) %collective-permute-start.52) | collective-permute-done | bytes 131104 | tf_op jit(solution)/shard_map/ppermute | solution.py:32
  384.2 5.6 %shard_map.124 = (f32[4,4,16,1024]{3,2,1,0:T(8,128)}, bf16[4,4,16,1024]{3,2,1,0:T(8,128)(2,1)}, f32[8,128]{1,0:T(8,128)}) custom-call(bf16[2,128,768]{2,1,0:T(8,128)(2,1)} %get-tuple-element.183.refs_0_.refs_6_, bf16[2,128,768]{2,1,0:T(8,128)(2,1)} %collective-permute-done.46.refs_12_.refs_1_.refs_7_, ...), custom_call_target="tpu_custom_call" | custom-call | flops 1 | bytes 1 | tf_op jit(solution)/shard_map/pallas_call | solution.py:65
  397.1 7.2 %collective-permute-done.56.refs_3_.refs_7_ = bf16[4,16,1024]{2,1,0:T(8,128)(2,1)} collective-permute-done((bf16[4,16,1024]{2,1,0:T(8,128)(2,1)}, bf16[4,16,1024]{2,1,0:T(8,128)(2,1)}, u32[]{:S(2)}, u32[]{:S(2)}) %collective-permute-start.56) | collective-permute-done | bytes 131104 | tf_op jit(solution)/shard_map/ppermute | solution.py:32
  411.0 11.3 %shard_map.126 = (bf16[2048,3328]{1,0:T(8,128)(2,1)}, bf16[2048,3328]{1,0:T(8,128)(2,1)}, bf16[3328,2048]{1,0:T(8,128)(2,1)}, f32[8,128]{1,0:T(8,128)}) custom-call(bf16[2048,512]{1,0:T(8,128)(2,1)} %get-tuple-element.172.refs_0_, bf16[512,2048]{1,0:T(8,128)(2,1)} %bitcast.17, ...), custom_call_target="tpu_custom_call", output_to_operand_aliasing={{0}: (10, {}), {1}: (11, {}), {2}: (12, {})} | custom-call | flops 1 | bytes 1 | tf_op jit(solution)/shard_map/pallas_call | solution.py:65
  429.4 9.4 %shard_map.128 = (bf16[2048,3328]{1,0:T(8,128)(2,1)}, bf16[2048,3328]{1,0:T(8,128)(2,1)}, bf16[3328,2048]{1,0:T(8,128)(2,1)}, f32[8,128]{1,0:T(8,128)}) custom-call(bf16[2048,512]{1,0:T(8,128)(2,1)} %get-tuple-element.172.refs_0_, bf16[512,2048]{1,0:T(8,128)(2,1)} %bitcast.18, ...), custom_call_target="tpu_custom_call", output_to_operand_aliasing={{0}: (10, {}), {1}: (11, {}), {2}: (12, {})} | custom-call | flops 1 | bytes 1 | tf_op jit(solution)/shard_map/pallas_call | solution.py:65
  445.6 3.3 collective-permute-done.67.refs_3_
  (157 shorter events, 102.4 us)
Async XLA Ops:
  6.5 11.9 %collective-permute-start.10 = (bf16[64,2048]{1,0:T(8,128)(2,1)}, bf16[64,2048]{1,0:T(8,128)(2,1)}, u32[]{:S(2)}, u32[]{:S(2)}) collective-permute-start(bf16[64,2048]{1,0:T(8,128)(2,1)} %refs_1_.8), channel_id=1, source_target_pairs={{0,24},{4,28},{8,16},{12,20},{16,8},{20,12},{24,0},{28,4},{1,25},{... | collective-permute-start | bytes 786440 | tf_op jit(solution)/shard_map/ppermute | solution.py:32
  12.3 12.4 %collective-permute-start.8 = (bf16[64,2048]{1,0:T(8,128)(2,1)}, bf16[64,2048]{1,0:T(8,128)(2,1)}, u32[]{:S(2)}, u32[]{:S(2)}) collective-permute-start(bf16[64,2048]{1,0:T(8,128)(2,1)} %refs_1_.8), channel_id=1, source_target_pairs={{0,8},{4,12},{8,0},{12,4},{16,24},{20,28},{24,16},{28,20},{1,9},{5... | collective-permute-start | bytes 786440 | tf_op jit(solution)/shard_map/ppermute | solution.py:32
  12.4 21.7 %collective-permute-start.9 = (bf16[64,2048]{1,0:T(8,128)(2,1)}, bf16[64,2048]{1,0:T(8,128)(2,1)}, u32[]{:S(2)}, u32[]{:S(2)}) collective-permute-start(bf16[64,2048]{1,0:T(8,128)(2,1)} %refs_1_.8), channel_id=1, source_target_pairs={{0,16},{4,20},{8,24},{12,28},{16,0},{20,4},{24,8},{28,12},{1,17},{... | collective-permute-start | bytes 786440 | tf_op jit(solution)/shard_map/ppermute | solution.py:32
  13.8 20.2 %collective-permute-start = (bf16[64,2048]{1,0:T(8,128)(2,1)S(1)}, bf16[64,2048]{1,0:T(8,128)(2,1)}, u32[]{:S(2)}, u32[]{:S(2)}) collective-permute-start(bf16[64,2048]{1,0:T(8,128)(2,1)S(1)} %bitcast.23), channel_id=1, source_target_pairs={{0,4},{4,0},{8,12},{12,8},{16,20},{20,16},{24,28},{28,24},{1,5},{5... | collective-permute-start | bytes 786440 | tf_op jit(solution)/shard_map/ppermute | solution.py:32
  37.3 23.4 %collective-permute-start.11 = (bf16[3,64,2048]{2,1,0:T(8,128)(2,1)}, bf16[3,64,2048]{2,1,0:T(8,128)(2,1)}, u32[]{:S(2)}, u32[]{:S(2)}) collective-permute-start(bf16[3,64,2048]{2,1,0:T(8,128)(2,1)} %get-tuple-element.125), channel_id=1, source_target_pairs={{0,4},{4,0},{8,12},{12,8},{16,20},{20,16},{24,28},{28,24},{1,5},{5... | collective-permute-start | bytes 2359304 | tf_op jit(solution)/shard_map/ppermute | solution.py:32
  38.8 12.6 %collective-permute-start.1 = (bf16[64,2048]{1,0:T(8,128)(2,1)}, bf16[64,2048]{1,0:T(8,128)(2,1)}, u32[]{:S(2)}, u32[]{:S(2)}) collective-permute-start(bf16[64,2048]{1,0:T(8,128)(2,1)} %bitcast.25), channel_id=1, source_target_pairs={{0,8},{4,12},{8,0},{12,4},{16,24},{20,28},{24,16},{28,20},{1,9},{5... | collective-permute-start | bytes 786440 | tf_op jit(solution)/shard_map/ppermute | solution.py:32
  38.8 21.9 %collective-permute-start.3 = (bf16[64,2048]{1,0:T(8,128)(2,1)}, bf16[64,2048]{1,0:T(8,128)(2,1)}, u32[]{:S(2)}, u32[]{:S(2)}) collective-permute-start(bf16[64,2048]{1,0:T(8,128)(2,1)} %bitcast.26), channel_id=1, source_target_pairs={{0,16},{4,20},{8,24},{12,28},{16,0},{20,4},{24,8},{28,12},{1,17},{... | collective-permute-start | bytes 786440 | tf_op jit(solution)/shard_map/ppermute | solution.py:32
  41.9 18.8 %collective-permute-start.5 = (bf16[64,2048]{1,0:T(8,128)(2,1)}, bf16[64,2048]{1,0:T(8,128)(2,1)}, u32[]{:S(2)}, u32[]{:S(2)}) collective-permute-start(bf16[64,2048]{1,0:T(8,128)(2,1)} %bitcast.27), channel_id=1, source_target_pairs={{0,24},{4,28},{8,16},{12,20},{16,8},{20,12},{24,0},{28,4},{1,25},{... | collective-permute-start | bytes 786440 | tf_op jit(solution)/shard_map/ppermute | solution.py:32
  73.1 21.5 %collective-permute-start.12 = (f32[2,128,1536]{2,1,0:T(8,128)}, f32[2,128,1536]{2,1,0:T(8,128)}, u32[]{:S(2)}, u32[]{:S(2)}) collective-permute-start(f32[2,128,1536]{2,1,0:T(8,128)} %get-tuple-element.130), channel_id=1, source_target_pairs={{0,1},{1,0},{2,3},{3,2},{4,5},{5,4},{6,7},{7,6},{8,9},{9,8},{10,11... | collective-permute-start | bytes 4718600 | tf_op jit(solution)/shard_map/ppermute | solution.py:28
  73.7 14.5 %collective-permute-start.4 = (bf16[64,2048]{1,0:T(8,128)(2,1)}, bf16[64,2048]{1,0:T(8,128)(2,1)}, u32[]{:S(2)}, u32[]{:S(2)}) collective-permute-start(bf16[64,2048]{1,0:T(8,128)(2,1)} %collective-permute-done.3.refs_10_.refs_5_), channel_id=1, source_target_pairs={{0,4},{4,0},{8,12},{12,8},{16,20},{20,16},{24,28},{28,24},{1,5},{5... | collective-permute-start | bytes 786440 | tf_op jit(solution)/shard_map/ppermute | solution.py:32
  75.2 19.4 %collective-permute-start.6 = (bf16[64,2048]{1,0:T(8,128)(2,1)}, bf16[64,2048]{1,0:T(8,128)(2,1)}, u32[]{:S(2)}, u32[]{:S(2)}) collective-permute-start(bf16[64,2048]{1,0:T(8,128)(2,1)} %collective-permute-done.5.refs_11_.refs_7_), channel_id=1, source_target_pairs={{0,4},{4,0},{8,12},{12,8},{16,20},{20,16},{24,28},{28,24},{1,5},{5... | collective-permute-start | bytes 786440 | tf_op jit(solution)/shard_map/ppermute | solution.py:32
  94.6 17.0 %collective-permute-start.14 = (f32[2,128,1024]{2,1,0:T(8,128)}, f32[2,128,1024]{2,1,0:T(8,128)}, u32[]{:S(2)}, u32[]{:S(2)}) collective-permute-start(f32[2,128,1024]{2,1,0:T(8,128)} %get-tuple-element.139), channel_id=1, source_target_pairs={{0,1},{1,0},{2,3},{3,2},{4,5},{5,4},{6,7},{7,6},{8,9},{9,8},{10,11... | collective-permute-start | bytes 3145736 | tf_op jit(solution)/shard_map/ppermute | solution.py:28
  109.5 22.9 %collective-permute-start.13 = (f32[2,2,128,512]{3,2,1,0:T(8,128)}, f32[2,2,128,512]{3,2,1,0:T(8,128)}, u32[]{:S(2)}, u32[]{:S(2)}) collective-permute-start(f32[2,2,128,512]{3,2,1,0:T(8,128)} %get-tuple-element.137), channel_id=1, source_target_pairs={{0,1},{1,0},{2,3},{3,2},{4,5},{5,4},{6,7},{7,6},{8,9},{9,8},{10,11... | collective-permute-start | bytes 3145736 | tf_op jit(solution)/shard_map/ppermute | solution.py:28
  131.9 13.2 %collective-permute-start.18 = (f32[2,128,768]{2,1,0:T(8,128)}, f32[2,128,768]{2,1,0:T(8,128)}, u32[]{:S(2)}, u32[]{:S(2)}) collective-permute-start(f32[2,128,768]{2,1,0:T(8,128)} %get-tuple-element.147), channel_id=1, source_target_pairs={{0,1},{1,0},{2,3},{3,2},{4,5},{5,4},{6,7},{7,6},{8,9},{9,8},{10,11... | collective-permute-start | bytes 2359304 | tf_op jit(solution)/shard_map/ppermute | solution.py:28
  143.4 36.7 %collective-permute-start.23 = (f32[2,2,128,1024]{3,2,1,0:T(8,128)}, f32[2,2,128,1024]{3,2,1,0:T(8,128)}, u32[]{:S(2)}, u32[]{:S(2)}) collective-permute-start(f32[2,2,128,1024]{3,2,1,0:T(8,128)} %get-tuple-element.154), channel_id=1, source_target_pairs={{0,1},{1,0},{2,3},{3,2},{4,5},{5,4},{6,7},{7,6},{8,9},{9,8},{10,11... | collective-permute-start | bytes 6291464 | tf_op jit(solution)/shard_map/ppermute | solution.py:28
  166.5 44.1 %collective-permute-start.28 = (f32[2,2,128,1024]{3,2,1,0:T(8,128)}, f32[2,2,128,1024]{3,2,1,0:T(8,128)}, u32[]{:S(2)}, u32[]{:S(2)}) collective-permute-start(f32[2,2,128,1024]{3,2,1,0:T(8,128)} %get-tuple-element.162), channel_id=1, source_target_pairs={{0,1},{1,0},{2,3},{3,2},{4,5},{5,4},{6,7},{7,6},{8,9},{9,8},{10,11... | collective-permute-start | bytes 6291464 | tf_op jit(solution)/shard_map/ppermute | solution.py:28
  166.5 11.8 %collective-permute-start.19 = (bf16[2,128,512]{2,1,0:T(8,128)(2,1)}, bf16[2,128,512]{2,1,0:T(8,128)(2,1)}, u32[]{:S(2)}, u32[]{:S(2)}) collective-permute-start(bf16[2,128,512]{2,1,0:T(8,128)(2,1)} %get-tuple-element.151.refs_6_), channel_id=1, source_target_pairs={{0,2},{1,3},{2,0},{3,1},{4,6},{5,7},{6,4},{7,5},{8,10},{9,11},{10,... | collective-permute-start | bytes 786440 | tf_op jit(solution)/shard_map/ppermute | solution.py:28
  191.9 52.5 %collective-permute-start.26 = (f32[2,2,128,768]{3,2,1,0:T(8,128)}, f32[2,2,128,768]{3,2,1,0:T(8,128)}, u32[]{:S(2)}, u32[]{:S(2)}) collective-permute-start(f32[2,2,128,768]{3,2,1,0:T(8,128)} %get-tuple-element.159), channel_id=1, source_target_pairs={{0,1},{1,0},{2,3},{3,2},{4,5},{5,4},{6,7},{7,6},{8,9},{9,8},{10,11... | collective-permute-start | bytes 4718600 | tf_op jit(solution)/shard_map/ppermute | solution.py:28
  192.2 18.4 %collective-permute-start.27 = (bf16[2,128,1024]{2,1,0:T(8,128)(2,1)}, bf16[2,128,1024]{2,1,0:T(8,128)(2,1)}, u32[]{:S(2)}, u32[]{:S(2)}) collective-permute-start(bf16[2,128,1024]{2,1,0:T(8,128)(2,1)} %get-tuple-element.160), channel_id=1, source_target_pairs={{0,2},{1,3},{2,0},{3,1},{4,6},{5,7},{6,4},{7,5},{8,10},{9,11},{10,... | collective-permute-start | bytes 1572872 | tf_op jit(solution)/shard_map/ppermute | solution.py:28
  193.8 16.8 %collective-permute-start.29 = (bf16[128,768]{1,0:T(8,128)(2,1)}, bf16[128,768]{1,0:T(8,128)(2,1)S(1)}, u32[]{:S(2)}, u32[]{:S(2)}) collective-permute-start(bf16[128,768]{1,0:T(8,128)(2,1)} %get-tuple-element.163), channel_id=1, source_target_pairs={{0,2},{1,3},{2,0},{3,1},{4,6},{5,7},{6,4},{7,5},{8,10},{9,11},{10,... | collective-permute-start | bytes 589832 | tf_op jit(solution)/shard_map/ppermute | solution.py:28
  218.8 15.2 %collective-permute-start.30 = (bf16[2,128,1024]{2,1,0:T(8,128)(2,1)}, bf16[2,128,1024]{2,1,0:T(8,128)(2,1)}, u32[]{:S(2)}, u32[]{:S(2)}) collective-permute-start(bf16[2,128,1024]{2,1,0:T(8,128)(2,1)} %get-tuple-element.166.refs_9_.refs_6_), channel_id=1, source_target_pairs={{0,2},{1,3},{2,0},{3,1},{4,6},{5,7},{6,4},{7,5},{8,10},{9,11},{10,... | collective-permute-start | bytes 1572872 | tf_op jit(solution)/shard_map/ppermute | solution.py:28
  220.4 24.0 %collective-permute-start.31 = (bf16[2,128,1024]{2,1,0:T(8,128)(2,1)}, bf16[2,128,1024]{2,1,0:T(8,128)(2,1)}, u32[]{:S(2)}, u32[]{:S(2)}) collective-permute-start(bf16[2,128,1024]{2,1,0:T(8,128)(2,1)} %get-tuple-element.166.refs_9_.refs_6_), channel_id=1, source_target_pairs={{0,1},{1,0},{2,3},{3,2},{4,5},{5,4},{6,7},{7,6},{8,9},{9,8},{10,11... | collective-permute-start | bytes 1572872 | tf_op jit(solution)/shard_map/ppermute | solution.py:28
  220.4 13.6 %collective-permute-start.32 = (bf16[1,128,1024]{2,1,0:T(8,128)(2,1)}, bf16[1,128,1024]{2,1,0:T(8,128)(2,1)}, u32[]{:S(2)}, u32[]{:S(2)}) collective-permute-start(bf16[1,128,1024]{2,1,0:T(8,128)(2,1)} %get-tuple-element.167.refs_0_.refs_2_), channel_id=1, source_target_pairs={{0,1},{1,0},{2,3},{3,2},{4,5},{5,4},{6,7},{7,6},{8,9},{9,8},{10,11... | collective-permute-start | bytes 786440 | tf_op jit(solution)/shard_map/ppermute | solution.py:28
  220.9 33.9 %collective-permute-start.34 = (bf16[2,128,1024]{2,1,0:T(8,128)(2,1)}, bf16[2,128,1024]{2,1,0:T(8,128)(2,1)}, u32[]{:S(2)}, u32[]{:S(2)}) collective-permute-start(bf16[2,128,1024]{2,1,0:T(8,128)(2,1)} %get-tuple-element.171), channel_id=1, source_target_pairs={{0,2},{1,3},{2,0},{3,1},{4,6},{5,7},{6,4},{7,5},{8,10},{9,11},{10,... | collective-permute-start | bytes 1572872 | tf_op jit(solution)/shard_map/ppermute | solution.py:28
  234.0 20.8 %collective-permute-start.36 = (bf16[2,128,1024]{2,1,0:T(8,128)(2,1)}, bf16[2,128,1024]{2,1,0:T(8,128)(2,1)}, u32[]{:S(2)}, u32[]{:S(2)}) collective-permute-start(bf16[2,128,1024]{2,1,0:T(8,128)(2,1)} %collective-permute-done.30.refs_2_.refs_11_.refs_8_), channel_id=1, source_target_pairs={{0,1},{1,0},{2,3},{3,2},{4,5},{5,4},{6,7},{7,6},{8,9},{9,8},{10,11... | collective-permute-start | bytes 1572872 | tf_op jit(solution)/shard_map/ppermute | solution.py:28
  234.0 20.8 %collective-permute-start.35 = (bf16[1,128,1024]{2,1,0:T(8,128)(2,1)}, bf16[1,128,1024]{2,1,0:T(8,128)(2,1)}, u32[]{:S(2)}, u32[]{:S(2)}) collective-permute-start(bf16[1,128,1024]{2,1,0:T(8,128)(2,1)} %get-tuple-element.167.refs_0_.refs_2_), channel_id=1, source_target_pairs={{0,2},{1,3},{2,0},{3,1},{4,6},{5,7},{6,4},{7,5},{8,10},{9,11},{10,... | collective-permute-start | bytes 786440 | tf_op jit(solution)/shard_map/ppermute | solution.py:28
  258.8 15.1 %collective-permute-start.45 = (bf16[2,128,1024]{2,1,0:T(8,128)(2,1)}, bf16[2,128,1024]{2,1,0:T(8,128)(2,1)}, u32[]{:S(2)}, u32[]{:S(2)}) collective-permute-start(bf16[2,128,1024]{2,1,0:T(8,128)(2,1)} %get-tuple-element.176.refs_0_.refs_6_), channel_id=1, source_target_pairs={{0,2},{1,3},{2,0},{3,1},{4,6},{5,7},{6,4},{7,5},{8,10},{9,11},{10,... | collective-permute-start | bytes 1572872 | tf_op jit(solution)/shard_map/ppermute | solution.py:28
  259.3 41.9 %collective-permute-start.39 = (bf16[2,128,1024]{2,1,0:T(8,128)(2,1)}, bf16[2,128,1024]{2,1,0:T(8,128)(2,1)}, u32[]{:S(2)}, u32[]{:S(2)}) collective-permute-start(bf16[2,128,1024]{2,1,0:T(8,128)(2,1)} %get-tuple-element.176.refs_0_.refs_6_), channel_id=1, source_target_pairs={{0,1},{1,0},{2,3},{3,2},{4,5},{5,4},{6,7},{7,6},{8,9},{9,8},{10,11... | collective-permute-start | bytes 1572872 | tf_op jit(solution)/shard_map/ppermute | solution.py:28
  259.8 41.4 %collective-permute-start.33 = (bf16[2,128,768]{2,1,0:T(8,128)(2,1)}, bf16[2,128,768]{2,1,0:T(8,128)(2,1)}, u32[]{:S(2)}, u32[]{:S(2)}) collective-permute-start(bf16[2,128,768]{2,1,0:T(8,128)(2,1)} %get-tuple-element.170), channel_id=1, source_target_pairs={{0,2},{1,3},{2,0},{3,1},{4,6},{5,7},{6,4},{7,5},{8,10},{9,11},{10,... | collective-permute-start | bytes 1179656 | tf_op jit(solution)/shard_map/ppermute | solution.py:28
  261.4 25.9 %collective-permute-start.37 = (bf16[1,128,1024]{2,1,0:T(8,128)(2,1)}, bf16[1,128,1024]{2,1,0:T(8,128)(2,1)}, u32[]{:S(2)}, u32[]{:S(2)}) collective-permute-start(bf16[1,128,1024]{2,1,0:T(8,128)(2,1)} %get-tuple-element.175.refs_0_.refs_2_), channel_id=1, source_target_pairs={{0,2},{1,3},{2,0},{3,1},{4,6},{5,7},{6,4},{7,5},{8,10},{9,11},{10,... | collective-permute-start | bytes 786440 | tf_op jit(solution)/shard_map/ppermute | solution.py:28
  261.8 39.4 %collective-permute-start.38 = (bf16[1,128,1024]{2,1,0:T(8,128)(2,1)}, bf16[1,128,1024]{2,1,0:T(8,128)(2,1)}, u32[]{:S(2)}, u32[]{:S(2)}) collective-permute-start(bf16[1,128,1024]{2,1,0:T(8,128)(2,1)} %get-tuple-element.175.refs_0_.refs_2_), channel_id=1, source_target_pairs={{0,1},{1,0},{2,3},{3,2},{4,5},{5,4},{6,7},{7,6},{8,9},{9,8},{10,11... | collective-permute-start | bytes 786440 | tf_op jit(solution)/shard_map/ppermute | solution.py:28
  273.9 58.3 %collective-permute-start.47 = (bf16[2,128,1024]{2,1,0:T(8,128)(2,1)}, bf16[2,128,1024]{2,1,0:T(8,128)(2,1)}, u32[]{:S(2)}, u32[]{:S(2)}) collective-permute-start(bf16[2,128,1024]{2,1,0:T(8,128)(2,1)} %collective-permute-done.45.refs_10_.refs_2_.refs_8_), channel_id=1, source_target_pairs={{0,1},{1,0},{2,3},{3,2},{4,5},{5,4},{6,7},{7,6},{8,9},{9,8},{10,11... | collective-permute-start | bytes 1572872 | tf_op jit(solution)/shard_map/ppermute | solution.py:28
  287.3 19.9 %collective-permute-start.44 = (bf16[1,128,1024]{2,1,0:T(8,128)(2,1)}, bf16[1,128,1024]{2,1,0:T(8,128)(2,1)}, u32[]{:S(2)}, u32[]{:S(2)}) collective-permute-start(bf16[1,128,1024]{2,1,0:T(8,128)(2,1)} %collective-permute-done.37.refs_7_.refs_2_.refs_4_), channel_id=1, source_target_pairs={{0,1},{1,0},{2,3},{3,2},{4,5},{5,4},{6,7},{7,6},{8,9},{9,8},{10,11... | collective-permute-start | bytes 786440 | tf_op jit(solution)/shard_map/ppermute | solution.py:28
  304.7 19.9 %collective-permute-start.46 = (bf16[2,128,768]{2,1,0:T(8,128)(2,1)}, bf16[2,128,768]{2,1,0:T(8,128)(2,1)}, u32[]{:S(2)}, u32[]{:S(2)}) collective-permute-start(bf16[2,128,768]{2,1,0:T(8,128)(2,1)} %get-tuple-element.183.refs_0_.refs_6_), channel_id=1, source_target_pairs={{0,1},{1,0},{2,3},{3,2},{4,5},{5,4},{6,7},{7,6},{8,9},{9,8},{10,11... | collective-permute-start | bytes 1179656 | tf_op jit(solution)/shard_map/ppermute | solution.py:28
  305.6 26.6 %collective-permute-start.48 = (bf16[2,128,768]{2,1,0:T(8,128)(2,1)}, bf16[2,128,768]{2,1,0:T(8,128)(2,1)}, u32[]{:S(2)}, u32[]{:S(2)}) collective-permute-start(bf16[2,128,768]{2,1,0:T(8,128)(2,1)} %get-tuple-element.183.refs_0_.refs_6_), channel_id=1, source_target_pairs={{0,2},{1,3},{2,0},{3,1},{4,6},{5,7},{6,4},{7,5},{8,10},{9,11},{10,... | collective-permute-start | bytes 1179656 | tf_op jit(solution)/shard_map/ppermute | solution.py:28
  307.2 17.3 %collective-permute-start.41 = (bf16[1,128,768]{2,1,0:T(8,128)(2,1)}, bf16[1,128,768]{2,1,0:T(8,128)(2,1)}, u32[]{:S(2)}, u32[]{:S(2)}) collective-permute-start(bf16[1,128,768]{2,1,0:T(8,128)(2,1)} %get-tuple-element.181.refs_0_.refs_2_), channel_id=1, source_target_pairs={{0,1},{1,0},{2,3},{3,2},{4,5},{5,4},{6,7},{7,6},{8,9},{9,8},{10,11... | collective-permute-start | bytes 589832 | tf_op jit(solution)/shard_map/ppermute | solution.py:28
  313.2 18.9 %collective-permute-start.43 = (bf16[1,128,768]{2,1,0:T(8,128)(2,1)}, bf16[1,128,768]{2,1,0:T(8,128)(2,1)S(1)}, u32[]{:S(2)}, u32[]{:S(2)}) collective-permute-start(bf16[1,128,768]{2,1,0:T(8,128)(2,1)} %collective-permute-done.42.refs_9_.refs_2_.refs_4_), channel_id=1, source_target_pairs={{0,1},{1,0},{2,3},{3,2},{4,5},{5,4},{6,7},{7,6},{8,9},{9,8},{10,11... | collective-permute-start | bytes 589832 | tf_op jit(solution)/shard_map/ppermute | solution.py:28
  336.8 14.7 %collective-permute-start.49 = (bf16[4,4,16,1024]{3,2,1,0:T(8,128)(2,1)}, bf16[4,4,16,1024]{3,2,1,0:T(8,128)(2,1)}, u32[]{:S(2)}, u32[]{:S(2)}) collective-permute-start(bf16[4,4,16,1024]{3,2,1,0:T(8,128)(2,1)} %get-tuple-element.192), channel_id=1, source_target_pairs={{0,4},{4,0},{8,12},{12,8},{16,20},{20,16},{24,28},{28,24},{1,5},{5... | collective-permute-start | bytes 1572872 | tf_op jit(solution)/shard_map/ppermute | solution.py:32
  357.6 24.5 %collective-permute-start.54 = (bf16[4,4,16,1024]{3,2,1,0:T(8,128)(2,1)}, bf16[4,4,16,1024]{3,2,1,0:T(8,128)(2,1)}, u32[]{:S(2)}, u32[]{:S(2)}) collective-permute-start(bf16[4,4,16,1024]{3,2,1,0:T(8,128)(2,1)} %get-tuple-element.202), channel_id=1, source_target_pairs={{0,4},{4,0},{8,12},{12,8},{16,20},{20,16},{24,28},{28,24},{1,5},{5... | collective-permute-start | bytes 1572872 | tf_op jit(solution)/shard_map/ppermute | solution.py:32
  363.7 31.2 %collective-permute-start.59 = (bf16[4,4,16,1024]{3,2,1,0:T(8,128)(2,1)}, bf16[4,4,16,1024]{3,2,1,0:T(8,128)(2,1)}, u32[]{:S(2)}, u32[]{:S(2)}) collective-permute-start(bf16[4,4,16,1024]{3,2,1,0:T(8,128)(2,1)} %get-tuple-element.214), channel_id=1, source_target_pairs={{0,4},{4,0},{8,12},{12,8},{16,20},{20,16},{24,28},{28,24},{1,5},{5... | collective-permute-start | bytes 1572872 | tf_op jit(solution)/shard_map/ppermute | solution.py:32
  369.5 12.5 %collective-permute-start.52 = (bf16[4,16,1024]{2,1,0:T(8,128)(2,1)}, bf16[4,16,1024]{2,1,0:T(8,128)(2,1)}, u32[]{:S(2)}, u32[]{:S(2)}) collective-permute-start(bf16[4,16,1024]{2,1,0:T(8,128)(2,1)} %get-tuple-element.198), channel_id=1, source_target_pairs={{0,16},{4,20},{8,24},{12,28},{16,0},{20,4},{24,8},{28,12},{1,17},{... | collective-permute-start | bytes 393224 | tf_op jit(solution)/shard_map/ppermute | solution.py:32
  389.8 32.5 %collective-permute-start.58 = (bf16[4,4,16,1024]{3,2,1,0:T(8,128)(2,1)}, bf16[4,4,16,1024]{3,2,1,0:T(8,128)(2,1)}, u32[]{:S(2)}, u32[]{:S(2)}) collective-permute-start(bf16[4,4,16,1024]{3,2,1,0:T(8,128)(2,1)} %get-tuple-element.212), channel_id=1, source_target_pairs={{0,4},{4,0},{8,12},{12,8},{16,20},{20,16},{24,28},{28,24},{1,5},{5... | collective-permute-start | bytes 1572872 | tf_op jit(solution)/shard_map/ppermute | solution.py:32
  392.4 11.9 %collective-permute-start.56 = (bf16[4,16,1024]{2,1,0:T(8,128)(2,1)}, bf16[4,16,1024]{2,1,0:T(8,128)(2,1)}, u32[]{:S(2)}, u32[]{:S(2)}) collective-permute-start(bf16[4,16,1024]{2,1,0:T(8,128)(2,1)} %get-tuple-element.208), channel_id=1, source_target_pairs={{0,16},{4,20},{8,24},{12,28},{16,0},{20,4},{24,8},{28,12},{1,17},{... | collective-permute-start | bytes 393224 | tf_op jit(solution)/shard_map/ppermute | solution.py:32
  406.5 15.8 %collective-permute-start.60 = (bf16[4,16,1024]{2,1,0:T(8,128)(2,1)}, bf16[4,16,1024]{2,1,0:T(8,128)(2,1)S(1)}, u32[]{:S(2)}, u32[]{:S(2)}) collective-permute-start(bf16[4,16,1024]{2,1,0:T(8,128)(2,1)} %get-tuple-element.216), channel_id=1, source_target_pairs={{0,8},{4,12},{8,0},{12,4},{16,24},{20,28},{24,16},{28,20},{1,9},{5... | collective-permute-start | bytes 393224 | tf_op jit(solution)/shard_map/ppermute | solution.py:32
  408.4 13.8 %collective-permute-start.61 = (bf16[4,16,1024]{2,1,0:T(8,128)(2,1)}, bf16[4,16,1024]{2,1,0:T(8,128)(2,1)}, u32[]{:S(2)}, u32[]{:S(2)}) collective-permute-start(bf16[4,16,1024]{2,1,0:T(8,128)(2,1)} %get-tuple-element.217), channel_id=1, source_target_pairs={{0,16},{4,20},{8,24},{12,28},{16,0},{20,4},{24,8},{28,12},{1,17},{... | collective-permute-start | bytes 393224 | tf_op jit(solution)/shard_map/ppermute | solution.py:32
  409.6 12.7 %collective-permute-start.62 = (bf16[4,16,1024]{2,1,0:T(8,128)(2,1)}, bf16[4,16,1024]{2,1,0:T(8,128)(2,1)}, u32[]{:S(2)}, u32[]{:S(2)}) collective-permute-start(bf16[4,16,1024]{2,1,0:T(8,128)(2,1)} %get-tuple-element.218), channel_id=1, source_target_pairs={{0,24},{4,28},{8,16},{12,20},{16,8},{20,12},{24,0},{28,4},{1,25},{... | collective-permute-start | bytes 393224 | tf_op jit(solution)/shard_map/ppermute | solution.py:32
  425.0 13.8 %collective-permute-start.63 = (bf16[4,16,1024]{2,1,0:T(8,128)(2,1)}, bf16[4,16,1024]{2,1,0:T(8,128)(2,1)S(1)}, u32[]{:S(2)}, u32[]{:S(2)}) collective-permute-start(bf16[4,16,1024]{2,1,0:T(8,128)(2,1)} %get-tuple-element.224), channel_id=1, source_target_pairs={{0,8},{4,12},{8,0},{12,4},{16,24},{20,28},{24,16},{28,20},{1,9},{5... | collective-permute-start | bytes 393224 | tf_op jit(solution)/shard_map/ppermute | solution.py:32
  426.0 12.9 %collective-permute-start.64 = (bf16[4,16,1024]{2,1,0:T(8,128)(2,1)}, bf16[4,16,1024]{2,1,0:T(8,128)(2,1)}, u32[]{:S(2)}, u32[]{:S(2)}) collective-permute-start(bf16[4,16,1024]{2,1,0:T(8,128)(2,1)} %get-tuple-element.225), channel_id=1, source_target_pairs={{0,16},{4,20},{8,24},{12,28},{16,0},{20,4},{24,8},{28,12},{1,17},{... | collective-permute-start | bytes 393224 | tf_op jit(solution)/shard_map/ppermute | solution.py:32
  (34 other events, 198.7 us)

commit v4 on v3

--- a/solution.py
+++ b/solution.py
@@ -10,6 +10,7 @@
 BF16, F32 = jnp.bfloat16, jnp.float32
 BLOCK = 256
 VMEM_LIMIT = 64 * 1024 * 1024 - 256 * 1024
+ORDER = (0, 2, 1, 3)
 NN = (((1,), (0,)), ((), ()))
 NT = (((1,), (1,)), ((), ()))
 TN = (((0,), (0,)), ((), ()))
@@ -80,6 +81,10 @@
         return res[:-1]
 
 
+def group(i):
+    return (i & 1) * 2 + (i >> 1)
+
+
 def join(chain, parts):
     rows, tile = parts[0].shape
     count, step = len(parts), rows // 4
@@ -116,7 +121,7 @@
         body,
         (4,),
         [
-            (p, (rows, tile), functools.partial(lambda at, g, s: (at + (s[0] ^ g), 0), at))
+            (p, (rows, tile), functools.partial(lambda at, i, s: (at + (s[0] ^ group(i)), 0), at))
             for p, at in slots
         ],
         outs,
@@ -125,95 +130,87 @@
     return [out.reshape(4 * q, tile), *rest]
 
 
-def parted(acc, q, keep, send):
-    for i in range(2):
-        keep[i] = acc[2 * i * q : (2 * i + 1) * q]
-        send[i] = acc[(2 * i + 1) * q : (2 * i + 2) * q]
-
-
 def back_part(chain, cot, down, base, blocks):
     tokens, tile = cot.shape
-    q, n = tokens // 4, blocks * BLOCK
+    half, n = tokens // 2, blocks * BLOCK
 
     def body(c, w, keep, send):
-        parted(dot(c[...], w[...], NT), q, keep, send)
-
-    out = ((2, q, n), F32, (2, q, BLOCK), lambda j: (0, 0, j))
+        acc = dot(c[...], w[...], NT)
+        keep[...] = acc[:half]
+        send[...] = acc[half:].astype(BF16)
+
+    block, at = (half, BLOCK), lambda j: (0, j)
+    outs = [((half, n), dtype, block, at) for dtype in (F32, BF16)]
     return chain(
         body,
         (blocks,),
         [(cot, cot.shape, lambda j: (0, 0)), (down, (BLOCK, tile), lambda j: (base + j, 0))],
-        [out, out],
+        outs,
         flops=2 * tokens * tile * n,
     )
 
 
 def gate_up_part(chain, act, gate, up, base, blocks):
     tokens, tile = act.shape
-    q, n = tokens // 4, blocks * BLOCK
+    half, n = tokens // 2, blocks * BLOCK
 
     def body(a, wg, wu, keep, send):
-        parted(dot(a[...], wg[...], NN), q, keep.at[:, 0], send.at[:, 0])
-        parted(dot(a[...], wu[...], NN), q, keep.at[:, 1], send.at[:, 1])
+        for k, w in enumerate((wg, wu)):
+            acc = dot(a[...], w[...], NN)
+            keep[k] = acc[:half]
+            send[k] = acc[half:].astype(BF16)
 
     weight = ((tile, BLOCK), lambda j: (0, base + j))
-    out = ((2, 2, q, n), F32, (2, 2, q, BLOCK), lambda j: (0, 0, 0, j))
+    block, at = (2, half, BLOCK), lambda j: (0, 0, j)
+    outs = [((2, half, n), dtype, block, at) for dtype in (F32, BF16)]
     return chain(
         body,
         (blocks,),
         [(act, act.shape, lambda j: (0, 0)), (gate, *weight), (up, *weight)],
-        [out, out],
+        outs,
         flops=4 * tokens * tile * n,
     )
 
 
 def add_away(chain, keep, got):
-    shape = keep.shape[1:]
-    zeros = (0,) * (len(shape) - 1)
-    block = (1, *shape[:-1], BLOCK)
+    lead, (half, n) = keep.shape[:-2], keep.shape[-2:]
+    zeros = (0,) * len(lead)
+    block = (*lead, half // 2, n)
 
     def body(a, b, out):
-        out[...] = (a[0] + b[0]).astype(BF16)
-
-    def at(j):
-        return (1, *zeros, j)
+        out[...] = (a[...] + b[...].astype(F32)).astype(BF16)
 
     (out,) = chain(
         body,
-        (shape[-1] // BLOCK,),
-        [(keep, block, at), (got, block, at)],
-        [(shape, BF16, block[1:], lambda j: (*zeros, j))],
+        (2,),
+        [(x, block, lambda i: (*zeros, 1 - i, 0)) for x in (keep, got)],
+        [(keep.shape, BF16, block, lambda i: (*zeros, i, 0))],
     )
     return out
 
 
-def activate(chain, keep_gu, got_gu, far_gu, keep_b, got_b, far_b, off):
-    n, q = far_gu.shape[-1], far_gu.shape[1]
-
-    def body(kg, gg, fg, kb, gb, fb, deltas, hidden):
-        gate = kg[0, 0] + gg[0, 0] + fg[0].astype(F32)
-        up = kg[0, 1] + gg[0, 1] + fg[1].astype(F32)
-        back = kb[0] + gb[0] + fb[...].astype(F32)
+def activate(chain, keep_gu, got_gu, far_gu, keep_b, got_b, far_b, off, blocks):
+    half, n = far_gu.shape[1:]
+    q = half // 2
+
+    def body(kg, gg, fg, kb, gb, fb, out):
+        gate = kg[0] + gg[0].astype(F32) + fg[0].astype(F32)
+        up = kg[1] + gg[1].astype(F32) + fg[1].astype(F32)
+        back = kb[...] + gb[...].astype(F32) + fb[...].astype(F32)
         active, slope = silu_parts(gate)
-        deltas[0] = (back * up * slope).astype(BF16)
-        deltas[1] = (back * active).astype(BF16)
-        hidden[0] = (active * up).astype(BF16)
-
-    four = ((1, 2, q, BLOCK), lambda j: (0, 0, 0, j))
-    three = ((1, q, BLOCK), lambda j: (0, 0, off + j))
-    return chain(
+        out[0] = (back * up * slope).astype(BF16)
+        out[1] = (back * active).astype(BF16)
+        out[2] = (active * up).astype(BF16)
+
+    two = ((2, half, BLOCK), lambda j: (0, 0, j))
+    one = ((half, BLOCK), lambda j: (0, off + j))
+    (out,) = chain(
         body,
         (n // BLOCK,),
-        [
-            (keep_gu, *four),
-            (got_gu, *four),
-            (far_gu, (2, q, BLOCK), lambda j: (0, 0, j)),
-            (keep_b, *three),
-            (got_b, *three),
-            (far_b, (q, BLOCK), lambda j: (0, off + j)),
-        ],
-        [((k, q, n), BF16, (k, q, BLOCK), lambda j: (0, 0, j)) for k in (2, 1)],
-    )
+        [(x, *two) for x in (keep_gu, got_gu, far_gu)] + [(x, *one) for x in (keep_b, got_b, far_b)],
+        [((3, half, n), BF16, (3, half, BLOCK), lambda j: (0, 0, j))],
+    )
+    return out
 
 
 def split_slots(acc, rows, keep, send):
@@ -223,21 +220,20 @@
         send[s] = view[:, 2 * s + 1].astype(BF16)
 
 
-def summed(chain, terms, base, blocks, halves=1, half=0, split=False):
-    kinds = sum(len(t[1]) for t in terms)
-    q, n = terms[0][0][0].shape[1:]
+def summed(chain, parts, terms, base, blocks, halves=1, half=0, split=False):
+    kinds = parts[0].shape[0]
+    half_rows, n = parts[0].shape[1:]
+    q = half_rows // 2
     rows = q // 8
     first_weight, dims = terms[0][1][0], terms[0][2]
     tile = first_weight.shape[1 if dims is NN else 0]
     width = tile // halves
     step = min(2 * BLOCK, width)
     off = half * (width // step)
-    ins, outs, alias, plan, moves = [], [], {}, [], []
-    for quarters, weights, dims, prev in terms:
-        refs, first = [], len(moves) // 4
-        for k in range(len(weights)):
-            moves += [(first + k, g, len(ins) + g, k) for g in range(4)]
-        ins += [(p, p.shape, lambda j: (0, 0, 0)) for p in quarters]
+    ins = [(p, p.shape, lambda j: (0, 0, 0)) for p in parts]
+    outs, alias, plan = [], {}, []
+    for first, weights, dims, prev in terms:
+        refs = []
         for w in weights:
             for i in range(blocks):
                 refs.append(len(ins))
@@ -267,8 +263,9 @@
 
         @pl.when(pl.program_id(0) == 0)
         def _():
-            for to, g, at, k in moves:
-                scratch[to, g * q : (g + 1) * q] = refs[at][k]
+            for g in range(2):
+                for k in range(kinds):
+                    scratch[k, g * half_rows : (g + 1) * half_rows] = refs[g][k]
 
         for first, count, dims, at, before, out in plan:
             total = None if before is None else refs[before][...]
@@ -288,28 +285,27 @@
         ins,
         outs,
         scratch=[pltpu.VMEM((kinds, 4 * q, n), BF16)],
-        flops=2 * kinds * 4 * q * n * width,
+        flops=6 * 4 * q * n * width,
         alias=alias,
     )
 
 
-def gradients(chain, act_t, cot, hidden, deltas, base, blocks, prev, units):
+def gradients(chain, act_t, cot, parts, base, blocks, prev, units):
     tile, tokens = act_t.shape
-    q = deltas[0].shape[1]
-    lead = 10
+    half = tokens // 2
+    lead = 4
 
     def body(*refs):
-        a, c, hid, dl = refs[0], refs[1], refs[2:6], refs[6:10]
+        a, c, own, near = refs[:lead]
         outs = refs[-3:]
         for k in range(2):
-            right = jnp.concatenate([p[k] for p in dl], axis=0)
+            right = jnp.concatenate([own[k], near[k]], axis=0)
             outs[k][...] = dot(a[...], right, NN).astype(BF16)
-        left = jnp.concatenate([p[0] for p in hid], axis=0)
+        left = jnp.concatenate([own[2], near[2]], axis=0)
         outs[2][...] = dot(left, c[...], TN).astype(BF16)
 
     ins = [(act_t, act_t.shape, lambda j: (0, 0)), (cot, cot.shape, lambda j: (0, 0))]
-    ins += [(p, (1, q, BLOCK), lambda j: (0, 0, j)) for p in hidden]
-    ins += [(p, (2, q, BLOCK), lambda j: (0, 0, j)) for p in deltas]
+    ins += [(p, (3, half, BLOCK), lambda j: (0, 0, j)) for p in parts]
     column = ((tile, units), BF16, (tile, BLOCK), lambda j: (0, base + j))
     outs = [column, column, ((units, tile), BF16, (BLOCK, tile), lambda j: (base + j, 0))]
     alias = {}
@@ -348,8 +344,8 @@
             for x in refs[4 * h + 1 : 4 * h + 4]:
                 total = total + x[...].astype(F32)
             columns = slice(h * width, (h + 1) * width)
-            for g in range(4):
-                rounded = total[g].astype(BF16)
+            for i, g in enumerate(ORDER):
+                rounded = total[i].astype(BF16)
                 if by_rows:
                     outs[0][s[0] ^ g, :, columns] = rounded
                 else:
@@ -407,13 +403,13 @@
     tile, units = gate_proj.shape
     sizes = chunk_sizes(units // BLOCK)
     chunks = [(sum(sizes[:c]), sizes[c]) for c in range(4)]
-    backs = [(0, sizes[0] + sizes[1]), chunks[2], chunks[3]]
-    back_of = [(0, 0), (0, sizes[0]), (1, 0), (2, 0)]
+    backs = [(0, chunks[2][0]), (chunks[2][0], sizes[2] + sizes[3])]
+    back_of = [(0, 0), (0, sizes[0]), (1, 0), (1, sizes[2])]
     chain = Chain()
 
     keep_b, got_b, far_b = {}, {}, {}
     keep_gu, got_gu, far_gu = {}, {}, {}
-    own, near, far, diag = {}, {}, {}, {}
+    own, near = {}, {}
     out = grad = grads = None
 
     def back(p):
@@ -432,34 +428,27 @@
 
     def elementwise(c):
         p, off = back_of[c]
-        res = activate(
-            chain, keep_gu[c], got_gu[c], far_gu[c], keep_b[p], got_b[p], far_b[p], off
+        own[c] = activate(
+            chain, keep_gu[c], got_gu[c], far_gu[c], keep_b[p], got_b[p], far_b[p], off, sizes[c]
         )
-        for kind, value in zip("dh", res):
-            name = (kind, c)
-            own[name], near[name], far[name] = value, swap(value, 1), swap(value, 2)
-            diag[name] = swap(far[name], 1)
-
-    def gathered(kind, c):
-        return [x[kind, c] for x in (own, near, far, diag)]
-
-    def out_term(c):
-        return (gathered("h", c), [down_proj], NN, out)
-
-    def grad_term(c):
-        return (gathered("d", c), [gate_proj, up_proj], NT, grad)
+        near[c] = swap(own[c], 1)
+
+    def out_term():
+        return (2, [down_proj], NN, out)
+
+    def grad_term():
+        return (0, [gate_proj, up_proj], NT, grad)
 
     def add_both(c):
         nonlocal out, grad
-        out, grad = summed(chain, [out_term(c), grad_term(c)], *chunks[c])
+        out, grad = summed(chain, (own[c], near[c]), [out_term(), grad_term()], *chunks[c])
 
     def all_grads(c):
         nonlocal grads
-        hid, delta = gathered("h", c), gathered("d", c)
-        grads = gradients(chain, act_t, cot, hid, delta, *chunks[c], grads, units)
+        grads = gradients(chain, act_t, cot, (own[c], near[c]), *chunks[c], grads, units)
 
     def last_part(term, half):
-        keep, send = summed(chain, [term], *chunks[3], 2, half, True)
+        keep, send = summed(chain, (own[3], near[3]), [term], *chunks[3], 2, half, True)
         return keep, swap_wide(send, 1)
 
     def across_z(keep, got):
@@ -476,61 +465,49 @@
     chain.after(*act_even[1:])
     (cot,) = arrange(chain, me, cot_even, cot_first, cot_odd, rows, tile)
     back(0)
-    chain.after(act_odd[0], act_odd[1])
+    chain.after(act_odd[0])
     back(1)
-    chain.after(act_odd[2])
-    back_x(0)
+    chain.after(act_odd[1], act_odd[2])
     act_odd = [(x, 0) for x in act_odd]
     act, act_t = arrange(chain, me, act_even, act_first, act_odd, rows, tile, True)
     gate_up(0)
+    back_x(0)
+    gate_up(1)
     chain.after(far_b[0])
     back_x(1)
-    back(2)
+    gate_up_x(0)
+    gate_up(2)
     chain.after(far_b[1])
-    gate_up_x(0)
-    gate_up(1)
-    chain.after(far_gu[0])
-    back_x(2)
+    gate_up_x(1)
     elementwise(0)
-    gate_up(2)
-    chain.after(far["d", 0], far["h", 0], near["d", 0], near["h", 0])
-    gate_up_x(1)
-    chain.after(diag["d", 0], diag["h", 0])
     gate_up(3)
-    chain.after(far_gu[1], far_b[2])
     gate_up_x(2)
+    chain.after(near[0])
     elementwise(1)
     add_both(0)
-    chain.after(far["d", 1], near["d", 1], near["h", 1])
     gate_up_x(3)
+    chain.after(near[1])
     all_grads(0)
-    chain.after(far["h", 1], far_gu[2], diag["d", 1])
     elementwise(2)
-    chain.after(diag["h", 1])
     add_both(1)
-    chain.after(far_gu[3], far["h", 2], near["h", 2], near["d", 2])
+    chain.after(far_gu[3], near[2])
     elementwise(3)
-    chain.after(diag["h", 2])
     all_grads(1)
-    chain.after(far["h", 3], far["d", 2], near["h", 3], near["d", 3])
-    (out,) = summed(chain, [out_term(2)], *chunks[2])
-    chain.after(diag["h", 3], diag["d", 2], far["d", 3])
-    pieces = [last_part(out_term(3), 0)]
-    chain.after(diag["d", 3])
-    (grad,) = summed(chain, [grad_term(2)], *chunks[2])
+    chain.after(near[3])
+    pieces = []
+    add_both(2)
+    pieces.append(last_part(out_term(), 0))
+    pieces.append(last_part(out_term(), 1))
+    pieces.append(last_part(grad_term(), 0))
+    pieces.append(last_part(grad_term(), 1))
     landed = [across_z(*pieces[0])]
-    pieces.append(last_part(out_term(3), 1))
-    pieces.append(last_part(grad_term(3), 0))
+    all_grads(2)
     chain.after(*landed[-1][1])
     landed.append(across_z(*pieces[1]))
-    pieces.append(last_part(grad_term(3), 1))
+    all_grads(3)
     chain.after(*landed[-1][1])
     landed.append(across_z(*pieces[2]))
-    all_grads(2)
-    chain.after(*landed[-1][1])
     landed.append(across_z(*pieces[3]))
-    all_grads(3)
-    chain.after(*landed[-1][1])
     block_output = finish(chain, me, landed[:2], True)
     groups = finish(chain, me, landed[2:], False)
     groups = [groups[0]] + [swap(groups[g], g) for g in range(1, 4)]

time: 454 us -> 370 us (0.81)
  waiting for transfers between devices: 164 us -> 105 us
  starting transfers between devices: 66.4 us -> 55.2 us
  Pallas kernels: 214 us -> 203 us
    ppermute x41 -> x19, waiting for transfers between devices: 94.7 us -> 48.9 us  [swap(): return lax.ppermute(value, 'narrow', [(i, i ^ mask) for i in range(4)])]
    ppermute x28, waiting for transfers between devices: 69.7 us -> 55.6 us  [swap_wide(): return lax.ppermute(value, 'wide', [(i, i ^ mask) for i in range(8)])]
    ppermute x41 -> x19, starting transfers between devices: 22.3 us -> 9.5 us  [swap(): return lax.ppermute(value, 'narrow', [(i, i ^ mask) for i in range(4)])]
    pallas_call x40 -> x37, Pallas kernels: 214 us -> 203 us  [__call__(): pl.pallas_call(kernel, grid_spec=pltpu.PrefetchScalarGridSpec(num_scalar_...]
  transfers between devices with their start and end apart: 70 -> 48, of which waited for: 26 -> 19; matrix products, arithmetic and copies ran while one was open for 0% -> 0% of each run, Pallas kernels for 39% -> 40%
where the time goes in v4:
time: 370 us; the launch traced here: 368 us
  Pallas kernels  203 us (55%)
  waiting for transfers between devices  105 us (28%)
  starting transfers between devices  55.2 us (15%)
  local copies, waits for them, and re-layouts  4.27 us (1%)
    pallas_call x37, Pallas kernels, __call__(): pl.pallas_call(kernel, grid_spec=pltpu.PrefetchScalarGridSpec(num_scalar_...  203 us
    ppermute x28, waiting for transfers between devices, swap_wide(): return lax.ppermute(value, 'wide', [(i, i ^ mask) for i in range(8)])  55.6 us
    ppermute x19, waiting for transfers between devices, swap(): return lax.ppermute(value, 'narrow', [(i, i ^ mask) for i in range(4)])  48.9 us
    ppermute x28, starting transfers between devices, swap_wide(): return lax.ppermute(value, 'wide', [(i, i ^ mask) for i in range(8)])  41.5 us
    ppermute x19, starting transfers between devices, swap(): return lax.ppermute(value, 'narrow', [(i, i ^ mask) for i in range(4)])  9.5 us
  transfers between devices with their start and end apart: 48, of which 19 were waited for; matrix products, arithmetic and copies ran while one was open for 0% of the time, Pallas kernels for 40%

profile of v4, /device:TPU:0, one launch (start us, length us, event | category | flops | bytes accessed | tf_op | source)
XLA Modules:
  0.0 368.1 jit_solution(3682605885574377961)
XLA Ops:
  2.3 4.2 %all-to-all-start = ((bf16[16,4,2048]{2,0,1:T(8,128)(2,1)}), bf16[16,4,2048]{2,0,1:T(8,128)(2,1)S(1)}, u32[]{:S(2)}, u32[]{:S(2)}) async-start(bf16[16,4,2048]{2,0,1:T(8,128)(2,1)} %bitcast.11), calls=%async_computation | async-start | bytes 524288 | tf_op jit(solution)/shard_map/all_to_all | solution.py:459
  6.5 3.3 collective-permute-start.9
  15.4 7.6 %collective-permute-done.9.refs_1_.refs_5_ = bf16[64,2048]{1,0:T(8,128)(2,1)} collective-permute-done((bf16[64,2048]{1,0:T(8,128)(2,1)}, bf16[64,2048]{1,0:T(8,128)(2,1)}, u32[]{:S(2)}, u32[]{:S(2)}) %collective-permute-start.9) | collective-permute-done | bytes 262176 | tf_op jit(solution)/shard_map/ppermute | solution.py:33
  23.0 6.5 %collective-permute-done.10.refs_2_.refs_7_ = bf16[64,2048]{1,0:T(8,128)(2,1)} collective-permute-done((bf16[64,2048]{1,0:T(8,128)(2,1)}, bf16[64,2048]{1,0:T(8,128)(2,1)}, u32[]{:S(2)}, u32[]{:S(2)}) %collective-permute-start.10) | collective-permute-done | bytes 262176 | tf_op jit(solution)/shard_map/ppermute | solution.py:33
  29.5 3.2 shard_map.92
  34.2 2.5 collective-permute-start.5
  36.7 4.6 %collective-permute-start.3 = (bf16[64,2048]{1,0:T(8,128)(2,1)}, bf16[64,2048]{1,0:T(8,128)(2,1)}, u32[]{:S(2)}, u32[]{:S(2)}) collective-permute-start(bf16[64,2048]{1,0:T(8,128)(2,1)} %bitcast.25), channel_id=1, source_target_pairs={{0,16},{4,20},{8,24},{12,28},{16,0},{20,4},{24,8},{28,12},{1,17},{... | collective-permute-start | bytes 786440 | tf_op jit(solution)/shard_map/ppermute | solution.py:33
  44.0 16.7 %collective-permute-done.3.refs_10_.refs_5_ = bf16[64,2048]{1,0:T(8,128)(2,1)} collective-permute-done((bf16[64,2048]{1,0:T(8,128)(2,1)}, bf16[64,2048]{1,0:T(8,128)(2,1)}, u32[]{:S(2)}, u32[]{:S(2)}) %collective-permute-start.3) | collective-permute-done | bytes 262176 | tf_op jit(solution)/shard_map/ppermute | solution.py:33
  60.7 3.8 %shard_map.93 = (bf16[4,8,16,2048]{3,2,1,0:T(8,128)(2,1)}, f32[8,128]{1,0:T(8,128)}) custom-call(s32[1]{0:T(128)} %bitcast.refs_0_, bf16[64,2048]{1,0:T(8,128)(2,1)} %refs_1_.7, bf16[64,2048]{1,0:T(8,128)(2,1)} %collective-permute-done.7.refs_4_.refs_2_, bf16[64,2048]{1,0:T(8,128)(2,1)} %collective-permute-done.8.refs_0_.refs_3_, ...), custom_call_target="tpu_custom_call" | custom-call | flops 1 | bytes 1 | tf_op jit(solution)/shard_map/pallas_call | solution.py:66
  64.5 8.4 %shard_map.94 = (f32[256,1536]{1,0:T(8,128)}, bf16[256,1536]{1,0:T(8,128)(2,1)}, f32[8,128]{1,0:T(8,128)}) custom-call(bf16[512,2048]{1,0:T(8,128)(2,1)} %bitcast.12, bf16[3328,2048]{1,0:T(8,128)(2,1)} %refs_4_.11, f32[8,128]{1,0:T(8,128)} %get-tuple-element.118.refs_2_), custom_call_target="tpu_custom_call" | custom-call | flops 1 | bytes 1 | tf_op jit(solution)/shard_map/pallas_call | solution.py:66
  75.4 6.9 %collective-permute-done.2.refs_2_.refs_4_ = bf16[64,2048]{1,0:T(8,128)(2,1)} collective-permute-done((bf16[64,2048]{1,0:T(8,128)(2,1)}, bf16[64,2048]{1,0:T(8,128)(2,1)}, u32[]{:S(2)}, u32[]{:S(2)}) %collective-permute-start.2) | collective-permute-done | bytes 262176 | tf_op jit(solution)/shard_map/ppermute | solution.py:33
  82.3 9.6 %shard_map.95 = (f32[256,1792]{1,0:T(8,128)}, bf16[256,1792]{1,0:T(8,128)(2,1)}, f32[8,128]{1,0:T(8,128)}) custom-call(bf16[512,2048]{1,0:T(8,128)(2,1)} %bitcast.13, bf16[3328,2048]{1,0:T(8,128)(2,1)} %refs_4_.11, bf16[64,2048]{1,0:T(8,128)(2,1)} %collective-permute-done.2.refs_2_.refs_4_, f32[8,128]{1,0:T(8,128)} %get-tuple-element.119.refs_3_), custom_call_target="tpu_custom_call" | custom-call | flops 1 | bytes 1 | tf_op jit(solution)/shard_map/pallas_call | solution.py:66
  93.1 4.4 %shard_map.96 = (bf16[4,8,16,2048]{3,2,1,0:T(8,128)(2,1)}, bf16[2048,512]{1,0:T(8,128)(2,1)}, f32[8,128]{1,0:T(8,128)}) custom-call(s32[1]{0:T(128)} %bitcast.refs_0_, bf16[64,2048]{1,0:T(8,128)(2,1)} %bitcast.27, bf16[64,2048]{1,0:T(8,128)(2,1)} %collective-permute-done.refs_5_.refs_2_, bf16[64,2048]{1,0:T(8,128)(2,1)} %collective-permute-done.1.refs_9_.refs_3_, ...), custom_call_target="tpu_custom_call" | custom-call | flops 1 | bytes 1 | tf_op jit(solution)/shard_map/pallas_call | solution.py:66
  97.6 6.0 %shard_map.97 = (f32[2,256,512]{2,1,0:T(8,128)}, bf16[2,256,512]{2,1,0:T(8,128)(2,1)}, f32[8,128]{1,0:T(8,128)}) custom-call(bf16[512,2048]{1,0:T(8,128)(2,1)} %bitcast.18, bf16[2048,3328]{1,0:T(8,128)(2,1)} %refs_4_.13, bf16[2048,3328]{1,0:T(8,128)(2,1)} %refs_7_.9, f32[8,128]{1,0:T(8,128)} %get-tuple-element.122.refs_3_), custom_call_target="tpu_custom_call" | custom-call | flops 1 | bytes 1 | tf_op jit(solution)/shard_map/pallas_call | solution.py:66
  103.6 2.4 shard_map.98
  107.3 8.8 %shard_map.99 = (f32[2,256,1024]{2,1,0:T(8,128)}, bf16[2,256,1024]{2,1,0:T(8,128)(2,1)}, f32[8,128]{1,0:T(8,128)}) custom-call(bf16[512,2048]{1,0:T(8,128)(2,1)} %bitcast.19, bf16[2048,3328]{1,0:T(8,128)(2,1)} %refs_4_.13, bf16[2048,3328]{1,0:T(8,128)(2,1)} %refs_7_.9, f32[8,128]{1,0:T(8,128)} %get-tuple-element.131.refs_3_), custom_call_target="tpu_custom_call" | custom-call | flops 1 | bytes 1 | tf_op jit(solution)/shard_map/pallas_call | solution.py:66
  116.1 9.3 %collective-permute-done.15.refs_2_.refs_5_ = bf16[256,1536]{1,0:T(8,128)(2,1)} collective-permute-done((bf16[256,1536]{1,0:T(8,128)(2,1)}, bf16[256,1536]{1,0:T(8,128)(2,1)}, u32[]{:S(2)}, u32[]{:S(2)}) %collective-permute-start.15) | collective-permute-done | bytes 786464 | tf_op jit(solution)/shard_map/ppermute | solution.py:29
  125.4 2.6 shard_map.100
  134.4 8.8 %shard_map.102 = (f32[2,256,1024]{2,1,0:T(8,128)}, bf16[2,256,1024]{2,1,0:T(8,128)(2,1)}, f32[8,128]{1,0:T(8,128)}) custom-call(bf16[512,2048]{1,0:T(8,128)(2,1)} %bitcast.20, bf16[2048,3328]{1,0:T(8,128)(2,1)} %refs_4_.13, bf16[2048,3328]{1,0:T(8,128)(2,1)} %refs_7_.9, f32[8,128]{1,0:T(8,128)} %get-tuple-element.138.refs_3_), custom_call_target="tpu_custom_call" | custom-call | flops 1 | bytes 1 | tf_op jit(solution)/shard_map/pallas_call | solution.py:66
  143.2 8.4 %collective-permute-done.18.refs_2_.refs_5_ = bf16[256,1792]{1,0:T(8,128)(2,1)} collective-permute-done((bf16[256,1792]{1,0:T(8,128)(2,1)}, bf16[256,1792]{1,0:T(8,128)(2,1)}, u32[]{:S(2)}, u32[]{:S(2)}) %collective-permute-start.18) | collective-permute-done | bytes 917536 | tf_op jit(solution)/shard_map/ppermute | solution.py:29
  151.6 2.7 shard_map.103
  155.7 7.2 %collective-permute-done.16.refs_2_ = bf16[2,256,512]{2,1,0:T(8,128)(2,1)} collective-permute-done((bf16[2,256,512]{2,1,0:T(8,128)(2,1)}, bf16[2,256,512]{2,1,0:T(8,128)(2,1)}, u32[]{:S(2)}, u32[]{:S(2)}) %collective-permute-start.16) | collective-permute-done | bytes 524320 | tf_op jit(solution)/shard_map/ppermute | solution.py:29
  162.8 2.9 shard_map.104
  165.7 7.4 %shard_map.105 = (f32[2,256,768]{2,1,0:T(8,128)}, bf16[2,256,768]{2,1,0:T(8,128)(2,1)}, f32[8,128]{1,0:T(8,128)}) custom-call(bf16[512,2048]{1,0:T(8,128)(2,1)} %bitcast.21, bf16[2048,3328]{1,0:T(8,128)(2,1)} %refs_4_.13, bf16[2048,3328]{1,0:T(8,128)(2,1)} %refs_7_.9, f32[8,128]{1,0:T(8,128)} %get-tuple-element.141.refs_3_), custom_call_target="tpu_custom_call" | custom-call | flops 1 | bytes 1 | tf_op jit(solution)/shard_map/pallas_call | solution.py:66
  173.1 2.8 shard_map.106
  175.9 7.1 %collective-permute-done.21.refs_2_ = bf16[2,256,1024]{2,1,0:T(8,128)(2,1)} collective-permute-done((bf16[2,256,1024]{2,1,0:T(8,128)(2,1)}, bf16[2,256,1024]{2,1,0:T(8,128)(2,1)}, u32[]{:S(2)}, u32[]{:S(2)}) %collective-permute-start.21) | collective-permute-done | bytes 1048608 | tf_op jit(solution)/shard_map/ppermute | solution.py:29
  183.1 4.9 %shard_map.107 = (bf16[3,256,1024]{2,1,0:T(8,128)(2,1)}, f32[8,128]{1,0:T(8,128)}) custom-call(f32[2,256,1024]{2,1,0:T(8,128)} %get-tuple-element.135.refs_0_, bf16[2,256,1024]{2,1,0:T(8,128)(2,1)} %collective-permute-done.17.refs_1_, bf16[2,256,1024]{2,1,0:T(8,128)(2,1)} %collective-permute-done.21.refs_2_, f32[256,1536]{1,0:T(8,128)} %get-tuple-element.127.refs_0_.refs_3_, ...), custom_call_target="tpu_custom_call" | custom-call | flops 1 | bytes 1 | tf_op jit(solution)/shard_map/pallas_call | solution.py:66
  189.5 8.8 %shard_map.108 = (f32[512,2048]{1,0:T(8,128)}, f32[512,2048]{1,0:T(8,128)}, f32[8,128]{1,0:T(8,128)}) custom-call(bf16[3,256,512]{2,1,0:T(8,128)(2,1)} %get-tuple-element.144.refs_0_.refs_2_, bf16[3,256,512]{2,1,0:T(8,128)(2,1)} %collective-permute-done.20.refs_6_.refs_1_.refs_3_, bf16[3328,2048]{1,0:T(8,128)(2,1)} %refs_4_.11, bf16[3328,2048]{1,0:T(8,128)(2,1)} %refs_4_.11, ...), custom_call_target="tpu_custom_call" | custom-call | flops 1 | bytes 1 | tf_op jit(solution)/shard_map/pallas_call | solution.py:66
  200.8 7.3 %shard_map.110 = (bf16[2048,3328]{1,0:T(8,128)(2,1)}, bf16[2048,3328]{1,0:T(8,128)(2,1)}, bf16[3328,2048]{1,0:T(8,128)(2,1)}, f32[8,128]{1,0:T(8,128)}) custom-call(bf16[2048,512]{1,0:T(8,128)(2,1)} %get-tuple-element.154.refs_0_, bf16[512,2048]{1,0:T(8,128)(2,1)} %bitcast.14, bf16[3,256,512]{2,1,0:T(8,128)(2,1)} %get-tuple-element.144.refs_0_.refs_2_, ...), custom_call_target="tpu_custom_call" | custom-call | flops 1 | bytes 1 | tf_op jit(solution)/shard_map/pallas_call | solution.py:66
  208.0 5.8 %collective-permute-done.24.refs_2_ = bf16[2,256,1024]{2,1,0:T(8,128)(2,1)} collective-permute-done((bf16[2,256,1024]{2,1,0:T(8,128)(2,1)}, bf16[2,256,1024]{2,1,0:T(8,128)(2,1)}, u32[]{:S(2)}, u32[]{:S(2)}) %collective-permute-start.24) | collective-permute-done | bytes 1048608 | tf_op jit(solution)/shard_map/ppermute | solution.py:29
  213.8 4.9 %shard_map.111 = (bf16[3,256,1024]{2,1,0:T(8,128)(2,1)}, f32[8,128]{1,0:T(8,128)}) custom-call(f32[2,256,1024]{2,1,0:T(8,128)} %get-tuple-element.146.refs_0_, bf16[2,256,1024]{2,1,0:T(8,128)(2,1)} %collective-permute-done.22.refs_1_, bf16[2,256,1024]{2,1,0:T(8,128)(2,1)} %collective-permute-done.24.refs_2_, f32[256,1792]{1,0:T(8,128)} %get-tuple-element.125.refs_0_.refs_3_, ...), custom_call_target="tpu_custom_call" | custom-call | flops 1 | bytes 1 | tf_op jit(solution)/shard_map/pallas_call | solution.py:66
  220.1 14.1 %shard_map.112 = (f32[512,2048]{1,0:T(8,128)}, f32[512,2048]{1,0:T(8,128)}, f32[8,128]{1,0:T(8,128)}) custom-call(bf16[3,256,1024]{2,1,0:T(8,128)(2,1)} %get-tuple-element.155.refs_0_.refs_2_, bf16[3,256,1024]{2,1,0:T(8,128)(2,1)} %collective-permute-done.25.refs_4_.refs_1_.refs_3_, ...), custom_call_target="tpu_custom_call", output_to_operand_aliasing={{0}: (6, {}), {1}: (15, {})} | custom-call | flops 1 | bytes 1 | tf_op jit(solution)/shard_map/pallas_call | solution.py:66
  234.3 4.7 %collective-permute-done.23.refs_2_.refs_6_ = bf16[2,256,768]{2,1,0:T(8,128)(2,1)} collective-permute-done((bf16[2,256,768]{2,1,0:T(8,128)(2,1)}, bf16[2,256,768]{2,1,0:T(8,128)(2,1)}, u32[]{:S(2)}, u32[]{:S(2)}) %collective-permute-start.23) | collective-permute-done | bytes 786464 | tf_op jit(solution)/shard_map/ppermute | solution.py:29
  239.0 4.3 %shard_map.113 = (bf16[3,256,768]{2,1,0:T(8,128)(2,1)}, f32[8,128]{1,0:T(8,128)}) custom-call(f32[2,256,768]{2,1,0:T(8,128)} %get-tuple-element.142.refs_0_, bf16[2,256,768]{2,1,0:T(8,128)(2,1)} %collective-permute-done.19.refs_1_, bf16[2,256,768]{2,1,0:T(8,128)(2,1)} %collective-permute-done.23.refs_2_.refs_6_, ...), custom_call_target="tpu_custom_call" | custom-call | flops 1 | bytes 1 | tf_op jit(solution)/shard_map/pallas_call | solution.py:66
  243.4 11.0 %shard_map.114 = (bf16[2048,3328]{1,0:T(8,128)(2,1)}, bf16[2048,3328]{1,0:T(8,128)(2,1)}, bf16[3328,2048]{1,0:T(8,128)(2,1)}, f32[8,128]{1,0:T(8,128)}) custom-call(bf16[2048,512]{1,0:T(8,128)(2,1)} %get-tuple-element.154.refs_0_, bf16[512,2048]{1,0:T(8,128)(2,1)} %bitcast.15, ...), custom_call_target="tpu_custom_call", output_to_operand_aliasing={{0}: (4, {}), {1}: (5, {}), {2}: (6, {})} | custom-call | flops 1 | bytes 1 | tf_op jit(solution)/shard_map/pallas_call | solution.py:66
  254.4 14.0 %shard_map.115 = (f32[512,2048]{1,0:T(8,128)}, f32[512,2048]{1,0:T(8,128)}, f32[8,128]{1,0:T(8,128)}) custom-call(bf16[3,256,1024]{2,1,0:T(8,128)(2,1)} %get-tuple-element.158.refs_0_.refs_2_, bf16[3,256,1024]{2,1,0:T(8,128)(2,1)} %collective-permute-done.26.refs_7_.refs_1_.refs_3_, ...), custom_call_target="tpu_custom_call", output_to_operand_aliasing={{0}: (6, {}), {1}: (15, {})} | custom-call | flops 1 | bytes 1 | tf_op jit(solution)/shard_map/pallas_call | solution.py:66
  268.3 4.4 %shard_map.116 = (f32[4,4,16,1024]{3,2,1,0:T(8,128)}, bf16[4,4,16,1024]{3,2,1,0:T(8,128)(2,1)}, f32[8,128]{1,0:T(8,128)}) custom-call(bf16[3,256,768]{2,1,0:T(8,128)(2,1)} %get-tuple-element.163.refs_0_.refs_2_, bf16[3,256,768]{2,1,0:T(8,128)(2,1)} %collective-permute-done.27.refs_16_.refs_1_.refs_3_, bf16[3328,2048]{1,0:T(8,128)(2,1)} %refs_4_.11, ...), custom_call_target="tpu_custom_call" | custom-call | flops 1 | bytes 1 | tf_op jit(solution)/shard_map/pallas_call | solution.py:66
  273.3 4.4 %shard_map.117 = (f32[4,4,16,1024]{3,2,1,0:T(8,128)}, bf16[4,4,16,1024]{3,2,1,0:T(8,128)(2,1)}, f32[8,128]{1,0:T(8,128)}) custom-call(bf16[3,256,768]{2,1,0:T(8,128)(2,1)} %get-tuple-element.163.refs_0_.refs_2_, bf16[3,256,768]{2,1,0:T(8,128)(2,1)} %collective-permute-done.27.refs_16_.refs_1_.refs_3_, bf16[3328,2048]{1,0:T(8,128)(2,1)} %refs_4_.11, ...), custom_call_target="tpu_custom_call" | custom-call | flops 1 | bytes 1 | tf_op jit(solution)/shard_map/pallas_call | solution.py:66
  279.3 5.8 %shard_map.118 = (f32[4,4,16,1024]{3,2,1,0:T(8,128)}, bf16[4,4,16,1024]{3,2,1,0:T(8,128)(2,1)}, f32[8,128]{1,0:T(8,128)}) custom-call(bf16[3,256,768]{2,1,0:T(8,128)(2,1)} %get-tuple-element.163.refs_0_.refs_2_, bf16[3,256,768]{2,1,0:T(8,128)(2,1)} %collective-permute-done.27.refs_16_.refs_1_.refs_3_, bf16[2048,3328]{1,0:T(8,128)(2,1)} %refs_4_.13, ...), custom_call_target="tpu_custom_call" | custom-call | flops 1 | bytes 1 | tf_op jit(solution)/shard_map/pallas_call | solution.py:66
  285.6 5.8 %shard_map.119 = (f32[4,4,16,1024]{3,2,1,0:T(8,128)}, bf16[4,4,16,1024]{3,2,1,0:T(8,128)(2,1)}, f32[8,128]{1,0:T(8,128)}) custom-call(bf16[3,256,768]{2,1,0:T(8,128)(2,1)} %get-tuple-element.163.refs_0_.refs_2_, bf16[3,256,768]{2,1,0:T(8,128)(2,1)} %collective-permute-done.27.refs_16_.refs_1_.refs_3_, bf16[2048,3328]{1,0:T(8,128)(2,1)} %refs_4_.13, ...), custom_call_target="tpu_custom_call" | custom-call | flops 1 | bytes 1 | tf_op jit(solution)/shard_map/pallas_call | solution.py:66
  295.2 3.0 collective-permute-start.30
  299.1 2.5 collective-permute-start.31
  301.5 11.0 %shard_map.121 = (bf16[2048,3328]{1,0:T(8,128)(2,1)}, bf16[2048,3328]{1,0:T(8,128)(2,1)}, bf16[3328,2048]{1,0:T(8,128)(2,1)}, f32[8,128]{1,0:T(8,128)}) custom-call(bf16[2048,512]{1,0:T(8,128)(2,1)} %get-tuple-element.154.refs_0_, bf16[512,2048]{1,0:T(8,128)(2,1)} %bitcast.16, ...), custom_call_target="tpu_custom_call", output_to_operand_aliasing={{0}: (4, {}), {1}: (5, {}), {2}: (6, {})} | custom-call | flops 1 | bytes 1 | tf_op jit(solution)/shard_map/pallas_call | solution.py:66
  317.2 2.5 collective-permute-start.35
  319.7 9.1 %shard_map.123 = (bf16[2048,3328]{1,0:T(8,128)(2,1)}, bf16[2048,3328]{1,0:T(8,128)(2,1)}, bf16[3328,2048]{1,0:T(8,128)(2,1)}, f32[8,128]{1,0:T(8,128)}) custom-call(bf16[2048,512]{1,0:T(8,128)(2,1)} %get-tuple-element.154.refs_0_, bf16[512,2048]{1,0:T(8,128)(2,1)} %bitcast.17, ...), custom_call_target="tpu_custom_call", output_to_operand_aliasing={{0}: (4, {}), {1}: (5, {}), {2}: (6, {})} | custom-call | flops 1 | bytes 1 | tf_op jit(solution)/shard_map/pallas_call | solution.py:66
  335.8 2.5 collective-permute-start.43
  347.7 9.5 %collective-permute-done.39.refs_3_ = bf16[4,16,1024]{2,1,0:T(8,128)(2,1)} collective-permute-done((bf16[4,16,1024]{2,1,0:T(8,128)(2,1)}, bf16[4,16,1024]{2,1,0:T(8,128)(2,1)}, u32[]{:S(2)}, u32[]{:S(2)}) %collective-permute-start.39) | collective-permute-done | bytes 131104 | tf_op jit(solution)/shard_map/ppermute | solution.py:33
  361.2 3.0 collective-permute-done.45.refs_3_
  (100 shorter events, 65.7 us)
Async XLA Ops:
  2.3 10.8 %all-to-all-start = ((bf16[16,4,2048]{2,0,1:T(8,128)(2,1)}), bf16[16,4,2048]{2,0,1:T(8,128)(2,1)S(1)}, u32[]{:S(2)}, u32[]{:S(2)}) async-start(bf16[16,4,2048]{2,0,1:T(8,128)(2,1)} %bitcast.11), calls=%async_computation | async-start | bytes 524288 | tf_op jit(solution)/shard_map/all_to_all | solution.py:459
  6.5 16.4 %collective-permute-start.9 = (bf16[64,2048]{1,0:T(8,128)(2,1)}, bf16[64,2048]{1,0:T(8,128)(2,1)}, u32[]{:S(2)}, u32[]{:S(2)}) collective-permute-start(bf16[64,2048]{1,0:T(8,128)(2,1)} %refs_1_.7), channel_id=1, source_target_pairs={{0,16},{4,20},{8,24},{12,28},{16,0},{20,4},{24,8},{28,12},{1,17},{... | collective-permute-start | bytes 786440 | tf_op jit(solution)/shard_map/ppermute | solution.py:33
  9.8 13.1 %collective-permute-start.8 = (bf16[64,2048]{1,0:T(8,128)(2,1)}, bf16[64,2048]{1,0:T(8,128)(2,1)}, u32[]{:S(2)}, u32[]{:S(2)}) collective-permute-start(bf16[64,2048]{1,0:T(8,128)(2,1)} %refs_1_.7), channel_id=1, source_target_pairs={{0,8},{4,12},{8,0},{12,4},{16,24},{20,28},{24,16},{28,20},{1,9},{5... | collective-permute-start | bytes 786440 | tf_op jit(solution)/shard_map/ppermute | solution.py:33
  11.4 11.6 %collective-permute-start.7 = (bf16[64,2048]{1,0:T(8,128)(2,1)}, bf16[64,2048]{1,0:T(8,128)(2,1)}, u32[]{:S(2)}, u32[]{:S(2)}) collective-permute-start(bf16[64,2048]{1,0:T(8,128)(2,1)} %refs_1_.7), channel_id=1, source_target_pairs={{0,4},{4,0},{8,12},{12,8},{16,20},{20,16},{24,28},{28,24},{1,5},{5... | collective-permute-start | bytes 786440 | tf_op jit(solution)/shard_map/ppermute | solution.py:33
  12.9 16.6 %collective-permute-start.10 = (bf16[64,2048]{1,0:T(8,128)(2,1)}, bf16[64,2048]{1,0:T(8,128)(2,1)}, u32[]{:S(2)}, u32[]{:S(2)}) collective-permute-start(bf16[64,2048]{1,0:T(8,128)(2,1)} %refs_1_.7), channel_id=1, source_target_pairs={{0,24},{4,28},{8,16},{12,20},{16,8},{20,12},{24,0},{28,4},{1,25},{... | collective-permute-start | bytes 786440 | tf_op jit(solution)/shard_map/ppermute | solution.py:33
  13.8 15.6 %collective-permute-start = (bf16[64,2048]{1,0:T(8,128)(2,1)S(1)}, bf16[64,2048]{1,0:T(8,128)(2,1)}, u32[]{:S(2)}, u32[]{:S(2)}) collective-permute-start(bf16[64,2048]{1,0:T(8,128)(2,1)S(1)} %bitcast.22), channel_id=1, source_target_pairs={{0,4},{4,0},{8,12},{12,8},{16,20},{20,16},{24,28},{28,24},{1,5},{5... | collective-permute-start | bytes 786440 | tf_op jit(solution)/shard_map/ppermute | solution.py:33
  32.7 28.0 %collective-permute-start.11 = (bf16[3,64,2048]{2,1,0:T(8,128)(2,1)}, bf16[3,64,2048]{2,1,0:T(8,128)(2,1)}, u32[]{:S(2)}, u32[]{:S(2)}) collective-permute-start(bf16[3,64,2048]{2,1,0:T(8,128)(2,1)} %get-tuple-element.115), channel_id=1, source_target_pairs={{0,4},{4,0},{8,12},{12,8},{16,20},{20,16},{24,28},{28,24},{1,5},{5... | collective-permute-start | bytes 2359304 | tf_op jit(solution)/shard_map/ppermute | solution.py:33
  34.2 9.7 %collective-permute-start.5 = (bf16[64,2048]{1,0:T(8,128)(2,1)}, bf16[64,2048]{1,0:T(8,128)(2,1)}, u32[]{:S(2)}, u32[]{:S(2)}) collective-permute-start(bf16[64,2048]{1,0:T(8,128)(2,1)} %bitcast.24), channel_id=1, source_target_pairs={{0,24},{4,28},{8,16},{12,20},{16,8},{20,12},{24,0},{28,4},{1,25},{... | collective-permute-start | bytes 786440 | tf_op jit(solution)/shard_map/ppermute | solution.py:33
  36.7 24.0 %collective-permute-start.3 = (bf16[64,2048]{1,0:T(8,128)(2,1)}, bf16[64,2048]{1,0:T(8,128)(2,1)}, u32[]{:S(2)}, u32[]{:S(2)}) collective-permute-start(bf16[64,2048]{1,0:T(8,128)(2,1)} %bitcast.25), channel_id=1, source_target_pairs={{0,16},{4,20},{8,24},{12,28},{16,0},{20,4},{24,8},{28,12},{1,17},{... | collective-permute-start | bytes 786440 | tf_op jit(solution)/shard_map/ppermute | solution.py:33
  41.3 19.4 %collective-permute-start.1 = (bf16[64,2048]{1,0:T(8,128)(2,1)}, bf16[64,2048]{1,0:T(8,128)(2,1)}, u32[]{:S(2)}, u32[]{:S(2)}) collective-permute-start(bf16[64,2048]{1,0:T(8,128)(2,1)} %bitcast.26), channel_id=1, source_target_pairs={{0,8},{4,12},{8,0},{12,4},{16,24},{20,28},{24,16},{28,20},{1,9},{5... | collective-permute-start | bytes 786440 | tf_op jit(solution)/shard_map/ppermute | solution.py:33
  72.9 30.7 %collective-permute-start.14 = (bf16[256,1536]{1,0:T(8,128)(2,1)}, bf16[256,1536]{1,0:T(8,128)(2,1)}, u32[]{:S(2)}, u32[]{:S(2)}) collective-permute-start(bf16[256,1536]{1,0:T(8,128)(2,1)} %get-tuple-element.128), channel_id=1, source_target_pairs={{0,1},{1,0},{2,3},{3,2},{4,5},{5,4},{6,7},{7,6},{8,9},{9,8},{10,11... | collective-permute-start | bytes 2359304 | tf_op jit(solution)/shard_map/ppermute | solution.py:29
  72.9 9.4 %collective-permute-start.2 = (bf16[64,2048]{1,0:T(8,128)(2,1)}, bf16[64,2048]{1,0:T(8,128)(2,1)}, u32[]{:S(2)}, u32[]{:S(2)}) collective-permute-start(bf16[64,2048]{1,0:T(8,128)(2,1)} %collective-permute-done.1.refs_9_.refs_3_), channel_id=1, source_target_pairs={{0,4},{4,0},{8,12},{12,8},{16,20},{20,16},{24,28},{28,24},{1,5},{5... | collective-permute-start | bytes 786440 | tf_op jit(solution)/shard_map/ppermute | solution.py:33
  73.4 18.5 %collective-permute-start.6 = (bf16[64,2048]{1,0:T(8,128)(2,1)}, bf16[64,2048]{1,0:T(8,128)(2,1)}, u32[]{:S(2)}, u32[]{:S(2)}) collective-permute-start(bf16[64,2048]{1,0:T(8,128)(2,1)} %collective-permute-done.5.refs_11_.refs_7_), channel_id=1, source_target_pairs={{0,4},{4,0},{8,12},{12,8},{16,20},{20,16},{24,28},{28,24},{1,5},{5... | collective-permute-start | bytes 786440 | tf_op jit(solution)/shard_map/ppermute | solution.py:33
  74.9 18.2 %collective-permute-start.4 = (bf16[64,2048]{1,0:T(8,128)(2,1)}, bf16[64,2048]{1,0:T(8,128)(2,1)}, u32[]{:S(2)}, u32[]{:S(2)}) collective-permute-start(bf16[64,2048]{1,0:T(8,128)(2,1)} %collective-permute-done.3.refs_10_.refs_5_), channel_id=1, source_target_pairs={{0,4},{4,0},{8,12},{12,8},{16,20},{20,16},{24,28},{28,24},{1,5},{5... | collective-permute-start | bytes 786440 | tf_op jit(solution)/shard_map/ppermute | solution.py:33
  91.9 24.2 %collective-permute-start.13 = (bf16[256,1792]{1,0:T(8,128)(2,1)}, bf16[256,1792]{1,0:T(8,128)(2,1)}, u32[]{:S(2)}, u32[]{:S(2)}) collective-permute-start(bf16[256,1792]{1,0:T(8,128)(2,1)} %get-tuple-element.126), channel_id=1, source_target_pairs={{0,1},{1,0},{2,3},{3,2},{4,5},{5,4},{6,7},{7,6},{8,9},{9,8},{10,11... | collective-permute-start | bytes 2752520 | tf_op jit(solution)/shard_map/ppermute | solution.py:29
  106.0 19.4 %collective-permute-start.15 = (bf16[256,1536]{1,0:T(8,128)(2,1)}, bf16[256,1536]{1,0:T(8,128)(2,1)}, u32[]{:S(2)}, u32[]{:S(2)}) collective-permute-start(bf16[256,1536]{1,0:T(8,128)(2,1)} %get-tuple-element.130), channel_id=1, source_target_pairs={{0,2},{1,3},{2,0},{3,1},{4,6},{5,7},{6,4},{7,5},{8,10},{9,11},{10,... | collective-permute-start | bytes 2359304 | tf_op jit(solution)/shard_map/ppermute | solution.py:29
  116.1 27.1 %collective-permute-start.17 = (bf16[2,256,1024]{2,1,0:T(8,128)(2,1)}, bf16[2,256,1024]{2,1,0:T(8,128)(2,1)}, u32[]{:S(2)}, u32[]{:S(2)}) collective-permute-start(bf16[2,256,1024]{2,1,0:T(8,128)(2,1)} %get-tuple-element.136), channel_id=1, source_target_pairs={{0,1},{1,0},{2,3},{3,2},{4,5},{5,4},{6,7},{7,6},{8,9},{9,8},{10,11... | collective-permute-start | bytes 3145736 | tf_op jit(solution)/shard_map/ppermute | solution.py:29
  128.0 23.6 %collective-permute-start.18 = (bf16[256,1792]{1,0:T(8,128)(2,1)}, bf16[256,1792]{1,0:T(8,128)(2,1)}, u32[]{:S(2)}, u32[]{:S(2)}) collective-permute-start(bf16[256,1792]{1,0:T(8,128)(2,1)} %get-tuple-element.137), channel_id=1, source_target_pairs={{0,2},{1,3},{2,0},{3,1},{4,6},{5,7},{6,4},{7,5},{8,10},{9,11},{10,... | collective-permute-start | bytes 2752520 | tf_op jit(solution)/shard_map/ppermute | solution.py:29
  129.3 2.3 collective-permute-start.12
  133.7 29.2 %collective-permute-start.16 = (bf16[2,256,512]{2,1,0:T(8,128)(2,1)}, bf16[2,256,512]{2,1,0:T(8,128)(2,1)}, u32[]{:S(2)}, u32[]{:S(2)}) collective-permute-start(bf16[2,256,512]{2,1,0:T(8,128)(2,1)} %get-tuple-element.134), channel_id=1, source_target_pairs={{0,2},{1,3},{2,0},{3,1},{4,6},{5,7},{6,4},{7,5},{8,10},{9,11},{10,... | collective-permute-start | bytes 1572872 | tf_op jit(solution)/shard_map/ppermute | solution.py:29
  143.2 30.0 %collective-permute-start.22 = (bf16[2,256,1024]{2,1,0:T(8,128)(2,1)}, bf16[2,256,1024]{2,1,0:T(8,128)(2,1)}, u32[]{:S(2)}, u32[]{:S(2)}) collective-permute-start(bf16[2,256,1024]{2,1,0:T(8,128)(2,1)} %get-tuple-element.147), channel_id=1, source_target_pairs={{0,1},{1,0},{2,3},{3,2},{4,5},{5,4},{6,7},{7,6},{8,9},{9,8},{10,11... | collective-permute-start | bytes 3145736 | tf_op jit(solution)/shard_map/ppermute | solution.py:29
  154.3 28.7 %collective-permute-start.21 = (bf16[2,256,1024]{2,1,0:T(8,128)(2,1)}, bf16[2,256,1024]{2,1,0:T(8,128)(2,1)}, u32[]{:S(2)}, u32[]{:S(2)}) collective-permute-start(bf16[2,256,1024]{2,1,0:T(8,128)(2,1)} %get-tuple-element.145), channel_id=1, source_target_pairs={{0,2},{1,3},{2,0},{3,1},{4,6},{5,7},{6,4},{7,5},{8,10},{9,11},{10,... | collective-permute-start | bytes 3145736 | tf_op jit(solution)/shard_map/ppermute | solution.py:29
  165.7 10.2 %collective-permute-start.20 = (bf16[3,256,512]{2,1,0:T(8,128)(2,1)}, bf16[3,256,512]{2,1,0:T(8,128)(2,1)}, u32[]{:S(2)}, u32[]{:S(2)}) collective-permute-start(bf16[3,256,512]{2,1,0:T(8,128)(2,1)} %get-tuple-element.144.refs_0_.refs_2_), channel_id=1, source_target_pairs={{0,1},{1,0},{2,3},{3,2},{4,5},{5,4},{6,7},{7,6},{8,9},{9,8},{10,11... | collective-permute-start | bytes 2359304 | tf_op jit(solution)/shard_map/ppermute | solution.py:29
  187.9 12.8 %collective-permute-start.25 = (bf16[3,256,1024]{2,1,0:T(8,128)(2,1)}, bf16[3,256,1024]{2,1,0:T(8,128)(2,1)}, u32[]{:S(2)}, u32[]{:S(2)}) collective-permute-start(bf16[3,256,1024]{2,1,0:T(8,128)(2,1)} %get-tuple-element.155.refs_0_.refs_2_), channel_id=1, source_target_pairs={{0,1},{1,0},{2,3},{3,2},{4,5},{5,4},{6,7},{7,6},{8,9},{9,8},{10,11... | collective-permute-start | bytes 4718600 | tf_op jit(solution)/shard_map/ppermute | solution.py:29
  187.9 25.9 %collective-permute-start.24 = (bf16[2,256,1024]{2,1,0:T(8,128)(2,1)}, bf16[2,256,1024]{2,1,0:T(8,128)(2,1)}, u32[]{:S(2)}, u32[]{:S(2)}) collective-permute-start(bf16[2,256,1024]{2,1,0:T(8,128)(2,1)} %get-tuple-element.153), channel_id=1, source_target_pairs={{0,2},{1,3},{2,0},{3,1},{4,6},{5,7},{6,4},{7,5},{8,10},{9,11},{10,... | collective-permute-start | bytes 3145736 | tf_op jit(solution)/shard_map/ppermute | solution.py:29
  189.3 9.0 %collective-permute-start.19 = (bf16[2,256,768]{2,1,0:T(8,128)(2,1)}, bf16[2,256,768]{2,1,0:T(8,128)(2,1)}, u32[]{:S(2)}, u32[]{:S(2)}) collective-permute-start(bf16[2,256,768]{2,1,0:T(8,128)(2,1)} %get-tuple-element.143), channel_id=1, source_target_pairs={{0,1},{1,0},{2,3},{3,2},{4,5},{5,4},{6,7},{7,6},{8,9},{9,8},{10,11... | collective-permute-start | bytes 2359304 | tf_op jit(solution)/shard_map/ppermute | solution.py:29
  218.7 20.3 %collective-permute-start.26 = (bf16[3,256,1024]{2,1,0:T(8,128)(2,1)}, bf16[3,256,1024]{2,1,0:T(8,128)(2,1)}, u32[]{:S(2)}, u32[]{:S(2)}) collective-permute-start(bf16[3,256,1024]{2,1,0:T(8,128)(2,1)} %get-tuple-element.158.refs_0_.refs_2_), channel_id=1, source_target_pairs={{0,1},{1,0},{2,3},{3,2},{4,5},{5,4},{6,7},{7,6},{8,9},{9,8},{10,11... | collective-permute-start | bytes 4718600 | tf_op jit(solution)/shard_map/ppermute | solution.py:29
  218.7 20.3 %collective-permute-start.23 = (bf16[2,256,768]{2,1,0:T(8,128)(2,1)}, bf16[2,256,768]{2,1,0:T(8,128)(2,1)}, u32[]{:S(2)}, u32[]{:S(2)}) collective-permute-start(bf16[2,256,768]{2,1,0:T(8,128)(2,1)} %get-tuple-element.152), channel_id=1, source_target_pairs={{0,2},{1,3},{2,0},{3,1},{4,6},{5,7},{6,4},{7,5},{8,10},{9,11},{10,... | collective-permute-start | bytes 2359304 | tf_op jit(solution)/shard_map/ppermute | solution.py:29
  243.3 11.0 %collective-permute-start.27 = (bf16[3,256,768]{2,1,0:T(8,128)(2,1)}, bf16[3,256,768]{2,1,0:T(8,128)(2,1)}, u32[]{:S(2)}, u32[]{:S(2)}) collective-permute-start(bf16[3,256,768]{2,1,0:T(8,128)(2,1)} %get-tuple-element.163.refs_0_.refs_2_), channel_id=1, source_target_pairs={{0,1},{1,0},{2,3},{3,2},{4,5},{5,4},{6,7},{7,6},{8,9},{9,8},{10,11... | collective-permute-start | bytes 3538952 | tf_op jit(solution)/shard_map/ppermute | solution.py:29
  272.8 20.2 %collective-permute-start.28 = (bf16[4,4,16,1024]{3,2,1,0:T(8,128)(2,1)}, bf16[4,4,16,1024]{3,2,1,0:T(8,128)(2,1)}, u32[]{:S(2)}, u32[]{:S(2)}) collective-permute-start(bf16[4,4,16,1024]{3,2,1,0:T(8,128)(2,1)} %get-tuple-element.174), channel_id=1, source_target_pairs={{0,4},{4,0},{8,12},{12,8},{16,20},{20,16},{24,28},{28,24},{1,5},{5... | collective-permute-start | bytes 1572872 | tf_op jit(solution)/shard_map/ppermute | solution.py:33
  277.7 21.3 %collective-permute-start.32 = (bf16[4,4,16,1024]{3,2,1,0:T(8,128)(2,1)}, bf16[4,4,16,1024]{3,2,1,0:T(8,128)(2,1)}, u32[]{:S(2)}, u32[]{:S(2)}) collective-permute-start(bf16[4,4,16,1024]{3,2,1,0:T(8,128)(2,1)} %get-tuple-element.185), channel_id=1, source_target_pairs={{0,4},{4,0},{8,12},{12,8},{16,20},{20,16},{24,28},{28,24},{1,5},{5... | collective-permute-start | bytes 1572872 | tf_op jit(solution)/shard_map/ppermute | solution.py:33
  285.1 43.7 %collective-permute-start.37 = (bf16[4,4,16,1024]{3,2,1,0:T(8,128)(2,1)}, bf16[4,4,16,1024]{3,2,1,0:T(8,128)(2,1)}, u32[]{:S(2)}, u32[]{:S(2)}) collective-permute-start(bf16[4,4,16,1024]{3,2,1,0:T(8,128)(2,1)} %get-tuple-element.198), channel_id=1, source_target_pairs={{0,4},{4,0},{8,12},{12,8},{16,20},{20,16},{24,28},{28,24},{1,5},{5... | collective-permute-start | bytes 1572872 | tf_op jit(solution)/shard_map/ppermute | solution.py:33
  291.5 40.2 %collective-permute-start.36 = (bf16[4,4,16,1024]{3,2,1,0:T(8,128)(2,1)}, bf16[4,4,16,1024]{3,2,1,0:T(8,128)(2,1)}, u32[]{:S(2)}, u32[]{:S(2)}) collective-permute-start(bf16[4,4,16,1024]{3,2,1,0:T(8,128)(2,1)} %get-tuple-element.196), channel_id=1, source_target_pairs={{0,4},{4,0},{8,12},{12,8},{16,20},{20,16},{24,28},{28,24},{1,5},{5... | collective-permute-start | bytes 1572872 | tf_op jit(solution)/shard_map/ppermute | solution.py:33
  295.1 17.3 %collective-permute-start.29 = (bf16[4,16,1024]{2,1,0:T(8,128)(2,1)}, bf16[4,16,1024]{2,1,0:T(8,128)(2,1)S(1)}, u32[]{:S(2)}, u32[]{:S(2)}) collective-permute-start(bf16[4,16,1024]{2,1,0:T(8,128)(2,1)} %get-tuple-element.181), channel_id=1, source_target_pairs={{0,8},{4,12},{8,0},{12,4},{16,24},{20,28},{24,16},{28,20},{1,9},{5... | collective-permute-start | bytes 393224 | tf_op jit(solution)/shard_map/ppermute | solution.py:33
  295.2 17.3 %collective-permute-start.30 = (bf16[4,16,1024]{2,1,0:T(8,128)(2,1)}, bf16[4,16,1024]{2,1,0:T(8,128)(2,1)}, u32[]{:S(2)}, u32[]{:S(2)}) collective-permute-start(bf16[4,16,1024]{2,1,0:T(8,128)(2,1)} %get-tuple-element.182), channel_id=1, source_target_pairs={{0,16},{4,20},{8,24},{12,28},{16,0},{20,4},{24,8},{28,12},{1,17},{... | collective-permute-start | bytes 393224 | tf_op jit(solution)/shard_map/ppermute | solution.py:33
  299.1 13.5 %collective-permute-start.31 = (bf16[4,16,1024]{2,1,0:T(8,128)(2,1)}, bf16[4,16,1024]{2,1,0:T(8,128)(2,1)}, u32[]{:S(2)}, u32[]{:S(2)}) collective-permute-start(bf16[4,16,1024]{2,1,0:T(8,128)(2,1)} %get-tuple-element.183), channel_id=1, source_target_pairs={{0,24},{4,28},{8,16},{12,20},{16,8},{20,12},{24,0},{28,4},{1,25},{... | collective-permute-start | bytes 393224 | tf_op jit(solution)/shard_map/ppermute | solution.py:33
  315.3 13.5 %collective-permute-start.33 = (bf16[4,16,1024]{2,1,0:T(8,128)(2,1)}, bf16[4,16,1024]{2,1,0:T(8,128)(2,1)S(1)}, u32[]{:S(2)}, u32[]{:S(2)}) collective-permute-start(bf16[4,16,1024]{2,1,0:T(8,128)(2,1)} %get-tuple-element.192), channel_id=1, source_target_pairs={{0,8},{4,12},{8,0},{12,4},{16,24},{20,28},{24,16},{28,20},{1,9},{5... | collective-permute-start | bytes 393224 | tf_op jit(solution)/shard_map/ppermute | solution.py:33
  315.3 13.5 %collective-permute-start.34 = (bf16[4,16,1024]{2,1,0:T(8,128)(2,1)}, bf16[4,16,1024]{2,1,0:T(8,128)(2,1)}, u32[]{:S(2)}, u32[]{:S(2)}) collective-permute-start(bf16[4,16,1024]{2,1,0:T(8,128)(2,1)} %get-tuple-element.193), channel_id=1, source_target_pairs={{0,16},{4,20},{8,24},{12,28},{16,0},{20,4},{24,8},{28,12},{1,17},{... | collective-permute-start | bytes 393224 | tf_op jit(solution)/shard_map/ppermute | solution.py:33
  317.2 11.6 %collective-permute-start.35 = (bf16[4,16,1024]{2,1,0:T(8,128)(2,1)}, bf16[4,16,1024]{2,1,0:T(8,128)(2,1)}, u32[]{:S(2)}, u32[]{:S(2)}) collective-permute-start(bf16[4,16,1024]{2,1,0:T(8,128)(2,1)} %get-tuple-element.194), channel_id=1, source_target_pairs={{0,24},{4,28},{8,16},{12,20},{16,8},{20,12},{24,0},{28,4},{1,25},{... | collective-permute-start | bytes 393224 | tf_op jit(solution)/shard_map/ppermute | solution.py:33
  333.8 8.6 %collective-permute-start.41 = (bf16[4,16,1024]{2,1,0:T(8,128)(2,1)}, bf16[4,16,1024]{2,1,0:T(8,128)(2,1)S(1)}, u32[]{:S(2)}, u32[]{:S(2)}) collective-permute-start(bf16[4,16,1024]{2,1,0:T(8,128)(2,1)} %get-tuple-element.212), channel_id=1, source_target_pairs={{0,8},{4,12},{8,0},{12,4},{16,24},{20,28},{24,16},{28,20},{1,9},{5... | collective-permute-start | bytes 393224 | tf_op jit(solution)/shard_map/ppermute | solution.py:33
  334.4 13.3 %collective-permute-start.42 = (bf16[4,16,1024]{2,1,0:T(8,128)(2,1)}, bf16[4,16,1024]{2,1,0:T(8,128)(2,1)}, u32[]{:S(2)}, u32[]{:S(2)}) collective-permute-start(bf16[4,16,1024]{2,1,0:T(8,128)(2,1)} %get-tuple-element.213), channel_id=1, source_target_pairs={{0,16},{4,20},{8,24},{12,28},{16,0},{20,4},{24,8},{28,12},{1,17},{... | collective-permute-start | bytes 393224 | tf_op jit(solution)/shard_map/ppermute | solution.py:33
  335.8 11.9 %collective-permute-start.43 = (bf16[4,16,1024]{2,1,0:T(8,128)(2,1)}, bf16[4,16,1024]{2,1,0:T(8,128)(2,1)}, u32[]{:S(2)}, u32[]{:S(2)}) collective-permute-start(bf16[4,16,1024]{2,1,0:T(8,128)(2,1)} %get-tuple-element.214), channel_id=1, source_target_pairs={{0,24},{4,28},{8,16},{12,20},{16,8},{20,12},{24,0},{28,4},{1,25},{... | collective-permute-start | bytes 393224 | tf_op jit(solution)/shard_map/ppermute | solution.py:33
  338.2 9.5 %collective-permute-start.38 = (bf16[4,16,1024]{2,1,0:T(8,128)(2,1)}, bf16[4,16,1024]{2,1,0:T(8,128)(2,1)}, u32[]{:S(2)}, u32[]{:S(2)}) collective-permute-start(bf16[4,16,1024]{2,1,0:T(8,128)(2,1)} %get-tuple-element.208), channel_id=1, source_target_pairs={{0,8},{4,12},{8,0},{12,4},{16,24},{20,28},{24,16},{28,20},{1,9},{5... | collective-permute-start | bytes 393224 | tf_op jit(solution)/shard_map/ppermute | solution.py:33
  338.3 19.0 %collective-permute-start.39 = (bf16[4,16,1024]{2,1,0:T(8,128)(2,1)}, bf16[4,16,1024]{2,1,0:T(8,128)(2,1)}, u32[]{:S(2)}, u32[]{:S(2)}) collective-permute-start(bf16[4,16,1024]{2,1,0:T(8,128)(2,1)} %get-tuple-element.209), channel_id=1, source_target_pairs={{0,16},{4,20},{8,24},{12,28},{16,0},{20,4},{24,8},{28,12},{1,17},{... | collective-permute-start | bytes 393224 | tf_op jit(solution)/shard_map/ppermute | solution.py:33
  342.4 14.8 %collective-permute-start.40 = (bf16[4,16,1024]{2,1,0:T(8,128)(2,1)}, bf16[4,16,1024]{2,1,0:T(8,128)(2,1)}, u32[]{:S(2)}, u32[]{:S(2)}) collective-permute-start(bf16[4,16,1024]{2,1,0:T(8,128)(2,1)} %get-tuple-element.210), channel_id=1, source_target_pairs={{0,24},{4,28},{8,16},{12,20},{16,8},{20,12},{24,0},{28,4},{1,25},{... | collective-permute-start | bytes 393224 | tf_op jit(solution)/shard_map/ppermute | solution.py:33
  359.4 1.9 collective-permute-start.44
  359.4 4.9 %collective-permute-start.45 = (bf16[16,2048]{1,0:T(8,128)(2,1)}, bf16[16,2048]{1,0:T(8,128)(2,1)S(1)}, u32[]{:S(2)}, u32[]{:S(2)}) collective-permute-start(bf16[16,2048]{1,0:T(8,128)(2,1)} %get-tuple-element.218), channel_id=1, source_target_pairs={{0,2},{1,3},{2,0},{3,1},{4,6},{5,7},{6,4},{7,5},{8,10},{9,11},{10,... | collective-permute-start | bytes 196616 | tf_op jit(solution)/shard_map/ppermute | solution.py:29
  360.7 4.5 %collective-permute-start.46 = (bf16[16,2048]{1,0:T(8,128)(2,1)}, bf16[16,2048]{1,0:T(8,128)(2,1)S(1)}, u32[]{:S(2)}, u32[]{:S(2)}) collective-permute-start(bf16[16,2048]{1,0:T(8,128)(2,1)} %get-tuple-element.219), channel_id=1, source_target_pairs={{0,3},{1,2},{2,1},{3,0},{4,7},{5,6},{6,5},{7,4},{8,11},{9,10},{10,... | collective-permute-start | bytes 196616 | tf_op jit(solution)/shard_map/ppermute | solution.py:29
  (7 other events, 22.6 us)

commit v5 on v4

--- a/solution.py
+++ b/solution.py
@@ -85,24 +85,7 @@
     return (i & 1) * 2 + (i >> 1)
 
 
-def join(chain, parts):
-    rows, tile = parts[0].shape
-    count, step = len(parts), rows // 4
-
-    def body(*refs):
-        for i in range(count):
-            refs[count][i] = refs[i][...]
-
-    (out,) = chain(
-        body,
-        (4,),
-        [(p, (step, tile), lambda j: (j, 0)) for p in parts],
-        [((count, rows, tile), BF16, (count, step, tile), lambda j: (0, j, 0))],
-    )
-    return out
-
-
-def arrange(chain, me, even, first, odd, rows, tile, turned=False):
+def arrange(chain, place, slots, rows, tile, turned=False):
     q = 8 * rows
 
     def body(_, *refs):
@@ -112,8 +95,6 @@
         if turned:
             refs[9][...] = out[0].reshape(q, tile).T
 
-    slots = [(even[0], 0), (first, 0), (even[1], 0), odd[0]]
-    slots += [(even[2], 0), odd[1], (even[3], 0), odd[2]]
     outs = [((4, 8, rows, tile), BF16, (1, 8, rows, tile), lambda g, s: (g, 0, 0, 0))]
     if turned:
         outs.append(((tile, 4 * q), BF16, (tile, q), lambda g, s: (0, g)))
@@ -121,11 +102,11 @@
         body,
         (4,),
         [
-            (p, (rows, tile), functools.partial(lambda at, i, s: (at + (s[0] ^ group(i)), 0), at))
+            (p, (rows, tile), functools.partial(lambda at, i, s: (at(s) + (s[0] ^ group(i)), 0), at))
             for p, at in slots
         ],
         outs,
-        scalar=me,
+        scalar=place,
     )
     return [out.reshape(4 * q, tile), *rest]
 
@@ -315,34 +296,34 @@
     return chain(body, (blocks,), ins, outs, flops=6 * tokens * tile * blocks * BLOCK, alias=alias)
 
 
-def over_z(chain, keep, got):
-    _, four, rows, width = keep.shape
-    step = min(width, 512)
+def pass_on(chain, keep, got):
+    slots = keep.shape[0]
+    rest = keep.shape[1:]
+    zeros = (0,) * len(rest)
 
     def body(k, g, *outs):
-        for s in range(4):
-            outs[s][...] = (k[s] + g[s].astype(F32)).astype(outs[s].dtype)
-
-    four_slots = ((4, four, rows, step), lambda j: (0, 0, 0, j))
-    one = ((four, rows, step), lambda j: (0, 0, j))
+        for i in range(slots // 2):
+            for out, s in zip(outs, (2 * i, 2 * i + 1)):
+                out[i] = (k[s] + g[s].astype(F32)).astype(out.dtype)
+
+    whole = ((slots, *rest), lambda j: (0, *zeros))
+    half = ((slots // 2, *rest), lambda j: (0, *zeros))
     return chain(
         body,
-        (width // step,),
-        [(keep, *four_slots), (got, *four_slots)],
-        [((four, rows, width), F32 if s == 0 else BF16, *one) for s in range(4)],
+        (1,),
+        [(keep, *whole), (got, *whole)],
+        [(half[0], dtype, *half) for dtype in (F32, BF16)],
     )
 
 
 def finish(chain, me, halves, by_rows):
-    four, rows, width = halves[0][0].shape
+    four, rows, width = halves[0][0].shape[1:]
     tile = width * len(halves)
 
     def body(s, *refs):
-        outs = refs[4 * len(halves) :]
+        outs = refs[2 * len(halves) :]
         for h in range(len(halves)):
-            total = refs[4 * h][...]
-            for x in refs[4 * h + 1 : 4 * h + 4]:
-                total = total + x[...].astype(F32)
+            total = refs[2 * h][0] + refs[2 * h + 1][0].astype(F32)
             columns = slice(h * width, (h + 1) * width)
             for i, g in enumerate(ORDER):
                 rounded = total[i].astype(BF16)
@@ -353,7 +334,7 @@
 
     ins = []
     for own, got in halves:
-        ins += [(x, (four, rows, width), lambda j, s: (0, 0, 0)) for x in (own, *got)]
+        ins += [(x, (1, four, rows, width), lambda j, s: (0, 0, 0, 0)) for x in (own, got)]
     if by_rows:
         outs = [((four, rows, tile), BF16, (four, rows, tile), lambda j, s: (0, 0, 0))]
     else:
@@ -382,23 +363,19 @@
     return out
 
 
-def gather_z(own):
-    return [own] + [swap_wide(own, k) for k in (2, 4, 6)]
-
-
 def spread(own):
     far = swap(own, 2)
     return [own, swap(own, 1), far, swap(far, 1)]
 
 
 def chunk_sizes(total):
-    first = max(1, total // 6)
-    rest = total - first
-    return [first, (rest + 2) // 3, (rest + 1) // 3, rest // 3]
+    last = max(1, total // 6)
+    rest = total - last
+    return [rest // 3, (rest + 2) // 3, (rest + 1) // 3, last]
 
 
 def local_eight(activations, cotangent, gate_proj, up_proj, down_proj):
-    me = lax.axis_index("narrow").astype(jnp.int32).reshape(1)
+    place = jnp.stack([lax.axis_index("narrow"), lax.axis_index("wide")]).astype(jnp.int32)
     rows = activations.shape[0]
     tile, units = gate_proj.shape
     sizes = chunk_sizes(units // BLOCK)
@@ -451,67 +428,62 @@
         keep, send = summed(chain, (own[3], near[3]), [term], *chunks[3], 2, half, True)
         return keep, swap_wide(send, 1)
 
-    def across_z(keep, got):
-        mine, *away = over_z(chain, keep, got)
-        return mine, [swap_wide(a, 2 * (i + 1)) for i, a in enumerate(away)]
-
-    cot_even, cot_first = gather_z(cotangent), swap_wide(cotangent, 1)
+    def over_z(pair, mask):
+        keep, send = pass_on(chain, *pair)
+        return keep, swap_wide(send, mask)
+
+    cot_all = lax.all_gather(cotangent, "wide", axis=0, tiled=True)
     tiles = lax.all_to_all(activations, "narrow", split_axis=1, concat_axis=0, tiled=True)
-    act_even, act_first = gather_z(tiles), swap_wide(tiles, 1)
-    act_odd = [swap_wide(x, 1) for x in act_even[1:]]
-    chain.after(tiles, cot_first, act_first)
-    cot_odd = swap_wide(join(chain, cot_even[1:]), 1)
-    cot_odd = [(cot_odd.reshape(12 * rows, tile), 4 * i) for i in range(3)]
-    chain.after(*act_even[1:])
-    (cot,) = arrange(chain, me, cot_even, cot_first, cot_odd, rows, tile)
+    pieces = {0: tiles, 1: swap_wide(tiles, 1)}
+    for k in (2, 4, 6):
+        pieces[k] = swap_wide(tiles, k)
+        pieces[k + 1] = swap_wide(pieces[k], 1)
+    slots = [(pieces[k], lambda s: 0) for k in range(8)]
+    act, act_t = arrange(chain, place, slots, rows, tile, True)
+    gate_up(0)
+    gate_up(1)
+    slots = [(cot_all, functools.partial(lambda k, s: (s[1] ^ k) * 4, k)) for k in range(8)]
+    (cot,) = arrange(chain, place, slots, rows, tile)
+    gate_up_x(0)
     back(0)
-    chain.after(act_odd[0])
+    gate_up_x(1)
+    gate_up(2)
+    chain.after(far_gu[0])
+    back_x(0)
     back(1)
-    chain.after(act_odd[1], act_odd[2])
-    act_odd = [(x, 0) for x in act_odd]
-    act, act_t = arrange(chain, me, act_even, act_first, act_odd, rows, tile, True)
-    gate_up(0)
-    back_x(0)
-    gate_up(1)
-    chain.after(far_b[0])
+    gate_up_x(2)
+    chain.after(far_gu[1])
+    gate_up(3)
     back_x(1)
-    gate_up_x(0)
-    gate_up(2)
-    chain.after(far_b[1])
-    gate_up_x(1)
     elementwise(0)
-    gate_up(3)
-    gate_up_x(2)
-    chain.after(near[0])
     elementwise(1)
+    gate_up_x(3)
     add_both(0)
-    gate_up_x(3)
-    chain.after(near[1])
     all_grads(0)
+    chain.after(far_gu[2])
+    add_both(1)
     elementwise(2)
-    add_both(1)
-    chain.after(far_gu[3], near[2])
+    all_grads(1)
     elementwise(3)
-    all_grads(1)
-    chain.after(near[3])
-    pieces = []
     add_both(2)
-    pieces.append(last_part(out_term(), 0))
-    pieces.append(last_part(out_term(), 1))
-    pieces.append(last_part(grad_term(), 0))
-    pieces.append(last_part(grad_term(), 1))
-    landed = [across_z(*pieces[0])]
+    parts = [last_part(out_term(), 0)]
+    parts.append(last_part(out_term(), 1))
+    parts.append(last_part(grad_term(), 0))
+    parts[0] = over_z(parts[0], 2)
+    parts.append(last_part(grad_term(), 1))
+    parts[1] = over_z(parts[1], 2)
+    parts[0] = over_z(parts[0], 4)
     all_grads(2)
-    chain.after(*landed[-1][1])
-    landed.append(across_z(*pieces[1]))
+    parts[2] = over_z(parts[2], 2)
+    parts[1] = over_z(parts[1], 4)
     all_grads(3)
-    chain.after(*landed[-1][1])
-    landed.append(across_z(*pieces[2]))
-    landed.append(across_z(*pieces[3]))
-    block_output = finish(chain, me, landed[:2], True)
-    groups = finish(chain, me, landed[2:], False)
+    parts[3] = over_z(parts[3], 2)
+    parts[2] = over_z(parts[2], 4)
+    block_output = finish(chain, place, parts[:2], True)
+    parts[3] = over_z(parts[3], 4)
+    groups = finish(chain, place, parts[2:], False)
     groups = [groups[0]] + [swap(groups[g], g) for g in range(1, 4)]
-    input_gradient = place_columns(chain, me, groups)
+    input_gradient = place_columns(chain, place, groups)
     return (block_output, input_gradient, *grads)
 
 

time: 370 us -> 381 us (1.030)
  starting transfers between devices: 55.2 us -> 32.2 us
  between operations: 0.81 us -> 14.2 us
  blocking collectives: 0 us -> 10 us
  Pallas kernels: 203 us -> 209 us
  waiting for transfers between devices: 105 us -> 110 us
    ppermute x28 -> x19, starting transfers between devices: 41.5 us -> 23.1 us  [swap_wide(): return lax.ppermute(value, 'wide', [(i, i ^ mask) for i in range(8)])]
    ppermute x28 -> x19, waiting for transfers between devices: 55.6 us -> 72.9 us  [swap_wide(): return lax.ppermute(value, 'wide', [(i, i ^ mask) for i in range(8)])]
    ppermute x19, waiting for transfers between devices: 48.9 us -> 36.8 us  [swap(): return lax.ppermute(value, 'narrow', [(i, i ^ mask) for i in range(4)])]
    all_to_all x0 -> x1, blocking collectives: none -> 10 us  [local_eight(): lax.all_to_all(activations, 'narrow', split_axis=1, concat_axis=0, tiled=...]
    pallas_call x37 -> x40, Pallas kernels: 203 us -> 209 us  [__call__(): pl.pallas_call(kernel, grid_spec=pltpu.PrefetchScalarGridSpec(num_scalar_...]
    all_to_all x1 -> x0, starting transfers between devices: 4.21 us -> none  [local_eight(): lax.all_to_all(activations, 'narrow', split_axis=1, concat_axis=0, tiled=...]
  transfers between devices with their start and end apart: 48 -> 39, of which waited for: 19 -> 18; matrix products, arithmetic and copies ran while one was open for 0% -> 0% of each run, Pallas kernels for 40% -> 49%
where the time goes in v5:
time: 381 us; the launch traced here: 379 us
  Pallas kernels  209 us (55%)
  waiting for transfers between devices  110 us (29%)
  starting transfers between devices  32.2 us (8%)
  between operations  14.2 us (4%)
  blocking collectives  10 us (3%)
    pallas_call x40, Pallas kernels, __call__(): pl.pallas_call(kernel, grid_spec=pltpu.PrefetchScalarGridSpec(num_scalar_...  209 us
    ppermute x19, waiting for transfers between devices, swap_wide(): return lax.ppermute(value, 'wide', [(i, i ^ mask) for i in range(8)])  72.9 us
    ppermute x19, waiting for transfers between devices, swap(): return lax.ppermute(value, 'narrow', [(i, i ^ mask) for i in range(4)])  36.8 us
    ppermute x19, starting transfers between devices, swap_wide(): return lax.ppermute(value, 'wide', [(i, i ^ mask) for i in range(8)])  23.1 us
    all_to_all x1, blocking collectives, local_eight(): lax.all_to_all(activations, 'narrow', split_axis=1, concat_axis=0, tiled=...  10 us
    ppermute x19, starting transfers between devices, swap(): return lax.ppermute(value, 'narrow', [(i, i ^ mask) for i in range(4)])  9.09 us
  transfers between devices with their start and end apart: 39, of which 18 were waited for; matrix products, arithmetic and copies ran while one was open for 0% of the time, Pallas kernels for 49%

profile of v5, /device:TPU:0, one launch (start us, length us, event | category | flops | bytes accessed | tf_op | source)
XLA Modules:
  0.0 379.0 jit_solution(17441373422923131291)
XLA Ops:
  8.9 10.0 %all_to_all.19 = bf16[16,4,2048]{2,0,1:T(8,128)(2,1)S(1)} all-to-all(bf16[16,4,2048]{2,0,1:T(8,128)(2,1)S(1)} %bitcast.27), channel_id=1, replica_groups=mesh['wide'=8,'narrow'=4] {'narrow'}, dimensions={1} | all-to-all | bytes 524288 | tf_op jit(solution)/shard_map/all_to_all | solution.py:436
  18.9 3.6 collective-permute-start.5
  24.8 9.0 %collective-permute-done.5.refs_7_ = bf16[64,2048]{1,0:T(8,128)(2,1)S(1)} collective-permute-done((bf16[64,2048]{1,0:T(8,128)(2,1)S(1)}, bf16[64,2048]{1,0:T(8,128)(2,1)S(1)}, u32[]{:S(2)}, u32[]{:S(2)}) %collective-permute-start.5) | collective-permute-done | bytes 262176 | tf_op jit(solution)/shard_map/ppermute | solution.py:33
  35.4 17.5 %collective-permute-done.3.refs_5_ = bf16[64,2048]{1,0:T(8,128)(2,1)S(1)} collective-permute-done((bf16[64,2048]{1,0:T(8,128)(2,1)S(1)}, bf16[64,2048]{1,0:T(8,128)(2,1)S(1)}, u32[]{:S(2)}, u32[]{:S(2)}) %collective-permute-start.3) | collective-permute-done | bytes 262176 | tf_op jit(solution)/shard_map/ppermute | solution.py:33
  55.6 11.7 %collective-permute-done.4.refs_6_ = bf16[64,2048]{1,0:T(8,128)(2,1)S(1)} collective-permute-done((bf16[64,2048]{1,0:T(8,128)(2,1)S(1)}, bf16[64,2048]{1,0:T(8,128)(2,1)S(1)}, u32[]{:S(2)}, u32[]{:S(2)}) %collective-permute-start.4) | collective-permute-done | bytes 262176 | tf_op jit(solution)/shard_map/ppermute | solution.py:33
  68.0 9.2 %collective-permute-done.2.refs_4_ = bf16[64,2048]{1,0:T(8,128)(2,1)} collective-permute-done((bf16[64,2048]{1,0:T(8,128)(2,1)S(1)}, bf16[64,2048]{1,0:T(8,128)(2,1)}, u32[]{:S(2)}, u32[]{:S(2)}) %collective-permute-start.2) | collective-permute-done | bytes 262176 | tf_op jit(solution)/shard_map/ppermute | solution.py:33
  77.2 5.1 %shard_map.92 = (bf16[4,8,16,2048]{3,2,1,0:T(8,128)(2,1)}, bf16[2048,512]{1,0:T(8,128)(2,1)}, f32[8,128]{1,0:T(8,128)}) custom-call(s32[2]{0:T(128)} %pad_add_fusion.refs_0_, bf16[64,2048]{1,0:T(8,128)(2,1)} %bitcast.26, bf16[64,2048]{1,0:T(8,128)(2,1)} %copy-done.4, bf16[64,2048]{1,0:T(8,128)(2,1)} %copy-done.3, ...), custom_call_target="tpu_custom_call" | custom-call | flops 1 | bytes 1 | tf_op jit(solution)/shard_map/pallas_call | solution.py:66
  82.3 7.4 %shard_map.93 = (f32[2,256,768]{2,1,0:T(8,128)}, bf16[2,256,768]{2,1,0:T(8,128)(2,1)}, f32[8,128]{1,0:T(8,128)}) custom-call(bf16[512,2048]{1,0:T(8,128)(2,1)} %bitcast.18, bf16[2048,3328]{1,0:T(8,128)(2,1)} %refs_3_.13, bf16[2048,3328]{1,0:T(8,128)(2,1)} %refs_5_.9, f32[8,128]{1,0:T(8,128)} %get-tuple-element.118.refs_3_), custom_call_target="tpu_custom_call" | custom-call | flops 1 | bytes 1 | tf_op jit(solution)/shard_map/pallas_call | solution.py:66
  89.7 8.8 %shard_map.94 = (f32[2,256,1024]{2,1,0:T(8,128)}, bf16[2,256,1024]{2,1,0:T(8,128)(2,1)}, f32[8,128]{1,0:T(8,128)}) custom-call(bf16[512,2048]{1,0:T(8,128)(2,1)} %bitcast.19, bf16[2048,3328]{1,0:T(8,128)(2,1)} %refs_3_.13, bf16[2048,3328]{1,0:T(8,128)(2,1)} %refs_5_.9, f32[8,128]{1,0:T(8,128)} %get-tuple-element.119.refs_3_), custom_call_target="tpu_custom_call" | custom-call | flops 1 | bytes 1 | tf_op jit(solution)/shard_map/pallas_call | solution.py:66
  99.0 4.5 %shard_map.95 = (bf16[4,8,16,2048]{3,2,1,0:T(8,128)(2,1)}, f32[8,128]{1,0:T(8,128)}) custom-call(s32[2]{0:T(128)} %pad_add_fusion.refs_0_, bf16[512,2048]{1,0:T(8,128)(2,1)} %all-gather.2.cloned.1.call-done.refs_1_.refs_2_.refs_3_.refs_4_.refs_5_.refs_6_.refs_7_.refs_8_, ...), custom_call_target="tpu_custom_call" | custom-call | flops 1 | bytes 1 | tf_op jit(solution)/shard_map/pallas_call | solution.py:66
  103.4 2.5 shard_map.96
  105.9 9.6 %shard_map.97 = (f32[256,1792]{1,0:T(8,128)}, bf16[256,1792]{1,0:T(8,128)(2,1)}, f32[8,128]{1,0:T(8,128)}) custom-call(bf16[512,2048]{1,0:T(8,128)(2,1)} %bitcast.12, bf16[3328,2048]{1,0:T(8,128)(2,1)} %refs_3_.11, f32[8,128]{1,0:T(8,128)} %get-tuple-element.127.refs_2_), custom_call_target="tpu_custom_call" | custom-call | flops 1 | bytes 1 | tf_op jit(solution)/shard_map/pallas_call | solution.py:66
  116.5 2.7 shard_map.98
  119.2 8.8 %shard_map.99 = (f32[2,256,1024]{2,1,0:T(8,128)}, bf16[2,256,1024]{2,1,0:T(8,128)(2,1)}, f32[8,128]{1,0:T(8,128)}) custom-call(bf16[512,2048]{1,0:T(8,128)(2,1)} %bitcast.20, bf16[2048,3328]{1,0:T(8,128)(2,1)} %refs_3_.13, bf16[2048,3328]{1,0:T(8,128)(2,1)} %refs_5_.9, f32[8,128]{1,0:T(8,128)} %get-tuple-element.130.refs_3_), custom_call_target="tpu_custom_call" | custom-call | flops 1 | bytes 1 | tf_op jit(solution)/shard_map/pallas_call | solution.py:66
  129.3 6.9 %collective-permute-done.12.refs_2_ = bf16[2,256,768]{2,1,0:T(8,128)(2,1)} collective-permute-done((bf16[2,256,768]{2,1,0:T(8,128)(2,1)}, bf16[2,256,768]{2,1,0:T(8,128)(2,1)}, u32[]{:S(2)}, u32[]{:S(2)}) %collective-permute-start.12) | collective-permute-done | bytes 786464 | tf_op jit(solution)/shard_map/ppermute | solution.py:29
  136.2 2.6 shard_map.100
  139.7 8.4 %shard_map.101 = (f32[256,1536]{1,0:T(8,128)}, bf16[256,1536]{1,0:T(8,128)(2,1)}, f32[8,128]{1,0:T(8,128)}) custom-call(bf16[512,2048]{1,0:T(8,128)(2,1)} %bitcast.13, bf16[3328,2048]{1,0:T(8,128)(2,1)} %refs_3_.11, f32[8,128]{1,0:T(8,128)} %get-tuple-element.137.refs_2_), custom_call_target="tpu_custom_call" | custom-call | flops 1 | bytes 1 | tf_op jit(solution)/shard_map/pallas_call | solution.py:66
  148.1 2.7 shard_map.102
  150.9 7.8 %collective-permute-done.9.refs_3_.refs_2_ = bf16[2,256,1024]{2,1,0:T(8,128)(2,1)} collective-permute-done((bf16[2,256,1024]{2,1,0:T(8,128)(2,1)}, bf16[2,256,1024]{2,1,0:T(8,128)(2,1)}, u32[]{:S(2)}, u32[]{:S(2)}) %collective-permute-start.9) | collective-permute-done | bytes 1048608 | tf_op jit(solution)/shard_map/ppermute | solution.py:29
  158.6 5.6 %shard_map.103 = (f32[2,256,512]{2,1,0:T(8,128)}, bf16[2,256,512]{2,1,0:T(8,128)(2,1)}, f32[8,128]{1,0:T(8,128)}) custom-call(bf16[512,2048]{1,0:T(8,128)(2,1)} %bitcast.21, bf16[2048,3328]{1,0:T(8,128)(2,1)} %refs_3_.13, bf16[2048,3328]{1,0:T(8,128)(2,1)} %refs_5_.9, bf16[2,256,1024]{2,1,0:T(8,128)(2,1)} %collective-permute-done.9.refs_3_.refs_2_, ...), custom_call_target="tpu_custom_call" | custom-call | flops 1 | bytes 1 | tf_op jit(solution)/shard_map/pallas_call | solution.py:66
  166.7 11.2 %collective-permute-done.14.refs_5_ = bf16[256,1792]{1,0:T(8,128)(2,1)} collective-permute-done((bf16[256,1792]{1,0:T(8,128)(2,1)}, bf16[256,1792]{1,0:T(8,128)(2,1)}, u32[]{:S(2)}, u32[]{:S(2)}) %collective-permute-start.14) | collective-permute-done | bytes 917536 | tf_op jit(solution)/shard_map/ppermute | solution.py:29
  177.9 4.3 %shard_map.105 = (bf16[3,256,768]{2,1,0:T(8,128)(2,1)}, f32[8,128]{1,0:T(8,128)}) custom-call(f32[2,256,768]{2,1,0:T(8,128)} %get-tuple-element.124.refs_0_, bf16[2,256,768]{2,1,0:T(8,128)(2,1)} %collective-permute-done.8.refs_1_, bf16[2,256,768]{2,1,0:T(8,128)(2,1)} %collective-permute-done.12.refs_2_, f32[256,1792]{1,0:T(8,128)} %get-tuple-element.133.refs_0_.refs_3_, ...), custom_call_target="tpu_custom_call" | custom-call | flops 1 | bytes 1 | tf_op jit(solution)/shard_map/pallas_call | solution.py:66
  182.2 4.9 %shard_map.106 = (bf16[3,256,1024]{2,1,0:T(8,128)(2,1)}, f32[8,128]{1,0:T(8,128)}) custom-call(f32[2,256,1024]{2,1,0:T(8,128)} %get-tuple-element.120.refs_0_, bf16[2,256,1024]{2,1,0:T(8,128)(2,1)} %collective-permute-done.7.refs_1_, bf16[2,256,1024]{2,1,0:T(8,128)(2,1)} %collective-permute-done.9.refs_3_.refs_2_, ...), custom_call_target="tpu_custom_call" | custom-call | flops 1 | bytes 1 | tf_op jit(solution)/shard_map/pallas_call | solution.py:66
  189.6 3.6 collective-permute-done.13.refs_1_
  195.3 10.7 %shard_map.108 = (f32[512,2048]{1,0:T(8,128)}, f32[512,2048]{1,0:T(8,128)}, f32[8,128]{1,0:T(8,128)}) custom-call(bf16[3,256,768]{2,1,0:T(8,128)(2,1)} %get-tuple-element.153.refs_0_.refs_2_, bf16[3,256,768]{2,1,0:T(8,128)(2,1)} %collective-permute-done.19.refs_1_.refs_3_, bf16[3328,2048]{1,0:T(8,128)(2,1)} %refs_3_.11, bf16[3328,2048]{1,0:T(8,128)(2,1)} %refs_3_.11, ...), custom_call_target="tpu_custom_call" | custom-call | flops 1 | bytes 1 | tf_op jit(solution)/shard_map/pallas_call | solution.py:66
  206.0 9.1 %shard_map.109 = (bf16[2048,3328]{1,0:T(8,128)(2,1)}, bf16[2048,3328]{1,0:T(8,128)(2,1)}, bf16[3328,2048]{1,0:T(8,128)(2,1)}, f32[8,128]{1,0:T(8,128)}) custom-call(bf16[2048,512]{1,0:T(8,128)(2,1)} %get-tuple-element.151.refs_0_, bf16[512,2048]{1,0:T(8,128)(2,1)} %bitcast.14, bf16[3,256,768]{2,1,0:T(8,128)(2,1)} %get-tuple-element.153.refs_0_.refs_2_, ...), custom_call_target="tpu_custom_call" | custom-call | flops 1 | bytes 1 | tf_op jit(solution)/shard_map/pallas_call | solution.py:66
  215.2 14.0 %shard_map.110 = (f32[512,2048]{1,0:T(8,128)}, f32[512,2048]{1,0:T(8,128)}, f32[8,128]{1,0:T(8,128)}) custom-call(bf16[3,256,1024]{2,1,0:T(8,128)(2,1)} %get-tuple-element.152.refs_0_.refs_2_, bf16[3,256,1024]{2,1,0:T(8,128)(2,1)} %collective-permute-done.18.refs_1_.refs_3_, ...), custom_call_target="tpu_custom_call", output_to_operand_aliasing={{0}: (6, {}), {1}: (15, {})} | custom-call | flops 1 | bytes 1 | tf_op jit(solution)/shard_map/pallas_call | solution.py:66
  229.9 4.9 %shard_map.111 = (bf16[3,256,1024]{2,1,0:T(8,128)(2,1)}, f32[8,128]{1,0:T(8,128)}) custom-call(f32[2,256,1024]{2,1,0:T(8,128)} %get-tuple-element.131.refs_0_, bf16[2,256,1024]{2,1,0:T(8,128)(2,1)} %collective-permute-done.10.refs_1_, bf16[2,256,1024]{2,1,0:T(8,128)(2,1)} %collective-permute-done.20.refs_16_.refs_2_, ...), custom_call_target="tpu_custom_call" | custom-call | flops 1 | bytes 1 | tf_op jit(solution)/shard_map/pallas_call | solution.py:66
  235.8 11.0 %shard_map.112 = (bf16[2048,3328]{1,0:T(8,128)(2,1)}, bf16[2048,3328]{1,0:T(8,128)(2,1)}, bf16[3328,2048]{1,0:T(8,128)(2,1)}, f32[8,128]{1,0:T(8,128)}) custom-call(bf16[2048,512]{1,0:T(8,128)(2,1)} %get-tuple-element.151.refs_0_, bf16[512,2048]{1,0:T(8,128)(2,1)} %bitcast.15, ...), custom_call_target="tpu_custom_call", output_to_operand_aliasing={{0}: (4, {}), {1}: (5, {}), {2}: (6, {})} | custom-call | flops 1 | bytes 1 | tf_op jit(solution)/shard_map/pallas_call | solution.py:66
  246.7 2.7 collective-permute-done.16.refs_2_
  249.4 2.9 shard_map.113
  252.3 14.0 %shard_map.114 = (f32[512,2048]{1,0:T(8,128)}, f32[512,2048]{1,0:T(8,128)}, f32[8,128]{1,0:T(8,128)}) custom-call(bf16[3,256,1024]{2,1,0:T(8,128)(2,1)} %get-tuple-element.167.refs_0_.refs_2_, bf16[3,256,1024]{2,1,0:T(8,128)(2,1)} %collective-permute-done.22.refs_1_.refs_3_, ...), custom_call_target="tpu_custom_call", output_to_operand_aliasing={{0}: (6, {}), {1}: (15, {})} | custom-call | flops 1 | bytes 1 | tf_op jit(solution)/shard_map/pallas_call | solution.py:66
  266.3 4.0 %shard_map.115 = (f32[4,4,16,1024]{3,2,1,0:T(8,128)}, bf16[4,4,16,1024]{3,2,1,0:T(8,128)(2,1)}, f32[8,128]{1,0:T(8,128)}) custom-call(bf16[3,256,512]{2,1,0:T(8,128)(2,1)} %get-tuple-element.166.refs_0_.refs_2_, bf16[3,256,512]{2,1,0:T(8,128)(2,1)} %collective-permute-done.21.refs_1_.refs_3_, bf16[3328,2048]{1,0:T(8,128)(2,1)} %refs_3_.11, ...), custom_call_target="tpu_custom_call" | custom-call | flops 1 | bytes 1 | tf_op jit(solution)/shard_map/pallas_call | solution.py:66
  271.2 3.8 %shard_map.116 = (f32[4,4,16,1024]{3,2,1,0:T(8,128)}, bf16[4,4,16,1024]{3,2,1,0:T(8,128)(2,1)}, f32[8,128]{1,0:T(8,128)}) custom-call(bf16[3,256,512]{2,1,0:T(8,128)(2,1)} %get-tuple-element.166.refs_0_.refs_2_, bf16[3,256,512]{2,1,0:T(8,128)(2,1)} %collective-permute-done.21.refs_1_.refs_3_, bf16[3328,2048]{1,0:T(8,128)(2,1)} %refs_3_.11, ...), custom_call_target="tpu_custom_call" | custom-call | flops 1 | bytes 1 | tf_op jit(solution)/shard_map/pallas_call | solution.py:66
  276.1 4.7 %shard_map.117 = (f32[4,4,16,1024]{3,2,1,0:T(8,128)}, bf16[4,4,16,1024]{3,2,1,0:T(8,128)(2,1)}, f32[8,128]{1,0:T(8,128)}) custom-call(bf16[3,256,512]{2,1,0:T(8,128)(2,1)} %get-tuple-element.166.refs_0_.refs_2_, bf16[3,256,512]{2,1,0:T(8,128)(2,1)} %collective-permute-done.21.refs_1_.refs_3_, bf16[2048,3328]{1,0:T(8,128)(2,1)} %refs_3_.13, ...), custom_call_target="tpu_custom_call" | custom-call | flops 1 | bytes 1 | tf_op jit(solution)/shard_map/pallas_call | solution.py:66
  281.8 3.5 collective-permute-done.23.refs_1_
  287.5 4.8 %shard_map.119 = (f32[4,4,16,1024]{3,2,1,0:T(8,128)}, bf16[4,4,16,1024]{3,2,1,0:T(8,128)(2,1)}, f32[8,128]{1,0:T(8,128)}) custom-call(bf16[3,256,512]{2,1,0:T(8,128)(2,1)} %get-tuple-element.166.refs_0_.refs_2_, bf16[3,256,512]{2,1,0:T(8,128)(2,1)} %collective-permute-done.21.refs_1_.refs_3_, bf16[2048,3328]{1,0:T(8,128)(2,1)} %refs_3_.13, ...), custom_call_target="tpu_custom_call" | custom-call | flops 1 | bytes 1 | tf_op jit(solution)/shard_map/pallas_call | solution.py:66
  302.7 11.0 %shard_map.122 = (bf16[2048,3328]{1,0:T(8,128)(2,1)}, bf16[2048,3328]{1,0:T(8,128)(2,1)}, bf16[3328,2048]{1,0:T(8,128)(2,1)}, f32[8,128]{1,0:T(8,128)}) custom-call(bf16[2048,512]{1,0:T(8,128)(2,1)} %get-tuple-element.151.refs_0_, bf16[512,2048]{1,0:T(8,128)(2,1)} %bitcast.16, ...), custom_call_target="tpu_custom_call", output_to_operand_aliasing={{0}: (4, {}), {1}: (5, {}), {2}: (6, {})} | custom-call | flops 1 | bytes 1 | tf_op jit(solution)/shard_map/pallas_call | solution.py:66
  319.6 7.3 %shard_map.125 = (bf16[2048,3328]{1,0:T(8,128)(2,1)}, bf16[2048,3328]{1,0:T(8,128)(2,1)}, bf16[3328,2048]{1,0:T(8,128)(2,1)}, f32[8,128]{1,0:T(8,128)}) custom-call(bf16[2048,512]{1,0:T(8,128)(2,1)} %get-tuple-element.151.refs_0_, bf16[512,2048]{1,0:T(8,128)(2,1)} %bitcast.17, ...), custom_call_target="tpu_custom_call", output_to_operand_aliasing={{0}: (4, {}), {1}: (5, {}), {2}: (6, {})} | custom-call | flops 1 | bytes 1 | tf_op jit(solution)/shard_map/pallas_call | solution.py:66
  329.5 3.2 collective-permute-start.26
  334.6 2.9 collective-permute-start.32
  337.5 7.5 %collective-permute-done.26.refs_2_ = bf16[1,4,16,1024]{3,2,1,0:T(8,128)(2,1)} collective-permute-done((bf16[1,4,16,1024]{3,2,1,0:T(8,128)(2,1)}, bf16[1,4,16,1024]{3,2,1,0:T(8,128)(2,1)}, u32[]{:S(2)}, u32[]{:S(2)}) %collective-permute-start.26) | collective-permute-done | bytes 131104 | tf_op jit(solution)/shard_map/ppermute | solution.py:33
  345.0 4.2 %collective-permute-done.29.refs_4_ = bf16[1,4,16,1024]{3,2,1,0:T(8,128)(2,1)} collective-permute-done((bf16[1,4,16,1024]{3,2,1,0:T(8,128)(2,1)}, bf16[1,4,16,1024]{3,2,1,0:T(8,128)(2,1)}, u32[]{:S(2)}, u32[]{:S(2)}) %collective-permute-start.29) | collective-permute-done | bytes 131104 | tf_op jit(solution)/shard_map/ppermute | solution.py:33
  349.2 2.5 shard_map.128
  353.6 6.7 %collective-permute-done.34.refs_4_ = bf16[1,4,16,1024]{3,2,1,0:T(8,128)(2,1)} collective-permute-done((bf16[1,4,16,1024]{3,2,1,0:T(8,128)(2,1)}, bf16[1,4,16,1024]{3,2,1,0:T(8,128)(2,1)}, u32[]{:S(2)}, u32[]{:S(2)}) %collective-permute-start.34) | collective-permute-done | bytes 131104 | tf_op jit(solution)/shard_map/ppermute | solution.py:33
  360.3 2.5 shard_map.130
  364.7 2.9 collective-permute-done.36.refs_3_
  369.2 2.9 shard_map.131
  (96 shorter events, 52.9 us)
Async XLA Ops:
  7.2 91.8 %all-gather.2.cloned.1.call-start = ((), (), s32[]{:S(2)}) async-start(), calls=%async_computation.1 | async-start | bytes 2359296 | tf_op jit(solution)/shard_map/all_gather | solution.py:435
  18.9 4.4 %copy-start = (bf16[16,4,2048]{2,0,1:T(8,128)(2,1)}, bf16[16,4,2048]{2,0,1:T(8,128)(2,1)S(1)}, u32[]{:S(2)}) copy-start(bf16[16,4,2048]{2,0,1:T(8,128)(2,1)S(1)} %all_to_all.19) | copy-start | bytes 786436
  18.9 14.9 %collective-permute-start.5 = (bf16[64,2048]{1,0:T(8,128)(2,1)S(1)}, bf16[64,2048]{1,0:T(8,128)(2,1)S(1)}, u32[]{:S(2)}, u32[]{:S(2)}) collective-permute-start(bf16[64,2048]{1,0:T(8,128)(2,1)S(1)} %bitcast.22), channel_id=1, source_target_pairs={{0,24},{4,28},{8,16},{12,20},{16,8},{20,12},{24,0},{28,4},{1,25},{... | collective-permute-start | bytes 786440 | tf_op jit(solution)/shard_map/ppermute | solution.py:33
  22.5 30.4 %collective-permute-start.3 = (bf16[64,2048]{1,0:T(8,128)(2,1)S(1)}, bf16[64,2048]{1,0:T(8,128)(2,1)S(1)}, u32[]{:S(2)}, u32[]{:S(2)}) collective-permute-start(bf16[64,2048]{1,0:T(8,128)(2,1)S(1)} %bitcast.23), channel_id=1, source_target_pairs={{0,16},{4,20},{8,24},{12,28},{16,0},{20,4},{24,8},{28,12},{1,17},{... | collective-permute-start | bytes 786440 | tf_op jit(solution)/shard_map/ppermute | solution.py:33
  22.5 31.9 %collective-permute-start.1 = (bf16[64,2048]{1,0:T(8,128)(2,1)S(1)}, bf16[64,2048]{1,0:T(8,128)(2,1)S(1)}, u32[]{:S(2)}, u32[]{:S(2)}) collective-permute-start(bf16[64,2048]{1,0:T(8,128)(2,1)S(1)} %bitcast.24), channel_id=1, source_target_pairs={{0,8},{4,12},{8,0},{12,4},{16,24},{20,28},{24,16},{28,20},{1,9},{5... | collective-permute-start | bytes 786440 | tf_op jit(solution)/shard_map/ppermute | solution.py:33
  23.3 32.3 %collective-permute-start = (bf16[64,2048]{1,0:T(8,128)(2,1)S(1)}, bf16[64,2048]{1,0:T(8,128)(2,1)S(1)}, u32[]{:S(2)}, u32[]{:S(2)}) collective-permute-start(bf16[64,2048]{1,0:T(8,128)(2,1)S(1)} %bitcast.25), channel_id=1, source_target_pairs={{0,4},{4,0},{8,12},{12,8},{16,20},{20,16},{24,28},{28,24},{1,5},{5... | collective-permute-start | bytes 786440 | tf_op jit(solution)/shard_map/ppermute | solution.py:33
  33.8 21.7 %copy-start.1 = (bf16[64,2048]{1,0:T(8,128)(2,1)}, bf16[64,2048]{1,0:T(8,128)(2,1)S(1)}, u32[]{:S(2)}) copy-start(bf16[64,2048]{1,0:T(8,128)(2,1)S(1)} %collective-permute-done.5.refs_7_) | copy-start | bytes 786436
  33.8 21.8 %collective-permute-start.6 = (bf16[64,2048]{1,0:T(8,128)(2,1)S(1)}, bf16[64,2048]{1,0:T(8,128)(2,1)S(1)}, u32[]{:S(2)}, u32[]{:S(2)}) collective-permute-start(bf16[64,2048]{1,0:T(8,128)(2,1)S(1)} %collective-permute-done.5.refs_7_), channel_id=1, source_target_pairs={{0,4},{4,0},{8,12},{12,8},{16,20},{20,16},{24,28},{28,24},{1,5},{5... | collective-permute-start | bytes 786440 | tf_op jit(solution)/shard_map/ppermute | solution.py:33
  52.9 2.7 copy-start.2
  52.9 14.4 %collective-permute-start.4 = (bf16[64,2048]{1,0:T(8,128)(2,1)S(1)}, bf16[64,2048]{1,0:T(8,128)(2,1)S(1)}, u32[]{:S(2)}, u32[]{:S(2)}) collective-permute-start(bf16[64,2048]{1,0:T(8,128)(2,1)S(1)} %collective-permute-done.3.refs_5_), channel_id=1, source_target_pairs={{0,4},{4,0},{8,12},{12,8},{16,20},{20,16},{24,28},{28,24},{1,5},{5... | collective-permute-start | bytes 786440 | tf_op jit(solution)/shard_map/ppermute | solution.py:33
  54.4 12.9 %copy-start.3 = (bf16[64,2048]{1,0:T(8,128)(2,1)}, bf16[64,2048]{1,0:T(8,128)(2,1)S(1)}, u32[]{:S(2)}) copy-start(bf16[64,2048]{1,0:T(8,128)(2,1)S(1)} %collective-permute-done.1.refs_3_) | copy-start | bytes 786436
  54.4 22.7 %collective-permute-start.2 = (bf16[64,2048]{1,0:T(8,128)(2,1)S(1)}, bf16[64,2048]{1,0:T(8,128)(2,1)}, u32[]{:S(2)}, u32[]{:S(2)}) collective-permute-start(bf16[64,2048]{1,0:T(8,128)(2,1)S(1)} %collective-permute-done.1.refs_3_), channel_id=1, source_target_pairs={{0,4},{4,0},{8,12},{12,8},{16,20},{20,16},{24,28},{28,24},{1,5},{5... | collective-permute-start | bytes 786440 | tf_op jit(solution)/shard_map/ppermute | solution.py:33
  55.6 11.7 %copy-start.4 = (bf16[64,2048]{1,0:T(8,128)(2,1)}, bf16[64,2048]{1,0:T(8,128)(2,1)S(1)}, u32[]{:S(2)}) copy-start(bf16[64,2048]{1,0:T(8,128)(2,1)S(1)} %collective-permute-done.refs_2_) | copy-start | bytes 786436
  55.6 11.7 %copy-start.5 = (bf16[64,2048]{1,0:T(8,128)(2,1)}, bf16[64,2048]{1,0:T(8,128)(2,1)S(1)}, u32[]{:S(2)}) copy-start(bf16[64,2048]{1,0:T(8,128)(2,1)S(1)} %collective-permute-done.6.refs_8_) | copy-start | bytes 786436
  89.7 13.8 %collective-permute-start.8 = (bf16[2,256,768]{2,1,0:T(8,128)(2,1)}, bf16[2,256,768]{2,1,0:T(8,128)(2,1)}, u32[]{:S(2)}, u32[]{:S(2)}) collective-permute-start(bf16[2,256,768]{2,1,0:T(8,128)(2,1)} %get-tuple-element.125), channel_id=1, source_target_pairs={{0,1},{1,0},{2,3},{3,2},{4,5},{5,4},{6,7},{7,6},{8,9},{9,8},{10,11... | collective-permute-start | bytes 2359304 | tf_op jit(solution)/shard_map/ppermute | solution.py:29
  98.5 18.0 %collective-permute-start.7 = (bf16[2,256,1024]{2,1,0:T(8,128)(2,1)}, bf16[2,256,1024]{2,1,0:T(8,128)(2,1)}, u32[]{:S(2)}, u32[]{:S(2)}) collective-permute-start(bf16[2,256,1024]{2,1,0:T(8,128)(2,1)} %get-tuple-element.121), channel_id=1, source_target_pairs={{0,1},{1,0},{2,3},{3,2},{4,5},{5,4},{6,7},{7,6},{8,9},{9,8},{10,11... | collective-permute-start | bytes 3145736 | tf_op jit(solution)/shard_map/ppermute | solution.py:29
  115.5 20.7 %collective-permute-start.11 = (bf16[256,1792]{1,0:T(8,128)(2,1)}, bf16[256,1792]{1,0:T(8,128)(2,1)}, u32[]{:S(2)}, u32[]{:S(2)}) collective-permute-start(bf16[256,1792]{1,0:T(8,128)(2,1)} %get-tuple-element.134), channel_id=1, source_target_pairs={{0,1},{1,0},{2,3},{3,2},{4,5},{5,4},{6,7},{7,6},{8,9},{9,8},{10,11... | collective-permute-start | bytes 2752520 | tf_op jit(solution)/shard_map/ppermute | solution.py:29
  115.5 20.7 %collective-permute-start.12 = (bf16[2,256,768]{2,1,0:T(8,128)(2,1)}, bf16[2,256,768]{2,1,0:T(8,128)(2,1)}, u32[]{:S(2)}, u32[]{:S(2)}) collective-permute-start(bf16[2,256,768]{2,1,0:T(8,128)(2,1)} %get-tuple-element.135), channel_id=1, source_target_pairs={{0,2},{1,3},{2,0},{3,1},{4,6},{5,7},{6,4},{7,5},{8,10},{9,11},{10,... | collective-permute-start | bytes 2359304 | tf_op jit(solution)/shard_map/ppermute | solution.py:29
  128.0 20.1 %collective-permute-start.10 = (bf16[2,256,1024]{2,1,0:T(8,128)(2,1)}, bf16[2,256,1024]{2,1,0:T(8,128)(2,1)}, u32[]{:S(2)}, u32[]{:S(2)}) collective-permute-start(bf16[2,256,1024]{2,1,0:T(8,128)(2,1)} %get-tuple-element.132), channel_id=1, source_target_pairs={{0,1},{1,0},{2,3},{3,2},{4,5},{5,4},{6,7},{7,6},{8,9},{9,8},{10,11... | collective-permute-start | bytes 3145736 | tf_op jit(solution)/shard_map/ppermute | solution.py:29
  128.2 30.4 %collective-permute-start.9 = (bf16[2,256,1024]{2,1,0:T(8,128)(2,1)}, bf16[2,256,1024]{2,1,0:T(8,128)(2,1)}, u32[]{:S(2)}, u32[]{:S(2)}) collective-permute-start(bf16[2,256,1024]{2,1,0:T(8,128)(2,1)} %get-tuple-element.129), channel_id=1, source_target_pairs={{0,2},{1,3},{2,0},{3,1},{4,6},{5,7},{6,4},{7,5},{8,10},{9,11},{10,... | collective-permute-start | bytes 3145736 | tf_op jit(solution)/shard_map/ppermute | solution.py:29
  138.8 39.1 %collective-permute-start.14 = (bf16[256,1792]{1,0:T(8,128)(2,1)}, bf16[256,1792]{1,0:T(8,128)(2,1)}, u32[]{:S(2)}, u32[]{:S(2)}) collective-permute-start(bf16[256,1792]{1,0:T(8,128)(2,1)} %get-tuple-element.142), channel_id=1, source_target_pairs={{0,2},{1,3},{2,0},{3,1},{4,6},{5,7},{6,4},{7,5},{8,10},{9,11},{10,... | collective-permute-start | bytes 2752520 | tf_op jit(solution)/shard_map/ppermute | solution.py:29
  148.1 16.2 %collective-permute-start.15 = (bf16[256,1536]{1,0:T(8,128)(2,1)}, bf16[256,1536]{1,0:T(8,128)(2,1)}, u32[]{:S(2)}, u32[]{:S(2)}) collective-permute-start(bf16[256,1536]{1,0:T(8,128)(2,1)} %get-tuple-element.144), channel_id=1, source_target_pairs={{0,1},{1,0},{2,3},{3,2},{4,5},{5,4},{6,7},{7,6},{8,9},{9,8},{10,11... | collective-permute-start | bytes 2359304 | tf_op jit(solution)/shard_map/ppermute | solution.py:29
  187.0 28.1 %collective-permute-start.18 = (bf16[3,256,1024]{2,1,0:T(8,128)(2,1)}, bf16[3,256,1024]{2,1,0:T(8,128)(2,1)}, u32[]{:S(2)}, u32[]{:S(2)}) collective-permute-start(bf16[3,256,1024]{2,1,0:T(8,128)(2,1)} %get-tuple-element.152.refs_0_.refs_2_), channel_id=1, source_target_pairs={{0,1},{1,0},{2,3},{3,2},{4,5},{5,4},{6,7},{7,6},{8,9},{9,8},{10,11... | collective-permute-start | bytes 4718600 | tf_op jit(solution)/shard_map/ppermute | solution.py:29
  187.0 8.3 %collective-permute-start.19 = (bf16[3,256,768]{2,1,0:T(8,128)(2,1)}, bf16[3,256,768]{2,1,0:T(8,128)(2,1)}, u32[]{:S(2)}, u32[]{:S(2)}) collective-permute-start(bf16[3,256,768]{2,1,0:T(8,128)(2,1)} %get-tuple-element.153.refs_0_.refs_2_), channel_id=1, source_target_pairs={{0,1},{1,0},{2,3},{3,2},{4,5},{5,4},{6,7},{7,6},{8,9},{9,8},{10,11... | collective-permute-start | bytes 3538952 | tf_op jit(solution)/shard_map/ppermute | solution.py:29
  187.5 27.6 %collective-permute-start.20 = (bf16[2,256,1024]{2,1,0:T(8,128)(2,1)}, bf16[2,256,1024]{2,1,0:T(8,128)(2,1)}, u32[]{:S(2)}, u32[]{:S(2)}) collective-permute-start(bf16[2,256,1024]{2,1,0:T(8,128)(2,1)} %get-tuple-element.159), channel_id=1, source_target_pairs={{0,2},{1,3},{2,0},{3,1},{4,6},{5,7},{6,4},{7,5},{8,10},{9,11},{10,... | collective-permute-start | bytes 3145736 | tf_op jit(solution)/shard_map/ppermute | solution.py:29
  188.5 41.4 %collective-permute-start.17 = (bf16[256,1536]{1,0:T(8,128)(2,1)}, bf16[256,1536]{1,0:T(8,128)(2,1)}, u32[]{:S(2)}, u32[]{:S(2)}) collective-permute-start(bf16[256,1536]{1,0:T(8,128)(2,1)} %get-tuple-element.150), channel_id=1, source_target_pairs={{0,2},{1,3},{2,0},{3,1},{4,6},{5,7},{6,4},{7,5},{8,10},{9,11},{10,... | collective-permute-start | bytes 2359304 | tf_op jit(solution)/shard_map/ppermute | solution.py:29
  189.6 3.7 collective-permute-start.13
  234.7 17.5 %collective-permute-start.22 = (bf16[3,256,1024]{2,1,0:T(8,128)(2,1)}, bf16[3,256,1024]{2,1,0:T(8,128)(2,1)}, u32[]{:S(2)}, u32[]{:S(2)}) collective-permute-start(bf16[3,256,1024]{2,1,0:T(8,128)(2,1)} %get-tuple-element.167.refs_0_.refs_2_), channel_id=1, source_target_pairs={{0,1},{1,0},{2,3},{3,2},{4,5},{5,4},{6,7},{7,6},{8,9},{9,8},{10,11... | collective-permute-start | bytes 4718600 | tf_op jit(solution)/shard_map/ppermute | solution.py:29
  234.8 14.6 %collective-permute-start.16 = (bf16[2,256,512]{2,1,0:T(8,128)(2,1)}, bf16[2,256,512]{2,1,0:T(8,128)(2,1)}, u32[]{:S(2)}, u32[]{:S(2)}) collective-permute-start(bf16[2,256,512]{2,1,0:T(8,128)(2,1)} %get-tuple-element.149), channel_id=1, source_target_pairs={{0,2},{1,3},{2,0},{3,1},{4,6},{5,7},{6,4},{7,5},{8,10},{9,11},{10,... | collective-permute-start | bytes 1572872 | tf_op jit(solution)/shard_map/ppermute | solution.py:29
  252.3 14.0 %collective-permute-start.21 = (bf16[3,256,512]{2,1,0:T(8,128)(2,1)}, bf16[3,256,512]{2,1,0:T(8,128)(2,1)}, u32[]{:S(2)}, u32[]{:S(2)}) collective-permute-start(bf16[3,256,512]{2,1,0:T(8,128)(2,1)} %get-tuple-element.166.refs_0_.refs_2_), channel_id=1, source_target_pairs={{0,1},{1,0},{2,3},{3,2},{4,5},{5,4},{6,7},{7,6},{8,9},{9,8},{10,11... | collective-permute-start | bytes 2359304 | tf_op jit(solution)/shard_map/ppermute | solution.py:29
  270.2 15.0 %collective-permute-start.23 = (bf16[4,4,16,1024]{3,2,1,0:T(8,128)(2,1)}, bf16[4,4,16,1024]{3,2,1,0:T(8,128)(2,1)}, u32[]{:S(2)}, u32[]{:S(2)}) collective-permute-start(bf16[4,4,16,1024]{3,2,1,0:T(8,128)(2,1)} %get-tuple-element.174), channel_id=1, source_target_pairs={{0,4},{4,0},{8,12},{12,8},{16,20},{20,16},{24,28},{28,24},{1,5},{5... | collective-permute-start | bytes 1572872 | tf_op jit(solution)/shard_map/ppermute | solution.py:33
  275.0 21.5 %collective-permute-start.25 = (bf16[4,4,16,1024]{3,2,1,0:T(8,128)(2,1)}, bf16[4,4,16,1024]{3,2,1,0:T(8,128)(2,1)}, u32[]{:S(2)}, u32[]{:S(2)}) collective-permute-start(bf16[4,4,16,1024]{3,2,1,0:T(8,128)(2,1)} %get-tuple-element.182), channel_id=1, source_target_pairs={{0,4},{4,0},{8,12},{12,8},{16,20},{20,16},{24,28},{28,24},{1,5},{5... | collective-permute-start | bytes 1572872 | tf_op jit(solution)/shard_map/ppermute | solution.py:33
  280.8 32.9 %collective-permute-start.28 = (bf16[4,4,16,1024]{3,2,1,0:T(8,128)(2,1)}, bf16[4,4,16,1024]{3,2,1,0:T(8,128)(2,1)}, u32[]{:S(2)}, u32[]{:S(2)}) collective-permute-start(bf16[4,4,16,1024]{3,2,1,0:T(8,128)(2,1)} %get-tuple-element.191), channel_id=1, source_target_pairs={{0,4},{4,0},{8,12},{12,8},{16,20},{20,16},{24,28},{28,24},{1,5},{5... | collective-permute-start | bytes 1572872 | tf_op jit(solution)/shard_map/ppermute | solution.py:33
  292.3 34.6 %collective-permute-start.31 = (bf16[4,4,16,1024]{3,2,1,0:T(8,128)(2,1)}, bf16[4,4,16,1024]{3,2,1,0:T(8,128)(2,1)}, u32[]{:S(2)}, u32[]{:S(2)}) collective-permute-start(bf16[4,4,16,1024]{3,2,1,0:T(8,128)(2,1)} %get-tuple-element.203), channel_id=1, source_target_pairs={{0,4},{4,0},{8,12},{12,8},{16,20},{20,16},{24,28},{28,24},{1,5},{5... | collective-permute-start | bytes 1572872 | tf_op jit(solution)/shard_map/ppermute | solution.py:33
  293.3 7.5 %collective-permute-start.24 = (bf16[2,4,16,1024]{3,2,1,0:T(8,128)(2,1)}, bf16[2,4,16,1024]{3,2,1,0:T(8,128)(2,1)}, u32[]{:S(2)}, u32[]{:S(2)}) collective-permute-start(bf16[2,4,16,1024]{3,2,1,0:T(8,128)(2,1)} %get-tuple-element.180), channel_id=1, source_target_pairs={{0,8},{4,12},{8,0},{12,4},{16,24},{20,28},{24,16},{28,20},{1,9},{5... | collective-permute-start | bytes 786440 | tf_op jit(solution)/shard_map/ppermute | solution.py:33
  298.8 18.9 %collective-permute-start.27 = (bf16[2,4,16,1024]{3,2,1,0:T(8,128)(2,1)}, bf16[2,4,16,1024]{3,2,1,0:T(8,128)(2,1)}, u32[]{:S(2)}, u32[]{:S(2)}) collective-permute-start(bf16[2,4,16,1024]{3,2,1,0:T(8,128)(2,1)} %get-tuple-element.189), channel_id=1, source_target_pairs={{0,8},{4,12},{8,0},{12,4},{16,24},{20,28},{24,16},{28,20},{1,9},{5... | collective-permute-start | bytes 786440 | tf_op jit(solution)/shard_map/ppermute | solution.py:33
  316.0 16.7 %collective-permute-start.30 = (bf16[2,4,16,1024]{3,2,1,0:T(8,128)(2,1)}, bf16[2,4,16,1024]{3,2,1,0:T(8,128)(2,1)}, u32[]{:S(2)}, u32[]{:S(2)}) collective-permute-start(bf16[2,4,16,1024]{3,2,1,0:T(8,128)(2,1)} %get-tuple-element.201), channel_id=1, source_target_pairs={{0,8},{4,12},{8,0},{12,4},{16,24},{20,28},{24,16},{28,20},{1,9},{5... | collective-permute-start | bytes 786440 | tf_op jit(solution)/shard_map/ppermute | solution.py:33
  329.2 22.5 %collective-permute-start.33 = (bf16[2,4,16,1024]{3,2,1,0:T(8,128)(2,1)}, bf16[2,4,16,1024]{3,2,1,0:T(8,128)(2,1)}, u32[]{:S(2)}, u32[]{:S(2)}) collective-permute-start(bf16[2,4,16,1024]{3,2,1,0:T(8,128)(2,1)} %get-tuple-element.215), channel_id=1, source_target_pairs={{0,8},{4,12},{8,0},{12,4},{16,24},{20,28},{24,16},{28,20},{1,9},{5... | collective-permute-start | bytes 786440 | tf_op jit(solution)/shard_map/ppermute | solution.py:33
  329.5 15.4 %collective-permute-start.26 = (bf16[1,4,16,1024]{3,2,1,0:T(8,128)(2,1)}, bf16[1,4,16,1024]{3,2,1,0:T(8,128)(2,1)}, u32[]{:S(2)}, u32[]{:S(2)}) collective-permute-start(bf16[1,4,16,1024]{3,2,1,0:T(8,128)(2,1)} %get-tuple-element.187), channel_id=1, source_target_pairs={{0,16},{4,20},{8,24},{12,28},{16,0},{20,4},{24,8},{28,12},{1,17},{... | collective-permute-start | bytes 393224 | tf_op jit(solution)/shard_map/ppermute | solution.py:33
  332.7 16.5 %collective-permute-start.29 = (bf16[1,4,16,1024]{3,2,1,0:T(8,128)(2,1)}, bf16[1,4,16,1024]{3,2,1,0:T(8,128)(2,1)}, u32[]{:S(2)}, u32[]{:S(2)}) collective-permute-start(bf16[1,4,16,1024]{3,2,1,0:T(8,128)(2,1)} %get-tuple-element.199), channel_id=1, source_target_pairs={{0,16},{4,20},{8,24},{12,28},{16,0},{20,4},{24,8},{28,12},{1,17},{... | collective-permute-start | bytes 393224 | tf_op jit(solution)/shard_map/ppermute | solution.py:33
  334.6 19.0 %collective-permute-start.32 = (bf16[1,4,16,1024]{3,2,1,0:T(8,128)(2,1)}, bf16[1,4,16,1024]{3,2,1,0:T(8,128)(2,1)S(1)}, u32[]{:S(2)}, u32[]{:S(2)}) collective-permute-start(bf16[1,4,16,1024]{3,2,1,0:T(8,128)(2,1)} %get-tuple-element.213), channel_id=1, source_target_pairs={{0,16},{4,20},{8,24},{12,28},{16,0},{20,4},{24,8},{28,12},{1,17},{... | collective-permute-start | bytes 393224 | tf_op jit(solution)/shard_map/ppermute | solution.py:33
  353.6 6.7 %collective-permute-start.34 = (bf16[1,4,16,1024]{3,2,1,0:T(8,128)(2,1)}, bf16[1,4,16,1024]{3,2,1,0:T(8,128)(2,1)}, u32[]{:S(2)}, u32[]{:S(2)}) collective-permute-start(bf16[1,4,16,1024]{3,2,1,0:T(8,128)(2,1)} %get-tuple-element.218), channel_id=1, source_target_pairs={{0,16},{4,20},{8,24},{12,28},{16,0},{20,4},{24,8},{28,12},{1,17},{... | collective-permute-start | bytes 393224 | tf_op jit(solution)/shard_map/ppermute | solution.py:33
  353.6 6.7 %copy-start.7 = (bf16[1,4,16,1024]{3,2,1,0:T(8,128)(2,1)}, bf16[1,4,16,1024]{3,2,1,0:T(8,128)(2,1)S(1)}, u32[]{:S(2)}) copy-start(bf16[1,4,16,1024]{3,2,1,0:T(8,128)(2,1)S(1)} %collective-permute-done.32.refs_2_) | copy-start | bytes 393220
  362.8 1.9 collective-permute-start.35
  362.8 4.8 %collective-permute-start.36 = (bf16[16,2048]{1,0:T(8,128)(2,1)}, bf16[16,2048]{1,0:T(8,128)(2,1)S(1)}, u32[]{:S(2)}, u32[]{:S(2)}) collective-permute-start(bf16[16,2048]{1,0:T(8,128)(2,1)} %get-tuple-element.222), channel_id=1, source_target_pairs={{0,2},{1,3},{2,0},{3,1},{4,6},{5,7},{6,4},{7,5},{8,10},{9,11},{10,... | collective-permute-start | bytes 196616 | tf_op jit(solution)/shard_map/ppermute | solution.py:29
  364.3 4.3 %collective-permute-start.37 = (bf16[16,2048]{1,0:T(8,128)(2,1)}, bf16[16,2048]{1,0:T(8,128)(2,1)S(1)}, u32[]{:S(2)}, u32[]{:S(2)}) collective-permute-start(bf16[16,2048]{1,0:T(8,128)(2,1)} %get-tuple-element.223), channel_id=1, source_target_pairs={{0,3},{1,2},{2,1},{3,0},{4,7},{5,6},{6,5},{7,4},{8,11},{9,10},{10,... | collective-permute-start | bytes 196616 | tf_op jit(solution)/shard_map/ppermute | solution.py:29
  364.7 3.9 %copy-start.8 = (bf16[16,2048]{1,0:T(8,128)(2,1)}, bf16[16,2048]{1,0:T(8,128)(2,1)S(1)}, u32[]{:S(2)}) copy-start(bf16[16,2048]{1,0:T(8,128)(2,1)S(1)} %collective-permute-done.35.refs_2_) | copy-start | bytes 196612
  367.6 1.0 copy-start.9
  (2 other events, 1.3 us)
Sparse Core Ops, SparseCore 0:
  10.1 75.4 all-gather.1

commit v6 on v5

--- a/solution.py
+++ b/solution.py
@@ -83,6 +83,23 @@
 
 def group(i):
     return (i & 1) * 2 + (i >> 1)
+
+
+def join(chain, parts):
+    rows, tile = parts[0].shape
+    count = len(parts)
+
+    def body(*refs):
+        for i in range(count):
+            refs[count][i] = refs[i][...]
+
+    (out,) = chain(
+        body,
+        (1,),
+        [(p, (rows, tile), lambda j: (0, 0)) for p in parts],
+        [((count, rows, tile), BF16, (count, rows, tile), lambda j: (0, 0, 0))],
+    )
+    return out
 
 
 def arrange(chain, place, slots, rows, tile, turned=False):
@@ -369,9 +386,9 @@
 
 
 def chunk_sizes(total):
-    last = max(1, total // 6)
-    rest = total - last
-    return [rest // 3, (rest + 2) // 3, (rest + 1) // 3, last]
+    small = max(1, total // 6)
+    rest = total - 2 * small
+    return [small, (rest + 1) // 2, rest // 2, small]
 
 
 def local_eight(activations, cotangent, gate_proj, up_proj, down_proj):
@@ -380,8 +397,8 @@
     tile, units = gate_proj.shape
     sizes = chunk_sizes(units // BLOCK)
     chunks = [(sum(sizes[:c]), sizes[c]) for c in range(4)]
-    backs = [(0, chunks[2][0]), (chunks[2][0], sizes[2] + sizes[3])]
-    back_of = [(0, 0), (0, sizes[0]), (1, 0), (1, sizes[2])]
+    backs = [chunks[0], chunks[1], (chunks[2][0], sizes[2] + sizes[3])]
+    back_of = [(0, 0), (1, 0), (2, 0), (2, sizes[2])]
     chain = Chain()
 
     keep_b, got_b, far_b = {}, {}, {}
@@ -424,66 +441,77 @@
         nonlocal grads
         grads = gradients(chain, act_t, cot, (own[c], near[c]), *chunks[c], grads, units)
 
-    def last_part(term, half):
-        keep, send = summed(chain, (own[3], near[3]), [term], *chunks[3], 2, half, True)
+    def last_part(term, halves=1, half=0):
+        keep, send = summed(chain, (own[3], near[3]), [term], *chunks[3], halves, half, True)
         return keep, swap_wide(send, 1)
 
     def over_z(pair, mask):
         keep, send = pass_on(chain, *pair)
         return keep, swap_wide(send, mask)
 
-    cot_all = lax.all_gather(cotangent, "wide", axis=0, tiled=True)
+    def gather_z(mine):
+        return [mine] + [swap_wide(mine, k) for k in (2, 4, 6)]
+
+    cot_even, cot_first = gather_z(cotangent), swap_wide(cotangent, 1)
     tiles = lax.all_to_all(activations, "narrow", split_axis=1, concat_axis=0, tiled=True)
-    pieces = {0: tiles, 1: swap_wide(tiles, 1)}
-    for k in (2, 4, 6):
-        pieces[k] = swap_wide(tiles, k)
-        pieces[k + 1] = swap_wide(pieces[k], 1)
-    slots = [(pieces[k], lambda s: 0) for k in range(8)]
-    act, act_t = arrange(chain, place, slots, rows, tile, True)
+    act_even, act_first = gather_z(tiles), swap_wide(tiles, 1)
+    act_odd = [swap_wide(x, 1) for x in act_even[1:]]
+    chain.after(tiles, cot_first, act_first)
+    cot_odd = swap_wide(join(chain, cot_even[1:]), 1).reshape(12 * rows, tile)
+
+    def slots(even, first, odd):
+        res = [(even[0], 0), (first, 0)]
+        for i in range(3):
+            res += [(even[i + 1], 0), odd[i]]
+        return [(x, functools.partial(lambda at, s: at, at)) for x, at in res]
+
+    chain.after(*act_even[1:])
+    cot_slots = slots(cot_even, cot_first, [(cot_odd, 4 * i) for i in range(3)])
+    (cot,) = arrange(chain, place, cot_slots, rows, tile)
+    back(0)
+    chain.after(*act_odd)
+    back(1)
+    back_x(0)
+    back(2)
+    back_x(1)
+    act_slots = slots(act_even, act_first, [(x, 0) for x in act_odd])
+    act, act_t = arrange(chain, place, act_slots, rows, tile, True)
+    chain.after(far_b[0])
     gate_up(0)
+    back_x(2)
+    chain.after(far_b[1], got_gu[0])
     gate_up(1)
-    slots = [(cot_all, functools.partial(lambda k, s: (s[1] ^ k) * 4, k)) for k in range(8)]
-    (cot,) = arrange(chain, place, slots, rows, tile)
     gate_up_x(0)
-    back(0)
+    chain.after(far_b[2])
+    gate_up(2)
     gate_up_x(1)
-    gate_up(2)
-    chain.after(far_gu[0])
-    back_x(0)
-    back(1)
+    gate_up(3)
     gate_up_x(2)
-    chain.after(far_gu[1])
-    gate_up(3)
-    back_x(1)
+    chain.after(got_gu[3])
     elementwise(0)
-    elementwise(1)
     gate_up_x(3)
     add_both(0)
     all_grads(0)
-    chain.after(far_gu[2])
+    elementwise(1)
     add_both(1)
     elementwise(2)
     all_grads(1)
     elementwise(3)
     add_both(2)
-    parts = [last_part(out_term(), 0)]
-    parts.append(last_part(out_term(), 1))
-    parts.append(last_part(grad_term(), 0))
-    parts[0] = over_z(parts[0], 2)
-    parts.append(last_part(grad_term(), 1))
-    parts[1] = over_z(parts[1], 2)
-    parts[0] = over_z(parts[0], 4)
+    grad_part = last_part(grad_term())
+    out_parts = [last_part(out_term(), 2, 0), last_part(out_term(), 2, 1)]
     all_grads(2)
-    parts[2] = over_z(parts[2], 2)
-    parts[1] = over_z(parts[1], 4)
     all_grads(3)
-    parts[3] = over_z(parts[3], 2)
-    parts[2] = over_z(parts[2], 4)
-    block_output = finish(chain, place, parts[:2], True)
-    parts[3] = over_z(parts[3], 4)
-    groups = finish(chain, place, parts[2:], False)
+    grad_part = over_z(grad_part, 2)
+    out_parts[0] = over_z(out_parts[0], 2)
+    grad_part = over_z(grad_part, 4)
+    out_parts[1] = over_z(out_parts[1], 2)
+    out_parts[0] = over_z(out_parts[0], 4)
+    groups = finish(chain, place, [grad_part], False)
     groups = [groups[0]] + [swap(groups[g], g) for g in range(1, 4)]
+    out_parts[1] = over_z(out_parts[1], 4)
     input_gradient = place_columns(chain, place, groups)
+    block_output = finish(chain, place, out_parts, True)
     return (block_output, input_gradient, *grads)
 
 

time: 381 us -> 343 us (0.900)
  waiting for transfers between devices: 110 us -> 84.1 us
  between operations: 14.2 us -> 0.75 us
  starting transfers between devices: 32.2 us -> 42.3 us
  blocking collectives: 10 us -> 0 us
    ppermute x19 -> x21, waiting for transfers between devices: 72.9 us -> 54.6 us  [swap_wide(): return lax.ppermute(value, 'wide', [(i, i ^ mask) for i in range(8)])]
    all_to_all x1 -> x0, blocking collectives: 10 us -> none  [local_eight(): lax.all_to_all(activations, 'narrow', split_axis=1, concat_axis=0, tiled=...]
    ppermute x19 -> x21, waiting for transfers between devices: 36.8 us -> 29.4 us  [swap(): return lax.ppermute(value, 'narrow', [(i, i ^ mask) for i in range(4)])]
    all_to_all x0 -> x1, starting transfers between devices: none -> 4.21 us  [local_eight(): lax.all_to_all(activations, 'narrow', split_axis=1, concat_axis=0, tiled=...]
    ppermute x19 -> x21, starting transfers between devices: 23.1 us -> 27.1 us  [swap_wide(): return lax.ppermute(value, 'wide', [(i, i ^ mask) for i in range(8)])]
    ppermute x19 -> x21, starting transfers between devices: 9.09 us -> 11 us  [swap(): return lax.ppermute(value, 'narrow', [(i, i ^ mask) for i in range(4)])]
  transfers between devices with their start and end apart: 39 -> 43, of which waited for: 18 -> 19; matrix products, arithmetic and copies ran while one was open for 0% -> 0% of each run, Pallas kernels for 49% -> 53%
where the time goes in v6:
time: 343 us; the launch traced here: 341 us
  Pallas kernels  210 us (61%)
  waiting for transfers between devices  84.1 us (25%)
  starting transfers between devices  42.3 us (12%)
    pallas_call x40, Pallas kernels, __call__(): pl.pallas_call(kernel, grid_spec=pltpu.PrefetchScalarGridSpec(num_scalar_...  210 us
    ppermute x21, waiting for transfers between devices, swap_wide(): return lax.ppermute(value, 'wide', [(i, i ^ mask) for i in range(8)])  54.6 us
    ppermute x21, waiting for transfers between devices, swap(): return lax.ppermute(value, 'narrow', [(i, i ^ mask) for i in range(4)])  29.4 us
    ppermute x21, starting transfers between devices, swap_wide(): return lax.ppermute(value, 'wide', [(i, i ^ mask) for i in range(8)])  27.1 us
    ppermute x21, starting transfers between devices, swap(): return lax.ppermute(value, 'narrow', [(i, i ^ mask) for i in range(4)])  11 us
  transfers between devices with their start and end apart: 43, of which 19 were waited for; matrix products, arithmetic and copies ran while one was open for 0% of the time, Pallas kernels for 53%

profile of v6, /device:TPU:0, one launch (start us, length us, event | category | flops | bytes accessed | tf_op | source)
XLA Modules:
  0.0 340.7 jit_solution(11453786946451490578)
XLA Ops:
  2.3 4.2 %all-to-all-start = ((bf16[16,4,2048]{2,0,1:T(8,128)(2,1)}), bf16[16,4,2048]{2,0,1:T(8,128)(2,1)S(1)}, u32[]{:S(2)}, u32[]{:S(2)}) async-start(bf16[16,4,2048]{2,0,1:T(8,128)(2,1)} %bitcast.12), calls=%async_computation | async-start | bytes 524288 | tf_op jit(solution)/shard_map/all_to_all | solution.py:456
  6.5 3.3 collective-permute-start.9
  15.4 7.6 %collective-permute-done.9.refs_1_.refs_5_ = bf16[64,2048]{1,0:T(8,128)(2,1)} collective-permute-done((bf16[64,2048]{1,0:T(8,128)(2,1)}, bf16[64,2048]{1,0:T(8,128)(2,1)}, u32[]{:S(2)}, u32[]{:S(2)}) %collective-permute-start.9) | collective-permute-done | bytes 262176 | tf_op jit(solution)/shard_map/ppermute | solution.py:33
  23.0 6.5 %collective-permute-done.10.refs_2_.refs_7_ = bf16[64,2048]{1,0:T(8,128)(2,1)} collective-permute-done((bf16[64,2048]{1,0:T(8,128)(2,1)}, bf16[64,2048]{1,0:T(8,128)(2,1)}, u32[]{:S(2)}, u32[]{:S(2)}) %collective-permute-start.10) | collective-permute-done | bytes 262176 | tf_op jit(solution)/shard_map/ppermute | solution.py:33
  33.0 2.5 collective-permute-start.5
  35.5 4.6 %collective-permute-start.3 = (bf16[64,2048]{1,0:T(8,128)(2,1)}, bf16[64,2048]{1,0:T(8,128)(2,1)}, u32[]{:S(2)}, u32[]{:S(2)}) collective-permute-start(bf16[64,2048]{1,0:T(8,128)(2,1)} %bitcast.27), channel_id=1, source_target_pairs={{0,16},{4,20},{8,24},{12,28},{16,0},{20,4},{24,8},{28,12},{1,17},{... | collective-permute-start | bytes 786440 | tf_op jit(solution)/shard_map/ppermute | solution.py:33
  43.3 16.2 %collective-permute-done.3.refs_10_.refs_5_ = bf16[64,2048]{1,0:T(8,128)(2,1)} collective-permute-done((bf16[64,2048]{1,0:T(8,128)(2,1)}, bf16[64,2048]{1,0:T(8,128)(2,1)}, u32[]{:S(2)}, u32[]{:S(2)}) %collective-permute-start.3) | collective-permute-done | bytes 262176 | tf_op jit(solution)/shard_map/ppermute | solution.py:33
  62.2 4.5 %shard_map.93 = (bf16[4,8,16,2048]{3,2,1,0:T(8,128)(2,1)}, f32[8,128]{1,0:T(8,128)}) custom-call(s32[2]{0:T(128)} %pad_add_fusion.refs_0_, bf16[64,2048]{1,0:T(8,128)(2,1)} %refs_1_.8, bf16[64,2048]{1,0:T(8,128)(2,1)} %collective-permute-done.7.refs_4_.refs_2_, bf16[64,2048]{1,0:T(8,128)(2,1)} %collective-permute-done.8.refs_0_.refs_3_, ...), custom_call_target="tpu_custom_call" | custom-call | flops 1 | bytes 1 | tf_op jit(solution)/shard_map/pallas_call | solution.py:66
  66.7 4.1 %shard_map.94 = (f32[256,512]{1,0:T(8,128)}, bf16[256,512]{1,0:T(8,128)(2,1)}, f32[8,128]{1,0:T(8,128)}) custom-call(bf16[512,2048]{1,0:T(8,128)(2,1)} %bitcast.13, bf16[3328,2048]{1,0:T(8,128)(2,1)} %refs_3_.11, f32[8,128]{1,0:T(8,128)} %get-tuple-element.118.refs_2_), custom_call_target="tpu_custom_call" | custom-call | flops 1 | bytes 1 | tf_op jit(solution)/shard_map/pallas_call | solution.py:66
  70.8 2.9 collective-permute-done.2.refs_2_.refs_4_
  73.7 7.5 %shard_map.95 = (f32[256,1280]{1,0:T(8,128)}, bf16[256,1280]{1,0:T(8,128)(2,1)}, f32[8,128]{1,0:T(8,128)}) custom-call(bf16[512,2048]{1,0:T(8,128)(2,1)} %bitcast.14, bf16[3328,2048]{1,0:T(8,128)(2,1)} %refs_3_.11, bf16[64,2048]{1,0:T(8,128)(2,1)} %collective-permute-done.2.refs_2_.refs_4_, bf16[64,2048]{1,0:T(8,128)(2,1)} %collective-permute-done.4.refs_3_.refs_6_, ...), custom_call_target="tpu_custom_call" | custom-call | flops 1 | bytes 1 | tf_op jit(solution)/shard_map/pallas_call | solution.py:66
  87.1 8.4 %shard_map.97 = (f32[256,1536]{1,0:T(8,128)}, bf16[256,1536]{1,0:T(8,128)(2,1)}, f32[8,128]{1,0:T(8,128)}) custom-call(bf16[512,2048]{1,0:T(8,128)(2,1)} %bitcast.15, bf16[3328,2048]{1,0:T(8,128)(2,1)} %refs_3_.11, f32[8,128]{1,0:T(8,128)} %get-tuple-element.125.refs_2_), custom_call_target="tpu_custom_call" | custom-call | flops 1 | bytes 1 | tf_op jit(solution)/shard_map/pallas_call | solution.py:66
  95.5 2.3 shard_map.98
  98.5 5.1 %shard_map.99 = (bf16[4,8,16,2048]{3,2,1,0:T(8,128)(2,1)}, bf16[2048,512]{1,0:T(8,128)(2,1)}, f32[8,128]{1,0:T(8,128)}) custom-call(s32[2]{0:T(128)} %pad_add_fusion.refs_0_, bf16[64,2048]{1,0:T(8,128)(2,1)} %bitcast.29, bf16[64,2048]{1,0:T(8,128)(2,1)} %collective-permute-done.refs_5_.refs_2_, bf16[64,2048]{1,0:T(8,128)(2,1)} %collective-permute-done.1.refs_9_.refs_3_, ...), custom_call_target="tpu_custom_call" | custom-call | flops 1 | bytes 1 | tf_op jit(solution)/shard_map/pallas_call | solution.py:66
  103.7 6.0 %shard_map.100 = (f32[2,256,512]{2,1,0:T(8,128)}, bf16[2,256,512]{2,1,0:T(8,128)(2,1)}, f32[8,128]{1,0:T(8,128)}) custom-call(bf16[512,2048]{1,0:T(8,128)(2,1)} %bitcast.20, bf16[2048,3328]{1,0:T(8,128)(2,1)} %refs_3_.9, bf16[2048,3328]{1,0:T(8,128)(2,1)} %refs_5_.7, bf16[256,512]{1,0:T(8,128)(2,1)} %collective-permute-done.15.refs_3_.refs_5_, ...), custom_call_target="tpu_custom_call" | custom-call | flops 1 | bytes 1 | tf_op jit(solution)/shard_map/pallas_call | solution.py:66
  109.9 2.4 shard_map.101
  115.3 10.4 %shard_map.102 = (f32[2,256,1280]{2,1,0:T(8,128)}, bf16[2,256,1280]{2,1,0:T(8,128)(2,1)}, f32[8,128]{1,0:T(8,128)}) custom-call(bf16[512,2048]{1,0:T(8,128)(2,1)} %bitcast.21, bf16[2048,3328]{1,0:T(8,128)(2,1)} %refs_3_.9, bf16[2048,3328]{1,0:T(8,128)(2,1)} %refs_5_.7, bf16[256,1280]{1,0:T(8,128)(2,1)} %collective-permute-done.14.refs_3_.refs_5_, ...), custom_call_target="tpu_custom_call" | custom-call | flops 1 | bytes 1 | tf_op jit(solution)/shard_map/pallas_call | solution.py:66
  127.8 4.5 %collective-permute-done.19.refs_3_.refs_5_ = bf16[256,1536]{1,0:T(8,128)(2,1)} collective-permute-done((bf16[256,1536]{1,0:T(8,128)(2,1)}, bf16[256,1536]{1,0:T(8,128)(2,1)}, u32[]{:S(2)}, u32[]{:S(2)}) %collective-permute-start.19) | collective-permute-done | bytes 786464 | tf_op jit(solution)/shard_map/ppermute | solution.py:29
  132.4 8.8 %shard_map.104 = (f32[2,256,1024]{2,1,0:T(8,128)}, bf16[2,256,1024]{2,1,0:T(8,128)(2,1)}, f32[8,128]{1,0:T(8,128)}) custom-call(bf16[512,2048]{1,0:T(8,128)(2,1)} %bitcast.22, bf16[2048,3328]{1,0:T(8,128)(2,1)} %refs_3_.9, bf16[2048,3328]{1,0:T(8,128)(2,1)} %refs_5_.7, bf16[256,1536]{1,0:T(8,128)(2,1)} %collective-permute-done.19.refs_3_.refs_5_, ...), custom_call_target="tpu_custom_call" | custom-call | flops 1 | bytes 1 | tf_op jit(solution)/shard_map/pallas_call | solution.py:66
  142.5 3.0 shard_map.105
  145.6 5.6 %shard_map.106 = (f32[2,256,512]{2,1,0:T(8,128)}, bf16[2,256,512]{2,1,0:T(8,128)(2,1)}, f32[8,128]{1,0:T(8,128)}) custom-call(bf16[512,2048]{1,0:T(8,128)(2,1)} %bitcast.23, bf16[2048,3328]{1,0:T(8,128)(2,1)} %refs_3_.9, bf16[2048,3328]{1,0:T(8,128)(2,1)} %refs_5_.7, f32[8,128]{1,0:T(8,128)} %get-tuple-element.144.refs_3_), custom_call_target="tpu_custom_call" | custom-call | flops 1 | bytes 1 | tf_op jit(solution)/shard_map/pallas_call | solution.py:66
  152.1 2.7 shard_map.107
  156.3 2.8 shard_map.108
  161.7 8.7 %shard_map.110 = (f32[512,2048]{1,0:T(8,128)}, f32[512,2048]{1,0:T(8,128)}, f32[8,128]{1,0:T(8,128)}) custom-call(bf16[3,256,512]{2,1,0:T(8,128)(2,1)} %get-tuple-element.156.refs_0_.refs_2_, bf16[3,256,512]{2,1,0:T(8,128)(2,1)} %collective-permute-done.25.refs_1_.refs_3_, bf16[3328,2048]{1,0:T(8,128)(2,1)} %refs_3_.11, bf16[3328,2048]{1,0:T(8,128)(2,1)} %refs_3_.11, ...), custom_call_target="tpu_custom_call" | custom-call | flops 1 | bytes 1 | tf_op jit(solution)/shard_map/pallas_call | solution.py:66
  170.4 7.3 %shard_map.111 = (bf16[2048,3328]{1,0:T(8,128)(2,1)}, bf16[2048,3328]{1,0:T(8,128)(2,1)}, bf16[3328,2048]{1,0:T(8,128)(2,1)}, f32[8,128]{1,0:T(8,128)}) custom-call(bf16[2048,512]{1,0:T(8,128)(2,1)} %get-tuple-element.154.refs_0_, bf16[512,2048]{1,0:T(8,128)(2,1)} %bitcast.16, bf16[3,256,512]{2,1,0:T(8,128)(2,1)} %get-tuple-element.156.refs_0_.refs_2_, ...), custom_call_target="tpu_custom_call" | custom-call | flops 1 | bytes 1 | tf_op jit(solution)/shard_map/pallas_call | solution.py:66
  177.7 6.2 %collective-permute-done.24.refs_2_ = bf16[2,256,1280]{2,1,0:T(8,128)(2,1)} collective-permute-done((bf16[2,256,1280]{2,1,0:T(8,128)(2,1)}, bf16[2,256,1280]{2,1,0:T(8,128)(2,1)}, u32[]{:S(2)}, u32[]{:S(2)}) %collective-permute-start.24) | collective-permute-done | bytes 1310752 | tf_op jit(solution)/shard_map/ppermute | solution.py:29
  183.9 6.3 %shard_map.112 = (bf16[3,256,1280]{2,1,0:T(8,128)(2,1)}, f32[8,128]{1,0:T(8,128)}) custom-call(f32[2,256,1280]{2,1,0:T(8,128)} %get-tuple-element.137.refs_0_, bf16[2,256,1280]{2,1,0:T(8,128)(2,1)} %collective-permute-done.18.refs_1_, bf16[2,256,1280]{2,1,0:T(8,128)(2,1)} %collective-permute-done.24.refs_2_, f32[256,1280]{1,0:T(8,128)} %get-tuple-element.120.refs_0_.refs_3_, ...), custom_call_target="tpu_custom_call" | custom-call | flops 1 | bytes 1 | tf_op jit(solution)/shard_map/pallas_call | solution.py:66
  191.5 2.9 collective-permute-done.26.refs_1_.refs_3_
  194.5 16.0 %shard_map.113 = (f32[512,2048]{1,0:T(8,128)}, f32[512,2048]{1,0:T(8,128)}, f32[8,128]{1,0:T(8,128)}) custom-call(bf16[3,256,1280]{2,1,0:T(8,128)(2,1)} %get-tuple-element.160.refs_0_.refs_2_, bf16[3,256,1280]{2,1,0:T(8,128)(2,1)} %collective-permute-done.26.refs_1_.refs_3_, ...), custom_call_target="tpu_custom_call", output_to_operand_aliasing={{0}: (7, {}), {1}: (18, {})} | custom-call | flops 1 | bytes 1 | tf_op jit(solution)/shard_map/pallas_call | solution.py:66
  210.5 5.5 %collective-permute-done.27.refs_2_ = bf16[2,256,1024]{2,1,0:T(8,128)(2,1)} collective-permute-done((bf16[2,256,1024]{2,1,0:T(8,128)(2,1)}, bf16[2,256,1024]{2,1,0:T(8,128)(2,1)}, u32[]{:S(2)}, u32[]{:S(2)}) %collective-permute-start.27) | collective-permute-done | bytes 1048608 | tf_op jit(solution)/shard_map/ppermute | solution.py:29
  216.0 4.9 %shard_map.114 = (bf16[3,256,1024]{2,1,0:T(8,128)(2,1)}, f32[8,128]{1,0:T(8,128)}) custom-call(f32[2,256,1024]{2,1,0:T(8,128)} %get-tuple-element.148.refs_0_, bf16[2,256,1024]{2,1,0:T(8,128)(2,1)} %collective-permute-done.22.refs_1_, bf16[2,256,1024]{2,1,0:T(8,128)(2,1)} %collective-permute-done.27.refs_2_, f32[256,1536]{1,0:T(8,128)} %get-tuple-element.133.refs_0_.refs_3_, ...), custom_call_target="tpu_custom_call" | custom-call | flops 1 | bytes 1 | tf_op jit(solution)/shard_map/pallas_call | solution.py:66
  222.3 12.8 %shard_map.115 = (bf16[2048,3328]{1,0:T(8,128)(2,1)}, bf16[2048,3328]{1,0:T(8,128)(2,1)}, bf16[3328,2048]{1,0:T(8,128)(2,1)}, f32[8,128]{1,0:T(8,128)}) custom-call(bf16[2048,512]{1,0:T(8,128)(2,1)} %get-tuple-element.154.refs_0_, bf16[512,2048]{1,0:T(8,128)(2,1)} %bitcast.17, ...), custom_call_target="tpu_custom_call", output_to_operand_aliasing={{0}: (4, {}), {1}: (5, {}), {2}: (6, {})} | custom-call | flops 1 | bytes 1 | tf_op jit(solution)/shard_map/pallas_call | solution.py:66
  235.6 2.9 shard_map.116
  238.5 13.9 %shard_map.117 = (f32[512,2048]{1,0:T(8,128)}, f32[512,2048]{1,0:T(8,128)}, f32[8,128]{1,0:T(8,128)}) custom-call(bf16[3,256,1024]{2,1,0:T(8,128)(2,1)} %get-tuple-element.172.refs_0_.refs_2_, bf16[3,256,1024]{2,1,0:T(8,128)(2,1)} %collective-permute-done.29.refs_1_.refs_3_, ...), custom_call_target="tpu_custom_call", output_to_operand_aliasing={{0}: (6, {}), {1}: (15, {})} | custom-call | flops 1 | bytes 1 | tf_op jit(solution)/shard_map/pallas_call | solution.py:66
  252.3 7.6 %shard_map.118 = (f32[4,4,16,2048]{3,2,1,0:T(8,128)}, bf16[4,4,16,2048]{3,2,1,0:T(8,128)(2,1)}, f32[8,128]{1,0:T(8,128)}) custom-call(bf16[3,256,512]{2,1,0:T(8,128)(2,1)} %get-tuple-element.171.refs_0_.refs_2_, bf16[3,256,512]{2,1,0:T(8,128)(2,1)} %collective-permute-done.28.refs_1_.refs_3_, bf16[2048,3328]{1,0:T(8,128)(2,1)} %refs_3_.9, ...), custom_call_target="tpu_custom_call" | custom-call | flops 1 | bytes 1 | tf_op jit(solution)/shard_map/pallas_call | solution.py:66
  260.4 3.9 %shard_map.119 = (f32[4,4,16,1024]{3,2,1,0:T(8,128)}, bf16[4,4,16,1024]{3,2,1,0:T(8,128)(2,1)}, f32[8,128]{1,0:T(8,128)}) custom-call(bf16[3,256,512]{2,1,0:T(8,128)(2,1)} %get-tuple-element.171.refs_0_.refs_2_, bf16[3,256,512]{2,1,0:T(8,128)(2,1)} %collective-permute-done.28.refs_1_.refs_3_, bf16[3328,2048]{1,0:T(8,128)(2,1)} %refs_3_.11, ...), custom_call_target="tpu_custom_call" | custom-call | flops 1 | bytes 1 | tf_op jit(solution)/shard_map/pallas_call | solution.py:66
  265.9 3.8 %shard_map.120 = (f32[4,4,16,1024]{3,2,1,0:T(8,128)}, bf16[4,4,16,1024]{3,2,1,0:T(8,128)(2,1)}, f32[8,128]{1,0:T(8,128)}) custom-call(bf16[3,256,512]{2,1,0:T(8,128)(2,1)} %get-tuple-element.171.refs_0_.refs_2_, bf16[3,256,512]{2,1,0:T(8,128)(2,1)} %collective-permute-done.28.refs_1_.refs_3_, bf16[3328,2048]{1,0:T(8,128)(2,1)} %refs_3_.11, ...), custom_call_target="tpu_custom_call" | custom-call | flops 1 | bytes 1 | tf_op jit(solution)/shard_map/pallas_call | solution.py:66
  269.6 11.0 %shard_map.121 = (bf16[2048,3328]{1,0:T(8,128)(2,1)}, bf16[2048,3328]{1,0:T(8,128)(2,1)}, bf16[3328,2048]{1,0:T(8,128)(2,1)}, f32[8,128]{1,0:T(8,128)}) custom-call(bf16[2048,512]{1,0:T(8,128)(2,1)} %get-tuple-element.154.refs_0_, bf16[512,2048]{1,0:T(8,128)(2,1)} %bitcast.18, ...), custom_call_target="tpu_custom_call", output_to_operand_aliasing={{0}: (4, {}), {1}: (5, {}), {2}: (6, {})} | custom-call | flops 1 | bytes 1 | tf_op jit(solution)/shard_map/pallas_call | solution.py:66
  280.6 7.3 %shard_map.122 = (bf16[2048,3328]{1,0:T(8,128)(2,1)}, bf16[2048,3328]{1,0:T(8,128)(2,1)}, bf16[3328,2048]{1,0:T(8,128)(2,1)}, f32[8,128]{1,0:T(8,128)}) custom-call(bf16[2048,512]{1,0:T(8,128)(2,1)} %get-tuple-element.154.refs_0_, bf16[512,2048]{1,0:T(8,128)(2,1)} %bitcast.19, ...), custom_call_target="tpu_custom_call", output_to_operand_aliasing={{0}: (4, {}), {1}: (5, {}), {2}: (6, {})} | custom-call | flops 1 | bytes 1 | tf_op jit(solution)/shard_map/pallas_call | solution.py:66
  287.9 3.2 shard_map.123
  292.3 5.1 %collective-permute-done.30.refs_1_ = bf16[4,4,16,1024]{3,2,1,0:T(8,128)(2,1)} collective-permute-done((bf16[4,4,16,1024]{3,2,1,0:T(8,128)(2,1)}, bf16[4,4,16,1024]{3,2,1,0:T(8,128)(2,1)}, u32[]{:S(2)}, u32[]{:S(2)}) %collective-permute-start.30) | collective-permute-done | bytes 524320 | tf_op jit(solution)/shard_map/ppermute | solution.py:33
  300.3 5.9 %collective-permute-done.34.refs_1_ = bf16[2,4,16,2048]{3,2,1,0:T(8,128)(2,1)} collective-permute-done((bf16[2,4,16,2048]{3,2,1,0:T(8,128)(2,1)}, bf16[2,4,16,2048]{3,2,1,0:T(8,128)(2,1)}, u32[]{:S(2)}, u32[]{:S(2)}) %collective-permute-start.34) | collective-permute-done | bytes 524320 | tf_op jit(solution)/shard_map/ppermute | solution.py:33
  310.1 2.3 shard_map.126
  316.2 8.2 %collective-permute-done.37.refs_2_ = bf16[1,4,16,2048]{3,2,1,0:T(8,128)(2,1)} collective-permute-done((bf16[1,4,16,2048]{3,2,1,0:T(8,128)(2,1)}, bf16[1,4,16,2048]{3,2,1,0:T(8,128)(2,1)}, u32[]{:S(2)}, u32[]{:S(2)}) %collective-permute-start.37) | collective-permute-done | bytes 262176 | tf_op jit(solution)/shard_map/ppermute | solution.py:33
  324.4 2.5 shard_map.128
  330.6 3.4 %collective-permute-done.40.refs_3_ = bf16[16,2048]{1,0:T(8,128)(2,1)} collective-permute-done((bf16[16,2048]{1,0:T(8,128)(2,1)}, bf16[16,2048]{1,0:T(8,128)(2,1)}, u32[]{:S(2)}, u32[]{:S(2)}) %collective-permute-start.40) | collective-permute-done | bytes 65568 | tf_op jit(solution)/shard_map/ppermute | solution.py:29
  334.5 2.9 shard_map.130
  338.1 2.5 shard_map.131
  (86 shorter events, 56.9 us)
Async XLA Ops:
  2.3 10.8 %all-to-all-start = ((bf16[16,4,2048]{2,0,1:T(8,128)(2,1)}), bf16[16,4,2048]{2,0,1:T(8,128)(2,1)S(1)}, u32[]{:S(2)}, u32[]{:S(2)}) async-start(bf16[16,4,2048]{2,0,1:T(8,128)(2,1)} %bitcast.12), calls=%async_computation | async-start | bytes 524288 | tf_op jit(solution)/shard_map/all_to_all | solution.py:456
  6.5 16.4 %collective-permute-start.9 = (bf16[64,2048]{1,0:T(8,128)(2,1)}, bf16[64,2048]{1,0:T(8,128)(2,1)}, u32[]{:S(2)}, u32[]{:S(2)}) collective-permute-start(bf16[64,2048]{1,0:T(8,128)(2,1)} %refs_1_.8), channel_id=1, source_target_pairs={{0,16},{4,20},{8,24},{12,28},{16,0},{20,4},{24,8},{28,12},{1,17},{... | collective-permute-start | bytes 786440 | tf_op jit(solution)/shard_map/ppermute | solution.py:33
  9.8 13.1 %collective-permute-start.8 = (bf16[64,2048]{1,0:T(8,128)(2,1)}, bf16[64,2048]{1,0:T(8,128)(2,1)}, u32[]{:S(2)}, u32[]{:S(2)}) collective-permute-start(bf16[64,2048]{1,0:T(8,128)(2,1)} %refs_1_.8), channel_id=1, source_target_pairs={{0,8},{4,12},{8,0},{12,4},{16,24},{20,28},{24,16},{28,20},{1,9},{5... | collective-permute-start | bytes 786440 | tf_op jit(solution)/shard_map/ppermute | solution.py:33
  11.4 11.6 %collective-permute-start.7 = (bf16[64,2048]{1,0:T(8,128)(2,1)}, bf16[64,2048]{1,0:T(8,128)(2,1)}, u32[]{:S(2)}, u32[]{:S(2)}) collective-permute-start(bf16[64,2048]{1,0:T(8,128)(2,1)} %refs_1_.8), channel_id=1, source_target_pairs={{0,4},{4,0},{8,12},{12,8},{16,20},{20,16},{24,28},{28,24},{1,5},{5... | collective-permute-start | bytes 786440 | tf_op jit(solution)/shard_map/ppermute | solution.py:33
  12.9 16.6 %collective-permute-start.10 = (bf16[64,2048]{1,0:T(8,128)(2,1)}, bf16[64,2048]{1,0:T(8,128)(2,1)}, u32[]{:S(2)}, u32[]{:S(2)}) collective-permute-start(bf16[64,2048]{1,0:T(8,128)(2,1)} %refs_1_.8), channel_id=1, source_target_pairs={{0,24},{4,28},{8,16},{12,20},{16,8},{20,12},{24,0},{28,4},{1,25},{... | collective-permute-start | bytes 786440 | tf_op jit(solution)/shard_map/ppermute | solution.py:33
  13.1 0.7 copy-start
  13.8 15.6 %collective-permute-start = (bf16[64,2048]{1,0:T(8,128)(2,1)S(1)}, bf16[64,2048]{1,0:T(8,128)(2,1)}, u32[]{:S(2)}, u32[]{:S(2)}) collective-permute-start(bf16[64,2048]{1,0:T(8,128)(2,1)S(1)} %bitcast.24), channel_id=1, source_target_pairs={{0,4},{4,0},{8,12},{12,8},{16,20},{20,16},{24,28},{28,24},{1,5},{5... | collective-permute-start | bytes 786440 | tf_op jit(solution)/shard_map/ppermute | solution.py:33
  31.5 30.7 %collective-permute-start.11 = (bf16[3,64,2048]{2,1,0:T(8,128)(2,1)}, bf16[3,64,2048]{2,1,0:T(8,128)(2,1)}, u32[]{:S(2)}, u32[]{:S(2)}) collective-permute-start(bf16[3,64,2048]{2,1,0:T(8,128)(2,1)} %get-tuple-element.115), channel_id=1, source_target_pairs={{0,4},{4,0},{8,12},{12,8},{16,20},{20,16},{24,28},{28,24},{1,5},{5... | collective-permute-start | bytes 2359304 | tf_op jit(solution)/shard_map/ppermute | solution.py:33
  33.0 9.7 %collective-permute-start.5 = (bf16[64,2048]{1,0:T(8,128)(2,1)}, bf16[64,2048]{1,0:T(8,128)(2,1)}, u32[]{:S(2)}, u32[]{:S(2)}) collective-permute-start(bf16[64,2048]{1,0:T(8,128)(2,1)} %bitcast.26), channel_id=1, source_target_pairs={{0,24},{4,28},{8,16},{12,20},{16,8},{20,12},{24,0},{28,4},{1,25},{... | collective-permute-start | bytes 786440 | tf_op jit(solution)/shard_map/ppermute | solution.py:33
  35.5 24.0 %collective-permute-start.3 = (bf16[64,2048]{1,0:T(8,128)(2,1)}, bf16[64,2048]{1,0:T(8,128)(2,1)}, u32[]{:S(2)}, u32[]{:S(2)}) collective-permute-start(bf16[64,2048]{1,0:T(8,128)(2,1)} %bitcast.27), channel_id=1, source_target_pairs={{0,16},{4,20},{8,24},{12,28},{16,0},{20,4},{24,8},{28,12},{1,17},{... | collective-permute-start | bytes 786440 | tf_op jit(solution)/shard_map/ppermute | solution.py:33
  40.1 19.9 %collective-permute-start.1 = (bf16[64,2048]{1,0:T(8,128)(2,1)}, bf16[64,2048]{1,0:T(8,128)(2,1)}, u32[]{:S(2)}, u32[]{:S(2)}) collective-permute-start(bf16[64,2048]{1,0:T(8,128)(2,1)} %bitcast.28), channel_id=1, source_target_pairs={{0,8},{4,12},{8,0},{12,4},{16,24},{20,28},{24,16},{28,20},{1,9},{5... | collective-permute-start | bytes 786440 | tf_op jit(solution)/shard_map/ppermute | solution.py:33
  42.8 28.0 %collective-permute-start.6 = (bf16[64,2048]{1,0:T(8,128)(2,1)}, bf16[64,2048]{1,0:T(8,128)(2,1)}, u32[]{:S(2)}, u32[]{:S(2)}) collective-permute-start(bf16[64,2048]{1,0:T(8,128)(2,1)} %collective-permute-done.5.refs_11_.refs_7_), channel_id=1, source_target_pairs={{0,4},{4,0},{8,12},{12,8},{16,20},{20,16},{24,28},{28,24},{1,5},{5... | collective-permute-start | bytes 786440 | tf_op jit(solution)/shard_map/ppermute | solution.py:33
  59.5 11.2 %collective-permute-start.4 = (bf16[64,2048]{1,0:T(8,128)(2,1)}, bf16[64,2048]{1,0:T(8,128)(2,1)}, u32[]{:S(2)}, u32[]{:S(2)}) collective-permute-start(bf16[64,2048]{1,0:T(8,128)(2,1)} %collective-permute-done.3.refs_10_.refs_5_), channel_id=1, source_target_pairs={{0,4},{4,0},{8,12},{12,8},{16,20},{20,16},{24,28},{28,24},{1,5},{5... | collective-permute-start | bytes 786440 | tf_op jit(solution)/shard_map/ppermute | solution.py:33
  60.0 13.7 %collective-permute-start.2 = (bf16[64,2048]{1,0:T(8,128)(2,1)}, bf16[64,2048]{1,0:T(8,128)(2,1)}, u32[]{:S(2)}, u32[]{:S(2)}) collective-permute-start(bf16[64,2048]{1,0:T(8,128)(2,1)} %collective-permute-done.1.refs_9_.refs_3_), channel_id=1, source_target_pairs={{0,4},{4,0},{8,12},{12,8},{16,20},{20,16},{24,28},{28,24},{1,5},{5... | collective-permute-start | bytes 786440 | tf_op jit(solution)/shard_map/ppermute | solution.py:33
  81.2 14.4 %collective-permute-start.12 = (bf16[256,1280]{1,0:T(8,128)(2,1)}, bf16[256,1280]{1,0:T(8,128)(2,1)}, u32[]{:S(2)}, u32[]{:S(2)}) collective-permute-start(bf16[256,1280]{1,0:T(8,128)(2,1)} %get-tuple-element.121), channel_id=1, source_target_pairs={{0,1},{1,0},{2,3},{3,2},{4,5},{5,4},{6,7},{7,6},{8,9},{9,8},{10,11... | collective-permute-start | bytes 1966088 | tf_op jit(solution)/shard_map/ppermute | solution.py:29
  81.2 2.8 collective-permute-start.13
  85.8 17.9 %collective-permute-start.15 = (bf16[256,512]{1,0:T(8,128)(2,1)}, bf16[256,512]{1,0:T(8,128)(2,1)}, u32[]{:S(2)}, u32[]{:S(2)}) collective-permute-start(bf16[256,512]{1,0:T(8,128)(2,1)} %get-tuple-element.130), channel_id=1, source_target_pairs={{0,2},{1,3},{2,0},{3,1},{4,6},{5,7},{6,4},{7,5},{8,10},{9,11},{10,... | collective-permute-start | bytes 786440 | tf_op jit(solution)/shard_map/ppermute | solution.py:29
  95.5 14.4 %collective-permute-start.17 = (bf16[256,1536]{1,0:T(8,128)(2,1)}, bf16[256,1536]{1,0:T(8,128)(2,1)}, u32[]{:S(2)}, u32[]{:S(2)}) collective-permute-start(bf16[256,1536]{1,0:T(8,128)(2,1)} %get-tuple-element.134), channel_id=1, source_target_pairs={{0,1},{1,0},{2,3},{3,2},{4,5},{5,4},{6,7},{7,6},{8,9},{9,8},{10,11... | collective-permute-start | bytes 2359304 | tf_op jit(solution)/shard_map/ppermute | solution.py:29
  97.8 17.4 %collective-permute-start.14 = (bf16[256,1280]{1,0:T(8,128)(2,1)}, bf16[256,1280]{1,0:T(8,128)(2,1)}, u32[]{:S(2)}, u32[]{:S(2)}) collective-permute-start(bf16[256,1280]{1,0:T(8,128)(2,1)} %get-tuple-element.129), channel_id=1, source_target_pairs={{0,2},{1,3},{2,0},{3,1},{4,6},{5,7},{6,4},{7,5},{8,10},{9,11},{10,... | collective-permute-start | bytes 1966088 | tf_op jit(solution)/shard_map/ppermute | solution.py:29
  109.7 3.9 %collective-permute-start.16 = (bf16[2,256,512]{2,1,0:T(8,128)(2,1)}, bf16[2,256,512]{2,1,0:T(8,128)(2,1)}, u32[]{:S(2)}, u32[]{:S(2)}) collective-permute-start(bf16[2,256,512]{2,1,0:T(8,128)(2,1)} %get-tuple-element.132), channel_id=1, source_target_pairs={{0,1},{1,0},{2,3},{3,2},{4,5},{5,4},{6,7},{7,6},{8,9},{9,8},{10,11... | collective-permute-start | bytes 1572872 | tf_op jit(solution)/shard_map/ppermute | solution.py:29
  112.3 20.1 %collective-permute-start.19 = (bf16[256,1536]{1,0:T(8,128)(2,1)}, bf16[256,1536]{1,0:T(8,128)(2,1)}, u32[]{:S(2)}, u32[]{:S(2)}) collective-permute-start(bf16[256,1536]{1,0:T(8,128)(2,1)} %get-tuple-element.139), channel_id=1, source_target_pairs={{0,2},{1,3},{2,0},{3,1},{4,6},{5,7},{6,4},{7,5},{8,10},{9,11},{10,... | collective-permute-start | bytes 2359304 | tf_op jit(solution)/shard_map/ppermute | solution.py:29
  125.7 16.8 %collective-permute-start.18 = (bf16[2,256,1280]{2,1,0:T(8,128)(2,1)}, bf16[2,256,1280]{2,1,0:T(8,128)(2,1)}, u32[]{:S(2)}, u32[]{:S(2)}) collective-permute-start(bf16[2,256,1280]{2,1,0:T(8,128)(2,1)} %get-tuple-element.138), channel_id=1, source_target_pairs={{0,1},{1,0},{2,3},{3,2},{4,5},{5,4},{6,7},{7,6},{8,9},{9,8},{10,11... | collective-permute-start | bytes 3932168 | tf_op jit(solution)/shard_map/ppermute | solution.py:29
  141.1 10.9 %collective-permute-start.22 = (bf16[2,256,1024]{2,1,0:T(8,128)(2,1)}, bf16[2,256,1024]{2,1,0:T(8,128)(2,1)}, u32[]{:S(2)}, u32[]{:S(2)}) collective-permute-start(bf16[2,256,1024]{2,1,0:T(8,128)(2,1)} %get-tuple-element.149), channel_id=1, source_target_pairs={{0,1},{1,0},{2,3},{3,2},{4,5},{5,4},{6,7},{7,6},{8,9},{9,8},{10,11... | collective-permute-start | bytes 3145736 | tf_op jit(solution)/shard_map/ppermute | solution.py:29
  141.1 15.1 %collective-permute-start.21 = (bf16[2,256,512]{2,1,0:T(8,128)(2,1)}, bf16[2,256,512]{2,1,0:T(8,128)(2,1)}, u32[]{:S(2)}, u32[]{:S(2)}) collective-permute-start(bf16[2,256,512]{2,1,0:T(8,128)(2,1)} %get-tuple-element.147), channel_id=1, source_target_pairs={{0,2},{1,3},{2,0},{3,1},{4,6},{5,7},{6,4},{7,5},{8,10},{9,11},{10,... | collective-permute-start | bytes 1572872 | tf_op jit(solution)/shard_map/ppermute | solution.py:29
  151.2 5.1 %collective-permute-start.20 = (bf16[2,256,512]{2,1,0:T(8,128)(2,1)}, bf16[2,256,512]{2,1,0:T(8,128)(2,1)}, u32[]{:S(2)}, u32[]{:S(2)}) collective-permute-start(bf16[2,256,512]{2,1,0:T(8,128)(2,1)} %get-tuple-element.146), channel_id=1, source_target_pairs={{0,1},{1,0},{2,3},{3,2},{4,5},{5,4},{6,7},{7,6},{8,9},{9,8},{10,11... | collective-permute-start | bytes 1572872 | tf_op jit(solution)/shard_map/ppermute | solution.py:29
  151.4 32.5 %collective-permute-start.24 = (bf16[2,256,1280]{2,1,0:T(8,128)(2,1)}, bf16[2,256,1280]{2,1,0:T(8,128)(2,1)}, u32[]{:S(2)}, u32[]{:S(2)}) collective-permute-start(bf16[2,256,1280]{2,1,0:T(8,128)(2,1)} %get-tuple-element.155), channel_id=1, source_target_pairs={{0,2},{1,3},{2,0},{3,1},{4,6},{5,7},{6,4},{7,5},{8,10},{9,11},{10,... | collective-permute-start | bytes 3932168 | tf_op jit(solution)/shard_map/ppermute | solution.py:29
  159.1 2.6 collective-permute-start.25
  190.2 4.3 %collective-permute-start.26 = (bf16[3,256,1280]{2,1,0:T(8,128)(2,1)}, bf16[3,256,1280]{2,1,0:T(8,128)(2,1)}, u32[]{:S(2)}, u32[]{:S(2)}) collective-permute-start(bf16[3,256,1280]{2,1,0:T(8,128)(2,1)} %get-tuple-element.160.refs_0_.refs_2_), channel_id=1, source_target_pairs={{0,1},{1,0},{2,3},{3,2},{4,5},{5,4},{6,7},{7,6},{8,9},{9,8},{10,11... | collective-permute-start | bytes 5898248 | tf_op jit(solution)/shard_map/ppermute | solution.py:29
  190.2 25.9 %collective-permute-start.27 = (bf16[2,256,1024]{2,1,0:T(8,128)(2,1)}, bf16[2,256,1024]{2,1,0:T(8,128)(2,1)}, u32[]{:S(2)}, u32[]{:S(2)}) collective-permute-start(bf16[2,256,1024]{2,1,0:T(8,128)(2,1)} %get-tuple-element.164), channel_id=1, source_target_pairs={{0,2},{1,3},{2,0},{3,1},{4,6},{5,7},{6,4},{7,5},{8,10},{9,11},{10,... | collective-permute-start | bytes 3145736 | tf_op jit(solution)/shard_map/ppermute | solution.py:29
  220.9 17.5 %collective-permute-start.29 = (bf16[3,256,1024]{2,1,0:T(8,128)(2,1)}, bf16[3,256,1024]{2,1,0:T(8,128)(2,1)}, u32[]{:S(2)}, u32[]{:S(2)}) collective-permute-start(bf16[3,256,1024]{2,1,0:T(8,128)(2,1)} %get-tuple-element.172.refs_0_.refs_2_), channel_id=1, source_target_pairs={{0,1},{1,0},{2,3},{3,2},{4,5},{5,4},{6,7},{7,6},{8,9},{9,8},{10,11... | collective-permute-start | bytes 4718600 | tf_op jit(solution)/shard_map/ppermute | solution.py:29
  220.9 14.6 %collective-permute-start.23 = (bf16[2,256,512]{2,1,0:T(8,128)(2,1)}, bf16[2,256,512]{2,1,0:T(8,128)(2,1)}, u32[]{:S(2)}, u32[]{:S(2)}) collective-permute-start(bf16[2,256,512]{2,1,0:T(8,128)(2,1)} %get-tuple-element.153), channel_id=1, source_target_pairs={{0,2},{1,3},{2,0},{3,1},{4,6},{5,7},{6,4},{7,5},{8,10},{9,11},{10,... | collective-permute-start | bytes 1572872 | tf_op jit(solution)/shard_map/ppermute | solution.py:29
  238.4 13.9 %collective-permute-start.28 = (bf16[3,256,512]{2,1,0:T(8,128)(2,1)}, bf16[3,256,512]{2,1,0:T(8,128)(2,1)}, u32[]{:S(2)}, u32[]{:S(2)}) collective-permute-start(bf16[3,256,512]{2,1,0:T(8,128)(2,1)} %get-tuple-element.171.refs_0_.refs_2_), channel_id=1, source_target_pairs={{0,1},{1,0},{2,3},{3,2},{4,5},{5,4},{6,7},{7,6},{8,9},{9,8},{10,11... | collective-permute-start | bytes 2359304 | tf_op jit(solution)/shard_map/ppermute | solution.py:29
  259.9 28.0 %collective-permute-start.31 = (bf16[4,4,16,2048]{3,2,1,0:T(8,128)(2,1)}, bf16[4,4,16,2048]{3,2,1,0:T(8,128)(2,1)}, u32[]{:S(2)}, u32[]{:S(2)}) collective-permute-start(bf16[4,4,16,2048]{3,2,1,0:T(8,128)(2,1)} %get-tuple-element.183), channel_id=1, source_target_pairs={{0,4},{4,0},{8,12},{12,8},{16,20},{20,16},{24,28},{28,24},{1,5},{5... | collective-permute-start | bytes 3145736 | tf_op jit(solution)/shard_map/ppermute | solution.py:33
  264.3 33.1 %collective-permute-start.30 = (bf16[4,4,16,1024]{3,2,1,0:T(8,128)(2,1)}, bf16[4,4,16,1024]{3,2,1,0:T(8,128)(2,1)}, u32[]{:S(2)}, u32[]{:S(2)}) collective-permute-start(bf16[4,4,16,1024]{3,2,1,0:T(8,128)(2,1)} %get-tuple-element.181), channel_id=1, source_target_pairs={{0,4},{4,0},{8,12},{12,8},{16,20},{20,16},{24,28},{28,24},{1,5},{5... | collective-permute-start | bytes 1572872 | tf_op jit(solution)/shard_map/ppermute | solution.py:33
  291.1 15.1 %collective-permute-start.34 = (bf16[2,4,16,2048]{3,2,1,0:T(8,128)(2,1)}, bf16[2,4,16,2048]{3,2,1,0:T(8,128)(2,1)}, u32[]{:S(2)}, u32[]{:S(2)}) collective-permute-start(bf16[2,4,16,2048]{3,2,1,0:T(8,128)(2,1)} %get-tuple-element.200), channel_id=1, source_target_pairs={{0,8},{4,12},{8,0},{12,4},{16,24},{20,28},{24,16},{28,20},{1,9},{5... | collective-permute-start | bytes 1572872 | tf_op jit(solution)/shard_map/ppermute | solution.py:33
  291.7 18.4 %collective-permute-start.33 = (bf16[4,4,16,1024]{3,2,1,0:T(8,128)(2,1)}, bf16[4,4,16,1024]{3,2,1,0:T(8,128)(2,1)}, u32[]{:S(2)}, u32[]{:S(2)}) collective-permute-start(bf16[4,4,16,1024]{3,2,1,0:T(8,128)(2,1)} %get-tuple-element.198), channel_id=1, source_target_pairs={{0,4},{4,0},{8,12},{12,8},{16,20},{20,16},{24,28},{28,24},{1,5},{5... | collective-permute-start | bytes 1572872 | tf_op jit(solution)/shard_map/ppermute | solution.py:33
  299.7 14.2 %collective-permute-start.32 = (bf16[2,4,16,1024]{3,2,1,0:T(8,128)(2,1)}, bf16[2,4,16,1024]{3,2,1,0:T(8,128)(2,1)}, u32[]{:S(2)}, u32[]{:S(2)}) collective-permute-start(bf16[2,4,16,1024]{3,2,1,0:T(8,128)(2,1)} %get-tuple-element.196), channel_id=1, source_target_pairs={{0,8},{4,12},{8,0},{12,4},{16,24},{20,28},{24,16},{28,20},{1,9},{5... | collective-permute-start | bytes 786440 | tf_op jit(solution)/shard_map/ppermute | solution.py:33
  308.5 15.9 %collective-permute-start.37 = (bf16[1,4,16,2048]{3,2,1,0:T(8,128)(2,1)}, bf16[1,4,16,2048]{3,2,1,0:T(8,128)(2,1)}, u32[]{:S(2)}, u32[]{:S(2)}) collective-permute-start(bf16[1,4,16,2048]{3,2,1,0:T(8,128)(2,1)} %get-tuple-element.209), channel_id=1, source_target_pairs={{0,16},{4,20},{8,24},{12,28},{16,0},{20,4},{24,8},{28,12},{1,17},{... | collective-permute-start | bytes 786440 | tf_op jit(solution)/shard_map/ppermute | solution.py:33
  312.5 14.4 %collective-permute-start.36 = (bf16[2,4,16,1024]{3,2,1,0:T(8,128)(2,1)}, bf16[2,4,16,1024]{3,2,1,0:T(8,128)(2,1)}, u32[]{:S(2)}, u32[]{:S(2)}) collective-permute-start(bf16[2,4,16,1024]{3,2,1,0:T(8,128)(2,1)} %get-tuple-element.207), channel_id=1, source_target_pairs={{0,8},{4,12},{8,0},{12,4},{16,24},{20,28},{24,16},{28,20},{1,9},{5... | collective-permute-start | bytes 786440 | tf_op jit(solution)/shard_map/ppermute | solution.py:33
  315.8 21.7 %collective-permute-start.35 = (bf16[1,4,16,1024]{3,2,1,0:T(8,128)(2,1)}, bf16[1,4,16,1024]{3,2,1,0:T(8,128)(2,1)S(1)}, u32[]{:S(2)}, u32[]{:S(2)}) collective-permute-start(bf16[1,4,16,1024]{3,2,1,0:T(8,128)(2,1)} %get-tuple-element.205), channel_id=1, source_target_pairs={{0,16},{4,20},{8,24},{12,28},{16,0},{20,4},{24,8},{28,12},{1,17},{... | collective-permute-start | bytes 393224 | tf_op jit(solution)/shard_map/ppermute | solution.py:33
  328.8 8.7 %collective-permute-start.38 = (bf16[1,4,16,1024]{3,2,1,0:T(8,128)(2,1)}, bf16[1,4,16,1024]{3,2,1,0:T(8,128)(2,1)}, u32[]{:S(2)}, u32[]{:S(2)}) collective-permute-start(bf16[1,4,16,1024]{3,2,1,0:T(8,128)(2,1)} %get-tuple-element.213), channel_id=1, source_target_pairs={{0,16},{4,20},{8,24},{12,28},{16,0},{20,4},{24,8},{28,12},{1,17},{... | collective-permute-start | bytes 393224 | tf_op jit(solution)/shard_map/ppermute | solution.py:33
  328.8 1.9 collective-permute-start.39
  328.8 5.3 %collective-permute-start.40 = (bf16[16,2048]{1,0:T(8,128)(2,1)}, bf16[16,2048]{1,0:T(8,128)(2,1)}, u32[]{:S(2)}, u32[]{:S(2)}) collective-permute-start(bf16[16,2048]{1,0:T(8,128)(2,1)} %get-tuple-element.216), channel_id=1, source_target_pairs={{0,2},{1,3},{2,0},{3,1},{4,6},{5,7},{6,4},{7,5},{8,10},{9,11},{10,... | collective-permute-start | bytes 196616 | tf_op jit(solution)/shard_map/ppermute | solution.py:29
  329.7 4.8 %collective-permute-start.41 = (bf16[16,2048]{1,0:T(8,128)(2,1)}, bf16[16,2048]{1,0:T(8,128)(2,1)}, u32[]{:S(2)}, u32[]{:S(2)}) collective-permute-start(bf16[16,2048]{1,0:T(8,128)(2,1)} %get-tuple-element.217), channel_id=1, source_target_pairs={{0,3},{1,2},{2,1},{3,0},{4,7},{5,6},{6,5},{7,4},{8,11},{9,10},{10,... | collective-permute-start | bytes 196616 | tf_op jit(solution)/shard_map/ppermute | solution.py:29
  330.6 3.9 %copy-start.2 = (bf16[16,2048]{1,0:T(8,128)(2,1)}, bf16[16,2048]{1,0:T(8,128)(2,1)S(1)}, u32[]{:S(2)}) copy-start(bf16[16,2048]{1,0:T(8,128)(2,1)S(1)} %collective-permute-done.39.refs_2_) | copy-start | bytes 196612
  337.5 0.7 copy-start.1

commit v7 on v6

--- a/solution.py
+++ b/solution.py
@@ -83,6 +83,21 @@
 
 def group(i):
     return (i & 1) * 2 + (i >> 1)
+
+
+def cut_columns(chain, rows_in):
+    rows, tile = rows_in.shape[0], rows_in.shape[1] // 4
+
+    def body(x, out):
+        out[0] = x[...]
+
+    (out,) = chain(
+        body,
+        (4,),
+        [(rows_in, (rows, tile), lambda j: (0, j))],
+        [((4, rows, tile), BF16, (1, rows, tile), lambda j: (j, 0, 0))],
+    )
+    return out
 
 
 def join(chain, parts):
@@ -450,13 +465,17 @@
         return keep, swap_wide(send, mask)
 
     def gather_z(mine):
-        return [mine] + [swap_wide(mine, k) for k in (2, 4, 6)]
+        neighbour, across = swap_wide(mine, 2), swap_wide(mine, 4)
+        return [mine, neighbour, across, swap_wide(across, 2)]
 
     cot_even, cot_first = gather_z(cotangent), swap_wide(cotangent, 1)
-    tiles = lax.all_to_all(activations, "narrow", split_axis=1, concat_axis=0, tiled=True)
+    chain.after(cot_first)
+    tiles = cut_columns(chain, activations)
+    tiles = lax.all_to_all(tiles, "narrow", split_axis=0, concat_axis=0, tiled=True)
+    tiles = tiles.reshape(4 * rows, tile)
     act_even, act_first = gather_z(tiles), swap_wide(tiles, 1)
     act_odd = [swap_wide(x, 1) for x in act_even[1:]]
-    chain.after(tiles, cot_first, act_first)
+    chain.after(tiles, act_first)
     cot_odd = swap_wide(join(chain, cot_even[1:]), 1).reshape(12 * rows, tile)
 
     def slots(even, first, odd):
@@ -495,14 +514,14 @@
     elementwise(1)
     add_both(1)
     elementwise(2)
+    add_both(2)
+    elementwise(3)
     all_grads(1)
-    elementwise(3)
-    add_both(2)
     grad_part = last_part(grad_term())
     out_parts = [last_part(out_term(), 2, 0), last_part(out_term(), 2, 1)]
     all_grads(2)
+    grad_part = over_z(grad_part, 2)
     all_grads(3)
-    grad_part = over_z(grad_part, 2)
     out_parts[0] = over_z(out_parts[0], 2)
     grad_part = over_z(grad_part, 4)
     out_parts[1] = over_z(out_parts[1], 2)

time: 343 us -> 343 us (level)
  waiting for transfers between devices: 84.1 us -> 73.3 us
  starting transfers between devices: 42.3 us -> 50.4 us
    ppermute x21, waiting for transfers between devices: 54.6 us -> 38.4 us  [swap_wide(): return lax.ppermute(value, 'wide', [(i, i ^ mask) for i in range(8)])]
    ppermute x21, starting transfers between devices: 27.1 us -> 35.7 us  [swap_wide(): return lax.ppermute(value, 'wide', [(i, i ^ mask) for i in range(8)])]
    all_to_all x1, waiting for transfers between devices: 0.01 us -> 3.72 us  [local_eight(): lax.all_to_all(tiles, 'narrow', split_axis=0, concat_axis=0, tiled=True)]
    pallas_call x40 -> x41, Pallas kernels: 210 us -> 213 us  [__call__(): pl.pallas_call(kernel, grid_spec=pltpu.PrefetchScalarGridSpec(num_scalar_...]
  transfers between devices with their start and end apart: 43 -> 43, of which waited for: 19 -> 21; matrix products, arithmetic and copies ran while one was open for 0% -> 0% of each run, Pallas kernels for 53% -> 53%
where the time goes in v7:
time: 343 us; the launch traced here: 341 us
  Pallas kernels  213 us (62%)
  waiting for transfers between devices  73.3 us (21%)
  starting transfers between devices  50.4 us (15%)
    pallas_call x41, Pallas kernels, __call__(): pl.pallas_call(kernel, grid_spec=pltpu.PrefetchScalarGridSpec(num_scalar_...  213 us
    ppermute x21, waiting for transfers between devices, swap_wide(): return lax.ppermute(value, 'wide', [(i, i ^ mask) for i in range(8)])  38.4 us
    ppermute x21, starting transfers between devices, swap_wide(): return lax.ppermute(value, 'wide', [(i, i ^ mask) for i in range(8)])  35.7 us
    ppermute x21, waiting for transfers between devices, swap(): return lax.ppermute(value, 'narrow', [(i, i ^ mask) for i in range(4)])  31.2 us
    ppermute x21, starting transfers between devices, swap(): return lax.ppermute(value, 'narrow', [(i, i ^ mask) for i in range(4)])  11.3 us
  transfers between devices with their start and end apart: 43, of which 21 were waited for; matrix products, arithmetic and copies ran while one was open for 0% of the time, Pallas kernels for 53%

profile of v7, /device:TPU:0, one launch (start us, length us, event | category | flops | bytes accessed | tf_op | source)
XLA Modules:
  0.0 340.8 jit_solution(2618166139313126099)
XLA Ops:
  0.6 3.0 collective-permute-start
  3.7 2.6 collective-permute-start.9
  6.3 4.0 %collective-permute-done.refs_1_.refs_2_ = bf16[64,2048]{1,0:T(8,128)(2,1)} collective-permute-done((bf16[64,2048]{1,0:T(8,128)(2,1)}, bf16[64,2048]{1,0:T(8,128)(2,1)}, u32[]{:S(2)}, u32[]{:S(2)}) %collective-permute-start) | collective-permute-done | bytes 262176 | tf_op jit(solution)/shard_map/ppermute | solution.py:33
  10.3 3.0 shard_map.92
  13.2 3.4 all-to-all-start
  18.9 3.7 %all-to-all-done = bf16[4,16,2048]{2,1,0:T(8,128)(2,1)S(1)} async-done(((bf16[4,16,2048]{2,1,0:T(8,128)(2,1)}), bf16[4,16,2048]{2,1,0:T(8,128)(2,1)S(1)}, u32[]{:S(2)}, u32[]{:S(2)}) %all-to-all-start) | async-done | bytes 262176 | tf_op jit(solution)/shard_map/all_to_all | solution.py:474
  26.0 5.2 %collective-permute-done.10.refs_2_.refs_7_ = bf16[64,2048]{1,0:T(8,128)(2,1)S(1)} collective-permute-done((bf16[64,2048]{1,0:T(8,128)(2,1)}, bf16[64,2048]{1,0:T(8,128)(2,1)S(1)}, u32[]{:S(2)}, u32[]{:S(2)}) %collective-permute-start.10) | collective-permute-done | bytes 262176 | tf_op jit(solution)/shard_map/ppermute | solution.py:33
  36.4 2.6 collective-permute-start.4
  40.5 10.3 %collective-permute-done.4.refs_10_.refs_5_ = bf16[64,2048]{1,0:T(8,128)(2,1)} collective-permute-done((bf16[64,2048]{1,0:T(8,128)(2,1)}, bf16[64,2048]{1,0:T(8,128)(2,1)}, u32[]{:S(2)}, u32[]{:S(2)}) %collective-permute-start.4) | collective-permute-done | bytes 262176 | tf_op jit(solution)/shard_map/ppermute | solution.py:33
  53.5 4.8 %collective-permute-done.6.refs_11_.refs_7_ = bf16[64,2048]{1,0:T(8,128)(2,1)} collective-permute-done((bf16[64,2048]{1,0:T(8,128)(2,1)}, bf16[64,2048]{1,0:T(8,128)(2,1)}, u32[]{:S(2)}, u32[]{:S(2)}) %collective-permute-start.6) | collective-permute-done | bytes 262176 | tf_op jit(solution)/shard_map/ppermute | solution.py:33
  59.4 4.5 %shard_map.94 = (bf16[4,8,16,2048]{3,2,1,0:T(8,128)(2,1)}, f32[8,128]{1,0:T(8,128)}) custom-call(s32[2]{0:T(128)} %pad_add_fusion.refs_0_, bf16[64,2048]{1,0:T(8,128)(2,1)} %refs_1_.8, bf16[64,2048]{1,0:T(8,128)(2,1)} %collective-permute-done.refs_1_.refs_2_, bf16[64,2048]{1,0:T(8,128)(2,1)} %copy-done.2, bf16[192,2048]{1,0:T(8,128)(2,1)} %bitcast.3.refs_4_.refs_6_.refs_8_, ...), custom_call_target="tpu_custom_call" | custom-call | flops 1 | bytes 1 | tf_op jit(solution)/shard_map/pallas_call | solution.py:66
  63.9 4.1 %shard_map.95 = (f32[256,512]{1,0:T(8,128)}, bf16[256,512]{1,0:T(8,128)(2,1)}, f32[8,128]{1,0:T(8,128)}) custom-call(bf16[512,2048]{1,0:T(8,128)(2,1)} %bitcast.7, bf16[3328,2048]{1,0:T(8,128)(2,1)} %refs_3_.11, f32[8,128]{1,0:T(8,128)} %get-tuple-element.122.refs_2_), custom_call_target="tpu_custom_call" | custom-call | flops 1 | bytes 1 | tf_op jit(solution)/shard_map/pallas_call | solution.py:66
  68.0 3.0 collective-permute-done.7.refs_4_.refs_8_
  70.9 7.5 %shard_map.96 = (f32[256,1280]{1,0:T(8,128)}, bf16[256,1280]{1,0:T(8,128)(2,1)}, f32[8,128]{1,0:T(8,128)}) custom-call(bf16[512,2048]{1,0:T(8,128)(2,1)} %bitcast.8, bf16[3328,2048]{1,0:T(8,128)(2,1)} %refs_3_.11, bf16[64,2048]{1,0:T(8,128)(2,1)} %collective-permute-done.3.refs_2_.refs_4_, bf16[64,2048]{1,0:T(8,128)(2,1)} %collective-permute-done.5.refs_3_.refs_6_, ...), custom_call_target="tpu_custom_call" | custom-call | flops 1 | bytes 1 | tf_op jit(solution)/shard_map/pallas_call | solution.py:66
  84.4 8.4 %shard_map.98 = (f32[256,1536]{1,0:T(8,128)}, bf16[256,1536]{1,0:T(8,128)(2,1)}, f32[8,128]{1,0:T(8,128)}) custom-call(bf16[512,2048]{1,0:T(8,128)(2,1)} %bitcast.9, bf16[3328,2048]{1,0:T(8,128)(2,1)} %refs_3_.11, f32[8,128]{1,0:T(8,128)} %get-tuple-element.129.refs_2_), custom_call_target="tpu_custom_call" | custom-call | flops 1 | bytes 1 | tf_op jit(solution)/shard_map/pallas_call | solution.py:66
  95.7 5.1 %shard_map.100 = (bf16[4,8,16,2048]{3,2,1,0:T(8,128)(2,1)}, bf16[2048,512]{1,0:T(8,128)(2,1)}, f32[8,128]{1,0:T(8,128)}) custom-call(s32[2]{0:T(128)} %pad_add_fusion.refs_0_, bf16[64,2048]{1,0:T(8,128)(2,1)} %bitcast.22, bf16[64,2048]{1,0:T(8,128)(2,1)} %copy-done.1, bf16[64,2048]{1,0:T(8,128)(2,1)} %collective-permute-done.2.refs_9_.refs_3_, ...), custom_call_target="tpu_custom_call" | custom-call | flops 1 | bytes 1 | tf_op jit(solution)/shard_map/pallas_call | solution.py:66
  100.8 6.0 %shard_map.101 = (f32[2,256,512]{2,1,0:T(8,128)}, bf16[2,256,512]{2,1,0:T(8,128)(2,1)}, f32[8,128]{1,0:T(8,128)}) custom-call(bf16[512,2048]{1,0:T(8,128)(2,1)} %bitcast.14, bf16[2048,3328]{1,0:T(8,128)(2,1)} %refs_3_.9, bf16[2048,3328]{1,0:T(8,128)(2,1)} %refs_5_.7, bf16[256,512]{1,0:T(8,128)(2,1)} %collective-permute-done.15.refs_3_.refs_5_, ...), custom_call_target="tpu_custom_call" | custom-call | flops 1 | bytes 1 | tf_op jit(solution)/shard_map/pallas_call | solution.py:66
  112.5 10.4 %shard_map.103 = (f32[2,256,1280]{2,1,0:T(8,128)}, bf16[2,256,1280]{2,1,0:T(8,128)(2,1)}, f32[8,128]{1,0:T(8,128)}) custom-call(bf16[512,2048]{1,0:T(8,128)(2,1)} %bitcast.15, bf16[2048,3328]{1,0:T(8,128)(2,1)} %refs_3_.9, bf16[2048,3328]{1,0:T(8,128)(2,1)} %refs_5_.7, bf16[256,1280]{1,0:T(8,128)(2,1)} %collective-permute-done.14.refs_3_.refs_5_, ...), custom_call_target="tpu_custom_call" | custom-call | flops 1 | bytes 1 | tf_op jit(solution)/shard_map/pallas_call | solution.py:66
  125.1 4.5 %collective-permute-done.19.refs_3_.refs_5_ = bf16[256,1536]{1,0:T(8,128)(2,1)} collective-permute-done((bf16[256,1536]{1,0:T(8,128)(2,1)}, bf16[256,1536]{1,0:T(8,128)(2,1)}, u32[]{:S(2)}, u32[]{:S(2)}) %collective-permute-start.19) | collective-permute-done | bytes 786464 | tf_op jit(solution)/shard_map/ppermute | solution.py:29
  129.5 8.8 %shard_map.105 = (f32[2,256,1024]{2,1,0:T(8,128)}, bf16[2,256,1024]{2,1,0:T(8,128)(2,1)}, f32[8,128]{1,0:T(8,128)}) custom-call(bf16[512,2048]{1,0:T(8,128)(2,1)} %bitcast.16, bf16[2048,3328]{1,0:T(8,128)(2,1)} %refs_3_.9, bf16[2048,3328]{1,0:T(8,128)(2,1)} %refs_5_.7, bf16[256,1536]{1,0:T(8,128)(2,1)} %collective-permute-done.19.refs_3_.refs_5_, ...), custom_call_target="tpu_custom_call" | custom-call | flops 1 | bytes 1 | tf_op jit(solution)/shard_map/pallas_call | solution.py:66
  139.8 3.1 shard_map.106
  142.8 5.6 %shard_map.107 = (f32[2,256,512]{2,1,0:T(8,128)}, bf16[2,256,512]{2,1,0:T(8,128)(2,1)}, f32[8,128]{1,0:T(8,128)}) custom-call(bf16[512,2048]{1,0:T(8,128)(2,1)} %bitcast.17, bf16[2048,3328]{1,0:T(8,128)(2,1)} %refs_3_.9, bf16[2048,3328]{1,0:T(8,128)(2,1)} %refs_5_.7, f32[8,128]{1,0:T(8,128)} %get-tuple-element.148.refs_3_), custom_call_target="tpu_custom_call" | custom-call | flops 1 | bytes 1 | tf_op jit(solution)/shard_map/pallas_call | solution.py:66
  149.3 2.7 shard_map.108
  153.4 2.8 shard_map.109
  158.9 8.8 %shard_map.111 = (f32[512,2048]{1,0:T(8,128)}, f32[512,2048]{1,0:T(8,128)}, f32[8,128]{1,0:T(8,128)}) custom-call(bf16[3,256,512]{2,1,0:T(8,128)(2,1)} %get-tuple-element.161.refs_0_.refs_2_, bf16[3,256,512]{2,1,0:T(8,128)(2,1)} %collective-permute-done.26.refs_1_.refs_3_, bf16[3328,2048]{1,0:T(8,128)(2,1)} %refs_3_.11, bf16[3328,2048]{1,0:T(8,128)(2,1)} %refs_3_.11, ...), custom_call_target="tpu_custom_call" | custom-call | flops 1 | bytes 1 | tf_op jit(solution)/shard_map/pallas_call | solution.py:66
  167.7 7.3 %shard_map.112 = (bf16[2048,3328]{1,0:T(8,128)(2,1)}, bf16[2048,3328]{1,0:T(8,128)(2,1)}, bf16[3328,2048]{1,0:T(8,128)(2,1)}, f32[8,128]{1,0:T(8,128)}) custom-call(bf16[2048,512]{1,0:T(8,128)(2,1)} %get-tuple-element.160.refs_0_, bf16[512,2048]{1,0:T(8,128)(2,1)} %bitcast.10, bf16[3,256,512]{2,1,0:T(8,128)(2,1)} %get-tuple-element.161.refs_0_.refs_2_, ...), custom_call_target="tpu_custom_call" | custom-call | flops 1 | bytes 1 | tf_op jit(solution)/shard_map/pallas_call | solution.py:66
  175.0 6.1 %collective-permute-done.25.refs_2_ = bf16[2,256,1280]{2,1,0:T(8,128)(2,1)} collective-permute-done((bf16[2,256,1280]{2,1,0:T(8,128)(2,1)}, bf16[2,256,1280]{2,1,0:T(8,128)(2,1)}, u32[]{:S(2)}, u32[]{:S(2)}) %collective-permute-start.25) | collective-permute-done | bytes 1310752 | tf_op jit(solution)/shard_map/ppermute | solution.py:29
  181.1 6.2 %shard_map.113 = (bf16[3,256,1280]{2,1,0:T(8,128)(2,1)}, f32[8,128]{1,0:T(8,128)}) custom-call(f32[2,256,1280]{2,1,0:T(8,128)} %get-tuple-element.141.refs_0_, bf16[2,256,1280]{2,1,0:T(8,128)(2,1)} %collective-permute-done.18.refs_1_, bf16[2,256,1280]{2,1,0:T(8,128)(2,1)} %collective-permute-done.25.refs_2_, f32[256,1280]{1,0:T(8,128)} %get-tuple-element.124.refs_0_.refs_3_, ...), custom_call_target="tpu_custom_call" | custom-call | flops 1 | bytes 1 | tf_op jit(solution)/shard_map/pallas_call | solution.py:66
  188.7 2.9 collective-permute-done.27.refs_1_.refs_3_
  191.6 16.1 %shard_map.114 = (f32[512,2048]{1,0:T(8,128)}, f32[512,2048]{1,0:T(8,128)}, f32[8,128]{1,0:T(8,128)}) custom-call(bf16[3,256,1280]{2,1,0:T(8,128)(2,1)} %get-tuple-element.165.refs_0_.refs_2_, bf16[3,256,1280]{2,1,0:T(8,128)(2,1)} %collective-permute-done.27.refs_1_.refs_3_, ...), custom_call_target="tpu_custom_call", output_to_operand_aliasing={{0}: (7, {}), {1}: (18, {})} | custom-call | flops 1 | bytes 1 | tf_op jit(solution)/shard_map/pallas_call | solution.py:66
  207.7 5.4 %collective-permute-done.24.refs_2_ = bf16[2,256,1024]{2,1,0:T(8,128)(2,1)} collective-permute-done((bf16[2,256,1024]{2,1,0:T(8,128)(2,1)}, bf16[2,256,1024]{2,1,0:T(8,128)(2,1)}, u32[]{:S(2)}, u32[]{:S(2)}) %collective-permute-start.24) | collective-permute-done | bytes 1048608 | tf_op jit(solution)/shard_map/ppermute | solution.py:29
  213.1 4.9 %shard_map.115 = (bf16[3,256,1024]{2,1,0:T(8,128)(2,1)}, f32[8,128]{1,0:T(8,128)}) custom-call(f32[2,256,1024]{2,1,0:T(8,128)} %get-tuple-element.152.refs_0_, bf16[2,256,1024]{2,1,0:T(8,128)(2,1)} %collective-permute-done.22.refs_1_, bf16[2,256,1024]{2,1,0:T(8,128)(2,1)} %collective-permute-done.24.refs_2_, f32[256,1536]{1,0:T(8,128)} %get-tuple-element.137.refs_0_.refs_3_, ...), custom_call_target="tpu_custom_call" | custom-call | flops 1 | bytes 1 | tf_op jit(solution)/shard_map/pallas_call | solution.py:66
  221.8 13.9 %shard_map.116 = (f32[512,2048]{1,0:T(8,128)}, f32[512,2048]{1,0:T(8,128)}, f32[8,128]{1,0:T(8,128)}) custom-call(bf16[3,256,1024]{2,1,0:T(8,128)(2,1)} %get-tuple-element.170.refs_0_.refs_2_, bf16[3,256,1024]{2,1,0:T(8,128)(2,1)} %collective-permute-done.28.refs_1_.refs_3_, ...), custom_call_target="tpu_custom_call", output_to_operand_aliasing={{0}: (6, {}), {1}: (15, {})} | custom-call | flops 1 | bytes 1 | tf_op jit(solution)/shard_map/pallas_call | solution.py:66
  235.7 2.9 shard_map.117
  238.8 12.8 %shard_map.118 = (bf16[2048,3328]{1,0:T(8,128)(2,1)}, bf16[2048,3328]{1,0:T(8,128)(2,1)}, bf16[3328,2048]{1,0:T(8,128)(2,1)}, f32[8,128]{1,0:T(8,128)}) custom-call(bf16[2048,512]{1,0:T(8,128)(2,1)} %get-tuple-element.160.refs_0_, bf16[512,2048]{1,0:T(8,128)(2,1)} %bitcast.11, ...), custom_call_target="tpu_custom_call", output_to_operand_aliasing={{0}: (4, {}), {1}: (5, {}), {2}: (6, {})} | custom-call | flops 1 | bytes 1 | tf_op jit(solution)/shard_map/pallas_call | solution.py:66
  251.6 7.6 %shard_map.119 = (f32[4,4,16,2048]{3,2,1,0:T(8,128)}, bf16[4,4,16,2048]{3,2,1,0:T(8,128)(2,1)}, f32[8,128]{1,0:T(8,128)}) custom-call(bf16[3,256,512]{2,1,0:T(8,128)(2,1)} %get-tuple-element.175.refs_0_.refs_2_, bf16[3,256,512]{2,1,0:T(8,128)(2,1)} %collective-permute-done.29.refs_1_.refs_3_, bf16[2048,3328]{1,0:T(8,128)(2,1)} %refs_3_.9, ...), custom_call_target="tpu_custom_call" | custom-call | flops 1 | bytes 1 | tf_op jit(solution)/shard_map/pallas_call | solution.py:66
  260.9 3.9 %shard_map.120 = (f32[4,4,16,1024]{3,2,1,0:T(8,128)}, bf16[4,4,16,1024]{3,2,1,0:T(8,128)(2,1)}, f32[8,128]{1,0:T(8,128)}) custom-call(bf16[3,256,512]{2,1,0:T(8,128)(2,1)} %get-tuple-element.175.refs_0_.refs_2_, bf16[3,256,512]{2,1,0:T(8,128)(2,1)} %collective-permute-done.29.refs_1_.refs_3_, bf16[3328,2048]{1,0:T(8,128)(2,1)} %refs_3_.11, ...), custom_call_target="tpu_custom_call" | custom-call | flops 1 | bytes 1 | tf_op jit(solution)/shard_map/pallas_call | solution.py:66
  265.1 3.8 %shard_map.121 = (f32[4,4,16,1024]{3,2,1,0:T(8,128)}, bf16[4,4,16,1024]{3,2,1,0:T(8,128)(2,1)}, f32[8,128]{1,0:T(8,128)}) custom-call(bf16[3,256,512]{2,1,0:T(8,128)(2,1)} %get-tuple-element.175.refs_0_.refs_2_, bf16[3,256,512]{2,1,0:T(8,128)(2,1)} %collective-permute-done.29.refs_1_.refs_3_, bf16[3328,2048]{1,0:T(8,128)(2,1)} %refs_3_.11, ...), custom_call_target="tpu_custom_call" | custom-call | flops 1 | bytes 1 | tf_op jit(solution)/shard_map/pallas_call | solution.py:66
  269.0 11.0 %shard_map.122 = (bf16[2048,3328]{1,0:T(8,128)(2,1)}, bf16[2048,3328]{1,0:T(8,128)(2,1)}, bf16[3328,2048]{1,0:T(8,128)(2,1)}, f32[8,128]{1,0:T(8,128)}) custom-call(bf16[2048,512]{1,0:T(8,128)(2,1)} %get-tuple-element.160.refs_0_, bf16[512,2048]{1,0:T(8,128)(2,1)} %bitcast.12, ...), custom_call_target="tpu_custom_call", output_to_operand_aliasing={{0}: (4, {}), {1}: (5, {}), {2}: (6, {})} | custom-call | flops 1 | bytes 1 | tf_op jit(solution)/shard_map/pallas_call | solution.py:66
  279.9 5.6 %collective-permute-done.31.refs_1_ = bf16[4,4,16,2048]{3,2,1,0:T(8,128)(2,1)} collective-permute-done((bf16[4,4,16,2048]{3,2,1,0:T(8,128)(2,1)}, bf16[4,4,16,2048]{3,2,1,0:T(8,128)(2,1)}, u32[]{:S(2)}, u32[]{:S(2)}) %collective-permute-start.31) | collective-permute-done | bytes 1048608 | tf_op jit(solution)/shard_map/ppermute | solution.py:33
  285.5 3.1 shard_map.123
  291.9 7.3 %shard_map.124 = (bf16[2048,3328]{1,0:T(8,128)(2,1)}, bf16[2048,3328]{1,0:T(8,128)(2,1)}, bf16[3328,2048]{1,0:T(8,128)(2,1)}, f32[8,128]{1,0:T(8,128)}) custom-call(bf16[2048,512]{1,0:T(8,128)(2,1)} %get-tuple-element.160.refs_0_, bf16[512,2048]{1,0:T(8,128)(2,1)} %bitcast.13, ...), custom_call_target="tpu_custom_call", output_to_operand_aliasing={{0}: (4, {}), {1}: (5, {}), {2}: (6, {})} | custom-call | flops 1 | bytes 1 | tf_op jit(solution)/shard_map/pallas_call | solution.py:66
  304.3 3.2 collective-permute-start.37
  313.3 2.6 collective-permute-start.35
  315.9 3.2 collective-permute-done.37.refs_2_
  324.8 3.9 %collective-permute-start.38 = (bf16[1,4,16,1024]{3,2,1,0:T(8,128)(2,1)}, bf16[1,4,16,1024]{3,2,1,0:T(8,128)(2,1)}, u32[]{:S(2)}, u32[]{:S(2)}) collective-permute-start(bf16[1,4,16,1024]{3,2,1,0:T(8,128)(2,1)} %get-tuple-element.217), channel_id=1, source_target_pairs={{0,16},{4,20},{8,24},{12,28},{16,0},{20,4},{24,8},{28,12},{1,17},{... | collective-permute-start | bytes 393224 | tf_op jit(solution)/shard_map/ppermute | solution.py:33
  330.6 3.2 collective-permute-done.40.refs_3_
  334.7 2.9 shard_map.131
  (92 shorter events, 72.5 us)
Async XLA Ops:
  0.6 9.7 %collective-permute-start = (bf16[64,2048]{1,0:T(8,128)(2,1)}, bf16[64,2048]{1,0:T(8,128)(2,1)}, u32[]{:S(2)}, u32[]{:S(2)}) collective-permute-start(bf16[64,2048]{1,0:T(8,128)(2,1)} %refs_1_.8), channel_id=1, source_target_pairs={{0,4},{4,0},{8,12},{12,8},{16,20},{20,16},{24,28},{28,24},{1,5},{5... | collective-permute-start | bytes 786440 | tf_op jit(solution)/shard_map/ppermute | solution.py:33
  3.7 14.9 %collective-permute-start.9 = (bf16[64,2048]{1,0:T(8,128)(2,1)}, bf16[64,2048]{1,0:T(8,128)(2,1)}, u32[]{:S(2)}, u32[]{:S(2)}) collective-permute-start(bf16[64,2048]{1,0:T(8,128)(2,1)} %refs_1_.8), channel_id=1, source_target_pairs={{0,16},{4,20},{8,24},{12,28},{16,0},{20,4},{24,8},{28,12},{1,17},{... | collective-permute-start | bytes 786440 | tf_op jit(solution)/shard_map/ppermute | solution.py:33
  13.2 9.4 %all-to-all-start = ((bf16[4,16,2048]{2,1,0:T(8,128)(2,1)}), bf16[4,16,2048]{2,1,0:T(8,128)(2,1)S(1)}, u32[]{:S(2)}, u32[]{:S(2)}) async-start(bf16[4,16,2048]{2,1,0:T(8,128)(2,1)} %get-tuple-element.117), calls=%async_computation | async-start | bytes 524288 | tf_op jit(solution)/shard_map/all_to_all | solution.py:474
  16.7 9.4 %collective-permute-start.8 = (bf16[64,2048]{1,0:T(8,128)(2,1)}, bf16[64,2048]{1,0:T(8,128)(2,1)S(1)}, u32[]{:S(2)}, u32[]{:S(2)}) collective-permute-start(bf16[64,2048]{1,0:T(8,128)(2,1)} %refs_1_.8), channel_id=1, source_target_pairs={{0,8},{4,12},{8,0},{12,4},{16,24},{20,28},{24,16},{28,20},{1,9},{5... | collective-permute-start | bytes 786440 | tf_op jit(solution)/shard_map/ppermute | solution.py:33
  18.5 12.7 %collective-permute-start.10 = (bf16[64,2048]{1,0:T(8,128)(2,1)}, bf16[64,2048]{1,0:T(8,128)(2,1)S(1)}, u32[]{:S(2)}, u32[]{:S(2)}) collective-permute-start(bf16[64,2048]{1,0:T(8,128)(2,1)} %collective-permute-done.9.refs_1_.refs_5_), channel_id=1, source_target_pairs={{0,8},{4,12},{8,0},{12,4},{16,24},{20,28},{24,16},{28,20},{1,9},{5... | collective-permute-start | bytes 786440 | tf_op jit(solution)/shard_map/ppermute | solution.py:33
  22.7 0.7 copy-start
  23.4 7.9 %collective-permute-start.1 = (bf16[64,2048]{1,0:T(8,128)(2,1)S(1)}, bf16[64,2048]{1,0:T(8,128)(2,1)S(1)}, u32[]{:S(2)}, u32[]{:S(2)}) collective-permute-start(bf16[64,2048]{1,0:T(8,128)(2,1)S(1)} %bitcast.18), channel_id=1, source_target_pairs={{0,4},{4,0},{8,12},{12,8},{16,20},{20,16},{24,28},{28,24},{1,5},{5... | collective-permute-start | bytes 786440 | tf_op jit(solution)/shard_map/ppermute | solution.py:33
  26.0 5.2 %copy-start.2 = (bf16[64,2048]{1,0:T(8,128)(2,1)}, bf16[64,2048]{1,0:T(8,128)(2,1)S(1)}, u32[]{:S(2)}) copy-start(bf16[64,2048]{1,0:T(8,128)(2,1)S(1)} %collective-permute-done.8.refs_0_.refs_3_) | copy-start | bytes 786436
  31.2 0.7 copy-start.3
  31.9 0.7 copy-start.1
  34.7 24.7 %collective-permute-start.11 = (bf16[3,64,2048]{2,1,0:T(8,128)(2,1)}, bf16[3,64,2048]{2,1,0:T(8,128)(2,1)}, u32[]{:S(2)}, u32[]{:S(2)}) collective-permute-start(bf16[3,64,2048]{2,1,0:T(8,128)(2,1)} %get-tuple-element.119), channel_id=1, source_target_pairs={{0,4},{4,0},{8,12},{12,8},{16,20},{20,16},{24,28},{28,24},{1,5},{5... | collective-permute-start | bytes 2359304 | tf_op jit(solution)/shard_map/ppermute | solution.py:33
  36.4 14.5 %collective-permute-start.4 = (bf16[64,2048]{1,0:T(8,128)(2,1)}, bf16[64,2048]{1,0:T(8,128)(2,1)}, u32[]{:S(2)}, u32[]{:S(2)}) collective-permute-start(bf16[64,2048]{1,0:T(8,128)(2,1)} %bitcast.20), channel_id=1, source_target_pairs={{0,16},{4,20},{8,24},{12,28},{16,0},{20,4},{24,8},{28,12},{1,17},{... | collective-permute-start | bytes 786440 | tf_op jit(solution)/shard_map/ppermute | solution.py:33
  39.0 13.0 %collective-permute-start.2 = (bf16[64,2048]{1,0:T(8,128)(2,1)}, bf16[64,2048]{1,0:T(8,128)(2,1)}, u32[]{:S(2)}, u32[]{:S(2)}) collective-permute-start(bf16[64,2048]{1,0:T(8,128)(2,1)} %bitcast.21), channel_id=1, source_target_pairs={{0,8},{4,12},{8,0},{12,4},{16,24},{20,28},{24,16},{28,20},{1,9},{5... | collective-permute-start | bytes 786440 | tf_op jit(solution)/shard_map/ppermute | solution.py:33
  50.9 7.4 %collective-permute-start.6 = (bf16[64,2048]{1,0:T(8,128)(2,1)}, bf16[64,2048]{1,0:T(8,128)(2,1)}, u32[]{:S(2)}, u32[]{:S(2)}) collective-permute-start(bf16[64,2048]{1,0:T(8,128)(2,1)} %collective-permute-done.4.refs_10_.refs_5_), channel_id=1, source_target_pairs={{0,8},{4,12},{8,0},{12,4},{16,24},{20,28},{24,16},{28,20},{1,9},{5... | collective-permute-start | bytes 786440 | tf_op jit(solution)/shard_map/ppermute | solution.py:33
  51.4 16.5 %collective-permute-start.5 = (bf16[64,2048]{1,0:T(8,128)(2,1)}, bf16[64,2048]{1,0:T(8,128)(2,1)}, u32[]{:S(2)}, u32[]{:S(2)}) collective-permute-start(bf16[64,2048]{1,0:T(8,128)(2,1)} %collective-permute-done.4.refs_10_.refs_5_), channel_id=1, source_target_pairs={{0,4},{4,0},{8,12},{12,8},{16,20},{20,16},{24,28},{28,24},{1,5},{5... | collective-permute-start | bytes 786440 | tf_op jit(solution)/shard_map/ppermute | solution.py:33
  52.0 16.0 %collective-permute-start.3 = (bf16[64,2048]{1,0:T(8,128)(2,1)}, bf16[64,2048]{1,0:T(8,128)(2,1)}, u32[]{:S(2)}, u32[]{:S(2)}) collective-permute-start(bf16[64,2048]{1,0:T(8,128)(2,1)} %collective-permute-done.2.refs_9_.refs_3_), channel_id=1, source_target_pairs={{0,4},{4,0},{8,12},{12,8},{16,20},{20,16},{24,28},{28,24},{1,5},{5... | collective-permute-start | bytes 786440 | tf_op jit(solution)/shard_map/ppermute | solution.py:33
  58.3 12.7 %collective-permute-start.7 = (bf16[64,2048]{1,0:T(8,128)(2,1)}, bf16[64,2048]{1,0:T(8,128)(2,1)}, u32[]{:S(2)}, u32[]{:S(2)}) collective-permute-start(bf16[64,2048]{1,0:T(8,128)(2,1)} %collective-permute-done.6.refs_11_.refs_7_), channel_id=1, source_target_pairs={{0,4},{4,0},{8,12},{12,8},{16,20},{20,16},{24,28},{28,24},{1,5},{5... | collective-permute-start | bytes 786440 | tf_op jit(solution)/shard_map/ppermute | solution.py:33
  78.4 14.4 %collective-permute-start.12 = (bf16[256,1280]{1,0:T(8,128)(2,1)}, bf16[256,1280]{1,0:T(8,128)(2,1)}, u32[]{:S(2)}, u32[]{:S(2)}) collective-permute-start(bf16[256,1280]{1,0:T(8,128)(2,1)} %get-tuple-element.125), channel_id=1, source_target_pairs={{0,1},{1,0},{2,3},{3,2},{4,5},{5,4},{6,7},{7,6},{8,9},{9,8},{10,11... | collective-permute-start | bytes 1966088 | tf_op jit(solution)/shard_map/ppermute | solution.py:29
  78.4 2.8 collective-permute-start.13
  83.0 17.8 %collective-permute-start.15 = (bf16[256,512]{1,0:T(8,128)(2,1)}, bf16[256,512]{1,0:T(8,128)(2,1)}, u32[]{:S(2)}, u32[]{:S(2)}) collective-permute-start(bf16[256,512]{1,0:T(8,128)(2,1)} %get-tuple-element.134), channel_id=1, source_target_pairs={{0,2},{1,3},{2,0},{3,1},{4,6},{5,7},{6,4},{7,5},{8,10},{9,11},{10,... | collective-permute-start | bytes 786440 | tf_op jit(solution)/shard_map/ppermute | solution.py:29
  92.8 14.2 %collective-permute-start.17 = (bf16[256,1536]{1,0:T(8,128)(2,1)}, bf16[256,1536]{1,0:T(8,128)(2,1)}, u32[]{:S(2)}, u32[]{:S(2)}) collective-permute-start(bf16[256,1536]{1,0:T(8,128)(2,1)} %get-tuple-element.138), channel_id=1, source_target_pairs={{0,1},{1,0},{2,3},{3,2},{4,5},{5,4},{6,7},{7,6},{8,9},{9,8},{10,11... | collective-permute-start | bytes 2359304 | tf_op jit(solution)/shard_map/ppermute | solution.py:29
  95.1 17.4 %collective-permute-start.14 = (bf16[256,1280]{1,0:T(8,128)(2,1)}, bf16[256,1280]{1,0:T(8,128)(2,1)}, u32[]{:S(2)}, u32[]{:S(2)}) collective-permute-start(bf16[256,1280]{1,0:T(8,128)(2,1)} %get-tuple-element.133), channel_id=1, source_target_pairs={{0,2},{1,3},{2,0},{3,1},{4,6},{5,7},{6,4},{7,5},{8,10},{9,11},{10,... | collective-permute-start | bytes 1966088 | tf_op jit(solution)/shard_map/ppermute | solution.py:29
  106.8 4.0 %collective-permute-start.16 = (bf16[2,256,512]{2,1,0:T(8,128)(2,1)}, bf16[2,256,512]{2,1,0:T(8,128)(2,1)}, u32[]{:S(2)}, u32[]{:S(2)}) collective-permute-start(bf16[2,256,512]{2,1,0:T(8,128)(2,1)} %get-tuple-element.136), channel_id=1, source_target_pairs={{0,1},{1,0},{2,3},{3,2},{4,5},{5,4},{6,7},{7,6},{8,9},{9,8},{10,11... | collective-permute-start | bytes 1572872 | tf_op jit(solution)/shard_map/ppermute | solution.py:29
  109.5 20.1 %collective-permute-start.19 = (bf16[256,1536]{1,0:T(8,128)(2,1)}, bf16[256,1536]{1,0:T(8,128)(2,1)}, u32[]{:S(2)}, u32[]{:S(2)}) collective-permute-start(bf16[256,1536]{1,0:T(8,128)(2,1)} %get-tuple-element.143), channel_id=1, source_target_pairs={{0,2},{1,3},{2,0},{3,1},{4,6},{5,7},{6,4},{7,5},{8,10},{9,11},{10,... | collective-permute-start | bytes 2359304 | tf_op jit(solution)/shard_map/ppermute | solution.py:29
  122.9 16.8 %collective-permute-start.18 = (bf16[2,256,1280]{2,1,0:T(8,128)(2,1)}, bf16[2,256,1280]{2,1,0:T(8,128)(2,1)}, u32[]{:S(2)}, u32[]{:S(2)}) collective-permute-start(bf16[2,256,1280]{2,1,0:T(8,128)(2,1)} %get-tuple-element.142), channel_id=1, source_target_pairs={{0,1},{1,0},{2,3},{3,2},{4,5},{5,4},{6,7},{7,6},{8,9},{9,8},{10,11... | collective-permute-start | bytes 3932168 | tf_op jit(solution)/shard_map/ppermute | solution.py:29
  138.3 11.0 %collective-permute-start.22 = (bf16[2,256,1024]{2,1,0:T(8,128)(2,1)}, bf16[2,256,1024]{2,1,0:T(8,128)(2,1)}, u32[]{:S(2)}, u32[]{:S(2)}) collective-permute-start(bf16[2,256,1024]{2,1,0:T(8,128)(2,1)} %get-tuple-element.153), channel_id=1, source_target_pairs={{0,1},{1,0},{2,3},{3,2},{4,5},{5,4},{6,7},{7,6},{8,9},{9,8},{10,11... | collective-permute-start | bytes 3145736 | tf_op jit(solution)/shard_map/ppermute | solution.py:29
  138.3 15.1 %collective-permute-start.21 = (bf16[2,256,512]{2,1,0:T(8,128)(2,1)}, bf16[2,256,512]{2,1,0:T(8,128)(2,1)}, u32[]{:S(2)}, u32[]{:S(2)}) collective-permute-start(bf16[2,256,512]{2,1,0:T(8,128)(2,1)} %get-tuple-element.151), channel_id=1, source_target_pairs={{0,2},{1,3},{2,0},{3,1},{4,6},{5,7},{6,4},{7,5},{8,10},{9,11},{10,... | collective-permute-start | bytes 1572872 | tf_op jit(solution)/shard_map/ppermute | solution.py:29
  148.5 5.0 %collective-permute-start.20 = (bf16[2,256,512]{2,1,0:T(8,128)(2,1)}, bf16[2,256,512]{2,1,0:T(8,128)(2,1)}, u32[]{:S(2)}, u32[]{:S(2)}) collective-permute-start(bf16[2,256,512]{2,1,0:T(8,128)(2,1)} %get-tuple-element.150), channel_id=1, source_target_pairs={{0,1},{1,0},{2,3},{3,2},{4,5},{5,4},{6,7},{7,6},{8,9},{9,8},{10,11... | collective-permute-start | bytes 1572872 | tf_op jit(solution)/shard_map/ppermute | solution.py:29
  148.6 32.4 %collective-permute-start.25 = (bf16[2,256,1280]{2,1,0:T(8,128)(2,1)}, bf16[2,256,1280]{2,1,0:T(8,128)(2,1)}, u32[]{:S(2)}, u32[]{:S(2)}) collective-permute-start(bf16[2,256,1280]{2,1,0:T(8,128)(2,1)} %get-tuple-element.159), channel_id=1, source_target_pairs={{0,2},{1,3},{2,0},{3,1},{4,6},{5,7},{6,4},{7,5},{8,10},{9,11},{10,... | collective-permute-start | bytes 3932168 | tf_op jit(solution)/shard_map/ppermute | solution.py:29
  156.3 2.6 collective-permute-start.26
  187.2 4.3 %collective-permute-start.27 = (bf16[3,256,1280]{2,1,0:T(8,128)(2,1)}, bf16[3,256,1280]{2,1,0:T(8,128)(2,1)}, u32[]{:S(2)}, u32[]{:S(2)}) collective-permute-start(bf16[3,256,1280]{2,1,0:T(8,128)(2,1)} %get-tuple-element.165.refs_0_.refs_2_), channel_id=1, source_target_pairs={{0,1},{1,0},{2,3},{3,2},{4,5},{5,4},{6,7},{7,6},{8,9},{9,8},{10,11... | collective-permute-start | bytes 5898248 | tf_op jit(solution)/shard_map/ppermute | solution.py:29
  187.2 25.9 %collective-permute-start.24 = (bf16[2,256,1024]{2,1,0:T(8,128)(2,1)}, bf16[2,256,1024]{2,1,0:T(8,128)(2,1)}, u32[]{:S(2)}, u32[]{:S(2)}) collective-permute-start(bf16[2,256,1024]{2,1,0:T(8,128)(2,1)} %get-tuple-element.158), channel_id=1, source_target_pairs={{0,2},{1,3},{2,0},{3,1},{4,6},{5,7},{6,4},{7,5},{8,10},{9,11},{10,... | collective-permute-start | bytes 3145736 | tf_op jit(solution)/shard_map/ppermute | solution.py:29
  218.0 3.8 %collective-permute-start.28 = (bf16[3,256,1024]{2,1,0:T(8,128)(2,1)}, bf16[3,256,1024]{2,1,0:T(8,128)(2,1)}, u32[]{:S(2)}, u32[]{:S(2)}) collective-permute-start(bf16[3,256,1024]{2,1,0:T(8,128)(2,1)} %get-tuple-element.170.refs_0_.refs_2_), channel_id=1, source_target_pairs={{0,1},{1,0},{2,3},{3,2},{4,5},{5,4},{6,7},{7,6},{8,9},{9,8},{10,11... | collective-permute-start | bytes 4718600 | tf_op jit(solution)/shard_map/ppermute | solution.py:29
  218.0 17.7 %collective-permute-start.23 = (bf16[2,256,512]{2,1,0:T(8,128)(2,1)}, bf16[2,256,512]{2,1,0:T(8,128)(2,1)}, u32[]{:S(2)}, u32[]{:S(2)}) collective-permute-start(bf16[2,256,512]{2,1,0:T(8,128)(2,1)} %get-tuple-element.157), channel_id=1, source_target_pairs={{0,2},{1,3},{2,0},{3,1},{4,6},{5,7},{6,4},{7,5},{8,10},{9,11},{10,... | collective-permute-start | bytes 1572872 | tf_op jit(solution)/shard_map/ppermute | solution.py:29
  238.6 12.9 %collective-permute-start.29 = (bf16[3,256,512]{2,1,0:T(8,128)(2,1)}, bf16[3,256,512]{2,1,0:T(8,128)(2,1)}, u32[]{:S(2)}, u32[]{:S(2)}) collective-permute-start(bf16[3,256,512]{2,1,0:T(8,128)(2,1)} %get-tuple-element.175.refs_0_.refs_2_), channel_id=1, source_target_pairs={{0,1},{1,0},{2,3},{3,2},{4,5},{5,4},{6,7},{7,6},{8,9},{9,8},{10,11... | collective-permute-start | bytes 2359304 | tf_op jit(solution)/shard_map/ppermute | solution.py:29
  259.2 26.3 %collective-permute-start.31 = (bf16[4,4,16,2048]{3,2,1,0:T(8,128)(2,1)}, bf16[4,4,16,2048]{3,2,1,0:T(8,128)(2,1)}, u32[]{:S(2)}, u32[]{:S(2)}) collective-permute-start(bf16[4,4,16,2048]{3,2,1,0:T(8,128)(2,1)} %get-tuple-element.195), channel_id=1, source_target_pairs={{0,4},{4,0},{8,12},{12,8},{16,20},{20,16},{24,28},{28,24},{1,5},{5... | collective-permute-start | bytes 3145736 | tf_op jit(solution)/shard_map/ppermute | solution.py:33
  264.8 34.4 %collective-permute-start.30 = (bf16[4,4,16,1024]{3,2,1,0:T(8,128)(2,1)}, bf16[4,4,16,1024]{3,2,1,0:T(8,128)(2,1)}, u32[]{:S(2)}, u32[]{:S(2)}) collective-permute-start(bf16[4,4,16,1024]{3,2,1,0:T(8,128)(2,1)} %get-tuple-element.185), channel_id=1, source_target_pairs={{0,4},{4,0},{8,12},{12,8},{16,20},{20,16},{24,28},{28,24},{1,5},{5... | collective-permute-start | bytes 1572872 | tf_op jit(solution)/shard_map/ppermute | solution.py:33
  288.6 13.3 %collective-permute-start.34 = (bf16[2,4,16,2048]{3,2,1,0:T(8,128)(2,1)}, bf16[2,4,16,2048]{3,2,1,0:T(8,128)(2,1)}, u32[]{:S(2)}, u32[]{:S(2)}) collective-permute-start(bf16[2,4,16,2048]{3,2,1,0:T(8,128)(2,1)} %get-tuple-element.204), channel_id=1, source_target_pairs={{0,8},{4,12},{8,0},{12,4},{16,24},{20,28},{24,16},{28,20},{1,9},{5... | collective-permute-start | bytes 1572872 | tf_op jit(solution)/shard_map/ppermute | solution.py:33
  290.4 17.1 %collective-permute-start.33 = (bf16[4,4,16,1024]{3,2,1,0:T(8,128)(2,1)}, bf16[4,4,16,1024]{3,2,1,0:T(8,128)(2,1)}, u32[]{:S(2)}, u32[]{:S(2)}) collective-permute-start(bf16[4,4,16,1024]{3,2,1,0:T(8,128)(2,1)} %get-tuple-element.202), channel_id=1, source_target_pairs={{0,4},{4,0},{8,12},{12,8},{16,20},{20,16},{24,28},{28,24},{1,5},{5... | collective-permute-start | bytes 1572872 | tf_op jit(solution)/shard_map/ppermute | solution.py:33
  301.5 10.0 %collective-permute-start.32 = (bf16[2,4,16,1024]{3,2,1,0:T(8,128)(2,1)}, bf16[2,4,16,1024]{3,2,1,0:T(8,128)(2,1)}, u32[]{:S(2)}, u32[]{:S(2)}) collective-permute-start(bf16[2,4,16,1024]{3,2,1,0:T(8,128)(2,1)} %get-tuple-element.200), channel_id=1, source_target_pairs={{0,8},{4,12},{8,0},{12,4},{16,24},{20,28},{24,16},{28,20},{1,9},{5... | collective-permute-start | bytes 786440 | tf_op jit(solution)/shard_map/ppermute | solution.py:33
  304.3 14.8 %collective-permute-start.37 = (bf16[1,4,16,2048]{3,2,1,0:T(8,128)(2,1)}, bf16[1,4,16,2048]{3,2,1,0:T(8,128)(2,1)}, u32[]{:S(2)}, u32[]{:S(2)}) collective-permute-start(bf16[1,4,16,2048]{3,2,1,0:T(8,128)(2,1)} %get-tuple-element.213), channel_id=1, source_target_pairs={{0,16},{4,20},{8,24},{12,28},{16,0},{20,4},{24,8},{28,12},{1,17},{... | collective-permute-start | bytes 786440 | tf_op jit(solution)/shard_map/ppermute | solution.py:33
  309.7 13.2 %collective-permute-start.36 = (bf16[2,4,16,1024]{3,2,1,0:T(8,128)(2,1)}, bf16[2,4,16,1024]{3,2,1,0:T(8,128)(2,1)}, u32[]{:S(2)}, u32[]{:S(2)}) collective-permute-start(bf16[2,4,16,1024]{3,2,1,0:T(8,128)(2,1)} %get-tuple-element.211), channel_id=1, source_target_pairs={{0,8},{4,12},{8,0},{12,4},{16,24},{20,28},{24,16},{28,20},{1,9},{5... | collective-permute-start | bytes 786440 | tf_op jit(solution)/shard_map/ppermute | solution.py:33
  313.3 24.3 %collective-permute-start.35 = (bf16[1,4,16,1024]{3,2,1,0:T(8,128)(2,1)}, bf16[1,4,16,1024]{3,2,1,0:T(8,128)(2,1)S(1)}, u32[]{:S(2)}, u32[]{:S(2)}) collective-permute-start(bf16[1,4,16,1024]{3,2,1,0:T(8,128)(2,1)} %get-tuple-element.209), channel_id=1, source_target_pairs={{0,16},{4,20},{8,24},{12,28},{16,0},{20,4},{24,8},{28,12},{1,17},{... | collective-permute-start | bytes 393224 | tf_op jit(solution)/shard_map/ppermute | solution.py:33
  324.8 12.8 %collective-permute-start.38 = (bf16[1,4,16,1024]{3,2,1,0:T(8,128)(2,1)}, bf16[1,4,16,1024]{3,2,1,0:T(8,128)(2,1)}, u32[]{:S(2)}, u32[]{:S(2)}) collective-permute-start(bf16[1,4,16,1024]{3,2,1,0:T(8,128)(2,1)} %get-tuple-element.217), channel_id=1, source_target_pairs={{0,16},{4,20},{8,24},{12,28},{16,0},{20,4},{24,8},{28,12},{1,17},{... | collective-permute-start | bytes 393224 | tf_op jit(solution)/shard_map/ppermute | solution.py:33
  328.7 1.9 collective-permute-start.39
  328.7 5.0 %collective-permute-start.40 = (bf16[16,2048]{1,0:T(8,128)(2,1)}, bf16[16,2048]{1,0:T(8,128)(2,1)}, u32[]{:S(2)}, u32[]{:S(2)}) collective-permute-start(bf16[16,2048]{1,0:T(8,128)(2,1)} %get-tuple-element.220), channel_id=1, source_target_pairs={{0,2},{1,3},{2,0},{3,1},{4,6},{5,7},{6,4},{7,5},{8,10},{9,11},{10,... | collective-permute-start | bytes 196616 | tf_op jit(solution)/shard_map/ppermute | solution.py:29
  330.1 4.6 %collective-permute-start.41 = (bf16[16,2048]{1,0:T(8,128)(2,1)}, bf16[16,2048]{1,0:T(8,128)(2,1)}, u32[]{:S(2)}, u32[]{:S(2)}) collective-permute-start(bf16[16,2048]{1,0:T(8,128)(2,1)} %get-tuple-element.221), channel_id=1, source_target_pairs={{0,3},{1,2},{2,1},{3,0},{4,7},{5,6},{6,5},{7,4},{8,11},{9,10},{10,... | collective-permute-start | bytes 196616 | tf_op jit(solution)/shard_map/ppermute | solution.py:29
  330.6 4.1 %copy-start.5 = (bf16[16,2048]{1,0:T(8,128)(2,1)}, bf16[16,2048]{1,0:T(8,128)(2,1)S(1)}, u32[]{:S(2)}) copy-start(bf16[16,2048]{1,0:T(8,128)(2,1)S(1)} %collective-permute-done.39.refs_2_) | copy-start | bytes 196612
  (1 other events, 0.7 us)

commit v8 on v7

--- a/solution.py
+++ b/solution.py
@@ -516,16 +516,16 @@
     elementwise(2)
     add_both(2)
     elementwise(3)
-    all_grads(1)
     grad_part = last_part(grad_term())
     out_parts = [last_part(out_term(), 2, 0), last_part(out_term(), 2, 1)]
+    all_grads(1)
+    grad_part = over_z(grad_part, 2)
     all_grads(2)
-    grad_part = over_z(grad_part, 2)
-    all_grads(3)
     out_parts[0] = over_z(out_parts[0], 2)
     grad_part = over_z(grad_part, 4)
     out_parts[1] = over_z(out_parts[1], 2)
     out_parts[0] = over_z(out_parts[0], 4)
+    all_grads(3)
     groups = finish(chain, place, [grad_part], False)
     groups = [groups[0]] + [swap(groups[g], g) for g in range(1, 4)]
     out_parts[1] = over_z(out_parts[1], 4)

time: 343 us -> 338 us (0.985)
  starting transfers between devices: 50.4 us -> 46 us
    ppermute x21, starting transfers between devices: 35.7 us -> 31.4 us  [swap_wide(): return lax.ppermute(value, 'wide', [(i, i ^ mask) for i in range(8)])]
where the time goes in v8:
time: 338 us; the launch traced here: 336 us
  Pallas kernels  213 us (63%)
  waiting for transfers between devices  73.2 us (22%)
  starting transfers between devices  46 us (14%)
    pallas_call x41, Pallas kernels, __call__(): pl.pallas_call(kernel, grid_spec=pltpu.PrefetchScalarGridSpec(num_scalar_...  213 us
    ppermute x21, waiting for transfers between devices, swap_wide(): return lax.ppermute(value, 'wide', [(i, i ^ mask) for i in range(8)])  36 us
    ppermute x21, waiting for transfers between devices, swap(): return lax.ppermute(value, 'narrow', [(i, i ^ mask) for i in range(4)])  33.5 us
    ppermute x21, starting transfers between devices, swap_wide(): return lax.ppermute(value, 'wide', [(i, i ^ mask) for i in range(8)])  31.4 us
    ppermute x21, starting transfers between devices, swap(): return lax.ppermute(value, 'narrow', [(i, i ^ mask) for i in range(4)])  11.3 us
  transfers between devices with their start and end apart: 43, of which 21 were waited for; matrix products, arithmetic and copies ran while one was open for 0% of the time, Pallas kernels for 53%

profile of v8, /device:TPU:0, one launch (start us, length us, event | category | flops | bytes accessed | tf_op | source)
XLA Modules:
  0.0 336.3 jit_solution(14624794030084862656)
XLA Ops:
  0.6 3.0 collective-permute-start
  3.7 2.6 collective-permute-start.9
  6.3 4.0 %collective-permute-done.refs_1_.refs_2_ = bf16[64,2048]{1,0:T(8,128)(2,1)} collective-permute-done((bf16[64,2048]{1,0:T(8,128)(2,1)}, bf16[64,2048]{1,0:T(8,128)(2,1)}, u32[]{:S(2)}, u32[]{:S(2)}) %collective-permute-start) | collective-permute-done | bytes 262176 | tf_op jit(solution)/shard_map/ppermute | solution.py:33
  10.3 3.0 shard_map.92
  13.2 3.4 %all-to-all-start = ((bf16[4,16,2048]{2,1,0:T(8,128)(2,1)}), bf16[4,16,2048]{2,1,0:T(8,128)(2,1)S(1)}, u32[]{:S(2)}, u32[]{:S(2)}) async-start(bf16[4,16,2048]{2,1,0:T(8,128)(2,1)} %get-tuple-element.117), calls=%async_computation | async-start | bytes 524288 | tf_op jit(solution)/shard_map/all_to_all | solution.py:474
  18.9 3.7 %all-to-all-done = bf16[4,16,2048]{2,1,0:T(8,128)(2,1)S(1)} async-done(((bf16[4,16,2048]{2,1,0:T(8,128)(2,1)}), bf16[4,16,2048]{2,1,0:T(8,128)(2,1)S(1)}, u32[]{:S(2)}, u32[]{:S(2)}) %all-to-all-start) | async-done | bytes 262176 | tf_op jit(solution)/shard_map/all_to_all | solution.py:474
  26.0 5.2 %collective-permute-done.10.refs_2_.refs_7_ = bf16[64,2048]{1,0:T(8,128)(2,1)S(1)} collective-permute-done((bf16[64,2048]{1,0:T(8,128)(2,1)}, bf16[64,2048]{1,0:T(8,128)(2,1)S(1)}, u32[]{:S(2)}, u32[]{:S(2)}) %collective-permute-start.10) | collective-permute-done | bytes 262176 | tf_op jit(solution)/shard_map/ppermute | solution.py:33
  36.4 2.6 collective-permute-start.4
  40.5 10.3 %collective-permute-done.4.refs_10_.refs_5_ = bf16[64,2048]{1,0:T(8,128)(2,1)} collective-permute-done((bf16[64,2048]{1,0:T(8,128)(2,1)}, bf16[64,2048]{1,0:T(8,128)(2,1)}, u32[]{:S(2)}, u32[]{:S(2)}) %collective-permute-start.4) | collective-permute-done | bytes 262176 | tf_op jit(solution)/shard_map/ppermute | solution.py:33
  53.5 4.8 %collective-permute-done.6.refs_11_.refs_7_ = bf16[64,2048]{1,0:T(8,128)(2,1)} collective-permute-done((bf16[64,2048]{1,0:T(8,128)(2,1)}, bf16[64,2048]{1,0:T(8,128)(2,1)}, u32[]{:S(2)}, u32[]{:S(2)}) %collective-permute-start.6) | collective-permute-done | bytes 262176 | tf_op jit(solution)/shard_map/ppermute | solution.py:33
  59.4 4.5 %shard_map.94 = (bf16[4,8,16,2048]{3,2,1,0:T(8,128)(2,1)}, f32[8,128]{1,0:T(8,128)}) custom-call(s32[2]{0:T(128)} %pad_add_fusion.refs_0_, bf16[64,2048]{1,0:T(8,128)(2,1)} %refs_1_.8, bf16[64,2048]{1,0:T(8,128)(2,1)} %collective-permute-done.refs_1_.refs_2_, bf16[64,2048]{1,0:T(8,128)(2,1)} %copy-done.2, bf16[192,2048]{1,0:T(8,128)(2,1)} %bitcast.3.refs_4_.refs_6_.refs_8_, ...), custom_call_target="tpu_custom_call" | custom-call | flops 1 | bytes 1 | tf_op jit(solution)/shard_map/pallas_call | solution.py:66
  63.9 4.1 %shard_map.95 = (f32[256,512]{1,0:T(8,128)}, bf16[256,512]{1,0:T(8,128)(2,1)}, f32[8,128]{1,0:T(8,128)}) custom-call(bf16[512,2048]{1,0:T(8,128)(2,1)} %bitcast.7, bf16[3328,2048]{1,0:T(8,128)(2,1)} %refs_3_.11, f32[8,128]{1,0:T(8,128)} %get-tuple-element.122.refs_2_), custom_call_target="tpu_custom_call" | custom-call | flops 1 | bytes 1 | tf_op jit(solution)/shard_map/pallas_call | solution.py:66
  68.0 3.0 collective-permute-done.7.refs_4_.refs_8_
  70.9 7.5 %shard_map.96 = (f32[256,1280]{1,0:T(8,128)}, bf16[256,1280]{1,0:T(8,128)(2,1)}, f32[8,128]{1,0:T(8,128)}) custom-call(bf16[512,2048]{1,0:T(8,128)(2,1)} %bitcast.8, bf16[3328,2048]{1,0:T(8,128)(2,1)} %refs_3_.11, bf16[64,2048]{1,0:T(8,128)(2,1)} %collective-permute-done.3.refs_2_.refs_4_, bf16[64,2048]{1,0:T(8,128)(2,1)} %collective-permute-done.5.refs_3_.refs_6_, ...), custom_call_target="tpu_custom_call" | custom-call | flops 1 | bytes 1 | tf_op jit(solution)/shard_map/pallas_call | solution.py:66
  84.4 8.4 %shard_map.98 = (f32[256,1536]{1,0:T(8,128)}, bf16[256,1536]{1,0:T(8,128)(2,1)}, f32[8,128]{1,0:T(8,128)}) custom-call(bf16[512,2048]{1,0:T(8,128)(2,1)} %bitcast.9, bf16[3328,2048]{1,0:T(8,128)(2,1)} %refs_3_.11, f32[8,128]{1,0:T(8,128)} %get-tuple-element.129.refs_2_), custom_call_target="tpu_custom_call" | custom-call | flops 1 | bytes 1 | tf_op jit(solution)/shard_map/pallas_call | solution.py:66
  95.7 5.1 %shard_map.100 = (bf16[4,8,16,2048]{3,2,1,0:T(8,128)(2,1)}, bf16[2048,512]{1,0:T(8,128)(2,1)}, f32[8,128]{1,0:T(8,128)}) custom-call(s32[2]{0:T(128)} %pad_add_fusion.refs_0_, bf16[64,2048]{1,0:T(8,128)(2,1)} %bitcast.22, bf16[64,2048]{1,0:T(8,128)(2,1)} %copy-done.1, bf16[64,2048]{1,0:T(8,128)(2,1)} %collective-permute-done.2.refs_9_.refs_3_, ...), custom_call_target="tpu_custom_call" | custom-call | flops 1 | bytes 1 | tf_op jit(solution)/shard_map/pallas_call | solution.py:66
  100.9 6.0 %shard_map.101 = (f32[2,256,512]{2,1,0:T(8,128)}, bf16[2,256,512]{2,1,0:T(8,128)(2,1)}, f32[8,128]{1,0:T(8,128)}) custom-call(bf16[512,2048]{1,0:T(8,128)(2,1)} %bitcast.14, bf16[2048,3328]{1,0:T(8,128)(2,1)} %refs_3_.9, bf16[2048,3328]{1,0:T(8,128)(2,1)} %refs_5_.7, bf16[256,512]{1,0:T(8,128)(2,1)} %collective-permute-done.15.refs_3_.refs_5_, ...), custom_call_target="tpu_custom_call" | custom-call | flops 1 | bytes 1 | tf_op jit(solution)/shard_map/pallas_call | solution.py:66
  112.5 10.4 %shard_map.103 = (f32[2,256,1280]{2,1,0:T(8,128)}, bf16[2,256,1280]{2,1,0:T(8,128)(2,1)}, f32[8,128]{1,0:T(8,128)}) custom-call(bf16[512,2048]{1,0:T(8,128)(2,1)} %bitcast.15, bf16[2048,3328]{1,0:T(8,128)(2,1)} %refs_3_.9, bf16[2048,3328]{1,0:T(8,128)(2,1)} %refs_5_.7, bf16[256,1280]{1,0:T(8,128)(2,1)} %collective-permute-done.14.refs_3_.refs_5_, ...), custom_call_target="tpu_custom_call" | custom-call | flops 1 | bytes 1 | tf_op jit(solution)/shard_map/pallas_call | solution.py:66
  125.1 4.4 %collective-permute-done.19.refs_3_.refs_5_ = bf16[256,1536]{1,0:T(8,128)(2,1)} collective-permute-done((bf16[256,1536]{1,0:T(8,128)(2,1)}, bf16[256,1536]{1,0:T(8,128)(2,1)}, u32[]{:S(2)}, u32[]{:S(2)}) %collective-permute-start.19) | collective-permute-done | bytes 786464 | tf_op jit(solution)/shard_map/ppermute | solution.py:29
  129.5 8.8 %shard_map.105 = (f32[2,256,1024]{2,1,0:T(8,128)}, bf16[2,256,1024]{2,1,0:T(8,128)(2,1)}, f32[8,128]{1,0:T(8,128)}) custom-call(bf16[512,2048]{1,0:T(8,128)(2,1)} %bitcast.16, bf16[2048,3328]{1,0:T(8,128)(2,1)} %refs_3_.9, bf16[2048,3328]{1,0:T(8,128)(2,1)} %refs_5_.7, bf16[256,1536]{1,0:T(8,128)(2,1)} %collective-permute-done.19.refs_3_.refs_5_, ...), custom_call_target="tpu_custom_call" | custom-call | flops 1 | bytes 1 | tf_op jit(solution)/shard_map/pallas_call | solution.py:66
  139.8 3.1 shard_map.106
  142.8 5.6 %shard_map.107 = (f32[2,256,512]{2,1,0:T(8,128)}, bf16[2,256,512]{2,1,0:T(8,128)(2,1)}, f32[8,128]{1,0:T(8,128)}) custom-call(bf16[512,2048]{1,0:T(8,128)(2,1)} %bitcast.17, bf16[2048,3328]{1,0:T(8,128)(2,1)} %refs_3_.9, bf16[2048,3328]{1,0:T(8,128)(2,1)} %refs_5_.7, f32[8,128]{1,0:T(8,128)} %get-tuple-element.148.refs_3_), custom_call_target="tpu_custom_call" | custom-call | flops 1 | bytes 1 | tf_op jit(solution)/shard_map/pallas_call | solution.py:66
  149.3 2.8 shard_map.108
  153.4 2.8 shard_map.109
  158.9 8.8 %shard_map.111 = (f32[512,2048]{1,0:T(8,128)}, f32[512,2048]{1,0:T(8,128)}, f32[8,128]{1,0:T(8,128)}) custom-call(bf16[3,256,512]{2,1,0:T(8,128)(2,1)} %get-tuple-element.161.refs_0_.refs_2_, bf16[3,256,512]{2,1,0:T(8,128)(2,1)} %collective-permute-done.26.refs_1_.refs_3_, bf16[3328,2048]{1,0:T(8,128)(2,1)} %refs_3_.11, bf16[3328,2048]{1,0:T(8,128)(2,1)} %refs_3_.11, ...), custom_call_target="tpu_custom_call" | custom-call | flops 1 | bytes 1 | tf_op jit(solution)/shard_map/pallas_call | solution.py:66
  167.7 7.3 %shard_map.112 = (bf16[2048,3328]{1,0:T(8,128)(2,1)}, bf16[2048,3328]{1,0:T(8,128)(2,1)}, bf16[3328,2048]{1,0:T(8,128)(2,1)}, f32[8,128]{1,0:T(8,128)}) custom-call(bf16[2048,512]{1,0:T(8,128)(2,1)} %get-tuple-element.160.refs_0_, bf16[512,2048]{1,0:T(8,128)(2,1)} %bitcast.10, bf16[3,256,512]{2,1,0:T(8,128)(2,1)} %get-tuple-element.161.refs_0_.refs_2_, ...), custom_call_target="tpu_custom_call" | custom-call | flops 1 | bytes 1 | tf_op jit(solution)/shard_map/pallas_call | solution.py:66
  175.0 6.1 %collective-permute-done.25.refs_2_ = bf16[2,256,1280]{2,1,0:T(8,128)(2,1)} collective-permute-done((bf16[2,256,1280]{2,1,0:T(8,128)(2,1)}, bf16[2,256,1280]{2,1,0:T(8,128)(2,1)}, u32[]{:S(2)}, u32[]{:S(2)}) %collective-permute-start.25) | collective-permute-done | bytes 1310752 | tf_op jit(solution)/shard_map/ppermute | solution.py:29
  181.1 6.2 %shard_map.113 = (bf16[3,256,1280]{2,1,0:T(8,128)(2,1)}, f32[8,128]{1,0:T(8,128)}) custom-call(f32[2,256,1280]{2,1,0:T(8,128)} %get-tuple-element.141.refs_0_, bf16[2,256,1280]{2,1,0:T(8,128)(2,1)} %collective-permute-done.18.refs_1_, bf16[2,256,1280]{2,1,0:T(8,128)(2,1)} %collective-permute-done.25.refs_2_, f32[256,1280]{1,0:T(8,128)} %get-tuple-element.124.refs_0_.refs_3_, ...), custom_call_target="tpu_custom_call" | custom-call | flops 1 | bytes 1 | tf_op jit(solution)/shard_map/pallas_call | solution.py:66
  188.7 2.9 collective-permute-done.27.refs_1_.refs_3_
  191.6 16.1 %shard_map.114 = (f32[512,2048]{1,0:T(8,128)}, f32[512,2048]{1,0:T(8,128)}, f32[8,128]{1,0:T(8,128)}) custom-call(bf16[3,256,1280]{2,1,0:T(8,128)(2,1)} %get-tuple-element.165.refs_0_.refs_2_, bf16[3,256,1280]{2,1,0:T(8,128)(2,1)} %collective-permute-done.27.refs_1_.refs_3_, ...), custom_call_target="tpu_custom_call", output_to_operand_aliasing={{0}: (7, {}), {1}: (18, {})} | custom-call | flops 1 | bytes 1 | tf_op jit(solution)/shard_map/pallas_call | solution.py:66
  207.7 5.4 %collective-permute-done.24.refs_2_ = bf16[2,256,1024]{2,1,0:T(8,128)(2,1)} collective-permute-done((bf16[2,256,1024]{2,1,0:T(8,128)(2,1)}, bf16[2,256,1024]{2,1,0:T(8,128)(2,1)}, u32[]{:S(2)}, u32[]{:S(2)}) %collective-permute-start.24) | collective-permute-done | bytes 1048608 | tf_op jit(solution)/shard_map/ppermute | solution.py:29
  213.1 4.9 %shard_map.115 = (bf16[3,256,1024]{2,1,0:T(8,128)(2,1)}, f32[8,128]{1,0:T(8,128)}) custom-call(f32[2,256,1024]{2,1,0:T(8,128)} %get-tuple-element.152.refs_0_, bf16[2,256,1024]{2,1,0:T(8,128)(2,1)} %collective-permute-done.22.refs_1_, bf16[2,256,1024]{2,1,0:T(8,128)(2,1)} %collective-permute-done.24.refs_2_, f32[256,1536]{1,0:T(8,128)} %get-tuple-element.137.refs_0_.refs_3_, ...), custom_call_target="tpu_custom_call" | custom-call | flops 1 | bytes 1 | tf_op jit(solution)/shard_map/pallas_call | solution.py:66
  221.8 13.9 %shard_map.116 = (f32[512,2048]{1,0:T(8,128)}, f32[512,2048]{1,0:T(8,128)}, f32[8,128]{1,0:T(8,128)}) custom-call(bf16[3,256,1024]{2,1,0:T(8,128)(2,1)} %get-tuple-element.170.refs_0_.refs_2_, bf16[3,256,1024]{2,1,0:T(8,128)(2,1)} %collective-permute-done.28.refs_1_.refs_3_, ...), custom_call_target="tpu_custom_call", output_to_operand_aliasing={{0}: (6, {}), {1}: (15, {})} | custom-call | flops 1 | bytes 1 | tf_op jit(solution)/shard_map/pallas_call | solution.py:66
  235.8 2.8 shard_map.117
  241.2 7.6 %shard_map.118 = (f32[4,4,16,2048]{3,2,1,0:T(8,128)}, bf16[4,4,16,2048]{3,2,1,0:T(8,128)(2,1)}, f32[8,128]{1,0:T(8,128)}) custom-call(bf16[3,256,512]{2,1,0:T(8,128)(2,1)} %get-tuple-element.175.refs_0_.refs_2_, bf16[3,256,512]{2,1,0:T(8,128)(2,1)} %collective-permute-done.29.refs_1_.refs_3_, bf16[2048,3328]{1,0:T(8,128)(2,1)} %refs_3_.9, ...), custom_call_target="tpu_custom_call" | custom-call | flops 1 | bytes 1 | tf_op jit(solution)/shard_map/pallas_call | solution.py:66
  250.5 3.9 %shard_map.119 = (f32[4,4,16,1024]{3,2,1,0:T(8,128)}, bf16[4,4,16,1024]{3,2,1,0:T(8,128)(2,1)}, f32[8,128]{1,0:T(8,128)}) custom-call(bf16[3,256,512]{2,1,0:T(8,128)(2,1)} %get-tuple-element.175.refs_0_.refs_2_, bf16[3,256,512]{2,1,0:T(8,128)(2,1)} %collective-permute-done.29.refs_1_.refs_3_, bf16[3328,2048]{1,0:T(8,128)(2,1)} %refs_3_.11, ...), custom_call_target="tpu_custom_call" | custom-call | flops 1 | bytes 1 | tf_op jit(solution)/shard_map/pallas_call | solution.py:66
  254.7 3.8 %shard_map.120 = (f32[4,4,16,1024]{3,2,1,0:T(8,128)}, bf16[4,4,16,1024]{3,2,1,0:T(8,128)(2,1)}, f32[8,128]{1,0:T(8,128)}) custom-call(bf16[3,256,512]{2,1,0:T(8,128)(2,1)} %get-tuple-element.175.refs_0_.refs_2_, bf16[3,256,512]{2,1,0:T(8,128)(2,1)} %collective-permute-done.29.refs_1_.refs_3_, bf16[3328,2048]{1,0:T(8,128)(2,1)} %refs_3_.11, ...), custom_call_target="tpu_custom_call" | custom-call | flops 1 | bytes 1 | tf_op jit(solution)/shard_map/pallas_call | solution.py:66
  258.5 12.8 %shard_map.121 = (bf16[2048,3328]{1,0:T(8,128)(2,1)}, bf16[2048,3328]{1,0:T(8,128)(2,1)}, bf16[3328,2048]{1,0:T(8,128)(2,1)}, f32[8,128]{1,0:T(8,128)}) custom-call(bf16[2048,512]{1,0:T(8,128)(2,1)} %get-tuple-element.160.refs_0_, bf16[512,2048]{1,0:T(8,128)(2,1)} %bitcast.11, ...), custom_call_target="tpu_custom_call", output_to_operand_aliasing={{0}: (4, {}), {1}: (5, {}), {2}: (6, {})} | custom-call | flops 1 | bytes 1 | tf_op jit(solution)/shard_map/pallas_call | solution.py:66
  271.3 3.8 %collective-permute-done.31.refs_1_ = bf16[4,4,16,2048]{3,2,1,0:T(8,128)(2,1)} collective-permute-done((bf16[4,4,16,2048]{3,2,1,0:T(8,128)(2,1)}, bf16[4,4,16,2048]{3,2,1,0:T(8,128)(2,1)}, u32[]{:S(2)}, u32[]{:S(2)}) %collective-permute-start.31) | collective-permute-done | bytes 1048608 | tf_op jit(solution)/shard_map/ppermute | solution.py:33
  275.1 3.1 shard_map.122
  281.5 11.0 %shard_map.123 = (bf16[2048,3328]{1,0:T(8,128)(2,1)}, bf16[2048,3328]{1,0:T(8,128)(2,1)}, bf16[3328,2048]{1,0:T(8,128)(2,1)}, f32[8,128]{1,0:T(8,128)}) custom-call(bf16[2048,512]{1,0:T(8,128)(2,1)} %get-tuple-element.160.refs_0_, bf16[512,2048]{1,0:T(8,128)(2,1)} %bitcast.12, ...), custom_call_target="tpu_custom_call", output_to_operand_aliasing={{0}: (4, {}), {1}: (5, {}), {2}: (6, {})} | custom-call | flops 1 | bytes 1 | tf_op jit(solution)/shard_map/pallas_call | solution.py:66
  297.5 2.6 collective-permute-start.37
  304.0 3.9 %collective-permute-done.32.refs_1_ = bf16[2,4,16,1024]{3,2,1,0:T(8,128)(2,1)} collective-permute-done((bf16[2,4,16,1024]{3,2,1,0:T(8,128)(2,1)}, bf16[2,4,16,1024]{3,2,1,0:T(8,128)(2,1)}, u32[]{:S(2)}, u32[]{:S(2)}) %collective-permute-start.32) | collective-permute-done | bytes 262176 | tf_op jit(solution)/shard_map/ppermute | solution.py:33
  309.7 7.3 %shard_map.128 = (bf16[2048,3328]{1,0:T(8,128)(2,1)}, bf16[2048,3328]{1,0:T(8,128)(2,1)}, bf16[3328,2048]{1,0:T(8,128)(2,1)}, f32[8,128]{1,0:T(8,128)}) custom-call(bf16[2048,512]{1,0:T(8,128)(2,1)} %get-tuple-element.160.refs_0_, bf16[512,2048]{1,0:T(8,128)(2,1)} %bitcast.13, ...), custom_call_target="tpu_custom_call", output_to_operand_aliasing={{0}: (4, {}), {1}: (5, {}), {2}: (6, {})} | custom-call | flops 1 | bytes 1 | tf_op jit(solution)/shard_map/pallas_call | solution.py:66
  321.5 2.9 collective-permute-start.38
  326.2 3.3 collective-permute-done.40.refs_3_
  330.2 2.9 shard_map.131
  333.8 2.5 shard_map.132
  (92 shorter events, 70.6 us)
Async XLA Ops:
  0.6 9.7 %collective-permute-start = (bf16[64,2048]{1,0:T(8,128)(2,1)}, bf16[64,2048]{1,0:T(8,128)(2,1)}, u32[]{:S(2)}, u32[]{:S(2)}) collective-permute-start(bf16[64,2048]{1,0:T(8,128)(2,1)} %refs_1_.8), channel_id=1, source_target_pairs={{0,4},{4,0},{8,12},{12,8},{16,20},{20,16},{24,28},{28,24},{1,5},{5... | collective-permute-start | bytes 786440 | tf_op jit(solution)/shard_map/ppermute | solution.py:33
  3.7 14.9 %collective-permute-start.9 = (bf16[64,2048]{1,0:T(8,128)(2,1)}, bf16[64,2048]{1,0:T(8,128)(2,1)}, u32[]{:S(2)}, u32[]{:S(2)}) collective-permute-start(bf16[64,2048]{1,0:T(8,128)(2,1)} %refs_1_.8), channel_id=1, source_target_pairs={{0,16},{4,20},{8,24},{12,28},{16,0},{20,4},{24,8},{28,12},{1,17},{... | collective-permute-start | bytes 786440 | tf_op jit(solution)/shard_map/ppermute | solution.py:33
  13.2 9.4 %all-to-all-start = ((bf16[4,16,2048]{2,1,0:T(8,128)(2,1)}), bf16[4,16,2048]{2,1,0:T(8,128)(2,1)S(1)}, u32[]{:S(2)}, u32[]{:S(2)}) async-start(bf16[4,16,2048]{2,1,0:T(8,128)(2,1)} %get-tuple-element.117), calls=%async_computation | async-start | bytes 524288 | tf_op jit(solution)/shard_map/all_to_all | solution.py:474
  16.7 9.4 %collective-permute-start.8 = (bf16[64,2048]{1,0:T(8,128)(2,1)}, bf16[64,2048]{1,0:T(8,128)(2,1)S(1)}, u32[]{:S(2)}, u32[]{:S(2)}) collective-permute-start(bf16[64,2048]{1,0:T(8,128)(2,1)} %refs_1_.8), channel_id=1, source_target_pairs={{0,8},{4,12},{8,0},{12,4},{16,24},{20,28},{24,16},{28,20},{1,9},{5... | collective-permute-start | bytes 786440 | tf_op jit(solution)/shard_map/ppermute | solution.py:33
  18.5 12.7 %collective-permute-start.10 = (bf16[64,2048]{1,0:T(8,128)(2,1)}, bf16[64,2048]{1,0:T(8,128)(2,1)S(1)}, u32[]{:S(2)}, u32[]{:S(2)}) collective-permute-start(bf16[64,2048]{1,0:T(8,128)(2,1)} %collective-permute-done.9.refs_1_.refs_5_), channel_id=1, source_target_pairs={{0,8},{4,12},{8,0},{12,4},{16,24},{20,28},{24,16},{28,20},{1,9},{5... | collective-permute-start | bytes 786440 | tf_op jit(solution)/shard_map/ppermute | solution.py:33
  22.7 0.7 copy-start
  23.4 7.9 %collective-permute-start.1 = (bf16[64,2048]{1,0:T(8,128)(2,1)S(1)}, bf16[64,2048]{1,0:T(8,128)(2,1)S(1)}, u32[]{:S(2)}, u32[]{:S(2)}) collective-permute-start(bf16[64,2048]{1,0:T(8,128)(2,1)S(1)} %bitcast.18), channel_id=1, source_target_pairs={{0,4},{4,0},{8,12},{12,8},{16,20},{20,16},{24,28},{28,24},{1,5},{5... | collective-permute-start | bytes 786440 | tf_op jit(solution)/shard_map/ppermute | solution.py:33
  26.0 5.2 %copy-start.2 = (bf16[64,2048]{1,0:T(8,128)(2,1)}, bf16[64,2048]{1,0:T(8,128)(2,1)S(1)}, u32[]{:S(2)}) copy-start(bf16[64,2048]{1,0:T(8,128)(2,1)S(1)} %collective-permute-done.8.refs_0_.refs_3_) | copy-start | bytes 786436
  31.2 0.7 copy-start.3
  31.9 0.7 copy-start.1
  34.7 24.7 %collective-permute-start.11 = (bf16[3,64,2048]{2,1,0:T(8,128)(2,1)}, bf16[3,64,2048]{2,1,0:T(8,128)(2,1)}, u32[]{:S(2)}, u32[]{:S(2)}) collective-permute-start(bf16[3,64,2048]{2,1,0:T(8,128)(2,1)} %get-tuple-element.119), channel_id=1, source_target_pairs={{0,4},{4,0},{8,12},{12,8},{16,20},{20,16},{24,28},{28,24},{1,5},{5... | collective-permute-start | bytes 2359304 | tf_op jit(solution)/shard_map/ppermute | solution.py:33
  36.4 14.5 %collective-permute-start.4 = (bf16[64,2048]{1,0:T(8,128)(2,1)}, bf16[64,2048]{1,0:T(8,128)(2,1)}, u32[]{:S(2)}, u32[]{:S(2)}) collective-permute-start(bf16[64,2048]{1,0:T(8,128)(2,1)} %bitcast.20), channel_id=1, source_target_pairs={{0,16},{4,20},{8,24},{12,28},{16,0},{20,4},{24,8},{28,12},{1,17},{... | collective-permute-start | bytes 786440 | tf_op jit(solution)/shard_map/ppermute | solution.py:33
  39.0 13.0 %collective-permute-start.2 = (bf16[64,2048]{1,0:T(8,128)(2,1)}, bf16[64,2048]{1,0:T(8,128)(2,1)}, u32[]{:S(2)}, u32[]{:S(2)}) collective-permute-start(bf16[64,2048]{1,0:T(8,128)(2,1)} %bitcast.21), channel_id=1, source_target_pairs={{0,8},{4,12},{8,0},{12,4},{16,24},{20,28},{24,16},{28,20},{1,9},{5... | collective-permute-start | bytes 786440 | tf_op jit(solution)/shard_map/ppermute | solution.py:33
  50.9 7.4 %collective-permute-start.6 = (bf16[64,2048]{1,0:T(8,128)(2,1)}, bf16[64,2048]{1,0:T(8,128)(2,1)}, u32[]{:S(2)}, u32[]{:S(2)}) collective-permute-start(bf16[64,2048]{1,0:T(8,128)(2,1)} %collective-permute-done.4.refs_10_.refs_5_), channel_id=1, source_target_pairs={{0,8},{4,12},{8,0},{12,4},{16,24},{20,28},{24,16},{28,20},{1,9},{5... | collective-permute-start | bytes 786440 | tf_op jit(solution)/shard_map/ppermute | solution.py:33
  51.4 16.5 %collective-permute-start.5 = (bf16[64,2048]{1,0:T(8,128)(2,1)}, bf16[64,2048]{1,0:T(8,128)(2,1)}, u32[]{:S(2)}, u32[]{:S(2)}) collective-permute-start(bf16[64,2048]{1,0:T(8,128)(2,1)} %collective-permute-done.4.refs_10_.refs_5_), channel_id=1, source_target_pairs={{0,4},{4,0},{8,12},{12,8},{16,20},{20,16},{24,28},{28,24},{1,5},{5... | collective-permute-start | bytes 786440 | tf_op jit(solution)/shard_map/ppermute | solution.py:33
  52.0 16.0 %collective-permute-start.3 = (bf16[64,2048]{1,0:T(8,128)(2,1)}, bf16[64,2048]{1,0:T(8,128)(2,1)}, u32[]{:S(2)}, u32[]{:S(2)}) collective-permute-start(bf16[64,2048]{1,0:T(8,128)(2,1)} %collective-permute-done.2.refs_9_.refs_3_), channel_id=1, source_target_pairs={{0,4},{4,0},{8,12},{12,8},{16,20},{20,16},{24,28},{28,24},{1,5},{5... | collective-permute-start | bytes 786440 | tf_op jit(solution)/shard_map/ppermute | solution.py:33
  58.3 12.7 %collective-permute-start.7 = (bf16[64,2048]{1,0:T(8,128)(2,1)}, bf16[64,2048]{1,0:T(8,128)(2,1)}, u32[]{:S(2)}, u32[]{:S(2)}) collective-permute-start(bf16[64,2048]{1,0:T(8,128)(2,1)} %collective-permute-done.6.refs_11_.refs_7_), channel_id=1, source_target_pairs={{0,4},{4,0},{8,12},{12,8},{16,20},{20,16},{24,28},{28,24},{1,5},{5... | collective-permute-start | bytes 786440 | tf_op jit(solution)/shard_map/ppermute | solution.py:33
  78.4 14.4 %collective-permute-start.12 = (bf16[256,1280]{1,0:T(8,128)(2,1)}, bf16[256,1280]{1,0:T(8,128)(2,1)}, u32[]{:S(2)}, u32[]{:S(2)}) collective-permute-start(bf16[256,1280]{1,0:T(8,128)(2,1)} %get-tuple-element.125), channel_id=1, source_target_pairs={{0,1},{1,0},{2,3},{3,2},{4,5},{5,4},{6,7},{7,6},{8,9},{9,8},{10,11... | collective-permute-start | bytes 1966088 | tf_op jit(solution)/shard_map/ppermute | solution.py:29
  78.4 2.8 collective-permute-start.13
  83.0 17.8 %collective-permute-start.15 = (bf16[256,512]{1,0:T(8,128)(2,1)}, bf16[256,512]{1,0:T(8,128)(2,1)}, u32[]{:S(2)}, u32[]{:S(2)}) collective-permute-start(bf16[256,512]{1,0:T(8,128)(2,1)} %get-tuple-element.134), channel_id=1, source_target_pairs={{0,2},{1,3},{2,0},{3,1},{4,6},{5,7},{6,4},{7,5},{8,10},{9,11},{10,... | collective-permute-start | bytes 786440 | tf_op jit(solution)/shard_map/ppermute | solution.py:29
  92.8 14.3 %collective-permute-start.17 = (bf16[256,1536]{1,0:T(8,128)(2,1)}, bf16[256,1536]{1,0:T(8,128)(2,1)}, u32[]{:S(2)}, u32[]{:S(2)}) collective-permute-start(bf16[256,1536]{1,0:T(8,128)(2,1)} %get-tuple-element.138), channel_id=1, source_target_pairs={{0,1},{1,0},{2,3},{3,2},{4,5},{5,4},{6,7},{7,6},{8,9},{9,8},{10,11... | collective-permute-start | bytes 2359304 | tf_op jit(solution)/shard_map/ppermute | solution.py:29
  95.1 17.4 %collective-permute-start.14 = (bf16[256,1280]{1,0:T(8,128)(2,1)}, bf16[256,1280]{1,0:T(8,128)(2,1)}, u32[]{:S(2)}, u32[]{:S(2)}) collective-permute-start(bf16[256,1280]{1,0:T(8,128)(2,1)} %get-tuple-element.133), channel_id=1, source_target_pairs={{0,2},{1,3},{2,0},{3,1},{4,6},{5,7},{6,4},{7,5},{8,10},{9,11},{10,... | collective-permute-start | bytes 1966088 | tf_op jit(solution)/shard_map/ppermute | solution.py:29
  106.8 4.0 %collective-permute-start.16 = (bf16[2,256,512]{2,1,0:T(8,128)(2,1)}, bf16[2,256,512]{2,1,0:T(8,128)(2,1)}, u32[]{:S(2)}, u32[]{:S(2)}) collective-permute-start(bf16[2,256,512]{2,1,0:T(8,128)(2,1)} %get-tuple-element.136), channel_id=1, source_target_pairs={{0,1},{1,0},{2,3},{3,2},{4,5},{5,4},{6,7},{7,6},{8,9},{9,8},{10,11... | collective-permute-start | bytes 1572872 | tf_op jit(solution)/shard_map/ppermute | solution.py:29
  109.5 20.1 %collective-permute-start.19 = (bf16[256,1536]{1,0:T(8,128)(2,1)}, bf16[256,1536]{1,0:T(8,128)(2,1)}, u32[]{:S(2)}, u32[]{:S(2)}) collective-permute-start(bf16[256,1536]{1,0:T(8,128)(2,1)} %get-tuple-element.143), channel_id=1, source_target_pairs={{0,2},{1,3},{2,0},{3,1},{4,6},{5,7},{6,4},{7,5},{8,10},{9,11},{10,... | collective-permute-start | bytes 2359304 | tf_op jit(solution)/shard_map/ppermute | solution.py:29
  123.0 16.8 %collective-permute-start.18 = (bf16[2,256,1280]{2,1,0:T(8,128)(2,1)}, bf16[2,256,1280]{2,1,0:T(8,128)(2,1)}, u32[]{:S(2)}, u32[]{:S(2)}) collective-permute-start(bf16[2,256,1280]{2,1,0:T(8,128)(2,1)} %get-tuple-element.142), channel_id=1, source_target_pairs={{0,1},{1,0},{2,3},{3,2},{4,5},{5,4},{6,7},{7,6},{8,9},{9,8},{10,11... | collective-permute-start | bytes 3932168 | tf_op jit(solution)/shard_map/ppermute | solution.py:29
  138.3 11.0 %collective-permute-start.22 = (bf16[2,256,1024]{2,1,0:T(8,128)(2,1)}, bf16[2,256,1024]{2,1,0:T(8,128)(2,1)}, u32[]{:S(2)}, u32[]{:S(2)}) collective-permute-start(bf16[2,256,1024]{2,1,0:T(8,128)(2,1)} %get-tuple-element.153), channel_id=1, source_target_pairs={{0,1},{1,0},{2,3},{3,2},{4,5},{5,4},{6,7},{7,6},{8,9},{9,8},{10,11... | collective-permute-start | bytes 3145736 | tf_op jit(solution)/shard_map/ppermute | solution.py:29
  138.3 15.1 %collective-permute-start.21 = (bf16[2,256,512]{2,1,0:T(8,128)(2,1)}, bf16[2,256,512]{2,1,0:T(8,128)(2,1)}, u32[]{:S(2)}, u32[]{:S(2)}) collective-permute-start(bf16[2,256,512]{2,1,0:T(8,128)(2,1)} %get-tuple-element.151), channel_id=1, source_target_pairs={{0,2},{1,3},{2,0},{3,1},{4,6},{5,7},{6,4},{7,5},{8,10},{9,11},{10,... | collective-permute-start | bytes 1572872 | tf_op jit(solution)/shard_map/ppermute | solution.py:29
  148.5 5.0 %collective-permute-start.20 = (bf16[2,256,512]{2,1,0:T(8,128)(2,1)}, bf16[2,256,512]{2,1,0:T(8,128)(2,1)}, u32[]{:S(2)}, u32[]{:S(2)}) collective-permute-start(bf16[2,256,512]{2,1,0:T(8,128)(2,1)} %get-tuple-element.150), channel_id=1, source_target_pairs={{0,1},{1,0},{2,3},{3,2},{4,5},{5,4},{6,7},{7,6},{8,9},{9,8},{10,11... | collective-permute-start | bytes 1572872 | tf_op jit(solution)/shard_map/ppermute | solution.py:29
  148.6 32.4 %collective-permute-start.25 = (bf16[2,256,1280]{2,1,0:T(8,128)(2,1)}, bf16[2,256,1280]{2,1,0:T(8,128)(2,1)}, u32[]{:S(2)}, u32[]{:S(2)}) collective-permute-start(bf16[2,256,1280]{2,1,0:T(8,128)(2,1)} %get-tuple-element.159), channel_id=1, source_target_pairs={{0,2},{1,3},{2,0},{3,1},{4,6},{5,7},{6,4},{7,5},{8,10},{9,11},{10,... | collective-permute-start | bytes 3932168 | tf_op jit(solution)/shard_map/ppermute | solution.py:29
  156.3 2.6 collective-permute-start.26
  187.3 4.3 %collective-permute-start.27 = (bf16[3,256,1280]{2,1,0:T(8,128)(2,1)}, bf16[3,256,1280]{2,1,0:T(8,128)(2,1)}, u32[]{:S(2)}, u32[]{:S(2)}) collective-permute-start(bf16[3,256,1280]{2,1,0:T(8,128)(2,1)} %get-tuple-element.165.refs_0_.refs_2_), channel_id=1, source_target_pairs={{0,1},{1,0},{2,3},{3,2},{4,5},{5,4},{6,7},{7,6},{8,9},{9,8},{10,11... | collective-permute-start | bytes 5898248 | tf_op jit(solution)/shard_map/ppermute | solution.py:29
  187.3 25.9 %collective-permute-start.24 = (bf16[2,256,1024]{2,1,0:T(8,128)(2,1)}, bf16[2,256,1024]{2,1,0:T(8,128)(2,1)}, u32[]{:S(2)}, u32[]{:S(2)}) collective-permute-start(bf16[2,256,1024]{2,1,0:T(8,128)(2,1)} %get-tuple-element.158), channel_id=1, source_target_pairs={{0,2},{1,3},{2,0},{3,1},{4,6},{5,7},{6,4},{7,5},{8,10},{9,11},{10,... | collective-permute-start | bytes 3145736 | tf_op jit(solution)/shard_map/ppermute | solution.py:29
  218.0 3.8 %collective-permute-start.28 = (bf16[3,256,1024]{2,1,0:T(8,128)(2,1)}, bf16[3,256,1024]{2,1,0:T(8,128)(2,1)}, u32[]{:S(2)}, u32[]{:S(2)}) collective-permute-start(bf16[3,256,1024]{2,1,0:T(8,128)(2,1)} %get-tuple-element.170.refs_0_.refs_2_), channel_id=1, source_target_pairs={{0,1},{1,0},{2,3},{3,2},{4,5},{5,4},{6,7},{7,6},{8,9},{9,8},{10,11... | collective-permute-start | bytes 4718600 | tf_op jit(solution)/shard_map/ppermute | solution.py:29
  218.0 17.7 %collective-permute-start.23 = (bf16[2,256,512]{2,1,0:T(8,128)(2,1)}, bf16[2,256,512]{2,1,0:T(8,128)(2,1)}, u32[]{:S(2)}, u32[]{:S(2)}) collective-permute-start(bf16[2,256,512]{2,1,0:T(8,128)(2,1)} %get-tuple-element.157), channel_id=1, source_target_pairs={{0,2},{1,3},{2,0},{3,1},{4,6},{5,7},{6,4},{7,5},{8,10},{9,11},{10,... | collective-permute-start | bytes 1572872 | tf_op jit(solution)/shard_map/ppermute | solution.py:29
  238.6 2.6 collective-permute-start.29
  248.8 26.3 %collective-permute-start.31 = (bf16[4,4,16,2048]{3,2,1,0:T(8,128)(2,1)}, bf16[4,4,16,2048]{3,2,1,0:T(8,128)(2,1)}, u32[]{:S(2)}, u32[]{:S(2)}) collective-permute-start(bf16[4,4,16,2048]{3,2,1,0:T(8,128)(2,1)} %get-tuple-element.191), channel_id=1, source_target_pairs={{0,4},{4,0},{8,12},{12,8},{16,20},{20,16},{24,28},{28,24},{1,5},{5... | collective-permute-start | bytes 3145736 | tf_op jit(solution)/shard_map/ppermute | solution.py:33
  254.4 38.1 %collective-permute-start.30 = (bf16[4,4,16,1024]{3,2,1,0:T(8,128)(2,1)}, bf16[4,4,16,1024]{3,2,1,0:T(8,128)(2,1)}, u32[]{:S(2)}, u32[]{:S(2)}) collective-permute-start(bf16[4,4,16,1024]{3,2,1,0:T(8,128)(2,1)} %get-tuple-element.181), channel_id=1, source_target_pairs={{0,4},{4,0},{8,12},{12,8},{16,20},{20,16},{24,28},{28,24},{1,5},{5... | collective-permute-start | bytes 1572872 | tf_op jit(solution)/shard_map/ppermute | solution.py:33
  278.2 17.0 %collective-permute-start.34 = (bf16[2,4,16,2048]{3,2,1,0:T(8,128)(2,1)}, bf16[2,4,16,2048]{3,2,1,0:T(8,128)(2,1)}, u32[]{:S(2)}, u32[]{:S(2)}) collective-permute-start(bf16[2,4,16,2048]{3,2,1,0:T(8,128)(2,1)} %get-tuple-element.200), channel_id=1, source_target_pairs={{0,8},{4,12},{8,0},{12,4},{16,24},{20,28},{24,16},{28,20},{1,9},{5... | collective-permute-start | bytes 1572872 | tf_op jit(solution)/shard_map/ppermute | solution.py:33
  280.0 20.1 %collective-permute-start.33 = (bf16[4,4,16,1024]{3,2,1,0:T(8,128)(2,1)}, bf16[4,4,16,1024]{3,2,1,0:T(8,128)(2,1)}, u32[]{:S(2)}, u32[]{:S(2)}) collective-permute-start(bf16[4,4,16,1024]{3,2,1,0:T(8,128)(2,1)} %get-tuple-element.198), channel_id=1, source_target_pairs={{0,4},{4,0},{8,12},{12,8},{16,20},{20,16},{24,28},{28,24},{1,5},{5... | collective-permute-start | bytes 1572872 | tf_op jit(solution)/shard_map/ppermute | solution.py:33
  294.8 13.1 %collective-permute-start.32 = (bf16[2,4,16,1024]{3,2,1,0:T(8,128)(2,1)}, bf16[2,4,16,1024]{3,2,1,0:T(8,128)(2,1)}, u32[]{:S(2)}, u32[]{:S(2)}) collective-permute-start(bf16[2,4,16,1024]{3,2,1,0:T(8,128)(2,1)} %get-tuple-element.196), channel_id=1, source_target_pairs={{0,8},{4,12},{8,0},{12,4},{16,24},{20,28},{24,16},{28,20},{1,9},{5... | collective-permute-start | bytes 786440 | tf_op jit(solution)/shard_map/ppermute | solution.py:33
  297.5 19.6 %collective-permute-start.37 = (bf16[1,4,16,2048]{3,2,1,0:T(8,128)(2,1)}, bf16[1,4,16,2048]{3,2,1,0:T(8,128)(2,1)}, u32[]{:S(2)}, u32[]{:S(2)}) collective-permute-start(bf16[1,4,16,2048]{3,2,1,0:T(8,128)(2,1)} %get-tuple-element.209), channel_id=1, source_target_pairs={{0,16},{4,20},{8,24},{12,28},{16,0},{20,4},{24,8},{28,12},{1,17},{... | collective-permute-start | bytes 786440 | tf_op jit(solution)/shard_map/ppermute | solution.py:33
  302.4 17.2 %collective-permute-start.36 = (bf16[2,4,16,1024]{3,2,1,0:T(8,128)(2,1)}, bf16[2,4,16,1024]{3,2,1,0:T(8,128)(2,1)}, u32[]{:S(2)}, u32[]{:S(2)}) collective-permute-start(bf16[2,4,16,1024]{3,2,1,0:T(8,128)(2,1)} %get-tuple-element.207), channel_id=1, source_target_pairs={{0,8},{4,12},{8,0},{12,4},{16,24},{20,28},{24,16},{28,20},{1,9},{5... | collective-permute-start | bytes 786440 | tf_op jit(solution)/shard_map/ppermute | solution.py:33
  309.7 23.4 %collective-permute-start.35 = (bf16[1,4,16,1024]{3,2,1,0:T(8,128)(2,1)}, bf16[1,4,16,1024]{3,2,1,0:T(8,128)(2,1)S(1)}, u32[]{:S(2)}, u32[]{:S(2)}) collective-permute-start(bf16[1,4,16,1024]{3,2,1,0:T(8,128)(2,1)} %get-tuple-element.205), channel_id=1, source_target_pairs={{0,16},{4,20},{8,24},{12,28},{16,0},{20,4},{24,8},{28,12},{1,17},{... | collective-permute-start | bytes 393224 | tf_op jit(solution)/shard_map/ppermute | solution.py:33
  321.5 11.7 %collective-permute-start.38 = (bf16[1,4,16,1024]{3,2,1,0:T(8,128)(2,1)}, bf16[1,4,16,1024]{3,2,1,0:T(8,128)(2,1)}, u32[]{:S(2)}, u32[]{:S(2)}) collective-permute-start(bf16[1,4,16,1024]{3,2,1,0:T(8,128)(2,1)} %get-tuple-element.217), channel_id=1, source_target_pairs={{0,16},{4,20},{8,24},{12,28},{16,0},{20,4},{24,8},{28,12},{1,17},{... | collective-permute-start | bytes 393224 | tf_op jit(solution)/shard_map/ppermute | solution.py:33
  324.4 1.9 collective-permute-start.39
  324.4 5.2 %collective-permute-start.40 = (bf16[16,2048]{1,0:T(8,128)(2,1)}, bf16[16,2048]{1,0:T(8,128)(2,1)}, u32[]{:S(2)}, u32[]{:S(2)}) collective-permute-start(bf16[16,2048]{1,0:T(8,128)(2,1)} %get-tuple-element.220), channel_id=1, source_target_pairs={{0,2},{1,3},{2,0},{3,1},{4,6},{5,7},{6,4},{7,5},{8,10},{9,11},{10,... | collective-permute-start | bytes 196616 | tf_op jit(solution)/shard_map/ppermute | solution.py:29
  325.6 4.7 %collective-permute-start.41 = (bf16[16,2048]{1,0:T(8,128)(2,1)}, bf16[16,2048]{1,0:T(8,128)(2,1)}, u32[]{:S(2)}, u32[]{:S(2)}) collective-permute-start(bf16[16,2048]{1,0:T(8,128)(2,1)} %get-tuple-element.221), channel_id=1, source_target_pairs={{0,3},{1,2},{2,1},{3,0},{4,7},{5,6},{6,5},{7,4},{8,11},{9,10},{10,... | collective-permute-start | bytes 196616 | tf_op jit(solution)/shard_map/ppermute | solution.py:29
  326.2 4.0 %copy-start.5 = (bf16[16,2048]{1,0:T(8,128)(2,1)}, bf16[16,2048]{1,0:T(8,128)(2,1)S(1)}, u32[]{:S(2)}) copy-start(bf16[16,2048]{1,0:T(8,128)(2,1)S(1)} %collective-permute-done.39.refs_2_) | copy-start | bytes 196612
  (1 other events, 0.7 us)

commit v9 on v8

--- a/solution.py
+++ b/solution.py
@@ -517,20 +517,18 @@
     add_both(2)
     elementwise(3)
     grad_part = last_part(grad_term())
-    out_parts = [last_part(out_term(), 2, 0), last_part(out_term(), 2, 1)]
+    out_part = last_part(out_term())
     all_grads(1)
     grad_part = over_z(grad_part, 2)
     all_grads(2)
-    out_parts[0] = over_z(out_parts[0], 2)
+    out_part = over_z(out_part, 2)
     grad_part = over_z(grad_part, 4)
-    out_parts[1] = over_z(out_parts[1], 2)
-    out_parts[0] = over_z(out_parts[0], 4)
     all_grads(3)
+    out_part = over_z(out_part, 4)
     groups = finish(chain, place, [grad_part], False)
     groups = [groups[0]] + [swap(groups[g], g) for g in range(1, 4)]
-    out_parts[1] = over_z(out_parts[1], 4)
     input_gradient = place_columns(chain, place, groups)
-    block_output = finish(chain, place, out_parts, True)
+    block_output = finish(chain, place, [out_part], True)
     return (block_output, input_gradient, *grads)
 
 

time: 338 us -> 339 us (level)
  waiting for transfers between devices: 73.2 us -> 81.6 us
  Pallas kernels: 213 us -> 209 us
    ppermute x21 -> x18, waiting for transfers between devices: 36 us -> 44.2 us  [swap_wide(): return lax.ppermute(value, 'wide', [(i, i ^ mask) for i in range(8)])]
    pallas_call x41 -> x38, Pallas kernels: 213 us -> 209 us  [__call__(): pl.pallas_call(kernel, grid_spec=pltpu.PrefetchScalarGridSpec(num_scalar_...]
    ppermute x21 -> x18, starting transfers between devices: 31.4 us -> 28.5 us  [swap_wide(): return lax.ppermute(value, 'wide', [(i, i ^ mask) for i in range(8)])]
  transfers between devices with their start and end apart: 43 -> 40, of which waited for: 21 -> 22; matrix products, arithmetic and copies ran while one was open for 0% -> 0% of each run, Pallas kernels for 53% -> 52%
where the time goes in v9:
time: 339 us; the launch traced here: 338 us
  Pallas kernels  209 us (62%)
  waiting for transfers between devices  81.6 us (24%)
  starting transfers between devices  43.2 us (13%)
    pallas_call x38, Pallas kernels, __call__(): pl.pallas_call(kernel, grid_spec=pltpu.PrefetchScalarGridSpec(num_scalar_...  209 us
    ppermute x18, waiting for transfers between devices, swap_wide(): return lax.ppermute(value, 'wide', [(i, i ^ mask) for i in range(8)])  44.2 us
    ppermute x21, waiting for transfers between devices, swap(): return lax.ppermute(value, 'narrow', [(i, i ^ mask) for i in range(4)])  33.6 us
    ppermute x18, starting transfers between devices, swap_wide(): return lax.ppermute(value, 'wide', [(i, i ^ mask) for i in range(8)])  28.5 us
    ppermute x21, starting transfers between devices, swap(): return lax.ppermute(value, 'narrow', [(i, i ^ mask) for i in range(4)])  11.3 us
  transfers between devices with their start and end apart: 40, of which 22 were waited for; matrix products, arithmetic and copies ran while one was open for 0% of the time, Pallas kernels for 52%

profile of v9, /device:TPU:0, one launch (start us, length us, event | category | flops | bytes accessed | tf_op | source)
XLA Modules:
  0.0 337.5 jit_solution(13288970514277856427)
XLA Ops:
  0.6 3.0 collective-permute-start
  3.7 2.6 collective-permute-start.9
  6.3 4.0 %collective-permute-done.refs_1_.refs_2_ = bf16[64,2048]{1,0:T(8,128)(2,1)} collective-permute-done((bf16[64,2048]{1,0:T(8,128)(2,1)}, bf16[64,2048]{1,0:T(8,128)(2,1)}, u32[]{:S(2)}, u32[]{:S(2)}) %collective-permute-start) | collective-permute-done | bytes 262176 | tf_op jit(solution)/shard_map/ppermute | solution.py:33
  10.3 3.0 shard_map.92
  13.2 3.4 %all-to-all-start = ((bf16[4,16,2048]{2,1,0:T(8,128)(2,1)}), bf16[4,16,2048]{2,1,0:T(8,128)(2,1)S(1)}, u32[]{:S(2)}, u32[]{:S(2)}) async-start(bf16[4,16,2048]{2,1,0:T(8,128)(2,1)} %get-tuple-element.108), calls=%async_computation | async-start | bytes 524288 | tf_op jit(solution)/shard_map/all_to_all | solution.py:474
  18.9 3.7 %all-to-all-done = bf16[4,16,2048]{2,1,0:T(8,128)(2,1)S(1)} async-done(((bf16[4,16,2048]{2,1,0:T(8,128)(2,1)}), bf16[4,16,2048]{2,1,0:T(8,128)(2,1)S(1)}, u32[]{:S(2)}, u32[]{:S(2)}) %all-to-all-start) | async-done | bytes 262176 | tf_op jit(solution)/shard_map/all_to_all | solution.py:474
  26.0 5.2 %collective-permute-done.10.refs_2_.refs_7_ = bf16[64,2048]{1,0:T(8,128)(2,1)S(1)} collective-permute-done((bf16[64,2048]{1,0:T(8,128)(2,1)}, bf16[64,2048]{1,0:T(8,128)(2,1)S(1)}, u32[]{:S(2)}, u32[]{:S(2)}) %collective-permute-start.10) | collective-permute-done | bytes 262176 | tf_op jit(solution)/shard_map/ppermute | solution.py:33
  36.4 2.6 collective-permute-start.4
  40.5 10.3 %collective-permute-done.4.refs_10_.refs_5_ = bf16[64,2048]{1,0:T(8,128)(2,1)} collective-permute-done((bf16[64,2048]{1,0:T(8,128)(2,1)}, bf16[64,2048]{1,0:T(8,128)(2,1)}, u32[]{:S(2)}, u32[]{:S(2)}) %collective-permute-start.4) | collective-permute-done | bytes 262176 | tf_op jit(solution)/shard_map/ppermute | solution.py:33
  53.5 4.8 %collective-permute-done.6.refs_11_.refs_7_ = bf16[64,2048]{1,0:T(8,128)(2,1)} collective-permute-done((bf16[64,2048]{1,0:T(8,128)(2,1)}, bf16[64,2048]{1,0:T(8,128)(2,1)}, u32[]{:S(2)}, u32[]{:S(2)}) %collective-permute-start.6) | collective-permute-done | bytes 262176 | tf_op jit(solution)/shard_map/ppermute | solution.py:33
  59.4 4.5 %shard_map.94 = (bf16[4,8,16,2048]{3,2,1,0:T(8,128)(2,1)}, f32[8,128]{1,0:T(8,128)}) custom-call(s32[2]{0:T(128)} %pad_add_fusion.refs_0_, bf16[64,2048]{1,0:T(8,128)(2,1)} %refs_1_.8, bf16[64,2048]{1,0:T(8,128)(2,1)} %collective-permute-done.refs_1_.refs_2_, bf16[64,2048]{1,0:T(8,128)(2,1)} %copy-done.2, bf16[192,2048]{1,0:T(8,128)(2,1)} %bitcast.3.refs_4_.refs_6_.refs_8_, ...), custom_call_target="tpu_custom_call" | custom-call | flops 1 | bytes 1 | tf_op jit(solution)/shard_map/pallas_call | solution.py:66
  63.9 4.1 %shard_map.95 = (f32[256,512]{1,0:T(8,128)}, bf16[256,512]{1,0:T(8,128)(2,1)}, f32[8,128]{1,0:T(8,128)}) custom-call(bf16[512,2048]{1,0:T(8,128)(2,1)} %bitcast.7, bf16[3328,2048]{1,0:T(8,128)(2,1)} %refs_3_.9, f32[8,128]{1,0:T(8,128)} %get-tuple-element.113.refs_2_), custom_call_target="tpu_custom_call" | custom-call | flops 1 | bytes 1 | tf_op jit(solution)/shard_map/pallas_call | solution.py:66
  68.0 2.9 collective-permute-done.7.refs_4_.refs_8_
  70.9 7.5 %shard_map.96 = (f32[256,1280]{1,0:T(8,128)}, bf16[256,1280]{1,0:T(8,128)(2,1)}, f32[8,128]{1,0:T(8,128)}) custom-call(bf16[512,2048]{1,0:T(8,128)(2,1)} %bitcast.8, bf16[3328,2048]{1,0:T(8,128)(2,1)} %refs_3_.9, bf16[64,2048]{1,0:T(8,128)(2,1)} %collective-permute-done.3.refs_2_.refs_4_, bf16[64,2048]{1,0:T(8,128)(2,1)} %collective-permute-done.5.refs_3_.refs_6_, ...), custom_call_target="tpu_custom_call" | custom-call | flops 1 | bytes 1 | tf_op jit(solution)/shard_map/pallas_call | solution.py:66
  84.4 8.4 %shard_map.98 = (f32[256,1536]{1,0:T(8,128)}, bf16[256,1536]{1,0:T(8,128)(2,1)}, f32[8,128]{1,0:T(8,128)}) custom-call(bf16[512,2048]{1,0:T(8,128)(2,1)} %bitcast.9, bf16[3328,2048]{1,0:T(8,128)(2,1)} %refs_3_.9, f32[8,128]{1,0:T(8,128)} %get-tuple-element.120.refs_2_), custom_call_target="tpu_custom_call" | custom-call | flops 1 | bytes 1 | tf_op jit(solution)/shard_map/pallas_call | solution.py:66
  95.7 5.1 %shard_map.100 = (bf16[4,8,16,2048]{3,2,1,0:T(8,128)(2,1)}, bf16[2048,512]{1,0:T(8,128)(2,1)}, f32[8,128]{1,0:T(8,128)}) custom-call(s32[2]{0:T(128)} %pad_add_fusion.refs_0_, bf16[64,2048]{1,0:T(8,128)(2,1)} %bitcast.22, bf16[64,2048]{1,0:T(8,128)(2,1)} %copy-done.1, bf16[64,2048]{1,0:T(8,128)(2,1)} %collective-permute-done.2.refs_9_.refs_3_, ...), custom_call_target="tpu_custom_call" | custom-call | flops 1 | bytes 1 | tf_op jit(solution)/shard_map/pallas_call | solution.py:66
  100.9 6.0 %shard_map.101 = (f32[2,256,512]{2,1,0:T(8,128)}, bf16[2,256,512]{2,1,0:T(8,128)(2,1)}, f32[8,128]{1,0:T(8,128)}) custom-call(bf16[512,2048]{1,0:T(8,128)(2,1)} %bitcast.14, bf16[2048,3328]{1,0:T(8,128)(2,1)} %refs_3_.8, bf16[2048,3328]{1,0:T(8,128)(2,1)} %refs_5_.7, bf16[256,512]{1,0:T(8,128)(2,1)} %collective-permute-done.15.refs_3_.refs_5_, ...), custom_call_target="tpu_custom_call" | custom-call | flops 1 | bytes 1 | tf_op jit(solution)/shard_map/pallas_call | solution.py:66
  112.5 10.4 %shard_map.103 = (f32[2,256,1280]{2,1,0:T(8,128)}, bf16[2,256,1280]{2,1,0:T(8,128)(2,1)}, f32[8,128]{1,0:T(8,128)}) custom-call(bf16[512,2048]{1,0:T(8,128)(2,1)} %bitcast.15, bf16[2048,3328]{1,0:T(8,128)(2,1)} %refs_3_.8, bf16[2048,3328]{1,0:T(8,128)(2,1)} %refs_5_.7, bf16[256,1280]{1,0:T(8,128)(2,1)} %collective-permute-done.14.refs_3_.refs_5_, ...), custom_call_target="tpu_custom_call" | custom-call | flops 1 | bytes 1 | tf_op jit(solution)/shard_map/pallas_call | solution.py:66
  125.1 4.4 %collective-permute-done.19.refs_3_.refs_5_ = bf16[256,1536]{1,0:T(8,128)(2,1)} collective-permute-done((bf16[256,1536]{1,0:T(8,128)(2,1)}, bf16[256,1536]{1,0:T(8,128)(2,1)}, u32[]{:S(2)}, u32[]{:S(2)}) %collective-permute-start.19) | collective-permute-done | bytes 786464 | tf_op jit(solution)/shard_map/ppermute | solution.py:29
  129.5 8.8 %shard_map.105 = (f32[2,256,1024]{2,1,0:T(8,128)}, bf16[2,256,1024]{2,1,0:T(8,128)(2,1)}, f32[8,128]{1,0:T(8,128)}) custom-call(bf16[512,2048]{1,0:T(8,128)(2,1)} %bitcast.16, bf16[2048,3328]{1,0:T(8,128)(2,1)} %refs_3_.8, bf16[2048,3328]{1,0:T(8,128)(2,1)} %refs_5_.7, bf16[256,1536]{1,0:T(8,128)(2,1)} %collective-permute-done.19.refs_3_.refs_5_, ...), custom_call_target="tpu_custom_call" | custom-call | flops 1 | bytes 1 | tf_op jit(solution)/shard_map/pallas_call | solution.py:66
  139.8 3.0 shard_map.106
  142.8 5.6 %shard_map.107 = (f32[2,256,512]{2,1,0:T(8,128)}, bf16[2,256,512]{2,1,0:T(8,128)(2,1)}, f32[8,128]{1,0:T(8,128)}) custom-call(bf16[512,2048]{1,0:T(8,128)(2,1)} %bitcast.17, bf16[2048,3328]{1,0:T(8,128)(2,1)} %refs_3_.8, bf16[2048,3328]{1,0:T(8,128)(2,1)} %refs_5_.7, f32[8,128]{1,0:T(8,128)} %get-tuple-element.139.refs_3_), custom_call_target="tpu_custom_call" | custom-call | flops 1 | bytes 1 | tf_op jit(solution)/shard_map/pallas_call | solution.py:66
  149.3 2.8 shard_map.108
  153.4 2.8 shard_map.109
  158.9 8.8 %shard_map.111 = (f32[512,2048]{1,0:T(8,128)}, f32[512,2048]{1,0:T(8,128)}, f32[8,128]{1,0:T(8,128)}) custom-call(bf16[3,256,512]{2,1,0:T(8,128)(2,1)} %get-tuple-element.152.refs_0_.refs_2_, bf16[3,256,512]{2,1,0:T(8,128)(2,1)} %collective-permute-done.26.refs_1_.refs_3_, bf16[3328,2048]{1,0:T(8,128)(2,1)} %refs_3_.9, bf16[3328,2048]{1,0:T(8,128)(2,1)} %refs_3_.9, ...), custom_call_target="tpu_custom_call" | custom-call | flops 1 | bytes 1 | tf_op jit(solution)/shard_map/pallas_call | solution.py:66
  167.7 7.3 %shard_map.112 = (bf16[2048,3328]{1,0:T(8,128)(2,1)}, bf16[2048,3328]{1,0:T(8,128)(2,1)}, bf16[3328,2048]{1,0:T(8,128)(2,1)}, f32[8,128]{1,0:T(8,128)}) custom-call(bf16[2048,512]{1,0:T(8,128)(2,1)} %get-tuple-element.151.refs_0_, bf16[512,2048]{1,0:T(8,128)(2,1)} %bitcast.10, bf16[3,256,512]{2,1,0:T(8,128)(2,1)} %get-tuple-element.152.refs_0_.refs_2_, ...), custom_call_target="tpu_custom_call" | custom-call | flops 1 | bytes 1 | tf_op jit(solution)/shard_map/pallas_call | solution.py:66
  175.0 6.1 %collective-permute-done.25.refs_2_ = bf16[2,256,1280]{2,1,0:T(8,128)(2,1)} collective-permute-done((bf16[2,256,1280]{2,1,0:T(8,128)(2,1)}, bf16[2,256,1280]{2,1,0:T(8,128)(2,1)}, u32[]{:S(2)}, u32[]{:S(2)}) %collective-permute-start.25) | collective-permute-done | bytes 1310752 | tf_op jit(solution)/shard_map/ppermute | solution.py:29
  181.1 6.2 %shard_map.113 = (bf16[3,256,1280]{2,1,0:T(8,128)(2,1)}, f32[8,128]{1,0:T(8,128)}) custom-call(f32[2,256,1280]{2,1,0:T(8,128)} %get-tuple-element.132.refs_0_, bf16[2,256,1280]{2,1,0:T(8,128)(2,1)} %collective-permute-done.18.refs_1_, bf16[2,256,1280]{2,1,0:T(8,128)(2,1)} %collective-permute-done.25.refs_2_, f32[256,1280]{1,0:T(8,128)} %get-tuple-element.115.refs_0_.refs_3_, ...), custom_call_target="tpu_custom_call" | custom-call | flops 1 | bytes 1 | tf_op jit(solution)/shard_map/pallas_call | solution.py:66
  188.7 2.9 collective-permute-done.27.refs_1_.refs_3_
  191.6 16.1 %shard_map.114 = (f32[512,2048]{1,0:T(8,128)}, f32[512,2048]{1,0:T(8,128)}, f32[8,128]{1,0:T(8,128)}) custom-call(bf16[3,256,1280]{2,1,0:T(8,128)(2,1)} %get-tuple-element.156.refs_0_.refs_2_, bf16[3,256,1280]{2,1,0:T(8,128)(2,1)} %collective-permute-done.27.refs_1_.refs_3_, ...), custom_call_target="tpu_custom_call", output_to_operand_aliasing={{0}: (7, {}), {1}: (18, {})} | custom-call | flops 1 | bytes 1 | tf_op jit(solution)/shard_map/pallas_call | solution.py:66
  207.7 5.5 %collective-permute-done.24.refs_2_ = bf16[2,256,1024]{2,1,0:T(8,128)(2,1)} collective-permute-done((bf16[2,256,1024]{2,1,0:T(8,128)(2,1)}, bf16[2,256,1024]{2,1,0:T(8,128)(2,1)}, u32[]{:S(2)}, u32[]{:S(2)}) %collective-permute-start.24) | collective-permute-done | bytes 1048608 | tf_op jit(solution)/shard_map/ppermute | solution.py:29
  213.1 4.9 %shard_map.115 = (bf16[3,256,1024]{2,1,0:T(8,128)(2,1)}, f32[8,128]{1,0:T(8,128)}) custom-call(f32[2,256,1024]{2,1,0:T(8,128)} %get-tuple-element.143.refs_0_, bf16[2,256,1024]{2,1,0:T(8,128)(2,1)} %collective-permute-done.22.refs_1_, bf16[2,256,1024]{2,1,0:T(8,128)(2,1)} %collective-permute-done.24.refs_2_, f32[256,1536]{1,0:T(8,128)} %get-tuple-element.128.refs_0_.refs_3_, ...), custom_call_target="tpu_custom_call" | custom-call | flops 1 | bytes 1 | tf_op jit(solution)/shard_map/pallas_call | solution.py:66
  221.8 13.9 %shard_map.116 = (f32[512,2048]{1,0:T(8,128)}, f32[512,2048]{1,0:T(8,128)}, f32[8,128]{1,0:T(8,128)}) custom-call(bf16[3,256,1024]{2,1,0:T(8,128)(2,1)} %get-tuple-element.161.refs_0_.refs_2_, bf16[3,256,1024]{2,1,0:T(8,128)(2,1)} %collective-permute-done.28.refs_1_.refs_3_, ...), custom_call_target="tpu_custom_call", output_to_operand_aliasing={{0}: (6, {}), {1}: (15, {})} | custom-call | flops 1 | bytes 1 | tf_op jit(solution)/shard_map/pallas_call | solution.py:66
  235.7 2.9 shard_map.117
  241.2 7.6 %shard_map.118 = (f32[4,4,16,2048]{3,2,1,0:T(8,128)}, bf16[4,4,16,2048]{3,2,1,0:T(8,128)(2,1)}, f32[8,128]{1,0:T(8,128)}) custom-call(bf16[3,256,512]{2,1,0:T(8,128)(2,1)} %get-tuple-element.166.refs_0_.refs_2_, bf16[3,256,512]{2,1,0:T(8,128)(2,1)} %collective-permute-done.29.refs_1_.refs_3_, bf16[2048,3328]{1,0:T(8,128)(2,1)} %refs_3_.8, ...), custom_call_target="tpu_custom_call" | custom-call | flops 1 | bytes 1 | tf_op jit(solution)/shard_map/pallas_call | solution.py:66
  250.5 6.4 %shard_map.119 = (f32[4,4,16,2048]{3,2,1,0:T(8,128)}, bf16[4,4,16,2048]{3,2,1,0:T(8,128)(2,1)}, f32[8,128]{1,0:T(8,128)}) custom-call(bf16[3,256,512]{2,1,0:T(8,128)(2,1)} %get-tuple-element.166.refs_0_.refs_2_, bf16[3,256,512]{2,1,0:T(8,128)(2,1)} %collective-permute-done.29.refs_1_.refs_3_, bf16[3328,2048]{1,0:T(8,128)(2,1)} %refs_3_.9, ...), custom_call_target="tpu_custom_call" | custom-call | flops 1 | bytes 1 | tf_op jit(solution)/shard_map/pallas_call | solution.py:66
  257.3 12.8 %shard_map.120 = (bf16[2048,3328]{1,0:T(8,128)(2,1)}, bf16[2048,3328]{1,0:T(8,128)(2,1)}, bf16[3328,2048]{1,0:T(8,128)(2,1)}, f32[8,128]{1,0:T(8,128)}) custom-call(bf16[2048,512]{1,0:T(8,128)(2,1)} %get-tuple-element.151.refs_0_, bf16[512,2048]{1,0:T(8,128)(2,1)} %bitcast.11, ...), custom_call_target="tpu_custom_call", output_to_operand_aliasing={{0}: (4, {}), {1}: (5, {}), {2}: (6, {})} | custom-call | flops 1 | bytes 1 | tf_op jit(solution)/shard_map/pallas_call | solution.py:66
  270.1 5.1 %collective-permute-done.31.refs_1_ = bf16[4,4,16,2048]{3,2,1,0:T(8,128)(2,1)} collective-permute-done((bf16[4,4,16,2048]{3,2,1,0:T(8,128)(2,1)}, bf16[4,4,16,2048]{3,2,1,0:T(8,128)(2,1)}, u32[]{:S(2)}, u32[]{:S(2)}) %collective-permute-start.31) | collective-permute-done | bytes 1048608 | tf_op jit(solution)/shard_map/ppermute | solution.py:33
  275.1 3.2 shard_map.121
  280.1 11.0 %shard_map.122 = (bf16[2048,3328]{1,0:T(8,128)(2,1)}, bf16[2048,3328]{1,0:T(8,128)(2,1)}, bf16[3328,2048]{1,0:T(8,128)(2,1)}, f32[8,128]{1,0:T(8,128)}) custom-call(bf16[2048,512]{1,0:T(8,128)(2,1)} %get-tuple-element.151.refs_0_, bf16[512,2048]{1,0:T(8,128)(2,1)} %bitcast.12, ...), custom_call_target="tpu_custom_call", output_to_operand_aliasing={{0}: (4, {}), {1}: (5, {}), {2}: (6, {})} | custom-call | flops 1 | bytes 1 | tf_op jit(solution)/shard_map/pallas_call | solution.py:66
  291.0 5.8 %collective-permute-done.30.refs_1_ = bf16[4,4,16,2048]{3,2,1,0:T(8,128)(2,1)} collective-permute-done((bf16[4,4,16,2048]{3,2,1,0:T(8,128)(2,1)}, bf16[4,4,16,2048]{3,2,1,0:T(8,128)(2,1)}, u32[]{:S(2)}, u32[]{:S(2)}) %collective-permute-start.30) | collective-permute-done | bytes 1048608 | tf_op jit(solution)/shard_map/ppermute | solution.py:33
  296.8 3.1 shard_map.123
  304.0 2.6 collective-permute-start.35
  306.6 7.3 %shard_map.125 = (bf16[2048,3328]{1,0:T(8,128)(2,1)}, bf16[2048,3328]{1,0:T(8,128)(2,1)}, bf16[3328,2048]{1,0:T(8,128)(2,1)}, f32[8,128]{1,0:T(8,128)}) custom-call(bf16[2048,512]{1,0:T(8,128)(2,1)} %get-tuple-element.151.refs_0_, bf16[512,2048]{1,0:T(8,128)(2,1)} %bitcast.13, ...), custom_call_target="tpu_custom_call", output_to_operand_aliasing={{0}: (4, {}), {1}: (5, {}), {2}: (6, {})} | custom-call | flops 1 | bytes 1 | tf_op jit(solution)/shard_map/pallas_call | solution.py:66
  313.9 5.1 %collective-permute-done.32.refs_1_ = bf16[2,4,16,2048]{3,2,1,0:T(8,128)(2,1)} collective-permute-done((bf16[2,4,16,2048]{3,2,1,0:T(8,128)(2,1)}, bf16[2,4,16,2048]{3,2,1,0:T(8,128)(2,1)}, u32[]{:S(2)}, u32[]{:S(2)}) %collective-permute-start.32) | collective-permute-done | bytes 524320 | tf_op jit(solution)/shard_map/ppermute | solution.py:33
  327.4 3.1 collective-permute-done.37.refs_3_
  332.1 2.9 shard_map.128
  335.0 2.5 shard_map.129
  (85 shorter events, 64.8 us)
Async XLA Ops:
  0.6 9.7 %collective-permute-start = (bf16[64,2048]{1,0:T(8,128)(2,1)}, bf16[64,2048]{1,0:T(8,128)(2,1)}, u32[]{:S(2)}, u32[]{:S(2)}) collective-permute-start(bf16[64,2048]{1,0:T(8,128)(2,1)} %refs_1_.8), channel_id=1, source_target_pairs={{0,4},{4,0},{8,12},{12,8},{16,20},{20,16},{24,28},{28,24},{1,5},{5... | collective-permute-start | bytes 786440 | tf_op jit(solution)/shard_map/ppermute | solution.py:33
  3.7 14.9 %collective-permute-start.9 = (bf16[64,2048]{1,0:T(8,128)(2,1)}, bf16[64,2048]{1,0:T(8,128)(2,1)}, u32[]{:S(2)}, u32[]{:S(2)}) collective-permute-start(bf16[64,2048]{1,0:T(8,128)(2,1)} %refs_1_.8), channel_id=1, source_target_pairs={{0,16},{4,20},{8,24},{12,28},{16,0},{20,4},{24,8},{28,12},{1,17},{... | collective-permute-start | bytes 786440 | tf_op jit(solution)/shard_map/ppermute | solution.py:33
  13.2 9.4 %all-to-all-start = ((bf16[4,16,2048]{2,1,0:T(8,128)(2,1)}), bf16[4,16,2048]{2,1,0:T(8,128)(2,1)S(1)}, u32[]{:S(2)}, u32[]{:S(2)}) async-start(bf16[4,16,2048]{2,1,0:T(8,128)(2,1)} %get-tuple-element.108), calls=%async_computation | async-start | bytes 524288 | tf_op jit(solution)/shard_map/all_to_all | solution.py:474
  16.7 9.4 %collective-permute-start.8 = (bf16[64,2048]{1,0:T(8,128)(2,1)}, bf16[64,2048]{1,0:T(8,128)(2,1)S(1)}, u32[]{:S(2)}, u32[]{:S(2)}) collective-permute-start(bf16[64,2048]{1,0:T(8,128)(2,1)} %refs_1_.8), channel_id=1, source_target_pairs={{0,8},{4,12},{8,0},{12,4},{16,24},{20,28},{24,16},{28,20},{1,9},{5... | collective-permute-start | bytes 786440 | tf_op jit(solution)/shard_map/ppermute | solution.py:33
  18.5 12.7 %collective-permute-start.10 = (bf16[64,2048]{1,0:T(8,128)(2,1)}, bf16[64,2048]{1,0:T(8,128)(2,1)S(1)}, u32[]{:S(2)}, u32[]{:S(2)}) collective-permute-start(bf16[64,2048]{1,0:T(8,128)(2,1)} %collective-permute-done.9.refs_1_.refs_5_), channel_id=1, source_target_pairs={{0,8},{4,12},{8,0},{12,4},{16,24},{20,28},{24,16},{28,20},{1,9},{5... | collective-permute-start | bytes 786440 | tf_op jit(solution)/shard_map/ppermute | solution.py:33
  22.7 0.7 copy-start
  23.4 7.9 %collective-permute-start.1 = (bf16[64,2048]{1,0:T(8,128)(2,1)S(1)}, bf16[64,2048]{1,0:T(8,128)(2,1)S(1)}, u32[]{:S(2)}, u32[]{:S(2)}) collective-permute-start(bf16[64,2048]{1,0:T(8,128)(2,1)S(1)} %bitcast.18), channel_id=1, source_target_pairs={{0,4},{4,0},{8,12},{12,8},{16,20},{20,16},{24,28},{28,24},{1,5},{5... | collective-permute-start | bytes 786440 | tf_op jit(solution)/shard_map/ppermute | solution.py:33
  26.0 5.2 %copy-start.2 = (bf16[64,2048]{1,0:T(8,128)(2,1)}, bf16[64,2048]{1,0:T(8,128)(2,1)S(1)}, u32[]{:S(2)}) copy-start(bf16[64,2048]{1,0:T(8,128)(2,1)S(1)} %collective-permute-done.8.refs_0_.refs_3_) | copy-start | bytes 786436
  31.2 0.7 copy-start.3
  31.9 0.7 copy-start.1
  34.7 24.7 %collective-permute-start.11 = (bf16[3,64,2048]{2,1,0:T(8,128)(2,1)}, bf16[3,64,2048]{2,1,0:T(8,128)(2,1)}, u32[]{:S(2)}, u32[]{:S(2)}) collective-permute-start(bf16[3,64,2048]{2,1,0:T(8,128)(2,1)} %get-tuple-element.110), channel_id=1, source_target_pairs={{0,4},{4,0},{8,12},{12,8},{16,20},{20,16},{24,28},{28,24},{1,5},{5... | collective-permute-start | bytes 2359304 | tf_op jit(solution)/shard_map/ppermute | solution.py:33
  36.4 14.5 %collective-permute-start.4 = (bf16[64,2048]{1,0:T(8,128)(2,1)}, bf16[64,2048]{1,0:T(8,128)(2,1)}, u32[]{:S(2)}, u32[]{:S(2)}) collective-permute-start(bf16[64,2048]{1,0:T(8,128)(2,1)} %bitcast.20), channel_id=1, source_target_pairs={{0,16},{4,20},{8,24},{12,28},{16,0},{20,4},{24,8},{28,12},{1,17},{... | collective-permute-start | bytes 786440 | tf_op jit(solution)/shard_map/ppermute | solution.py:33
  39.0 13.0 %collective-permute-start.2 = (bf16[64,2048]{1,0:T(8,128)(2,1)}, bf16[64,2048]{1,0:T(8,128)(2,1)}, u32[]{:S(2)}, u32[]{:S(2)}) collective-permute-start(bf16[64,2048]{1,0:T(8,128)(2,1)} %bitcast.21), channel_id=1, source_target_pairs={{0,8},{4,12},{8,0},{12,4},{16,24},{20,28},{24,16},{28,20},{1,9},{5... | collective-permute-start | bytes 786440 | tf_op jit(solution)/shard_map/ppermute | solution.py:33
  50.9 7.4 %collective-permute-start.6 = (bf16[64,2048]{1,0:T(8,128)(2,1)}, bf16[64,2048]{1,0:T(8,128)(2,1)}, u32[]{:S(2)}, u32[]{:S(2)}) collective-permute-start(bf16[64,2048]{1,0:T(8,128)(2,1)} %collective-permute-done.4.refs_10_.refs_5_), channel_id=1, source_target_pairs={{0,8},{4,12},{8,0},{12,4},{16,24},{20,28},{24,16},{28,20},{1,9},{5... | collective-permute-start | bytes 786440 | tf_op jit(solution)/shard_map/ppermute | solution.py:33
  51.4 16.5 %collective-permute-start.5 = (bf16[64,2048]{1,0:T(8,128)(2,1)}, bf16[64,2048]{1,0:T(8,128)(2,1)}, u32[]{:S(2)}, u32[]{:S(2)}) collective-permute-start(bf16[64,2048]{1,0:T(8,128)(2,1)} %collective-permute-done.4.refs_10_.refs_5_), channel_id=1, source_target_pairs={{0,4},{4,0},{8,12},{12,8},{16,20},{20,16},{24,28},{28,24},{1,5},{5... | collective-permute-start | bytes 786440 | tf_op jit(solution)/shard_map/ppermute | solution.py:33
  52.0 16.0 %collective-permute-start.3 = (bf16[64,2048]{1,0:T(8,128)(2,1)}, bf16[64,2048]{1,0:T(8,128)(2,1)}, u32[]{:S(2)}, u32[]{:S(2)}) collective-permute-start(bf16[64,2048]{1,0:T(8,128)(2,1)} %collective-permute-done.2.refs_9_.refs_3_), channel_id=1, source_target_pairs={{0,4},{4,0},{8,12},{12,8},{16,20},{20,16},{24,28},{28,24},{1,5},{5... | collective-permute-start | bytes 786440 | tf_op jit(solution)/shard_map/ppermute | solution.py:33
  58.3 12.7 %collective-permute-start.7 = (bf16[64,2048]{1,0:T(8,128)(2,1)}, bf16[64,2048]{1,0:T(8,128)(2,1)}, u32[]{:S(2)}, u32[]{:S(2)}) collective-permute-start(bf16[64,2048]{1,0:T(8,128)(2,1)} %collective-permute-done.6.refs_11_.refs_7_), channel_id=1, source_target_pairs={{0,4},{4,0},{8,12},{12,8},{16,20},{20,16},{24,28},{28,24},{1,5},{5... | collective-permute-start | bytes 786440 | tf_op jit(solution)/shard_map/ppermute | solution.py:33
  78.4 14.4 %collective-permute-start.12 = (bf16[256,1280]{1,0:T(8,128)(2,1)}, bf16[256,1280]{1,0:T(8,128)(2,1)}, u32[]{:S(2)}, u32[]{:S(2)}) collective-permute-start(bf16[256,1280]{1,0:T(8,128)(2,1)} %get-tuple-element.116), channel_id=1, source_target_pairs={{0,1},{1,0},{2,3},{3,2},{4,5},{5,4},{6,7},{7,6},{8,9},{9,8},{10,11... | collective-permute-start | bytes 1966088 | tf_op jit(solution)/shard_map/ppermute | solution.py:29
  78.4 2.8 collective-permute-start.13
  83.0 17.8 %collective-permute-start.15 = (bf16[256,512]{1,0:T(8,128)(2,1)}, bf16[256,512]{1,0:T(8,128)(2,1)}, u32[]{:S(2)}, u32[]{:S(2)}) collective-permute-start(bf16[256,512]{1,0:T(8,128)(2,1)} %get-tuple-element.125), channel_id=1, source_target_pairs={{0,2},{1,3},{2,0},{3,1},{4,6},{5,7},{6,4},{7,5},{8,10},{9,11},{10,... | collective-permute-start | bytes 786440 | tf_op jit(solution)/shard_map/ppermute | solution.py:29
  92.8 14.3 %collective-permute-start.17 = (bf16[256,1536]{1,0:T(8,128)(2,1)}, bf16[256,1536]{1,0:T(8,128)(2,1)}, u32[]{:S(2)}, u32[]{:S(2)}) collective-permute-start(bf16[256,1536]{1,0:T(8,128)(2,1)} %get-tuple-element.129), channel_id=1, source_target_pairs={{0,1},{1,0},{2,3},{3,2},{4,5},{5,4},{6,7},{7,6},{8,9},{9,8},{10,11... | collective-permute-start | bytes 2359304 | tf_op jit(solution)/shard_map/ppermute | solution.py:29
  95.1 17.4 %collective-permute-start.14 = (bf16[256,1280]{1,0:T(8,128)(2,1)}, bf16[256,1280]{1,0:T(8,128)(2,1)}, u32[]{:S(2)}, u32[]{:S(2)}) collective-permute-start(bf16[256,1280]{1,0:T(8,128)(2,1)} %get-tuple-element.124), channel_id=1, source_target_pairs={{0,2},{1,3},{2,0},{3,1},{4,6},{5,7},{6,4},{7,5},{8,10},{9,11},{10,... | collective-permute-start | bytes 1966088 | tf_op jit(solution)/shard_map/ppermute | solution.py:29
  106.8 4.0 %collective-permute-start.16 = (bf16[2,256,512]{2,1,0:T(8,128)(2,1)}, bf16[2,256,512]{2,1,0:T(8,128)(2,1)}, u32[]{:S(2)}, u32[]{:S(2)}) collective-permute-start(bf16[2,256,512]{2,1,0:T(8,128)(2,1)} %get-tuple-element.127), channel_id=1, source_target_pairs={{0,1},{1,0},{2,3},{3,2},{4,5},{5,4},{6,7},{7,6},{8,9},{9,8},{10,11... | collective-permute-start | bytes 1572872 | tf_op jit(solution)/shard_map/ppermute | solution.py:29
  109.5 20.1 %collective-permute-start.19 = (bf16[256,1536]{1,0:T(8,128)(2,1)}, bf16[256,1536]{1,0:T(8,128)(2,1)}, u32[]{:S(2)}, u32[]{:S(2)}) collective-permute-start(bf16[256,1536]{1,0:T(8,128)(2,1)} %get-tuple-element.134), channel_id=1, source_target_pairs={{0,2},{1,3},{2,0},{3,1},{4,6},{5,7},{6,4},{7,5},{8,10},{9,11},{10,... | collective-permute-start | bytes 2359304 | tf_op jit(solution)/shard_map/ppermute | solution.py:29
  123.0 16.8 %collective-permute-start.18 = (bf16[2,256,1280]{2,1,0:T(8,128)(2,1)}, bf16[2,256,1280]{2,1,0:T(8,128)(2,1)}, u32[]{:S(2)}, u32[]{:S(2)}) collective-permute-start(bf16[2,256,1280]{2,1,0:T(8,128)(2,1)} %get-tuple-element.133), channel_id=1, source_target_pairs={{0,1},{1,0},{2,3},{3,2},{4,5},{5,4},{6,7},{7,6},{8,9},{9,8},{10,11... | collective-permute-start | bytes 3932168 | tf_op jit(solution)/shard_map/ppermute | solution.py:29
  138.3 10.9 %collective-permute-start.22 = (bf16[2,256,1024]{2,1,0:T(8,128)(2,1)}, bf16[2,256,1024]{2,1,0:T(8,128)(2,1)}, u32[]{:S(2)}, u32[]{:S(2)}) collective-permute-start(bf16[2,256,1024]{2,1,0:T(8,128)(2,1)} %get-tuple-element.144), channel_id=1, source_target_pairs={{0,1},{1,0},{2,3},{3,2},{4,5},{5,4},{6,7},{7,6},{8,9},{9,8},{10,11... | collective-permute-start | bytes 3145736 | tf_op jit(solution)/shard_map/ppermute | solution.py:29
  138.3 15.1 %collective-permute-start.21 = (bf16[2,256,512]{2,1,0:T(8,128)(2,1)}, bf16[2,256,512]{2,1,0:T(8,128)(2,1)}, u32[]{:S(2)}, u32[]{:S(2)}) collective-permute-start(bf16[2,256,512]{2,1,0:T(8,128)(2,1)} %get-tuple-element.142), channel_id=1, source_target_pairs={{0,2},{1,3},{2,0},{3,1},{4,6},{5,7},{6,4},{7,5},{8,10},{9,11},{10,... | collective-permute-start | bytes 1572872 | tf_op jit(solution)/shard_map/ppermute | solution.py:29
  148.5 5.0 %collective-permute-start.20 = (bf16[2,256,512]{2,1,0:T(8,128)(2,1)}, bf16[2,256,512]{2,1,0:T(8,128)(2,1)}, u32[]{:S(2)}, u32[]{:S(2)}) collective-permute-start(bf16[2,256,512]{2,1,0:T(8,128)(2,1)} %get-tuple-element.141), channel_id=1, source_target_pairs={{0,1},{1,0},{2,3},{3,2},{4,5},{5,4},{6,7},{7,6},{8,9},{9,8},{10,11... | collective-permute-start | bytes 1572872 | tf_op jit(solution)/shard_map/ppermute | solution.py:29
  148.6 32.5 %collective-permute-start.25 = (bf16[2,256,1280]{2,1,0:T(8,128)(2,1)}, bf16[2,256,1280]{2,1,0:T(8,128)(2,1)}, u32[]{:S(2)}, u32[]{:S(2)}) collective-permute-start(bf16[2,256,1280]{2,1,0:T(8,128)(2,1)} %get-tuple-element.150), channel_id=1, source_target_pairs={{0,2},{1,3},{2,0},{3,1},{4,6},{5,7},{6,4},{7,5},{8,10},{9,11},{10,... | collective-permute-start | bytes 3932168 | tf_op jit(solution)/shard_map/ppermute | solution.py:29
  156.3 2.6 collective-permute-start.26
  187.3 4.3 %collective-permute-start.27 = (bf16[3,256,1280]{2,1,0:T(8,128)(2,1)}, bf16[3,256,1280]{2,1,0:T(8,128)(2,1)}, u32[]{:S(2)}, u32[]{:S(2)}) collective-permute-start(bf16[3,256,1280]{2,1,0:T(8,128)(2,1)} %get-tuple-element.156.refs_0_.refs_2_), channel_id=1, source_target_pairs={{0,1},{1,0},{2,3},{3,2},{4,5},{5,4},{6,7},{7,6},{8,9},{9,8},{10,11... | collective-permute-start | bytes 5898248 | tf_op jit(solution)/shard_map/ppermute | solution.py:29
  187.3 25.9 %collective-permute-start.24 = (bf16[2,256,1024]{2,1,0:T(8,128)(2,1)}, bf16[2,256,1024]{2,1,0:T(8,128)(2,1)}, u32[]{:S(2)}, u32[]{:S(2)}) collective-permute-start(bf16[2,256,1024]{2,1,0:T(8,128)(2,1)} %get-tuple-element.149), channel_id=1, source_target_pairs={{0,2},{1,3},{2,0},{3,1},{4,6},{5,7},{6,4},{7,5},{8,10},{9,11},{10,... | collective-permute-start | bytes 3145736 | tf_op jit(solution)/shard_map/ppermute | solution.py:29
  218.1 3.8 %collective-permute-start.28 = (bf16[3,256,1024]{2,1,0:T(8,128)(2,1)}, bf16[3,256,1024]{2,1,0:T(8,128)(2,1)}, u32[]{:S(2)}, u32[]{:S(2)}) collective-permute-start(bf16[3,256,1024]{2,1,0:T(8,128)(2,1)} %get-tuple-element.161.refs_0_.refs_2_), channel_id=1, source_target_pairs={{0,1},{1,0},{2,3},{3,2},{4,5},{5,4},{6,7},{7,6},{8,9},{9,8},{10,11... | collective-permute-start | bytes 4718600 | tf_op jit(solution)/shard_map/ppermute | solution.py:29
  218.1 17.7 %collective-permute-start.23 = (bf16[2,256,512]{2,1,0:T(8,128)(2,1)}, bf16[2,256,512]{2,1,0:T(8,128)(2,1)}, u32[]{:S(2)}, u32[]{:S(2)}) collective-permute-start(bf16[2,256,512]{2,1,0:T(8,128)(2,1)} %get-tuple-element.148), channel_id=1, source_target_pairs={{0,2},{1,3},{2,0},{3,1},{4,6},{5,7},{6,4},{7,5},{8,10},{9,11},{10,... | collective-permute-start | bytes 1572872 | tf_op jit(solution)/shard_map/ppermute | solution.py:29
  238.6 2.6 collective-permute-start.29
  248.8 26.3 %collective-permute-start.31 = (bf16[4,4,16,2048]{3,2,1,0:T(8,128)(2,1)}, bf16[4,4,16,2048]{3,2,1,0:T(8,128)(2,1)}, u32[]{:S(2)}, u32[]{:S(2)}) collective-permute-start(bf16[4,4,16,2048]{3,2,1,0:T(8,128)(2,1)} %get-tuple-element.181), channel_id=1, source_target_pairs={{0,4},{4,0},{8,12},{12,8},{16,20},{20,16},{24,28},{28,24},{1,5},{5... | collective-permute-start | bytes 3145736 | tf_op jit(solution)/shard_map/ppermute | solution.py:33
  256.9 39.9 %collective-permute-start.30 = (bf16[4,4,16,2048]{3,2,1,0:T(8,128)(2,1)}, bf16[4,4,16,2048]{3,2,1,0:T(8,128)(2,1)}, u32[]{:S(2)}, u32[]{:S(2)}) collective-permute-start(bf16[4,4,16,2048]{3,2,1,0:T(8,128)(2,1)} %get-tuple-element.172), channel_id=1, source_target_pairs={{0,4},{4,0},{8,12},{12,8},{16,20},{20,16},{24,28},{28,24},{1,5},{5... | collective-permute-start | bytes 3145736 | tf_op jit(solution)/shard_map/ppermute | solution.py:33
  278.3 23.3 %collective-permute-start.33 = (bf16[2,4,16,2048]{3,2,1,0:T(8,128)(2,1)}, bf16[2,4,16,2048]{3,2,1,0:T(8,128)(2,1)}, u32[]{:S(2)}, u32[]{:S(2)}) collective-permute-start(bf16[2,4,16,2048]{3,2,1,0:T(8,128)(2,1)} %get-tuple-element.191), channel_id=1, source_target_pairs={{0,8},{4,12},{8,0},{12,4},{16,24},{20,28},{24,16},{28,20},{1,9},{5... | collective-permute-start | bytes 1572872 | tf_op jit(solution)/shard_map/ppermute | solution.py:33
  299.9 19.1 %collective-permute-start.32 = (bf16[2,4,16,2048]{3,2,1,0:T(8,128)(2,1)}, bf16[2,4,16,2048]{3,2,1,0:T(8,128)(2,1)}, u32[]{:S(2)}, u32[]{:S(2)}) collective-permute-start(bf16[2,4,16,2048]{3,2,1,0:T(8,128)(2,1)} %get-tuple-element.186), channel_id=1, source_target_pairs={{0,8},{4,12},{8,0},{12,4},{16,24},{20,28},{24,16},{28,20},{1,9},{5... | collective-permute-start | bytes 1572872 | tf_op jit(solution)/shard_map/ppermute | solution.py:33
  304.0 19.1 %collective-permute-start.35 = (bf16[1,4,16,2048]{3,2,1,0:T(8,128)(2,1)}, bf16[1,4,16,2048]{3,2,1,0:T(8,128)(2,1)}, u32[]{:S(2)}, u32[]{:S(2)}) collective-permute-start(bf16[1,4,16,2048]{3,2,1,0:T(8,128)(2,1)} %get-tuple-element.198), channel_id=1, source_target_pairs={{0,16},{4,20},{8,24},{12,28},{16,0},{20,4},{24,8},{28,12},{1,17},{... | collective-permute-start | bytes 786440 | tf_op jit(solution)/shard_map/ppermute | solution.py:33
  321.3 13.8 %collective-permute-start.34 = (bf16[1,4,16,2048]{3,2,1,0:T(8,128)(2,1)}, bf16[1,4,16,2048]{3,2,1,0:T(8,128)(2,1)}, u32[]{:S(2)}, u32[]{:S(2)}) collective-permute-start(bf16[1,4,16,2048]{3,2,1,0:T(8,128)(2,1)} %get-tuple-element.196), channel_id=1, source_target_pairs={{0,16},{4,20},{8,24},{12,28},{16,0},{20,4},{24,8},{28,12},{1,17},{... | collective-permute-start | bytes 786440 | tf_op jit(solution)/shard_map/ppermute | solution.py:33
  325.6 1.9 collective-permute-start.36
  325.6 4.9 %collective-permute-start.37 = (bf16[16,2048]{1,0:T(8,128)(2,1)}, bf16[16,2048]{1,0:T(8,128)(2,1)S(1)}, u32[]{:S(2)}, u32[]{:S(2)}) collective-permute-start(bf16[16,2048]{1,0:T(8,128)(2,1)} %get-tuple-element.202), channel_id=1, source_target_pairs={{0,2},{1,3},{2,0},{3,1},{4,6},{5,7},{6,4},{7,5},{8,10},{9,11},{10,... | collective-permute-start | bytes 196616 | tf_op jit(solution)/shard_map/ppermute | solution.py:29
  326.9 4.6 %collective-permute-start.38 = (bf16[16,2048]{1,0:T(8,128)(2,1)}, bf16[16,2048]{1,0:T(8,128)(2,1)S(1)}, u32[]{:S(2)}, u32[]{:S(2)}) collective-permute-start(bf16[16,2048]{1,0:T(8,128)(2,1)} %get-tuple-element.203), channel_id=1, source_target_pairs={{0,3},{1,2},{2,1},{3,0},{4,7},{5,6},{6,5},{7,4},{8,11},{9,10},{10,... | collective-permute-start | bytes 196616 | tf_op jit(solution)/shard_map/ppermute | solution.py:29
  327.4 4.0 %copy-start.4 = (bf16[16,2048]{1,0:T(8,128)(2,1)}, bf16[16,2048]{1,0:T(8,128)(2,1)S(1)}, u32[]{:S(2)}) copy-start(bf16[16,2048]{1,0:T(8,128)(2,1)S(1)} %collective-permute-done.36.refs_2_) | copy-start | bytes 196612
  330.5 1.0 copy-start.5
  331.5 0.6 copy-start.6

commit v10 on v8

--- a/solution.py
+++ b/solution.py
@@ -513,12 +513,12 @@
     all_grads(0)
     elementwise(1)
     add_both(1)
+    all_grads(1)
     elementwise(2)
     add_both(2)
     elementwise(3)
     grad_part = last_part(grad_term())
     out_parts = [last_part(out_term(), 2, 0), last_part(out_term(), 2, 1)]
-    all_grads(1)
     grad_part = over_z(grad_part, 2)
     all_grads(2)
     out_parts[0] = over_z(out_parts[0], 2)

time: 338 us -> 345 us (1.021)
  waiting for transfers between devices: 73.2 us -> 80.6 us
    ppermute x21, waiting for transfers between devices: 36 us -> 48.7 us  [swap_wide(): return lax.ppermute(value, 'wide', [(i, i ^ mask) for i in range(8)])]
    ppermute x21, waiting for transfers between devices: 33.5 us -> 28.2 us  [swap(): return lax.ppermute(value, 'narrow', [(i, i ^ mask) for i in range(4)])]
  transfers between devices with their start and end apart: 43 -> 43, of which waited for: 21 -> 20; matrix products, arithmetic and copies ran while one was open for 0% -> 0% of each run, Pallas kernels for 53% -> 52%
where the time goes in v10:
time: 345 us; the launch traced here: 344 us
  Pallas kernels  213 us (62%)
  waiting for transfers between devices  80.6 us (23%)
  starting transfers between devices  46.1 us (13%)
    pallas_call x41, Pallas kernels, __call__(): pl.pallas_call(kernel, grid_spec=pltpu.PrefetchScalarGridSpec(num_scalar_...  213 us
    ppermute x21, waiting for transfers between devices, swap_wide(): return lax.ppermute(value, 'wide', [(i, i ^ mask) for i in range(8)])  48.7 us
    ppermute x21, starting transfers between devices, swap_wide(): return lax.ppermute(value, 'wide', [(i, i ^ mask) for i in range(8)])  31.4 us
    ppermute x21, waiting for transfers between devices, swap(): return lax.ppermute(value, 'narrow', [(i, i ^ mask) for i in range(4)])  28.2 us
    ppermute x21, starting transfers between devices, swap(): return lax.ppermute(value, 'narrow', [(i, i ^ mask) for i in range(4)])  11.3 us
  transfers between devices with their start and end apart: 43, of which 20 were waited for; matrix products, arithmetic and copies ran while one was open for 0% of the time, Pallas kernels for 52%

profile of v10, /device:TPU:0, one launch (start us, length us, event | category | flops | bytes accessed | tf_op | source)
XLA Modules:
  0.0 343.6 jit_solution(7827539920915349845)
XLA Ops:
  0.6 3.0 collective-permute-start
  3.7 2.6 collective-permute-start.9
  6.3 4.0 %collective-permute-done.refs_1_.refs_2_ = bf16[64,2048]{1,0:T(8,128)(2,1)} collective-permute-done((bf16[64,2048]{1,0:T(8,128)(2,1)}, bf16[64,2048]{1,0:T(8,128)(2,1)}, u32[]{:S(2)}, u32[]{:S(2)}) %collective-permute-start) | collective-permute-done | bytes 262176 | tf_op jit(solution)/shard_map/ppermute | solution.py:33
  10.3 3.0 shard_map.92
  13.2 3.4 all-to-all-start
  18.9 3.7 %all-to-all-done = bf16[4,16,2048]{2,1,0:T(8,128)(2,1)S(1)} async-done(((bf16[4,16,2048]{2,1,0:T(8,128)(2,1)}), bf16[4,16,2048]{2,1,0:T(8,128)(2,1)S(1)}, u32[]{:S(2)}, u32[]{:S(2)}) %all-to-all-start) | async-done | bytes 262176 | tf_op jit(solution)/shard_map/all_to_all | solution.py:474
  26.0 5.2 %collective-permute-done.10.refs_2_.refs_7_ = bf16[64,2048]{1,0:T(8,128)(2,1)S(1)} collective-permute-done((bf16[64,2048]{1,0:T(8,128)(2,1)}, bf16[64,2048]{1,0:T(8,128)(2,1)S(1)}, u32[]{:S(2)}, u32[]{:S(2)}) %collective-permute-start.10) | collective-permute-done | bytes 262176 | tf_op jit(solution)/shard_map/ppermute | solution.py:33
  36.4 2.6 collective-permute-start.4
  40.5 10.3 %collective-permute-done.4.refs_10_.refs_5_ = bf16[64,2048]{1,0:T(8,128)(2,1)} collective-permute-done((bf16[64,2048]{1,0:T(8,128)(2,1)}, bf16[64,2048]{1,0:T(8,128)(2,1)}, u32[]{:S(2)}, u32[]{:S(2)}) %collective-permute-start.4) | collective-permute-done | bytes 262176 | tf_op jit(solution)/shard_map/ppermute | solution.py:33
  53.5 4.8 %collective-permute-done.6.refs_11_.refs_7_ = bf16[64,2048]{1,0:T(8,128)(2,1)} collective-permute-done((bf16[64,2048]{1,0:T(8,128)(2,1)}, bf16[64,2048]{1,0:T(8,128)(2,1)}, u32[]{:S(2)}, u32[]{:S(2)}) %collective-permute-start.6) | collective-permute-done | bytes 262176 | tf_op jit(solution)/shard_map/ppermute | solution.py:33
  59.4 4.5 %shard_map.94 = (bf16[4,8,16,2048]{3,2,1,0:T(8,128)(2,1)}, f32[8,128]{1,0:T(8,128)}) custom-call(s32[2]{0:T(128)} %pad_add_fusion.refs_0_, bf16[64,2048]{1,0:T(8,128)(2,1)} %refs_1_.8, bf16[64,2048]{1,0:T(8,128)(2,1)} %collective-permute-done.refs_1_.refs_2_, bf16[64,2048]{1,0:T(8,128)(2,1)} %copy-done.2, bf16[192,2048]{1,0:T(8,128)(2,1)} %bitcast.3.refs_4_.refs_6_.refs_8_, ...), custom_call_target="tpu_custom_call" | custom-call | flops 1 | bytes 1 | tf_op jit(solution)/shard_map/pallas_call | solution.py:66
  63.9 4.1 %shard_map.95 = (f32[256,512]{1,0:T(8,128)}, bf16[256,512]{1,0:T(8,128)(2,1)}, f32[8,128]{1,0:T(8,128)}) custom-call(bf16[512,2048]{1,0:T(8,128)(2,1)} %bitcast.7, bf16[3328,2048]{1,0:T(8,128)(2,1)} %refs_3_.11, f32[8,128]{1,0:T(8,128)} %get-tuple-element.122.refs_2_), custom_call_target="tpu_custom_call" | custom-call | flops 1 | bytes 1 | tf_op jit(solution)/shard_map/pallas_call | solution.py:66
  68.0 3.0 collective-permute-done.7.refs_4_.refs_8_
  70.9 7.5 %shard_map.96 = (f32[256,1280]{1,0:T(8,128)}, bf16[256,1280]{1,0:T(8,128)(2,1)}, f32[8,128]{1,0:T(8,128)}) custom-call(bf16[512,2048]{1,0:T(8,128)(2,1)} %bitcast.8, bf16[3328,2048]{1,0:T(8,128)(2,1)} %refs_3_.11, bf16[64,2048]{1,0:T(8,128)(2,1)} %collective-permute-done.3.refs_2_.refs_4_, bf16[64,2048]{1,0:T(8,128)(2,1)} %collective-permute-done.5.refs_3_.refs_6_, ...), custom_call_target="tpu_custom_call" | custom-call | flops 1 | bytes 1 | tf_op jit(solution)/shard_map/pallas_call | solution.py:66
  84.4 8.4 %shard_map.98 = (f32[256,1536]{1,0:T(8,128)}, bf16[256,1536]{1,0:T(8,128)(2,1)}, f32[8,128]{1,0:T(8,128)}) custom-call(bf16[512,2048]{1,0:T(8,128)(2,1)} %bitcast.9, bf16[3328,2048]{1,0:T(8,128)(2,1)} %refs_3_.11, f32[8,128]{1,0:T(8,128)} %get-tuple-element.129.refs_2_), custom_call_target="tpu_custom_call" | custom-call | flops 1 | bytes 1 | tf_op jit(solution)/shard_map/pallas_call | solution.py:66
  95.8 5.1 %shard_map.100 = (bf16[4,8,16,2048]{3,2,1,0:T(8,128)(2,1)}, bf16[2048,512]{1,0:T(8,128)(2,1)}, f32[8,128]{1,0:T(8,128)}) custom-call(s32[2]{0:T(128)} %pad_add_fusion.refs_0_, bf16[64,2048]{1,0:T(8,128)(2,1)} %bitcast.22, bf16[64,2048]{1,0:T(8,128)(2,1)} %copy-done.1, bf16[64,2048]{1,0:T(8,128)(2,1)} %collective-permute-done.2.refs_9_.refs_3_, ...), custom_call_target="tpu_custom_call" | custom-call | flops 1 | bytes 1 | tf_op jit(solution)/shard_map/pallas_call | solution.py:66
  100.9 6.0 %shard_map.101 = (f32[2,256,512]{2,1,0:T(8,128)}, bf16[2,256,512]{2,1,0:T(8,128)(2,1)}, f32[8,128]{1,0:T(8,128)}) custom-call(bf16[512,2048]{1,0:T(8,128)(2,1)} %bitcast.14, bf16[2048,3328]{1,0:T(8,128)(2,1)} %refs_3_.9, bf16[2048,3328]{1,0:T(8,128)(2,1)} %refs_5_.7, bf16[256,512]{1,0:T(8,128)(2,1)} %collective-permute-done.15.refs_3_.refs_5_, ...), custom_call_target="tpu_custom_call" | custom-call | flops 1 | bytes 1 | tf_op jit(solution)/shard_map/pallas_call | solution.py:66
  112.6 10.4 %shard_map.103 = (f32[2,256,1280]{2,1,0:T(8,128)}, bf16[2,256,1280]{2,1,0:T(8,128)(2,1)}, f32[8,128]{1,0:T(8,128)}) custom-call(bf16[512,2048]{1,0:T(8,128)(2,1)} %bitcast.15, bf16[2048,3328]{1,0:T(8,128)(2,1)} %refs_3_.9, bf16[2048,3328]{1,0:T(8,128)(2,1)} %refs_5_.7, bf16[256,1280]{1,0:T(8,128)(2,1)} %collective-permute-done.14.refs_3_.refs_5_, ...), custom_call_target="tpu_custom_call" | custom-call | flops 1 | bytes 1 | tf_op jit(solution)/shard_map/pallas_call | solution.py:66
  125.1 4.5 %collective-permute-done.19.refs_3_.refs_5_ = bf16[256,1536]{1,0:T(8,128)(2,1)} collective-permute-done((bf16[256,1536]{1,0:T(8,128)(2,1)}, bf16[256,1536]{1,0:T(8,128)(2,1)}, u32[]{:S(2)}, u32[]{:S(2)}) %collective-permute-start.19) | collective-permute-done | bytes 786464 | tf_op jit(solution)/shard_map/ppermute | solution.py:29
  129.6 8.8 %shard_map.105 = (f32[2,256,1024]{2,1,0:T(8,128)}, bf16[2,256,1024]{2,1,0:T(8,128)(2,1)}, f32[8,128]{1,0:T(8,128)}) custom-call(bf16[512,2048]{1,0:T(8,128)(2,1)} %bitcast.16, bf16[2048,3328]{1,0:T(8,128)(2,1)} %refs_3_.9, bf16[2048,3328]{1,0:T(8,128)(2,1)} %refs_5_.7, bf16[256,1536]{1,0:T(8,128)(2,1)} %collective-permute-done.19.refs_3_.refs_5_, ...), custom_call_target="tpu_custom_call" | custom-call | flops 1 | bytes 1 | tf_op jit(solution)/shard_map/pallas_call | solution.py:66
  139.8 3.0 shard_map.106
  142.9 5.6 %shard_map.107 = (f32[2,256,512]{2,1,0:T(8,128)}, bf16[2,256,512]{2,1,0:T(8,128)(2,1)}, f32[8,128]{1,0:T(8,128)}) custom-call(bf16[512,2048]{1,0:T(8,128)(2,1)} %bitcast.17, bf16[2048,3328]{1,0:T(8,128)(2,1)} %refs_3_.9, bf16[2048,3328]{1,0:T(8,128)(2,1)} %refs_5_.7, f32[8,128]{1,0:T(8,128)} %get-tuple-element.148.refs_3_), custom_call_target="tpu_custom_call" | custom-call | flops 1 | bytes 1 | tf_op jit(solution)/shard_map/pallas_call | solution.py:66
  149.3 2.8 shard_map.108
  153.5 2.8 shard_map.109
  158.9 8.7 %shard_map.111 = (f32[512,2048]{1,0:T(8,128)}, f32[512,2048]{1,0:T(8,128)}, f32[8,128]{1,0:T(8,128)}) custom-call(bf16[3,256,512]{2,1,0:T(8,128)(2,1)} %get-tuple-element.161.refs_0_.refs_2_, bf16[3,256,512]{2,1,0:T(8,128)(2,1)} %collective-permute-done.26.refs_1_.refs_3_, bf16[3328,2048]{1,0:T(8,128)(2,1)} %refs_3_.11, bf16[3328,2048]{1,0:T(8,128)(2,1)} %refs_3_.11, ...), custom_call_target="tpu_custom_call" | custom-call | flops 1 | bytes 1 | tf_op jit(solution)/shard_map/pallas_call | solution.py:66
  167.7 7.3 %shard_map.112 = (bf16[2048,3328]{1,0:T(8,128)(2,1)}, bf16[2048,3328]{1,0:T(8,128)(2,1)}, bf16[3328,2048]{1,0:T(8,128)(2,1)}, f32[8,128]{1,0:T(8,128)}) custom-call(bf16[2048,512]{1,0:T(8,128)(2,1)} %get-tuple-element.159.refs_0_, bf16[512,2048]{1,0:T(8,128)(2,1)} %bitcast.10, bf16[3,256,512]{2,1,0:T(8,128)(2,1)} %get-tuple-element.161.refs_0_.refs_2_, ...), custom_call_target="tpu_custom_call" | custom-call | flops 1 | bytes 1 | tf_op jit(solution)/shard_map/pallas_call | solution.py:66
  175.0 6.2 %collective-permute-done.25.refs_2_ = bf16[2,256,1280]{2,1,0:T(8,128)(2,1)} collective-permute-done((bf16[2,256,1280]{2,1,0:T(8,128)(2,1)}, bf16[2,256,1280]{2,1,0:T(8,128)(2,1)}, u32[]{:S(2)}, u32[]{:S(2)}) %collective-permute-start.25) | collective-permute-done | bytes 1310752 | tf_op jit(solution)/shard_map/ppermute | solution.py:29
  181.1 6.3 %shard_map.113 = (bf16[3,256,1280]{2,1,0:T(8,128)(2,1)}, f32[8,128]{1,0:T(8,128)}) custom-call(f32[2,256,1280]{2,1,0:T(8,128)} %get-tuple-element.141.refs_0_, bf16[2,256,1280]{2,1,0:T(8,128)(2,1)} %collective-permute-done.18.refs_1_, bf16[2,256,1280]{2,1,0:T(8,128)(2,1)} %collective-permute-done.25.refs_2_, f32[256,1280]{1,0:T(8,128)} %get-tuple-element.124.refs_0_.refs_3_, ...), custom_call_target="tpu_custom_call" | custom-call | flops 1 | bytes 1 | tf_op jit(solution)/shard_map/pallas_call | solution.py:66
  188.8 2.9 collective-permute-done.27.refs_1_.refs_3_
  191.7 16.0 %shard_map.114 = (f32[512,2048]{1,0:T(8,128)}, f32[512,2048]{1,0:T(8,128)}, f32[8,128]{1,0:T(8,128)}) custom-call(bf16[3,256,1280]{2,1,0:T(8,128)(2,1)} %get-tuple-element.165.refs_0_.refs_2_, bf16[3,256,1280]{2,1,0:T(8,128)(2,1)} %collective-permute-done.27.refs_1_.refs_3_, ...), custom_call_target="tpu_custom_call", output_to_operand_aliasing={{0}: (7, {}), {1}: (18, {})} | custom-call | flops 1 | bytes 1 | tf_op jit(solution)/shard_map/pallas_call | solution.py:66
  207.7 12.8 %shard_map.115 = (bf16[2048,3328]{1,0:T(8,128)(2,1)}, bf16[2048,3328]{1,0:T(8,128)(2,1)}, bf16[3328,2048]{1,0:T(8,128)(2,1)}, f32[8,128]{1,0:T(8,128)}) custom-call(bf16[2048,512]{1,0:T(8,128)(2,1)} %get-tuple-element.159.refs_0_, bf16[512,2048]{1,0:T(8,128)(2,1)} %bitcast.11, ...), custom_call_target="tpu_custom_call", output_to_operand_aliasing={{0}: (4, {}), {1}: (5, {}), {2}: (6, {})} | custom-call | flops 1 | bytes 1 | tf_op jit(solution)/shard_map/pallas_call | solution.py:66
  220.6 4.9 %shard_map.116 = (bf16[3,256,1024]{2,1,0:T(8,128)(2,1)}, f32[8,128]{1,0:T(8,128)}) custom-call(f32[2,256,1024]{2,1,0:T(8,128)} %get-tuple-element.152.refs_0_, bf16[2,256,1024]{2,1,0:T(8,128)(2,1)} %collective-permute-done.22.refs_1_, bf16[2,256,1024]{2,1,0:T(8,128)(2,1)} %collective-permute-done.24.refs_2_, f32[256,1536]{1,0:T(8,128)} %get-tuple-element.137.refs_0_.refs_3_, ...), custom_call_target="tpu_custom_call" | custom-call | flops 1 | bytes 1 | tf_op jit(solution)/shard_map/pallas_call | solution.py:66
  229.2 13.9 %shard_map.117 = (f32[512,2048]{1,0:T(8,128)}, f32[512,2048]{1,0:T(8,128)}, f32[8,128]{1,0:T(8,128)}) custom-call(bf16[3,256,1024]{2,1,0:T(8,128)(2,1)} %get-tuple-element.174.refs_0_.refs_2_, bf16[3,256,1024]{2,1,0:T(8,128)(2,1)} %collective-permute-done.28.refs_1_.refs_3_, ...), custom_call_target="tpu_custom_call", output_to_operand_aliasing={{0}: (6, {}), {1}: (15, {})} | custom-call | flops 1 | bytes 1 | tf_op jit(solution)/shard_map/pallas_call | solution.py:66
  243.1 2.9 shard_map.118
  246.1 2.5 collective-permute-done.29.refs_1_.refs_3_
  248.6 7.6 %shard_map.119 = (f32[4,4,16,2048]{3,2,1,0:T(8,128)}, bf16[4,4,16,2048]{3,2,1,0:T(8,128)(2,1)}, f32[8,128]{1,0:T(8,128)}) custom-call(bf16[3,256,512]{2,1,0:T(8,128)(2,1)} %get-tuple-element.179.refs_0_.refs_2_, bf16[3,256,512]{2,1,0:T(8,128)(2,1)} %collective-permute-done.29.refs_1_.refs_3_, bf16[2048,3328]{1,0:T(8,128)(2,1)} %refs_3_.9, ...), custom_call_target="tpu_custom_call" | custom-call | flops 1 | bytes 1 | tf_op jit(solution)/shard_map/pallas_call | solution.py:66
  257.9 3.9 %shard_map.120 = (f32[4,4,16,1024]{3,2,1,0:T(8,128)}, bf16[4,4,16,1024]{3,2,1,0:T(8,128)(2,1)}, f32[8,128]{1,0:T(8,128)}) custom-call(bf16[3,256,512]{2,1,0:T(8,128)(2,1)} %get-tuple-element.179.refs_0_.refs_2_, bf16[3,256,512]{2,1,0:T(8,128)(2,1)} %collective-permute-done.29.refs_1_.refs_3_, bf16[3328,2048]{1,0:T(8,128)(2,1)} %refs_3_.11, ...), custom_call_target="tpu_custom_call" | custom-call | flops 1 | bytes 1 | tf_op jit(solution)/shard_map/pallas_call | solution.py:66
  262.1 3.8 %shard_map.121 = (f32[4,4,16,1024]{3,2,1,0:T(8,128)}, bf16[4,4,16,1024]{3,2,1,0:T(8,128)(2,1)}, f32[8,128]{1,0:T(8,128)}) custom-call(bf16[3,256,512]{2,1,0:T(8,128)(2,1)} %get-tuple-element.179.refs_0_.refs_2_, bf16[3,256,512]{2,1,0:T(8,128)(2,1)} %collective-permute-done.29.refs_1_.refs_3_, bf16[3328,2048]{1,0:T(8,128)(2,1)} %refs_3_.11, ...), custom_call_target="tpu_custom_call" | custom-call | flops 1 | bytes 1 | tf_op jit(solution)/shard_map/pallas_call | solution.py:66
  265.9 16.6 %collective-permute-done.31.refs_1_ = bf16[4,4,16,2048]{3,2,1,0:T(8,128)(2,1)} collective-permute-done((bf16[4,4,16,2048]{3,2,1,0:T(8,128)(2,1)}, bf16[4,4,16,2048]{3,2,1,0:T(8,128)(2,1)}, u32[]{:S(2)}, u32[]{:S(2)}) %collective-permute-start.31) | collective-permute-done | bytes 1048608 | tf_op jit(solution)/shard_map/ppermute | solution.py:33
  282.5 3.1 shard_map.122
  288.9 11.0 %shard_map.123 = (bf16[2048,3328]{1,0:T(8,128)(2,1)}, bf16[2048,3328]{1,0:T(8,128)(2,1)}, bf16[3328,2048]{1,0:T(8,128)(2,1)}, f32[8,128]{1,0:T(8,128)}) custom-call(bf16[2048,512]{1,0:T(8,128)(2,1)} %get-tuple-element.159.refs_0_, bf16[512,2048]{1,0:T(8,128)(2,1)} %bitcast.12, ...), custom_call_target="tpu_custom_call", output_to_operand_aliasing={{0}: (4, {}), {1}: (5, {}), {2}: (6, {})} | custom-call | flops 1 | bytes 1 | tf_op jit(solution)/shard_map/pallas_call | solution.py:66
  304.9 2.6 collective-permute-start.37
  311.3 3.7 %collective-permute-done.32.refs_1_ = bf16[2,4,16,1024]{3,2,1,0:T(8,128)(2,1)} collective-permute-done((bf16[2,4,16,1024]{3,2,1,0:T(8,128)(2,1)}, bf16[2,4,16,1024]{3,2,1,0:T(8,128)(2,1)}, u32[]{:S(2)}, u32[]{:S(2)}) %collective-permute-start.32) | collective-permute-done | bytes 262176 | tf_op jit(solution)/shard_map/ppermute | solution.py:33
  316.9 7.3 %shard_map.128 = (bf16[2048,3328]{1,0:T(8,128)(2,1)}, bf16[2048,3328]{1,0:T(8,128)(2,1)}, bf16[3328,2048]{1,0:T(8,128)(2,1)}, f32[8,128]{1,0:T(8,128)}) custom-call(bf16[2048,512]{1,0:T(8,128)(2,1)} %get-tuple-element.159.refs_0_, bf16[512,2048]{1,0:T(8,128)(2,1)} %bitcast.13, ...), custom_call_target="tpu_custom_call", output_to_operand_aliasing={{0}: (4, {}), {1}: (5, {}), {2}: (6, {})} | custom-call | flops 1 | bytes 1 | tf_op jit(solution)/shard_map/pallas_call | solution.py:66
  328.6 2.9 collective-permute-start.38
  333.4 3.2 collective-permute-done.40.refs_3_
  337.5 2.9 shard_map.131
  341.1 2.5 shard_map.132
  (92 shorter events, 68.3 us)
Async XLA Ops:
  0.6 9.7 %collective-permute-start = (bf16[64,2048]{1,0:T(8,128)(2,1)}, bf16[64,2048]{1,0:T(8,128)(2,1)}, u32[]{:S(2)}, u32[]{:S(2)}) collective-permute-start(bf16[64,2048]{1,0:T(8,128)(2,1)} %refs_1_.8), channel_id=1, source_target_pairs={{0,4},{4,0},{8,12},{12,8},{16,20},{20,16},{24,28},{28,24},{1,5},{5... | collective-permute-start | bytes 786440 | tf_op jit(solution)/shard_map/ppermute | solution.py:33
  3.7 14.9 %collective-permute-start.9 = (bf16[64,2048]{1,0:T(8,128)(2,1)}, bf16[64,2048]{1,0:T(8,128)(2,1)}, u32[]{:S(2)}, u32[]{:S(2)}) collective-permute-start(bf16[64,2048]{1,0:T(8,128)(2,1)} %refs_1_.8), channel_id=1, source_target_pairs={{0,16},{4,20},{8,24},{12,28},{16,0},{20,4},{24,8},{28,12},{1,17},{... | collective-permute-start | bytes 786440 | tf_op jit(solution)/shard_map/ppermute | solution.py:33
  13.2 9.4 %all-to-all-start = ((bf16[4,16,2048]{2,1,0:T(8,128)(2,1)}), bf16[4,16,2048]{2,1,0:T(8,128)(2,1)S(1)}, u32[]{:S(2)}, u32[]{:S(2)}) async-start(bf16[4,16,2048]{2,1,0:T(8,128)(2,1)} %get-tuple-element.117), calls=%async_computation | async-start | bytes 524288 | tf_op jit(solution)/shard_map/all_to_all | solution.py:474
  16.7 9.4 %collective-permute-start.8 = (bf16[64,2048]{1,0:T(8,128)(2,1)}, bf16[64,2048]{1,0:T(8,128)(2,1)S(1)}, u32[]{:S(2)}, u32[]{:S(2)}) collective-permute-start(bf16[64,2048]{1,0:T(8,128)(2,1)} %refs_1_.8), channel_id=1, source_target_pairs={{0,8},{4,12},{8,0},{12,4},{16,24},{20,28},{24,16},{28,20},{1,9},{5... | collective-permute-start | bytes 786440 | tf_op jit(solution)/shard_map/ppermute | solution.py:33
  18.5 12.7 %collective-permute-start.10 = (bf16[64,2048]{1,0:T(8,128)(2,1)}, bf16[64,2048]{1,0:T(8,128)(2,1)S(1)}, u32[]{:S(2)}, u32[]{:S(2)}) collective-permute-start(bf16[64,2048]{1,0:T(8,128)(2,1)} %collective-permute-done.9.refs_1_.refs_5_), channel_id=1, source_target_pairs={{0,8},{4,12},{8,0},{12,4},{16,24},{20,28},{24,16},{28,20},{1,9},{5... | collective-permute-start | bytes 786440 | tf_op jit(solution)/shard_map/ppermute | solution.py:33
  22.7 0.7 copy-start
  23.4 7.9 %collective-permute-start.1 = (bf16[64,2048]{1,0:T(8,128)(2,1)S(1)}, bf16[64,2048]{1,0:T(8,128)(2,1)S(1)}, u32[]{:S(2)}, u32[]{:S(2)}) collective-permute-start(bf16[64,2048]{1,0:T(8,128)(2,1)S(1)} %bitcast.18), channel_id=1, source_target_pairs={{0,4},{4,0},{8,12},{12,8},{16,20},{20,16},{24,28},{28,24},{1,5},{5... | collective-permute-start | bytes 786440 | tf_op jit(solution)/shard_map/ppermute | solution.py:33
  26.0 5.2 %copy-start.2 = (bf16[64,2048]{1,0:T(8,128)(2,1)}, bf16[64,2048]{1,0:T(8,128)(2,1)S(1)}, u32[]{:S(2)}) copy-start(bf16[64,2048]{1,0:T(8,128)(2,1)S(1)} %collective-permute-done.8.refs_0_.refs_3_) | copy-start | bytes 786436
  31.2 0.7 copy-start.3
  31.9 0.7 copy-start.1
  34.7 24.7 %collective-permute-start.11 = (bf16[3,64,2048]{2,1,0:T(8,128)(2,1)}, bf16[3,64,2048]{2,1,0:T(8,128)(2,1)}, u32[]{:S(2)}, u32[]{:S(2)}) collective-permute-start(bf16[3,64,2048]{2,1,0:T(8,128)(2,1)} %get-tuple-element.119), channel_id=1, source_target_pairs={{0,4},{4,0},{8,12},{12,8},{16,20},{20,16},{24,28},{28,24},{1,5},{5... | collective-permute-start | bytes 2359304 | tf_op jit(solution)/shard_map/ppermute | solution.py:33
  36.4 14.5 %collective-permute-start.4 = (bf16[64,2048]{1,0:T(8,128)(2,1)}, bf16[64,2048]{1,0:T(8,128)(2,1)}, u32[]{:S(2)}, u32[]{:S(2)}) collective-permute-start(bf16[64,2048]{1,0:T(8,128)(2,1)} %bitcast.20), channel_id=1, source_target_pairs={{0,16},{4,20},{8,24},{12,28},{16,0},{20,4},{24,8},{28,12},{1,17},{... | collective-permute-start | bytes 786440 | tf_op jit(solution)/shard_map/ppermute | solution.py:33
  39.0 13.0 %collective-permute-start.2 = (bf16[64,2048]{1,0:T(8,128)(2,1)}, bf16[64,2048]{1,0:T(8,128)(2,1)}, u32[]{:S(2)}, u32[]{:S(2)}) collective-permute-start(bf16[64,2048]{1,0:T(8,128)(2,1)} %bitcast.21), channel_id=1, source_target_pairs={{0,8},{4,12},{8,0},{12,4},{16,24},{20,28},{24,16},{28,20},{1,9},{5... | collective-permute-start | bytes 786440 | tf_op jit(solution)/shard_map/ppermute | solution.py:33
  50.9 7.4 %collective-permute-start.6 = (bf16[64,2048]{1,0:T(8,128)(2,1)}, bf16[64,2048]{1,0:T(8,128)(2,1)}, u32[]{:S(2)}, u32[]{:S(2)}) collective-permute-start(bf16[64,2048]{1,0:T(8,128)(2,1)} %collective-permute-done.4.refs_10_.refs_5_), channel_id=1, source_target_pairs={{0,8},{4,12},{8,0},{12,4},{16,24},{20,28},{24,16},{28,20},{1,9},{5... | collective-permute-start | bytes 786440 | tf_op jit(solution)/shard_map/ppermute | solution.py:33
  51.4 16.5 %collective-permute-start.5 = (bf16[64,2048]{1,0:T(8,128)(2,1)}, bf16[64,2048]{1,0:T(8,128)(2,1)}, u32[]{:S(2)}, u32[]{:S(2)}) collective-permute-start(bf16[64,2048]{1,0:T(8,128)(2,1)} %collective-permute-done.4.refs_10_.refs_5_), channel_id=1, source_target_pairs={{0,4},{4,0},{8,12},{12,8},{16,20},{20,16},{24,28},{28,24},{1,5},{5... | collective-permute-start | bytes 786440 | tf_op jit(solution)/shard_map/ppermute | solution.py:33
  52.0 16.0 %collective-permute-start.3 = (bf16[64,2048]{1,0:T(8,128)(2,1)}, bf16[64,2048]{1,0:T(8,128)(2,1)}, u32[]{:S(2)}, u32[]{:S(2)}) collective-permute-start(bf16[64,2048]{1,0:T(8,128)(2,1)} %collective-permute-done.2.refs_9_.refs_3_), channel_id=1, source_target_pairs={{0,4},{4,0},{8,12},{12,8},{16,20},{20,16},{24,28},{28,24},{1,5},{5... | collective-permute-start | bytes 786440 | tf_op jit(solution)/shard_map/ppermute | solution.py:33
  58.3 12.7 %collective-permute-start.7 = (bf16[64,2048]{1,0:T(8,128)(2,1)}, bf16[64,2048]{1,0:T(8,128)(2,1)}, u32[]{:S(2)}, u32[]{:S(2)}) collective-permute-start(bf16[64,2048]{1,0:T(8,128)(2,1)} %collective-permute-done.6.refs_11_.refs_7_), channel_id=1, source_target_pairs={{0,4},{4,0},{8,12},{12,8},{16,20},{20,16},{24,28},{28,24},{1,5},{5... | collective-permute-start | bytes 786440 | tf_op jit(solution)/shard_map/ppermute | solution.py:33
  78.4 14.4 %collective-permute-start.12 = (bf16[256,1280]{1,0:T(8,128)(2,1)}, bf16[256,1280]{1,0:T(8,128)(2,1)}, u32[]{:S(2)}, u32[]{:S(2)}) collective-permute-start(bf16[256,1280]{1,0:T(8,128)(2,1)} %get-tuple-element.125), channel_id=1, source_target_pairs={{0,1},{1,0},{2,3},{3,2},{4,5},{5,4},{6,7},{7,6},{8,9},{9,8},{10,11... | collective-permute-start | bytes 1966088 | tf_op jit(solution)/shard_map/ppermute | solution.py:29
  78.4 2.8 collective-permute-start.13
  83.0 17.9 %collective-permute-start.15 = (bf16[256,512]{1,0:T(8,128)(2,1)}, bf16[256,512]{1,0:T(8,128)(2,1)}, u32[]{:S(2)}, u32[]{:S(2)}) collective-permute-start(bf16[256,512]{1,0:T(8,128)(2,1)} %get-tuple-element.134), channel_id=1, source_target_pairs={{0,2},{1,3},{2,0},{3,1},{4,6},{5,7},{6,4},{7,5},{8,10},{9,11},{10,... | collective-permute-start | bytes 786440 | tf_op jit(solution)/shard_map/ppermute | solution.py:29
  92.8 14.3 %collective-permute-start.17 = (bf16[256,1536]{1,0:T(8,128)(2,1)}, bf16[256,1536]{1,0:T(8,128)(2,1)}, u32[]{:S(2)}, u32[]{:S(2)}) collective-permute-start(bf16[256,1536]{1,0:T(8,128)(2,1)} %get-tuple-element.138), channel_id=1, source_target_pairs={{0,1},{1,0},{2,3},{3,2},{4,5},{5,4},{6,7},{7,6},{8,9},{9,8},{10,11... | collective-permute-start | bytes 2359304 | tf_op jit(solution)/shard_map/ppermute | solution.py:29
  95.1 17.4 %collective-permute-start.14 = (bf16[256,1280]{1,0:T(8,128)(2,1)}, bf16[256,1280]{1,0:T(8,128)(2,1)}, u32[]{:S(2)}, u32[]{:S(2)}) collective-permute-start(bf16[256,1280]{1,0:T(8,128)(2,1)} %get-tuple-element.133), channel_id=1, source_target_pairs={{0,2},{1,3},{2,0},{3,1},{4,6},{5,7},{6,4},{7,5},{8,10},{9,11},{10,... | collective-permute-start | bytes 1966088 | tf_op jit(solution)/shard_map/ppermute | solution.py:29
  106.9 4.0 %collective-permute-start.16 = (bf16[2,256,512]{2,1,0:T(8,128)(2,1)}, bf16[2,256,512]{2,1,0:T(8,128)(2,1)}, u32[]{:S(2)}, u32[]{:S(2)}) collective-permute-start(bf16[2,256,512]{2,1,0:T(8,128)(2,1)} %get-tuple-element.136), channel_id=1, source_target_pairs={{0,1},{1,0},{2,3},{3,2},{4,5},{5,4},{6,7},{7,6},{8,9},{9,8},{10,11... | collective-permute-start | bytes 1572872 | tf_op jit(solution)/shard_map/ppermute | solution.py:29
  109.5 20.1 %collective-permute-start.19 = (bf16[256,1536]{1,0:T(8,128)(2,1)}, bf16[256,1536]{1,0:T(8,128)(2,1)}, u32[]{:S(2)}, u32[]{:S(2)}) collective-permute-start(bf16[256,1536]{1,0:T(8,128)(2,1)} %get-tuple-element.143), channel_id=1, source_target_pairs={{0,2},{1,3},{2,0},{3,1},{4,6},{5,7},{6,4},{7,5},{8,10},{9,11},{10,... | collective-permute-start | bytes 2359304 | tf_op jit(solution)/shard_map/ppermute | solution.py:29
  123.0 16.8 %collective-permute-start.18 = (bf16[2,256,1280]{2,1,0:T(8,128)(2,1)}, bf16[2,256,1280]{2,1,0:T(8,128)(2,1)}, u32[]{:S(2)}, u32[]{:S(2)}) collective-permute-start(bf16[2,256,1280]{2,1,0:T(8,128)(2,1)} %get-tuple-element.142), channel_id=1, source_target_pairs={{0,1},{1,0},{2,3},{3,2},{4,5},{5,4},{6,7},{7,6},{8,9},{9,8},{10,11... | collective-permute-start | bytes 3932168 | tf_op jit(solution)/shard_map/ppermute | solution.py:29
  138.4 10.9 %collective-permute-start.22 = (bf16[2,256,1024]{2,1,0:T(8,128)(2,1)}, bf16[2,256,1024]{2,1,0:T(8,128)(2,1)}, u32[]{:S(2)}, u32[]{:S(2)}) collective-permute-start(bf16[2,256,1024]{2,1,0:T(8,128)(2,1)} %get-tuple-element.153), channel_id=1, source_target_pairs={{0,1},{1,0},{2,3},{3,2},{4,5},{5,4},{6,7},{7,6},{8,9},{9,8},{10,11... | collective-permute-start | bytes 3145736 | tf_op jit(solution)/shard_map/ppermute | solution.py:29
  138.4 15.1 %collective-permute-start.21 = (bf16[2,256,512]{2,1,0:T(8,128)(2,1)}, bf16[2,256,512]{2,1,0:T(8,128)(2,1)}, u32[]{:S(2)}, u32[]{:S(2)}) collective-permute-start(bf16[2,256,512]{2,1,0:T(8,128)(2,1)} %get-tuple-element.151), channel_id=1, source_target_pairs={{0,2},{1,3},{2,0},{3,1},{4,6},{5,7},{6,4},{7,5},{8,10},{9,11},{10,... | collective-permute-start | bytes 1572872 | tf_op jit(solution)/shard_map/ppermute | solution.py:29
  148.5 5.0 %collective-permute-start.20 = (bf16[2,256,512]{2,1,0:T(8,128)(2,1)}, bf16[2,256,512]{2,1,0:T(8,128)(2,1)}, u32[]{:S(2)}, u32[]{:S(2)}) collective-permute-start(bf16[2,256,512]{2,1,0:T(8,128)(2,1)} %get-tuple-element.150), channel_id=1, source_target_pairs={{0,1},{1,0},{2,3},{3,2},{4,5},{5,4},{6,7},{7,6},{8,9},{9,8},{10,11... | collective-permute-start | bytes 1572872 | tf_op jit(solution)/shard_map/ppermute | solution.py:29
  148.7 32.5 %collective-permute-start.25 = (bf16[2,256,1280]{2,1,0:T(8,128)(2,1)}, bf16[2,256,1280]{2,1,0:T(8,128)(2,1)}, u32[]{:S(2)}, u32[]{:S(2)}) collective-permute-start(bf16[2,256,1280]{2,1,0:T(8,128)(2,1)} %get-tuple-element.160), channel_id=1, source_target_pairs={{0,2},{1,3},{2,0},{3,1},{4,6},{5,7},{6,4},{7,5},{8,10},{9,11},{10,... | collective-permute-start | bytes 3932168 | tf_op jit(solution)/shard_map/ppermute | solution.py:29
  156.3 2.6 collective-permute-start.26
  187.4 4.3 %collective-permute-start.27 = (bf16[3,256,1280]{2,1,0:T(8,128)(2,1)}, bf16[3,256,1280]{2,1,0:T(8,128)(2,1)}, u32[]{:S(2)}, u32[]{:S(2)}) collective-permute-start(bf16[3,256,1280]{2,1,0:T(8,128)(2,1)} %get-tuple-element.165.refs_0_.refs_2_), channel_id=1, source_target_pairs={{0,1},{1,0},{2,3},{3,2},{4,5},{5,4},{6,7},{7,6},{8,9},{9,8},{10,11... | collective-permute-start | bytes 5898248 | tf_op jit(solution)/shard_map/ppermute | solution.py:29
  187.4 33.2 %collective-permute-start.24 = (bf16[2,256,1024]{2,1,0:T(8,128)(2,1)}, bf16[2,256,1024]{2,1,0:T(8,128)(2,1)}, u32[]{:S(2)}, u32[]{:S(2)}) collective-permute-start(bf16[2,256,1024]{2,1,0:T(8,128)(2,1)} %get-tuple-element.158), channel_id=1, source_target_pairs={{0,2},{1,3},{2,0},{3,1},{4,6},{5,7},{6,4},{7,5},{8,10},{9,11},{10,... | collective-permute-start | bytes 3145736 | tf_op jit(solution)/shard_map/ppermute | solution.py:29
  225.5 3.8 %collective-permute-start.28 = (bf16[3,256,1024]{2,1,0:T(8,128)(2,1)}, bf16[3,256,1024]{2,1,0:T(8,128)(2,1)}, u32[]{:S(2)}, u32[]{:S(2)}) collective-permute-start(bf16[3,256,1024]{2,1,0:T(8,128)(2,1)} %get-tuple-element.174.refs_0_.refs_2_), channel_id=1, source_target_pairs={{0,1},{1,0},{2,3},{3,2},{4,5},{5,4},{6,7},{7,6},{8,9},{9,8},{10,11... | collective-permute-start | bytes 4718600 | tf_op jit(solution)/shard_map/ppermute | solution.py:29
  225.6 17.5 %collective-permute-start.23 = (bf16[2,256,512]{2,1,0:T(8,128)(2,1)}, bf16[2,256,512]{2,1,0:T(8,128)(2,1)}, u32[]{:S(2)}, u32[]{:S(2)}) collective-permute-start(bf16[2,256,512]{2,1,0:T(8,128)(2,1)} %get-tuple-element.157), channel_id=1, source_target_pairs={{0,2},{1,3},{2,0},{3,1},{4,6},{5,7},{6,4},{7,5},{8,10},{9,11},{10,... | collective-permute-start | bytes 1572872 | tf_op jit(solution)/shard_map/ppermute | solution.py:29
  246.0 2.6 collective-permute-start.29
  256.2 26.3 %collective-permute-start.31 = (bf16[4,4,16,2048]{3,2,1,0:T(8,128)(2,1)}, bf16[4,4,16,2048]{3,2,1,0:T(8,128)(2,1)}, u32[]{:S(2)}, u32[]{:S(2)}) collective-permute-start(bf16[4,4,16,2048]{3,2,1,0:T(8,128)(2,1)} %get-tuple-element.190), channel_id=1, source_target_pairs={{0,4},{4,0},{8,12},{12,8},{16,20},{20,16},{24,28},{28,24},{1,5},{5... | collective-permute-start | bytes 3145736 | tf_op jit(solution)/shard_map/ppermute | solution.py:33
  261.7 38.1 %collective-permute-start.30 = (bf16[4,4,16,1024]{3,2,1,0:T(8,128)(2,1)}, bf16[4,4,16,1024]{3,2,1,0:T(8,128)(2,1)}, u32[]{:S(2)}, u32[]{:S(2)}) collective-permute-start(bf16[4,4,16,1024]{3,2,1,0:T(8,128)(2,1)} %get-tuple-element.185), channel_id=1, source_target_pairs={{0,4},{4,0},{8,12},{12,8},{16,20},{20,16},{24,28},{28,24},{1,5},{5... | collective-permute-start | bytes 1572872 | tf_op jit(solution)/shard_map/ppermute | solution.py:33
  285.6 17.0 %collective-permute-start.34 = (bf16[2,4,16,2048]{3,2,1,0:T(8,128)(2,1)}, bf16[2,4,16,2048]{3,2,1,0:T(8,128)(2,1)}, u32[]{:S(2)}, u32[]{:S(2)}) collective-permute-start(bf16[2,4,16,2048]{3,2,1,0:T(8,128)(2,1)} %get-tuple-element.200), channel_id=1, source_target_pairs={{0,8},{4,12},{8,0},{12,4},{16,24},{20,28},{24,16},{28,20},{1,9},{5... | collective-permute-start | bytes 1572872 | tf_op jit(solution)/shard_map/ppermute | solution.py:33
  287.3 20.1 %collective-permute-start.33 = (bf16[4,4,16,1024]{3,2,1,0:T(8,128)(2,1)}, bf16[4,4,16,1024]{3,2,1,0:T(8,128)(2,1)}, u32[]{:S(2)}, u32[]{:S(2)}) collective-permute-start(bf16[4,4,16,1024]{3,2,1,0:T(8,128)(2,1)} %get-tuple-element.198), channel_id=1, source_target_pairs={{0,4},{4,0},{8,12},{12,8},{16,20},{20,16},{24,28},{28,24},{1,5},{5... | collective-permute-start | bytes 1572872 | tf_op jit(solution)/shard_map/ppermute | solution.py:33
  302.1 12.9 %collective-permute-start.32 = (bf16[2,4,16,1024]{3,2,1,0:T(8,128)(2,1)}, bf16[2,4,16,1024]{3,2,1,0:T(8,128)(2,1)}, u32[]{:S(2)}, u32[]{:S(2)}) collective-permute-start(bf16[2,4,16,1024]{3,2,1,0:T(8,128)(2,1)} %get-tuple-element.196), channel_id=1, source_target_pairs={{0,8},{4,12},{8,0},{12,4},{16,24},{20,28},{24,16},{28,20},{1,9},{5... | collective-permute-start | bytes 786440 | tf_op jit(solution)/shard_map/ppermute | solution.py:33
  304.9 19.4 %collective-permute-start.37 = (bf16[1,4,16,2048]{3,2,1,0:T(8,128)(2,1)}, bf16[1,4,16,2048]{3,2,1,0:T(8,128)(2,1)}, u32[]{:S(2)}, u32[]{:S(2)}) collective-permute-start(bf16[1,4,16,2048]{3,2,1,0:T(8,128)(2,1)} %get-tuple-element.209), channel_id=1, source_target_pairs={{0,16},{4,20},{8,24},{12,28},{16,0},{20,4},{24,8},{28,12},{1,17},{... | collective-permute-start | bytes 786440 | tf_op jit(solution)/shard_map/ppermute | solution.py:33
  309.8 17.0 %collective-permute-start.36 = (bf16[2,4,16,1024]{3,2,1,0:T(8,128)(2,1)}, bf16[2,4,16,1024]{3,2,1,0:T(8,128)(2,1)}, u32[]{:S(2)}, u32[]{:S(2)}) collective-permute-start(bf16[2,4,16,1024]{3,2,1,0:T(8,128)(2,1)} %get-tuple-element.207), channel_id=1, source_target_pairs={{0,8},{4,12},{8,0},{12,4},{16,24},{20,28},{24,16},{28,20},{1,9},{5... | collective-permute-start | bytes 786440 | tf_op jit(solution)/shard_map/ppermute | solution.py:33
  316.9 23.5 %collective-permute-start.35 = (bf16[1,4,16,1024]{3,2,1,0:T(8,128)(2,1)}, bf16[1,4,16,1024]{3,2,1,0:T(8,128)(2,1)S(1)}, u32[]{:S(2)}, u32[]{:S(2)}) collective-permute-start(bf16[1,4,16,1024]{3,2,1,0:T(8,128)(2,1)} %get-tuple-element.205), channel_id=1, source_target_pairs={{0,16},{4,20},{8,24},{12,28},{16,0},{20,4},{24,8},{28,12},{1,17},{... | collective-permute-start | bytes 393224 | tf_op jit(solution)/shard_map/ppermute | solution.py:33
  328.6 11.8 %collective-permute-start.38 = (bf16[1,4,16,1024]{3,2,1,0:T(8,128)(2,1)}, bf16[1,4,16,1024]{3,2,1,0:T(8,128)(2,1)}, u32[]{:S(2)}, u32[]{:S(2)}) collective-permute-start(bf16[1,4,16,1024]{3,2,1,0:T(8,128)(2,1)} %get-tuple-element.217), channel_id=1, source_target_pairs={{0,16},{4,20},{8,24},{12,28},{16,0},{20,4},{24,8},{28,12},{1,17},{... | collective-permute-start | bytes 393224 | tf_op jit(solution)/shard_map/ppermute | solution.py:33
  331.5 1.9 collective-permute-start.39
  331.5 5.1 %collective-permute-start.40 = (bf16[16,2048]{1,0:T(8,128)(2,1)}, bf16[16,2048]{1,0:T(8,128)(2,1)}, u32[]{:S(2)}, u32[]{:S(2)}) collective-permute-start(bf16[16,2048]{1,0:T(8,128)(2,1)} %get-tuple-element.220), channel_id=1, source_target_pairs={{0,2},{1,3},{2,0},{3,1},{4,6},{5,7},{6,4},{7,5},{8,10},{9,11},{10,... | collective-permute-start | bytes 196616 | tf_op jit(solution)/shard_map/ppermute | solution.py:29
  332.8 4.7 %collective-permute-start.41 = (bf16[16,2048]{1,0:T(8,128)(2,1)}, bf16[16,2048]{1,0:T(8,128)(2,1)}, u32[]{:S(2)}, u32[]{:S(2)}) collective-permute-start(bf16[16,2048]{1,0:T(8,128)(2,1)} %get-tuple-element.221), channel_id=1, source_target_pairs={{0,3},{1,2},{2,1},{3,0},{4,7},{5,6},{6,5},{7,4},{8,11},{9,10},{10,... | collective-permute-start | bytes 196616 | tf_op jit(solution)/shard_map/ppermute | solution.py:29
  333.4 4.1 %copy-start.5 = (bf16[16,2048]{1,0:T(8,128)(2,1)}, bf16[16,2048]{1,0:T(8,128)(2,1)S(1)}, u32[]{:S(2)}) copy-start(bf16[16,2048]{1,0:T(8,128)(2,1)S(1)} %collective-permute-done.39.refs_2_) | copy-start | bytes 196612
  (1 other events, 0.7 us)
